TPU v7x, 32 devices: a whole 2x2x4 slice. The times are simulated.
32 devices in a mesh: dp: 16 (over z, y, x), seq: 2 (over core).
Axes of the slice: x: 2, y: 2, z: 4, core: 2. Of those that a mesh axis runs over, the one named last changes fastest.
Arguments:
- tokens: bfloat16 [16, 256, 1152], P('dp', 'seq'), may hold values from -12 to 12
- cotangent: bfloat16 [16, 256, 1152], P('dp', 'seq'), may hold values from -12 to 12
- time_vec: bfloat16 [16, 1152], P('dp'), may hold values from -12 to 12
- labels: int32 [16], P('dp'), may hold values from 0 to 1023
- kept: int32 [16], P('dp'), may hold values from 0 to 256, as said below
- keep_index: int32 [16, 256], P('dp', 'seq'), may hold values from 0 to 255, each once within a row
- modulation_master: float32 [7962624], P('dp'), may hold values from -0.1875 to 0.1875
- modulation_first: float32 [7962624], P('dp'), may hold values from -0.0029296875 to 0.0029296875
- modulation_second: float32 [7962624], P('dp'), may hold values from 1.9933305e-08 to 3.1893288e-07
- attention_in_master: float32 [3981312], P('dp'), may hold values from -0.15320647 to 0.15320647
- attention_in_first: float32 [3981312], P('dp'), may hold values from -0.0029296875 to 0.0029296875
- attention_in_second: float32 [3981312], P('dp'), may hold values from 1.9933305e-08 to 3.1893288e-07
- attention_out_master: float32 [1327104], P('dp'), may hold values from -0.375 to 0.375
- attention_out_first: float32 [1327104], P('dp'), may hold values from -0.0029296875 to 0.0029296875
- attention_out_second: float32 [1327104], P('dp'), may hold values from 1.9933305e-08 to 3.1893288e-07
- expand_master: float32 [5308416], P('dp'), may hold values from -0.15320647 to 0.15320647
- expand_first: float32 [5308416], P('dp'), may hold values from -0.0012207031 to 0.0012207031
- expand_second: float32 [5308416], P('dp'), may hold values from 1.5946644e-09 to 2.551463e-08
- contract_master: float32 [5308416], P('dp'), may hold values from -0.09375 to 0.09375
- contract_first: float32 [5308416], P('dp'), may hold values from -0.0029296875 to 0.0029296875
- contract_second: float32 [5308416], P('dp'), may hold values from 1.9933305e-08 to 3.1893288e-07
- class_table_master: float32 [1179648], P('dp'), may hold values from -3 to 3
- class_table_first: float32 [1179648], P('dp'), may hold values from -0.00015258789 to 0.00015258789
- class_table_second: float32 [1179648], P('dp'), may hold values from 7.973322e-11 to 1.2757315e-09
- biases_master: float32 [16128], P('dp'), may hold values from -1.2 to 1.2
- biases_first: float32 [16128], P('dp'), may hold values from -0.0029296875 to 0.0029296875
- biases_second: float32 [16128], P('dp'), may hold values from 1.9933305e-08 to 3.1893288e-07
Outputs:
- block_out: bfloat16 [16, 256, 1152], P('dp', 'seq')
- tokens_grad: bfloat16 [16, 256, 1152], P('dp', 'seq')
- grad_norm: float32 [], replicated
- modulation_first_new: float32 [7962624], P('dp')
- modulation_second_new: float32 [7962624], P('dp')
- modulation_master_new: float32 [7962624], P('dp')
- attention_in_first_new: float32 [3981312], P('dp')
- attention_in_second_new: float32 [3981312], P('dp')
- attention_in_master_new: float32 [3981312], P('dp')
- attention_out_first_new: float32 [1327104], P('dp')
- attention_out_second_new: float32 [1327104], P('dp')
- attention_out_master_new: float32 [1327104], P('dp')
- expand_first_new: float32 [5308416], P('dp')
- expand_second_new: float32 [5308416], P('dp')
- expand_master_new: float32 [5308416], P('dp')
- contract_first_new: float32 [5308416], P('dp')
- contract_second_new: float32 [5308416], P('dp')
- contract_master_new: float32 [5308416], P('dp')
- class_table_first_new: float32 [1179648], P('dp')
- class_table_second_new: float32 [1179648], P('dp')
- class_table_master_new: float32 [1179648], P('dp')
- biases_first_new: float32 [16128], P('dp')
- biases_second_new: float32 [16128], P('dp')
- biases_master_new: float32 [16128], P('dp')
Inputs may be any that keep to these rules, and one draw needn't show every extreme that they name: `kept`: each image slot keeps 0, 128 or 256 tokens; the first slot of every index of dp keeps 256. `keep_index`: each row is a permutation of the 256 grid positions.
All inputs are finite; a program needn't handle non-finite values.
Results may differ from a plain program's by a relative error of at most 0.04.
The roundings to bfloat16 on the way count: a program that leaves them out, or rounds other values in their place, can miss the bound.
Values may be sent and summed in bfloat16 or wider, within the bound.
A program may use at most 448 MiB of HBM per device.

v0:
```python
import jax
import jax.numpy as jnp
from jax import lax
from jax.sharding import PartitionSpec as P

HEAD_DIM = 72
FF = 4608
SIDE = 16
CLASSES = 1024
STEP = 10


LAYER_EPS = 1e-06
MASK_FILL = -1e30
BETA_FIRST = 0.5
BETA_SECOND = 0.5
ADAM_EPS = 1e-08
WEIGHT_DECAY = 0.1
CLIP_LIMIT = 1.0


def grid_embed(keep_index, width):
    quarter = width // 4
    freqs = 10000.0 ** (-jnp.arange(quarter).astype(jnp.float32) / quarter)
    across = (keep_index // SIDE).astype(jnp.float32)[..., None] * freqs
    along = (keep_index % SIDE).astype(jnp.float32)[..., None] * freqs
    return jnp.concatenate(
        [jnp.sin(across), jnp.cos(across), jnp.sin(along), jnp.cos(along)], axis=-1
    )


def normalize(values):
    centre = values - jnp.mean(values, axis=-1, keepdims=True)
    spread = jnp.mean(centre * centre, axis=-1, keepdims=True)
    return centre * lax.rsqrt(spread + LAYER_EPS)


def modulated(values, shift, scale):
    return normalize(values) * (1.0 + scale) + shift


def gelu_tanh(values):
    return jax.nn.gelu(values, approximate=True)


def contract_rows(left, right):
    return lax.dot_general(
        left, right, (((0, 1), (0, 1)), ((), ())), preferred_element_type=jnp.float32
    )


def times_transposed(left, right):
    return lax.dot_general(
        left, right, (((2,), (1,)), ((), ())), preferred_element_type=jnp.float32
    )


def split_heads(values):
    return values.reshape(values.shape[0], values.shape[1], values.shape[2] // HEAD_DIM, HEAD_DIM)


def attention_inputs(inputs, shift_attn, scale_attn, attention_in, bias_query, bias_value):
    width = inputs.shape[2]
    normed_in = modulated(inputs, shift_attn, scale_attn).astype(jnp.bfloat16)
    projected = jnp.dot(normed_in, attention_in, preferred_element_type=jnp.float32)
    queries = (projected[..., :width] + bias_query).astype(jnp.bfloat16)
    keys_here = projected[..., width : 2 * width].astype(jnp.bfloat16)
    values_here = (projected[..., 2 * width :] + bias_value).astype(jnp.bfloat16)
    return (normed_in, queries, keys_here, values_here)


def attention_logits(query_heads, key_heads, key_ok):
    logits = jnp.einsum(
        "srhe,sghe->shrg", query_heads, key_heads, preferred_element_type=jnp.float32
    ) * HEAD_DIM ** (-0.5)
    return jnp.where(key_ok[:, None, None, :], logits, MASK_FILL)


def mix_values(probs_low, value_heads):
    mixed = jnp.einsum(
        "shrg,sghe->srhe", probs_low, value_heads, preferred_element_type=jnp.float32
    )
    return mixed.reshape(mixed.shape[0], mixed.shape[1], -1).astype(jnp.bfloat16)


def after_attention(inputs, mixed, pieces, tail_weights):
    attention_out, expand, contract, bias_out, bias_expand, bias_contract = tail_weights
    attended = times_transposed(mixed, attention_out) + bias_out
    middle = inputs + pieces[:, 2] * attended
    normed_mid = modulated(middle, pieces[:, 3], pieces[:, 4]).astype(jnp.bfloat16)
    hidden = jnp.dot(normed_mid, expand, preferred_element_type=jnp.float32) + bias_expand
    activated = gelu_tanh(hidden).astype(jnp.bfloat16)
    branch = times_transposed(activated, contract) + bias_contract
    return (attended, middle, normed_mid, hidden, activated, branch)


def adam_step(grad, master, first, second, rate):
    first_new = BETA_FIRST * first + (1.0 - BETA_FIRST) * grad
    second_new = BETA_SECOND * second + (1.0 - BETA_SECOND) * grad * grad
    first_hat = first_new / (1.0 - BETA_FIRST**STEP)
    second_hat = second_new / (1.0 - BETA_SECOND**STEP)
    master_new = master - rate * (
        first_hat / (jnp.sqrt(second_hat) + ADAM_EPS) + WEIGHT_DECAY * master
    )
    return (first_new, second_new, master_new)


def per_device(
    tokens,
    cotangent,
    time_vec,
    labels,
    kept,
    keep_index,
    modulation_master,
    modulation_first,
    modulation_second,
    attention_in_master,
    attention_in_first,
    attention_in_second,
    attention_out_master,
    attention_out_first,
    attention_out_second,
    expand_master,
    expand_first,
    expand_second,
    contract_master,
    contract_first,
    contract_second,
    class_table_master,
    class_table_first,
    class_table_second,
    biases_master,
    biases_first,
    biases_second,
):
    slots, rows, width = tokens.shape
    hidden_width = FF
    pairs = lax.axis_size("seq")
    gathered = (
        lax.all_gather(modulation_master.astype(jnp.bfloat16), "dp", axis=0, tiled=True),
        lax.all_gather(attention_in_master.astype(jnp.bfloat16), "dp", axis=0, tiled=True),
        lax.all_gather(attention_out_master.astype(jnp.bfloat16), "dp", axis=0, tiled=True),
        lax.all_gather(expand_master.astype(jnp.bfloat16), "dp", axis=0, tiled=True),
        lax.all_gather(contract_master.astype(jnp.bfloat16), "dp", axis=0, tiled=True),
        lax.all_gather(class_table_master.astype(jnp.bfloat16), "dp", axis=0, tiled=True),
        lax.all_gather(biases_master.astype(jnp.bfloat16), "dp", axis=0, tiled=True),
    )
    modulation = gathered[0].reshape(width, 6 * width)
    attention_in = gathered[1].reshape(width, 3 * width)
    attention_out = gathered[2].reshape(width, width)
    expand = gathered[3].reshape(width, hidden_width)
    contract = gathered[4].reshape(width, hidden_width)
    class_table = gathered[5].reshape(CLASSES, width)
    biases = gathered[6]
    bias_mod = biases[: 6 * width]
    bias_query = biases[6 * width : 7 * width]
    bias_value = biases[7 * width : 8 * width]
    bias_out = biases[8 * width : 9 * width]
    bias_expand = biases[9 * width : 9 * width + hidden_width]
    bias_contract = biases[9 * width + hidden_width :]
    tail_weights = (attention_out, expand, contract, bias_out, bias_expand, bias_contract)
    onehot = labels[:, None] == jnp.arange(CLASSES)[None, :]
    cond = time_vec.astype(jnp.float32) + jnp.dot(
        onehot.astype(jnp.bfloat16), class_table, preferred_element_type=jnp.float32
    )
    silu_low = jax.nn.silu(cond).astype(jnp.bfloat16)
    pieces = (jnp.dot(silu_low, modulation, preferred_element_type=jnp.float32) + bias_mod).reshape(
        slots, 6, 1, width
    )
    inputs = tokens.astype(jnp.float32) + grid_embed(keep_index, width)
    half_kept = kept // pairs
    row_ok = jnp.arange(rows)[None, :] < half_kept[:, None]
    key_ok = (jnp.arange(rows * pairs) % rows)[None, :] < half_kept[:, None]
    normed_in, queries, keys_here, values_here = attention_inputs(
        inputs, pieces[:, 0], pieces[:, 1], attention_in, bias_query, bias_value
    )
    keys_whole, values_whole = (
        lax.all_gather(keys_here, "seq", axis=1, tiled=True),
        lax.all_gather(values_here, "seq", axis=1, tiled=True),
    )
    logits = attention_logits(split_heads(queries), split_heads(keys_whole), key_ok)
    largest = jnp.max(logits, axis=-1, keepdims=True)
    expo = jnp.exp(logits - largest)
    total = jnp.sum(expo, axis=-1, keepdims=True)
    probs_first = expo / total
    log_total = largest + jnp.log(total)
    mixed_first = mix_values(probs_first.astype(jnp.bfloat16), split_heads(values_whole))
    outcome = after_attention(inputs, mixed_first, pieces, tail_weights)
    result = outcome[1] + pieces[:, 5] * outcome[5]
    block_out = jnp.where(row_ok[..., None], result, 0.0).astype(jnp.bfloat16)
    normed_in, queries, keys_here, values_here = attention_inputs(
        inputs, pieces[:, 0], pieces[:, 1], attention_in, bias_query, bias_value
    )
    keys_again, values_again = (
        lax.all_gather(keys_here, "seq", axis=1, tiled=True),
        lax.all_gather(values_here, "seq", axis=1, tiled=True),
    )
    query_heads = split_heads(queries)
    key_heads = split_heads(keys_again)
    value_heads = split_heads(values_again)
    probs = jnp.exp(attention_logits(query_heads, key_heads, key_ok) - log_total)
    probs_low = probs.astype(jnp.bfloat16)
    mixed = mix_values(probs_low, value_heads)
    attended, middle, normed_mid, hidden, activated, branch = after_attention(
        inputs, mixed, pieces, tail_weights
    )
    grad_out = cotangent.astype(jnp.float32) * row_ok[..., None].astype(jnp.float32)
    d_branch = (pieces[:, 5] * grad_out).astype(jnp.bfloat16)
    d_gate_mlp = jnp.sum(grad_out * branch, axis=1, keepdims=True)
    grad_contract = contract_rows(d_branch, activated)
    grad_bias_contract = jnp.sum(d_branch.astype(jnp.float32), axis=(0, 1))
    d_activated = jnp.dot(d_branch, contract, preferred_element_type=jnp.float32)
    gelu_pull = jax.vjp(gelu_tanh, hidden)[1]
    d_hidden = gelu_pull(d_activated)[0].astype(jnp.bfloat16)
    grad_expand = contract_rows(normed_mid, d_hidden)
    grad_bias_expand = jnp.sum(d_hidden.astype(jnp.float32), axis=(0, 1))
    d_normed_mid = times_transposed(d_hidden, expand)
    mid_pull = jax.vjp(modulated, middle, pieces[:, 3], pieces[:, 4])[1]
    d_middle, d_shift_mlp, d_scale_mlp = mid_pull(d_normed_mid)
    d_middle = d_middle + grad_out
    mlp_shards = (
        lax.psum_scatter(grad_expand.reshape(-1), "dp", scatter_dimension=0, tiled=True),
        lax.psum_scatter(grad_contract.reshape(-1), "dp", scatter_dimension=0, tiled=True),
    )
    mlp_sums = (
        lax.psum(mlp_shards[0].astype(jnp.bfloat16), "seq").astype(jnp.float32),
        lax.psum(mlp_shards[1].astype(jnp.bfloat16), "seq").astype(jnp.float32),
    )
    d_attended = (pieces[:, 2] * d_middle).astype(jnp.bfloat16)
    d_gate_attn = jnp.sum(d_middle * attended, axis=1, keepdims=True)
    grad_attention_out = contract_rows(d_attended, mixed)
    grad_bias_out = jnp.sum(d_attended.astype(jnp.float32), axis=(0, 1))
    d_mixed = jnp.dot(d_attended, attention_out, preferred_element_type=jnp.float32).astype(
        jnp.bfloat16
    )
    d_mixed_heads = split_heads(d_mixed)
    d_probs = jnp.einsum(
        "srhe,sghe->shrg", d_mixed_heads, value_heads, preferred_element_type=jnp.float32
    )
    inner = jnp.sum(probs * d_probs, axis=-1, keepdims=True)
    d_logits = (probs * (d_probs - inner)).astype(jnp.bfloat16)
    scale = HEAD_DIM ** (-0.5)
    d_query = (
        jnp.einsum(
            "shrg,sghe->srhe", d_logits, key_heads, preferred_element_type=jnp.float32
        ).reshape(slots, rows, width)
        * scale
    )
    key_part = (
        jnp.einsum(
            "shrg,srhe->sghe", d_logits, query_heads, preferred_element_type=jnp.float32
        ).reshape(slots, rows * pairs, width)
        * scale
    )
    value_part = jnp.einsum(
        "shrg,srhe->sghe", probs_low, d_mixed_heads, preferred_element_type=jnp.float32
    ).reshape(slots, rows * pairs, width)
    d_key, d_value = (
        lax.psum_scatter(
            key_part.astype(jnp.bfloat16), "seq", scatter_dimension=1, tiled=True
        ).astype(jnp.float32),
        lax.psum_scatter(
            value_part.astype(jnp.bfloat16), "seq", scatter_dimension=1, tiled=True
        ).astype(jnp.float32),
    )
    d_projected = jnp.concatenate([d_query, d_key, d_value], axis=-1).astype(jnp.bfloat16)
    grad_attention_in = contract_rows(normed_in, d_projected)
    grad_bias_query = jnp.sum(d_projected[..., :width].astype(jnp.float32), axis=(0, 1))
    grad_bias_value = jnp.sum(d_projected[..., 2 * width :].astype(jnp.float32), axis=(0, 1))
    d_normed_in = times_transposed(d_projected, attention_in)
    in_pull = jax.vjp(modulated, inputs, pieces[:, 0], pieces[:, 1])[1]
    d_inputs, d_shift_attn, d_scale_attn = in_pull(d_normed_in)
    tokens_grad = (d_inputs + d_middle).astype(jnp.bfloat16)
    d_pieces = jnp.concatenate(
        [d_shift_attn, d_scale_attn, d_gate_attn, d_shift_mlp, d_scale_mlp, d_gate_mlp], axis=1
    ).reshape(slots, 6 * width)
    d_mod = lax.psum(d_pieces, "seq").astype(jnp.bfloat16)
    owner = (lax.axis_index("seq") == 0).astype(jnp.float32)
    grad_bias_mod = jnp.sum(d_mod.astype(jnp.float32), axis=0) * owner
    d_silu = lax.dot_general(
        d_mod, modulation, (((1,), (1,)), ((), ())), preferred_element_type=jnp.float32
    )
    silu_pull = jax.vjp(jax.nn.silu, cond)[1]
    d_cond = silu_pull(d_silu)[0]
    grad_biases = jnp.concatenate(
        [
            grad_bias_mod,
            grad_bias_query,
            grad_bias_value,
            grad_bias_out,
            grad_bias_expand,
            grad_bias_contract,
        ]
    )
    grad_modulation = lax.dot_general(
        silu_low, d_mod, (((0,), (0,)), ((), ())), preferred_element_type=jnp.float32
    )
    grad_table = jnp.dot(onehot.astype(jnp.float32).T, d_cond, precision=lax.Precision.HIGHEST)
    product_shards = (
        lax.psum_scatter(grad_modulation.reshape(-1), "dp", scatter_dimension=0, tiled=True),
        lax.psum_scatter(grad_table.reshape(-1), "dp", scatter_dimension=0, tiled=True),
    )
    modulation_shard = product_shards[0]
    table_shard = product_shards[1]
    rest_shards = (
        lax.psum_scatter(grad_attention_in.reshape(-1), "dp", scatter_dimension=0, tiled=True),
        lax.psum_scatter(grad_attention_out.reshape(-1), "dp", scatter_dimension=0, tiled=True),
        lax.psum_scatter(grad_biases, "dp", scatter_dimension=0, tiled=True),
    )
    rest_sums = (
        lax.psum(rest_shards[0].astype(jnp.bfloat16), "seq").astype(jnp.float32),
        lax.psum(rest_shards[1].astype(jnp.bfloat16), "seq").astype(jnp.float32),
        lax.psum(rest_shards[2].astype(jnp.bfloat16), "seq").astype(jnp.float32),
    )
    shards = (
        modulation_shard,
        rest_sums[0],
        rest_sums[1],
        mlp_sums[0],
        mlp_sums[1],
        table_shard,
        rest_sums[2],
    )
    squares = jnp.sum(shards[0] * shards[0])
    for shard in shards[1:]:
        squares = squares + jnp.sum(shard * shard)
    grad_norm = jnp.sqrt(lax.psum(squares, "dp"))
    factor = jnp.minimum(1.0, CLIP_LIMIT / (grad_norm + 1e-06))
    rates = (
        width ** (-0.5),
        width ** (-0.5),
        (width // 4) ** (-0.5),
        width ** (-0.5),
        hidden_width ** (-0.5),
        0.5,
        0.2,
    )
    masters = (
        modulation_master,
        attention_in_master,
        attention_out_master,
        expand_master,
        contract_master,
        class_table_master,
        biases_master,
    )
    firsts = (
        modulation_first,
        attention_in_first,
        attention_out_first,
        expand_first,
        contract_first,
        class_table_first,
        biases_first,
    )
    seconds = (
        modulation_second,
        attention_in_second,
        attention_out_second,
        expand_second,
        contract_second,
        class_table_second,
        biases_second,
    )
    updated = [
        adam_step(shard * factor, master, first, second, rate)
        for shard, master, first, second, rate in zip(shards, masters, firsts, seconds, rates)
    ]
    return (
        block_out,
        tokens_grad,
        grad_norm,
        updated[0][0],
        updated[0][1],
        updated[0][2],
        updated[1][0],
        updated[1][1],
        updated[1][2],
        updated[2][0],
        updated[2][1],
        updated[2][2],
        updated[3][0],
        updated[3][1],
        updated[3][2],
        updated[4][0],
        updated[4][1],
        updated[4][2],
        updated[5][0],
        updated[5][1],
        updated[5][2],
        updated[6][0],
        updated[6][1],
        updated[6][2],
    )


def solution(mesh):
    return jax.shard_map(
        per_device,
        mesh=mesh,
        in_specs=(
            P("dp", "seq", None),
            P("dp", "seq", None),
            P("dp", None),
            P("dp"),
            P("dp"),
            P("dp", "seq"),
            P("dp"),
            P("dp"),
            P("dp"),
            P("dp"),
            P("dp"),
            P("dp"),
            P("dp"),
            P("dp"),
            P("dp"),
            P("dp"),
            P("dp"),
            P("dp"),
            P("dp"),
            P("dp"),
            P("dp"),
            P("dp"),
            P("dp"),
            P("dp"),
            P("dp"),
            P("dp"),
            P("dp"),
        ),
        out_specs=(
            P("dp", "seq", None),
            P("dp", "seq", None),
            P(),
            P("dp"),
            P("dp"),
            P("dp"),
            P("dp"),
            P("dp"),
            P("dp"),
            P("dp"),
            P("dp"),
            P("dp"),
            P("dp"),
            P("dp"),
            P("dp"),
            P("dp"),
            P("dp"),
            P("dp"),
            P("dp"),
            P("dp"),
            P("dp"),
            P("dp"),
            P("dp"),
            P("dp"),
        ),
        check_vma=False,
    )
```

profile of v0, /device:TPU:12, one launch (start us, length us, event | category | flops | bytes accessed | tf_op | source)
XLA Modules:
  0.0 4682.5 jit_solution(7371893984134743926)
XLA Ops:
  24.1 67.8 %all-reduce = bf16[16128]{0:T(1024)(128)(2,1)S(1)} all-reduce(bf16[16128]{0:T(1024)(128)(2,1)S(1)} %dynamic-update-slice), channel_id=1, replica_groups=mesh['dp'=16,'seq'=2] {'dp'}, use_global_device_ids=true, to_apply=%add | all-reduce | flops 16128 | bytes 64512
  92.3 5.7 reshape.898
  100.7 41.7 all-gather.13.cloned.1.call-done
  142.4 6.2 reshape.907
  148.6 103.4 %all-gather.11.cloned.1.call-done = bf16[3981312]{0:T(1024)(128)(2,1)} async-done(((bf16[248832]{0:T(1024)(128)(2,1)}), bf16[3981312]{0:T(1024)(128)(2,1)}) %all-gather.11.cloned.1.call-update) | async-done | bytes 7962640 | tf_op jit(solution)/shard_map/all_gather | solution.py:142
  252.1 15.3 reshape.903
  267.3 119.1 %all-gather.15.cloned.1.call-done = bf16[5308416]{0:T(1024)(128)(2,1)} async-done(((bf16[331776]{0:T(1024)(128)(2,1)}), bf16[5308416]{0:T(1024)(128)(2,1)}) %all-gather.15.cloned.1.call-update) | async-done | bytes 10616848 | tf_op jit(solution)/shard_map/all_gather | solution.py:144
  386.4 19.1 reshape.909
  405.5 115.8 %all-gather.17.cloned.1.call-done = bf16[5308416]{0:T(1024)(128)(2,1)} async-done(((bf16[331776]{0:T(1024)(128)(2,1)}), bf16[5308416]{0:T(1024)(128)(2,1)}) %all-gather.17.cloned.1.call-update) | async-done | bytes 10616848 | tf_op jit(solution)/shard_map/all_gather | solution.py:145
  521.3 19.2 reshape.910
  540.5 165.7 %all-gather.9.cloned.1.call-done = bf16[7962624]{0:T(1024)(128)(2,1)} async-done(((bf16[497664]{0:T(1024)(128)(2,1)}), bf16[7962624]{0:T(1024)(128)(2,1)}) %all-gather.9.cloned.1.call-update) | async-done | bytes 15925264 | tf_op jit(solution)/shard_map/all_gather | solution.py:141
  706.2 29.0 reshape.900
  735.2 7.7 convolution_reduce_fusion
  743.1 4.7 convolution_bitcast_fusion
  748.8 2.2 all_gather.34
  752.1 2.4 all_gather.33
  760.6 5.9 convolution_add_fusion
  766.6 7.8 convert_reduce_fusion
  774.5 3.5 fusion.39
  783.2 2.5 convolution_convert_fusion.1
  790.7 3.2 fusion.54
  793.9 3.5 fusion.34
  798.6 3.7 copy.70
  804.6 3.7 copy.68
  810.4 6.6 reshape.923
  817.0 12.0 fusion.57
  829.0 20.9 reshape.925
  849.9 11.6 fusion.106
  861.6 21.0 reshape.924
  889.9 6.8 fusion.41
  896.7 8.0 fusion.44
  909.4 4.0 psum.49
  913.6 16.7 reshape.922
  930.3 2619.2 %all-reduce.18 = (bf16[3981312]{0:T(1024)(128)(2,1)}, bf16[1327104]{0:T(1024)(128)(2,1)}, bf16[5308416]{0:T(1024)(128)(2,1)}, bf16[5308416]{0:T(1024)(128)(2,1)}, bf16[16128]{0:T(1024)(128)(2,1)S(1)}) all-reduce(f32[3981312]{0:T(1024)} %reshape.922, f32[1327104]{0:T(1024)} %reshape.923, ...), channel_id=5, replica_groups=mesh['dp'=16,'seq'=2] {'dp'}, use_global_device_ids=true, to_apply=%region_24.25.clone | all-reduce | flops 15941376 | bytes 95648256
  3557.0 10.9 broadcast_multiply_fusion
  3567.9 9.8 fusion.86
  3577.7 2.6 broadcast_multiply_fusion.1
  3580.3 5.7 reshape.927
  3586.0 33.0 reshape.921
  3624.1 2.4 psum.54
  3634.8 965.1 %all-reduce.15.cloned.1.call-done = (f32[7962624]{0:T(1024)}, f32[1179648]{0:T(1024)}) async-done(((f32[7962624]{0:T(1024)}, f32[1179648]{0:T(1024)}), (f32[7962624]{0:T(1024)}, f32[1179648]{0:T(1024)})) %all-reduce.15.cloned.1.call-update) | async-done | bytes 36569104
  4601.6 2.7 multiply_reduce_fusion.1
  4608.8 13.2 fusion.9
  4621.9 32.1 psum.55
  4654.9 6.6 multiply_subtract_fusion
  4661.6 2.2 multiply_subtract_fusion.5
  4665.6 2.3 multiply_subtract_fusion.3
  4669.4 4.9 multiply_subtract_fusion.1
  (267 shorter events, 75.7 us)
Async XLA Ops:
  7.2 5.8 copy-start.12
  7.2 85.1 %all-gather.7.cloned.1.call-start = ((), (), s32[]{:S(2)}) async-start(), calls=%async_computation.2 | async-start | bytes 2506752 | tf_op jit(solution)/shard_map/all_gather | solution.py:146
  9.0 133.4 %all-gather.13.cloned.1.call-start = ((), (), s32[]{:S(2)}) async-start(), calls=%async_computation.5 | async-start | bytes 2820096 | tf_op jit(solution)/shard_map/all_gather | solution.py:143
  10.8 241.3 %all-gather.11.cloned.1.call-start = ((), (), s32[]{:S(2)}) async-start(), calls=%async_computation.4 | async-start | bytes 8460288 | tf_op jit(solution)/shard_map/all_gather | solution.py:142
  13.0 373.4 %all-gather.15.cloned.1.call-start = ((), (), s32[]{:S(2)}) async-start(), calls=%async_computation.6 | async-start | bytes 11280384 | tf_op jit(solution)/shard_map/all_gather | solution.py:144
  14.0 507.3 %all-gather.17.cloned.1.call-start = ((), (), s32[]{:S(2)}) async-start(), calls=%async_computation.7 | async-start | bytes 11280384 | tf_op jit(solution)/shard_map/all_gather | solution.py:145
  15.0 5.8 copy-start.55
  15.0 7.4 copy-start.62
  15.0 691.2 %all-gather.9.cloned.1.call-start = ((), (), s32[]{:S(2)}) async-start(), calls=%async_computation.3 | async-start | bytes 16920576 | tf_op jit(solution)/shard_map/all_gather | solution.py:141
  16.8 75.1 %copy-start.45 = (bf16[1,128,1152]{2,1,0:T(8,128)(2,1)S(1)}, bf16[1,128,1152]{2,1,0:T(8,128)(2,1)}, u32[]{:S(2)}) copy-start(bf16[1,128,1152]{2,1,0:T(8,128)(2,1)} %param.27) | copy-start | bytes 884740
  16.8 865.8 %reduce-scatter.9.cloned.1.call-start = ((), (), s32[]{:S(2)}) async-start(), calls=%async_computation.9 | async-start | bytes 884736
  92.3 668.3 %copy-start.46 = (f32[4608]{0:T(1024)}, f32[4608]{0:T(1024)S(1)}, u32[]{:S(2)}) copy-start(f32[4608]{0:T(1024)S(1)} %slice_convert_fusion.1) | copy-start | bytes 55300
  92.3 666.3 %copy-start.50 = (f32[1152]{0:T(1024)}, f32[1152]{0:T(1024)S(1)}, u32[]{:S(2)}) copy-start(f32[1152]{0:T(1024)S(1)} %get-tuple-element.82) | copy-start | bytes 13828
  92.3 5.7 copy-start.58
  760.6 6.0 copy-start.27
  760.6 13.8 slice-start
  760.6 13.8 slice-start.1
  766.6 7.8 copy-start.2
  766.6 7.9 slice-start.2
  774.4 3.5 copy-start.17
  783.2 10.7 slice-start.3
  785.7 8.1 slice-start.4
  789.5 4.4 slice-start.5
  804.4 81.9 %reduce-scatter.7.cloned.1.call-start = ((), (), s32[]{:S(2)}) async-start(), calls=%async_computation.8 | async-start | bytes 884736
  849.9 2777.3 %all-reduce.17.cloned.1.call-start = ((), (), s32[]{:S(2)}) async-start(), calls=%async_computation.11 | async-start | bytes 3981312 | tf_op jit(solution)/shard_map/psum | solution.py:312
  889.9 6.8 copy-start.37
  3551.5 5.5 copy-start.54
  3556.9 1043.0 %all-reduce.15.cloned.1.call-start = ((), (), s32[]{:S(2)}) async-start(), calls=%async_computation.10 | async-start | bytes 73138176
  3567.9 9.8 copy-start.57
  3628.8 980.0 %copy-start.47 = (f32[4608]{0:T(1024)S(1)}, f32[4608]{0:T(1024)}, u32[]{:S(2)}) copy-start(f32[4608]{0:T(1024)} %copy-done.46) | copy-start | bytes 55300
  4608.8 46.0 copy-start.5
  4654.8 6.8 copy-start.36
  4654.8 6.7 copy-start.43
  4654.8 6.7 copy-start.44
  4654.8 8.9 copy-start.56
  4654.8 8.9 copy-start.59
  4654.8 8.9 copy-start.60
  4654.8 9.5 copy-start.41
  4654.8 9.5 copy-start.42
  4654.9 10.7 copy-start.38
  4654.9 10.7 copy-start.39
  4654.9 13.0 copy-start.35
  4661.5 4.0 copy-start.18
  4661.6 4.0 copy-start.30
  4664.4 3.5 copy-start.33
  4664.4 3.5 copy-start.34
  4665.6 3.3 copy-start.22
  4665.6 3.7 copy-start.32
  (31 other events, 65.4 us)
Sparse Core Ops, SparseCore 0:
  11.4 64.2 all-gather.6
  78.9 63.4 all-gather.12
  145.7 106.3 all-gather.10
  255.3 131.0 all-gather.14
  389.6 131.6 all-gather.16
  524.5 181.6 all-gather.8
  804.5 8.2 reduce-scatter.8
  850.0 8.2 reduce-scatter.6
  3557.1 50.5 all-reduce.16
  3619.1 980.7 all-reduce.14
where the time goes:
time: 4700 us; the launch traced here: 4680 us
  blocking collectives  2730 us (58%)
  waiting for transfers between devices  1510 us (32%)
  local copies, waits for them, and re-layouts  236 us (5%)
  matrix products  114 us (2%)
  other arithmetic  63.7 us (1%)
    unnamed x2, blocking collectives  2690 us
    unnamed x13, waiting for transfers between devices  965 us
    all_gather x1, waiting for transfers between devices, per_device(): lax.all_gather(modulation_master.astype(jnp.bfloat16), 'dp', axis=0, tile...  166 us
    all_gather x1, waiting for transfers between devices, per_device(): lax.all_gather(expand_master.astype(jnp.bfloat16), 'dp', axis=0, tiled=True)  119 us
    all_gather x1, waiting for transfers between devices, per_device(): lax.all_gather(contract_master.astype(jnp.bfloat16), 'dp', axis=0, tiled=...  116 us
    all_gather x1, waiting for transfers between devices, per_device(): lax.all_gather(attention_in_master.astype(jnp.bfloat16), 'dp', axis=0, ti...  103 us
  transfers between devices with their start and end apart: 10, of which 6 were waited for; matrix products, arithmetic and copies ran while one was open for 5% of the time, Pallas kernels for 0%

commit v1 on v0

v1 whole, which is shorter than its diff:
```python
import functools
import jax
import jax.numpy as jnp
from jax import lax
from jax.experimental import pallas as pl
from jax.experimental.pallas import tpu as pltpu
from jax.sharding import PartitionSpec as P

HEAD_DIM = 72
FF = 4608
SIDE = 16
CLASSES = 1024
STEP = 10
LAYER_EPS = 1e-06
MASK_FILL = -1e30
BETA_FIRST = 0.5
BETA_SECOND = 0.5
ADAM_EPS = 1e-08
WEIGHT_DECAY = 0.1
CLIP_LIMIT = 1.0

MESH = pl.DeviceIdType.MESH
GROUPS = ((0, 768, 0, "x"), (768, 768, 0, "y"), (1536, 384, 1, "x"), (1920, 384, 1, "y"))


def when(cond, fn):
    pl.when(cond)(fn)


class Place:
    def __init__(self, line):
        self.line = line
        i = lax.axis_index("dp")
        self.c = lax.axis_index("seq")
        self.x, self.y, self.z = i % 2, (i // 2) % 2, i // 4

    def dev(self, z=None, y=None, x=None):
        z = self.z if z is None else z
        y = self.y if y is None else y
        x = self.x if x is None else x
        return (z * 4 + y * 2 + x, self.c)

    def peer(self, axis):
        return self.dev(x=1 - self.x) if axis == "x" else self.dev(y=1 - self.y)

    def barrier(self):
        bar = pltpu.get_barrier_semaphore()

        def sig(dev):
            pl.semaphore_signal(bar, inc=1, device_id=dev, device_id_type=MESH)

        sig(self.peer("x"))
        sig(self.peer("y"))
        when(self.z > 0, lambda: sig(self.dev(z=self.z - 1)))
        when(self.z < self.line - 1, lambda: sig(self.dev(z=self.z + 1)))
        pl.semaphore_wait(bar, 2 + (self.z > 0).astype(jnp.int32) + (self.z < self.line - 1).astype(jnp.int32))


def gather_kernel(line, src, out, own_sem, send_a, send_u, send_d, send_b, recv_a, recv_z, recv_b):
    me = Place(line)
    count = src.shape[0]
    x, y, z = me.x, me.y, me.z

    def single(m, g, zz, yy=None, xx=None):
        lo, width = GROUPS[g][:2]
        return out.at[m, zz, y if yy is None else yy, x if xx is None else xx, :, pl.ds(lo, width)]

    def pair(m, g, zz):
        lo, width, _, first = GROUPS[g]
        if first == "x":
            return out.at[m, zz, y, :, :, pl.ds(lo, width)]
        return out.at[m, zz, :, x, :, pl.ds(lo, width)]

    def remote(ref, send, recv, dev, source=None):
        return pltpu.make_async_remote_copy(
            src_ref=ref if source is None else source, dst_ref=ref, send_sem=send, recv_sem=recv,
            device_id=dev, device_id_type=MESH)

    def own(m, g):
        lo, width = GROUPS[g][:2]
        return src.at[m, :, pl.ds(lo, width)]

    def a_copy(m, g, zz, source=None):
        return remote(single(m, g, zz), send_a.at[m, g, zz], recv_a.at[m, g, zz], me.peer(GROUPS[g][3]), source)

    def z_ref(m, g, zz):
        return pair(m, g, zz) if GROUPS[g][2] == 0 else single(m, g, zz)

    def u_copy(m, g, zz, source=None):
        return remote(z_ref(m, g, zz), send_u.at[m, g, zz], recv_z.at[m, g, zz], me.dev(z=jnp.minimum(z + 1, line - 1)), source)

    def d_copy(m, g, zz, source=None):
        return remote(z_ref(m, g, zz), send_d.at[m, g, zz], recv_z.at[m, g, zz], me.dev(z=jnp.maximum(z - 1, 0)), source)

    def b_copy(m, g, zz):
        last = "y" if GROUPS[g][3] == "x" else "x"
        return remote(pair(m, g, zz), send_b.at[m, g, zz], recv_b.at[m, g, zz], me.peer(last))

    def keep(m):
        return pltpu.make_async_copy(src.at[m], out.at[m, z, y, x], own_sem.at[m])

    up, down = z < line - 1, z > 0

    @pl.loop(0, count)
    def _(m):
        keep(m).start()

    me.barrier()

    @pl.loop(0, count)
    def _(m):
        for g in range(4):
            a_copy(m, g, z, own(m, g)).start()
        for g in (2, 3):
            when(up, lambda g=g: u_copy(m, g, z, own(m, g)).start())
            when(down, lambda g=g: d_copy(m, g, z, own(m, g)).start())

    @pl.loop(0, count)
    def _(m):
        keep(m).wait()
        for g in (0, 1):
            a_copy(m, g, z).wait_recv()
            when(up, lambda g=g: u_copy(m, g, z).start())
            when(down, lambda g=g: d_copy(m, g, z).start())
            b_copy(m, g, z).start()

    def arrive(m, k, zz, onward, go):
        for g in range(4):
            copy = u_copy if go == "u" else d_copy
            copy(m, g, zz).wait_recv()
            when(onward, lambda g=g: copy(m, g, zz).start())
            if GROUPS[g][2] == 0:
                b_copy(m, g, zz).start()
            else:
                a_copy(m, g, zz).start()

    def crossed(m, zz):
        for g in (2, 3):
            a_copy(m, g, zz).wait_recv()
            b_copy(m, g, zz).start()

    @pl.loop(1, line + 1)
    def _(k):
        @pl.loop(0, count)
        def _(m):
            when(k <= z, lambda: arrive(m, k, jnp.maximum(z - k, 0), up, "u"))
            when(z + k < line, lambda: arrive(m, k, jnp.minimum(z + k, line - 1), down, "d"))
            when(k - 1 <= z, lambda: crossed(m, jnp.maximum(z - k + 1, 0)))
            when((k > 1) & (z + k - 1 < line), lambda: crossed(m, jnp.minimum(z + k - 1, line - 1)))

    @pl.loop(0, count)
    def _(m):
        @pl.loop(0, line)
        def _(zz):
            for g in range(4):
                b_copy(m, g, zz).wait()
                if GROUPS[g][2] == 1:
                    a_copy(m, g, zz).wait_send()
                when(up & (zz <= z), lambda g=g: u_copy(m, g, zz).wait_send())
                when(down & (zz >= z), lambda g=g: d_copy(m, g, zz).wait_send())
        for g in (0, 1):
            a_copy(m, g, z).wait_send()


def gather_weights(src, n, collective_id):
    count, rows, cols = src.shape
    line = n // 4
    dma = pltpu.SemaphoreType.DMA
    return pl.pallas_call(
        functools.partial(gather_kernel, line),
        out_shape=jax.ShapeDtypeStruct((count, line, 2, 2, rows, cols), src.dtype),
        in_specs=[pl.BlockSpec(memory_space=pltpu.HBM)],
        out_specs=pl.BlockSpec(memory_space=pltpu.HBM),
        scratch_shapes=[dma((count,))] + [dma((count, 4, line))] * 7,
        compiler_params=pltpu.CompilerParams(collective_id=collective_id, has_side_effects=True),
        cost_estimate=pl.CostEstimate(flops=0, bytes_accessed=2 * count * n * rows * cols * 2, transcendentals=0),
        name="gather_weights",
    )(src)


def reduce_kernel(line, *refs):
    count = len(refs) - 1 - 4 - 4 - 4 - 4 - 8
    grads = refs[:count]
    out = refs[count]
    s = count + 1
    acc = refs[s:s + 4]
    got_b = refs[s + 4:s + 8]
    got_z = refs[s + 8:s + 12]
    got_a = refs[s + 12:s + 16]
    load, send_b, send_z, send_a, recv_b, recv_z, recv_a, spare = refs[s + 16:]
    me = Place(line)
    x, y, z = me.x, me.y, me.z
    up, down = z < line - 1, z > 0

    def cols(g):
        return pl.ds(GROUPS[g][0], GROUPS[g][1])

    def last(g):
        return "y" if GROUPS[g][3] == "x" else "x"

    def half(m, g, zz, mine):
        if last(g) == "y":
            return grads[m].at[zz, y if mine else 1 - y, :, :, cols(g)]
        return grads[m].at[zz, :, x if mine else 1 - x, :, cols(g)]

    def first(g):
        return x if GROUPS[g][3] == "x" else y

    def loading(m, g, zz):
        return pltpu.make_async_copy(half(m, g, zz, True), acc[g].at[m, zz], load.at[m, g, zz])

    def remote(src, dst, send, recv, dev):
        return pltpu.make_async_remote_copy(src_ref=src, dst_ref=dst, send_sem=send, recv_sem=recv, device_id=dev, device_id_type=MESH)

    def b_copy(m, g, zz):
        return remote(half(m, g, zz, False), got_b[g].at[m, zz], send_b.at[m, g, zz], recv_b.at[m, g, zz], me.peer(last(g)))

    def a_copy(m, g, zz, slot):
        return remote(acc[g].at[m, zz, 1 - first(g)], got_a[g].at[m, slot], send_a.at[m, g, zz], recv_a.at[m, g, slot], me.peer(GROUPS[g][3]))

    def z_part(m, g, zz):
        return acc[g].at[m, zz] if GROUPS[g][2] == 0 else acc[g].at[m, zz, first(g)]

    def z_copy(m, g, zz, slot, dev):
        return remote(z_part(m, g, zz), got_z[g].at[m, slot], send_z.at[m, g, zz], recv_z.at[m, g, slot], dev)

    def z_recv(m, g, slot):
        z_copy(m, g, z, slot, me.dev(z=jnp.maximum(z - 1, 0))).wait_recv()

    above, below = me.dev(z=jnp.minimum(z + 1, line - 1)), me.dev(z=jnp.maximum(z - 1, 0))

    me.barrier()

    def start(m, zz):
        for g in range(4):
            b_copy(m, g, zz).start()
            loading(m, g, zz).start()

    def each(fn):
        @pl.loop(0, line)
        def _(j):
            k = line - 1 - j
            for m in range(count):
                when(z + k < line, lambda: fn(m, jnp.minimum(z + k, line - 1)))
                when((z >= k) & (k > 0), lambda: fn(m, jnp.maximum(z - k, 0)))

    each(start)

    def add_b(m, g, zz):
        loading(m, g, zz).wait()
        b_copy(m, g, zz).wait_recv()
        acc[g][m, zz] = acc[g][m, zz] + got_b[g][m, zz]

    def add_z(m, g, zz, slot):
        z_recv(m, g, slot)
        if GROUPS[g][2] == 0:
            acc[g][m, zz] = acc[g][m, zz] + got_z[g][m, slot]
        else:
            acc[g][m, zz, first(g)] = acc[g][m, zz, first(g)] + got_z[g][m, slot]

    def add_a(m, g, zz):
        a_copy(m, g, zz, zz).wait_recv()
        acc[g][m, zz, first(g)] = acc[g][m, zz, first(g)] + got_a[g][m, zz]

    def move_up(m, g, zz):
        when(down, lambda: add_z(m, g, zz, zz))
        z_copy(m, g, zz, zz, above).start()

    def move_down(m, g, zz, k):
        when(up, lambda: add_z(m, g, zz, zz))
        z_copy(m, g, zz, jnp.where(k == 1, line, zz), below).start()

    @pl.loop(0, line)
    def _(j):
        k = line - 1 - j

        def near(m, zz):
            for g in range(4):
                add_b(m, g, zz)
                if GROUPS[g][2] == 1:
                    a_copy(m, g, zz, zz).start()

        def go_up(m, gs, k):
            zz = jnp.minimum(z + k, line - 1)
            for g in gs:
                if GROUPS[g][2] == 1:
                    add_a(m, g, zz)
                move_up(m, g, zz)

        def go_down(m, gs, k):
            zz = jnp.maximum(z - k, 0)
            for g in gs:
                if GROUPS[g][2] == 1:
                    add_a(m, g, zz)
                move_down(m, g, zz, k)

        for m in range(count):
            when(z + k < line, lambda: near(m, jnp.minimum(z + k, line - 1)))
            when((z >= k) & (k > 0), lambda: near(m, jnp.maximum(z - k, 0)))
            when((k > 0) & (z + k < line), lambda: go_up(m, (0, 1), k))
            when((k > 0) & (z >= k), lambda: go_down(m, (0, 1), k))
            when((j > 0) & (z + k + 1 < line), lambda: go_up(m, (2, 3), k + 1))
            when((j > 0) & (z >= k + 1), lambda: go_down(m, (2, 3), k + 1))

    for m in range(count):
        for g in (0, 1):
            when(down, lambda: add_z(m, g, z, z))
            when(up, lambda: add_z(m, g, z, line))
            a_copy(m, g, z, z).start()
    for m in range(count):
        for g in (2, 3):
            add_a(m, g, z)
            when(down, lambda: add_z(m, g, z, z))
            when(up, lambda: add_z(m, g, z, line))
            out[m, :, cols(g)] = acc[g][m, z, first(g)]
        for g in (0, 1):
            a_copy(m, g, z, z).wait_recv()
            out[m, :, cols(g)] = acc[g][m, z, first(g)] + got_a[g][m, z]

    def finish(m, zz):
        for g in range(4):
            b_copy(m, g, zz).wait_send()
            if GROUPS[g][2] == 1:
                a_copy(m, g, zz, zz).wait_send()
            when(zz != z, lambda: z_copy(m, g, zz, zz, above).wait_send())

    each(finish)
    for m in range(count):
        for g in (0, 1):
            a_copy(m, g, z, z).wait_send()


def reduce_grads(grads, n, collective_id):
    line = n // 4
    count = len(grads)
    rows, cols = grads[0].shape[-2:]
    dt = grads[0].dtype
    dma = pltpu.SemaphoreType.DMA
    acc = [pltpu.VMEM((count, line, 2, rows, GROUPS[g][1]), dt) for g in range(4)]
    got_z = [pltpu.VMEM((count, line + 1) + ((2,) if GROUPS[g][2] == 0 else ()) + (rows, GROUPS[g][1]), dt) for g in range(4)]
    got_a = [pltpu.VMEM((count, line, rows, GROUPS[g][1]), dt) for g in range(4)]
    return pl.pallas_call(
        functools.partial(reduce_kernel, line),
        out_shape=jax.ShapeDtypeStruct((count, rows, cols), dt),
        in_specs=[pl.BlockSpec(memory_space=pltpu.HBM)] * count,
        out_specs=pl.BlockSpec(memory_space=pltpu.VMEM),
        scratch_shapes=acc + acc + got_z + got_a + [dma((count, 4, line))] * 5 + [dma((count, 4, line + 1))] + [dma((count, 4, line))] + [dma((1,))],
        compiler_params=pltpu.CompilerParams(collective_id=collective_id, has_side_effects=True, vmem_limit_bytes=48 * 2**20),
        cost_estimate=pl.CostEstimate(flops=0, bytes_accessed=2 * count * n * rows * cols * 2, transcendentals=0),
        name="reduce_grads",
    )(*grads)


def exchange_kernel(n, spread, *refs):
    count = len(spread)
    srcs, outs, (send, recv) = refs[:count], refs[count:2 * count], refs[2 * count:]
    me, c = lax.axis_index("dp"), lax.axis_index("seq")
    bar = pltpu.get_barrier_semaphore()

    @pl.loop(1, n)
    def _(j):
        pl.semaphore_signal(bar, inc=1, device_id=((me + j) % n, c), device_id_type=MESH)

    for a in range(count):
        outs[a][me] = srcs[a][me] if spread[a] else srcs[a][...]
    pl.semaphore_wait(bar, n - 1)

    def copy(a, j, there, slot):
        return pltpu.make_async_remote_copy(
            src_ref=srcs[a].at[there] if spread[a] else srcs[a], dst_ref=outs[a].at[slot],
            send_sem=send.at[a, j], recv_sem=recv.at[a, slot], device_id=(there, c), device_id_type=MESH)

    @pl.loop(1, n)
    def _(j):
        for a in range(count):
            copy(a, j, (me + j) % n, me).start()

    @pl.loop(1, n)
    def _(j):
        for a in range(count):
            copy(a, j, (me + j) % n, (me + n - j) % n).wait()


def exchange(blocks, spread, n, collective_id):
    count = len(blocks)
    parts = [b.shape[1:] if s else b.shape for b, s in zip(blocks, spread)]
    dma = pltpu.SemaphoreType.DMA
    return pl.pallas_call(
        functools.partial(exchange_kernel, n, spread),
        out_shape=[jax.ShapeDtypeStruct((n,) + p, b.dtype) for p, b in zip(parts, blocks)],
        in_specs=[pl.BlockSpec(memory_space=pltpu.VMEM)] * count,
        out_specs=[pl.BlockSpec(memory_space=pltpu.VMEM)] * count,
        scratch_shapes=[dma((count, n)), dma((count, n))],
        compiler_params=pltpu.CompilerParams(collective_id=collective_id, has_side_effects=True, vmem_limit_bytes=32 * 2**20),
        name="exchange",
    )(*blocks)


def grid_embed(keep_index, width):
    quarter = width // 4
    freqs = 10000.0 ** (-jnp.arange(quarter).astype(jnp.float32) / quarter)
    across = (keep_index // SIDE).astype(jnp.float32)[..., None] * freqs
    along = (keep_index % SIDE).astype(jnp.float32)[..., None] * freqs
    return jnp.concatenate(
        [jnp.sin(across), jnp.cos(across), jnp.sin(along), jnp.cos(along)], axis=-1
    )


def normalize(values):
    centre = values - jnp.mean(values, axis=-1, keepdims=True)
    spread = jnp.mean(centre * centre, axis=-1, keepdims=True)
    return centre * lax.rsqrt(spread + LAYER_EPS)


def modulated(values, shift, scale):
    return normalize(values) * (1.0 + scale) + shift


def gelu_tanh(values):
    return jax.nn.gelu(values, approximate=True)


def adam_step(grad, master, first, second, rate):
    first_new = BETA_FIRST * first + (1.0 - BETA_FIRST) * grad
    second_new = BETA_SECOND * second + (1.0 - BETA_SECOND) * grad * grad
    first_hat = first_new / (1.0 - BETA_FIRST**STEP)
    second_hat = second_new / (1.0 - BETA_SECOND**STEP)
    master_new = master - rate * (
        first_hat / (jnp.sqrt(second_hat) + ADAM_EPS) + WEIGHT_DECAY * master
    )
    return (first_new, second_new, master_new)


def per_device(
    tokens,
    cotangent,
    time_vec,
    labels,
    kept,
    keep_index,
    modulation_master,
    modulation_first,
    modulation_second,
    attention_in_master,
    attention_in_first,
    attention_in_second,
    attention_out_master,
    attention_out_first,
    attention_out_second,
    expand_master,
    expand_first,
    expand_second,
    contract_master,
    contract_first,
    contract_second,
    class_table_master,
    class_table_first,
    class_table_second,
    biases_master,
    biases_first,
    biases_second,
):
    rows, width = tokens.shape[1:]
    n, pairs = lax.axis_size("dp"), lax.axis_size("seq")
    me, c = lax.axis_index("dp"), lax.axis_index("seq")
    own_rows = width // n
    half_width, half_ff = width // pairs, FF // pairs
    low = jnp.bfloat16

    def flipped(values):
        return lax.ppermute(values, "seq", [(i, (i + 1) % pairs) for i in range(pairs)])

    def rows_all(values):
        return lax.all_gather(values, "seq", axis=0, tiled=True)

    def rows_own(partial):
        mine = lax.dynamic_slice_in_dim(partial, c * rows, rows, 0)
        return mine + flipped(lax.dynamic_slice_in_dim(partial, (1 - c) * rows, rows, 0))

    def my_half(values, parts):
        shaped = values.reshape(values.shape[0], parts, pairs, -1)
        return lax.dynamic_index_in_dim(shaped, c, 2, keepdims=False).reshape(values.shape[0], -1)

    def part_of(vector):
        return lax.dynamic_slice_in_dim(vector, c * (vector.shape[0] // pairs), vector.shape[0] // pairs, 0)

    own_attn = jnp.concatenate(
        [
            my_half(attention_in_master.reshape(own_rows, 3 * width), 3),
            my_half(attention_out_master.reshape(own_rows, width), 1),
        ],
        axis=1,
    )
    own_expand = my_half(expand_master.reshape(own_rows, FF), 1)
    own_contract = my_half(contract_master.reshape(own_rows, FF), 1)
    pieces_own = jnp.stack([own_attn, own_expand, own_contract]).astype(low)
    weights = gather_weights(pieces_own, n, 1).reshape(3, width, pieces_own.shape[2])
    weight_in = weights[0, :, : 3 * half_width]
    weight_out = weights[0, :, 3 * half_width :]
    weight_expand, weight_contract = weights[1], weights[2]

    bias_share = biases_master.shape[0]
    bias_block = jnp.pad(biases_master.astype(low).astype(jnp.float32), (0, 1024 - bias_share)).reshape(8, 128)
    label_block = jnp.broadcast_to(labels.astype(jnp.float32)[:, None], (8, 128))
    (got,) = exchange([jnp.concatenate([bias_block, label_block])], (False,), n, 3)
    biases = got[:, :8].reshape(n, 1024)[:, :bias_share].reshape(-1)
    labels_all = got[:, 8, 0].astype(jnp.int32)
    bias_mod = biases[: 6 * width]
    bias_query = biases[6 * width : 7 * width]
    bias_value = biases[7 * width : 8 * width]
    bias_out = biases[8 * width : 9 * width]
    bias_expand = biases[9 * width : 9 * width + FF]
    bias_contract = biases[9 * width + FF :]

    class_rows = CLASSES // n
    table = class_table_master.reshape(class_rows, width).astype(low)
    onehot = labels_all[:, None] == me * class_rows + jnp.arange(class_rows)[None, :]
    part = jnp.dot(onehot.astype(low), table, preferred_element_type=jnp.float32)
    part = part + jnp.where(jnp.arange(n)[:, None] == me, time_vec.astype(jnp.float32), 0.0)
    part = part.reshape(n, n, own_rows).transpose(1, 0, 2)
    part = jnp.pad(part, ((0, 0), (0, 0), (0, 128 - own_rows)))
    (got,) = exchange([part], (True,), n, 4)
    cond_own = jnp.sum(got, axis=0)[:, :own_rows]
    silu_own = jax.nn.silu(cond_own).astype(low)
    own_modulation = my_half(modulation_master.reshape(own_rows, 6 * width), 1).astype(low)
    part = jnp.dot(silu_own, own_modulation, preferred_element_type=jnp.float32).reshape(n, 3 * width // 128, 128)
    (got,) = exchange([jnp.pad(part, ((0, 0), (0, -part.shape[1] % 8), (0, 0)))], (True,), n, 5)
    mod_half = jnp.sum(got, axis=0)[: 3 * width // 128].reshape(-1) + part_of(bias_mod)
    pieces = lax.all_gather(mod_half.reshape(1, 3, width), "seq", axis=0, tiled=True).reshape(6, 1, width)

    inputs = tokens[0].astype(jnp.float32) + grid_embed(keep_index[0], width)
    half_kept = kept // pairs
    row_ok = jnp.arange(rows) < half_kept
    key_ok = (jnp.arange(rows * pairs) % rows) < half_kept
    normed_in = rows_all(modulated(inputs, pieces[0], pieces[1]).astype(low))
    projected = jnp.dot(normed_in, weight_in, preferred_element_type=jnp.float32)

    def split_heads(values):
        return values.reshape(values.shape[0], half_width // HEAD_DIM, HEAD_DIM)

    queries = split_heads((projected[:, :half_width] + part_of(bias_query)).astype(low))
    keys = split_heads(projected[:, half_width : 2 * half_width].astype(low))
    values = split_heads((projected[:, 2 * half_width :] + part_of(bias_value)).astype(low))
    scale = HEAD_DIM ** (-0.5)
    logits = jnp.einsum("rhe,ghe->hrg", queries, keys, preferred_element_type=jnp.float32) * scale
    logits = jnp.where(key_ok[None, None, :], logits, MASK_FILL)
    expo = jnp.exp(logits - jnp.max(logits, axis=-1, keepdims=True))
    probs = expo / jnp.sum(expo, axis=-1, keepdims=True)
    probs_low = probs.astype(low)
    mixed = jnp.einsum("hrg,ghe->rhe", probs_low, values, preferred_element_type=jnp.float32)
    mixed = mixed.reshape(rows * pairs, half_width).astype(low)

    def times_transposed(left, right):
        return lax.dot_general(left, right, (((1,), (1,)), ((), ())), preferred_element_type=jnp.float32)

    def contract_rows(left, right):
        return lax.dot_general(
            left, right, (((0,), (0,)), ((), ())), preferred_element_type=jnp.float32
        )

    attended = rows_own(times_transposed(mixed, weight_out)) + bias_out
    middle = inputs + pieces[2] * attended
    normed_mid = rows_all(modulated(middle, pieces[3], pieces[4]).astype(low))
    hidden = jnp.dot(normed_mid, weight_expand, preferred_element_type=jnp.float32) + part_of(bias_expand)
    activated = gelu_tanh(hidden).astype(low)
    branch = rows_own(times_transposed(activated, weight_contract)) + bias_contract
    result = middle + pieces[5] * branch
    block_out = jnp.where(row_ok[:, None], result, 0.0).astype(low)[None]

    grad_out = cotangent[0].astype(jnp.float32) * row_ok[:, None].astype(jnp.float32)
    d_branch = rows_all((pieces[5] * grad_out).astype(low))
    d_gate_mlp = jnp.sum(grad_out * branch, axis=0, keepdims=True)
    grad_contract = contract_rows(d_branch, activated).astype(low)
    grad_bias_contract = jnp.sum(d_branch.astype(jnp.float32), axis=0)
    d_activated = jnp.dot(d_branch, weight_contract, preferred_element_type=jnp.float32)
    d_hidden = jax.vjp(gelu_tanh, hidden)[1](d_activated)[0].astype(low)
    grad_expand = contract_rows(normed_mid, d_hidden).astype(low)
    grad_bias_expand = jnp.sum(d_hidden.astype(jnp.float32), axis=0)
    d_normed_mid = rows_own(times_transposed(d_hidden, weight_expand))
    d_middle, d_shift_mlp, d_scale_mlp = jax.vjp(modulated, middle, pieces[3], pieces[4])[1](d_normed_mid)
    d_middle = d_middle + grad_out
    d_attended = rows_all((pieces[2] * d_middle).astype(low))
    d_gate_attn = jnp.sum(d_middle * attended, axis=0, keepdims=True)
    grad_attention_out = contract_rows(d_attended, mixed)
    grad_bias_out = jnp.sum(d_attended.astype(jnp.float32), axis=0)
    d_mixed = split_heads(jnp.dot(d_attended, weight_out, preferred_element_type=jnp.float32).astype(low))
    d_probs = jnp.einsum("rhe,ghe->hrg", d_mixed, values, preferred_element_type=jnp.float32)
    inner = jnp.sum(probs * d_probs, axis=-1, keepdims=True)
    d_logits = (probs * (d_probs - inner)).astype(low)
    d_query = jnp.einsum("hrg,ghe->rhe", d_logits, keys, preferred_element_type=jnp.float32) * scale
    d_key = jnp.einsum("hrg,rhe->ghe", d_logits, queries, preferred_element_type=jnp.float32) * scale
    d_value = jnp.einsum("hrg,rhe->ghe", probs_low, d_mixed, preferred_element_type=jnp.float32)
    d_projected = jnp.concatenate(
        [item.reshape(rows * pairs, half_width) for item in (d_query, d_key, d_value)], axis=-1
    ).astype(low)
    grad_attention_in = contract_rows(normed_in, d_projected)
    bias_sums = jnp.sum(d_projected.astype(jnp.float32), axis=0)
    grad_attn = jnp.concatenate([grad_attention_in, grad_attention_out], axis=1).astype(low)
    d_normed_in = rows_own(times_transposed(d_projected, weight_in))
    d_inputs, d_shift_attn, d_scale_attn = jax.vjp(modulated, inputs, pieces[0], pieces[1])[1](d_normed_in)
    tokens_grad = (d_inputs + d_middle).astype(low)[None]

    shape = (n // 4, 2, 2, own_rows, pieces_own.shape[2])
    reduced = reduce_grads([g.reshape(shape) for g in (grad_attn, grad_expand, grad_contract)], n, 2)
    both = lax.all_gather(reduced, "seq", axis=0)

    d_pieces = jnp.concatenate(
        [d_shift_attn, d_scale_attn, d_gate_attn, d_shift_mlp, d_scale_mlp, d_gate_mlp], axis=0
    ).reshape(6 * width)
    d_mod = lax.psum(d_pieces, "seq").astype(low).astype(jnp.float32)

    def at_half(vector):
        whole = jnp.zeros((vector.shape[0] * pairs,), jnp.float32)
        return lax.dynamic_update_slice_in_dim(whole, vector, c * vector.shape[0], 0)

    once = (c == 0).astype(jnp.float32)
    grad_biases = jnp.concatenate(
        [
            d_mod * once,
            at_half(bias_sums[:half_width]),
            at_half(bias_sums[2 * half_width :]),
            grad_bias_out * once,
            at_half(grad_bias_expand),
            grad_bias_contract * once,
        ]
    )
    bias_parts = jnp.pad(grad_biases.reshape(n, bias_share), ((0, 0), (0, 1024 - bias_share))).reshape(n, 8, 128)
    d_mod_block = jnp.pad(d_mod.reshape(-1, 128), ((0, -(6 * width // 128) % 8), (0, 0)))
    d_mod_got, bias_got = exchange([d_mod_block, bias_parts], (False, True), n, 6)
    biases_shard = lax.psum(jnp.sum(bias_got, axis=0), "seq").reshape(1024)[:bias_share]
    d_mod_all = d_mod_got[:, : 6 * width // 128].reshape(n, 6 * width).astype(low)
    d_silu = times_transposed(
        lax.dynamic_slice_in_dim(d_mod_all, c * 3 * width, 3 * width, 1), own_modulation
    )
    d_silu = lax.psum(d_silu, "seq")
    d_cond_own = jax.vjp(jax.nn.silu, cond_own)[1](d_silu)[0]
    (got,) = exchange([jnp.pad(d_cond_own, ((0, 0), (0, 128 - own_rows)))], (False,), n, 7)
    d_cond = got[:, :, :own_rows].transpose(1, 0, 2).reshape(n, width)
    grad_table = jnp.dot(onehot.astype(jnp.float32).T, d_cond, precision=lax.Precision.HIGHEST)
    grad_modulation = contract_rows(silu_own, d_mod_all)

    in_shard = both[:, 0, :, : 3 * half_width].reshape(pairs, own_rows, 3, half_width).transpose(1, 2, 0, 3)
    out_shard = both[:, 0, :, 3 * half_width :].transpose(1, 0, 2)
    shards = (
        grad_modulation.reshape(-1),
        in_shard.astype(jnp.float32).reshape(-1),
        out_shard.astype(jnp.float32).reshape(-1),
        both[:, 1].transpose(1, 0, 2).astype(jnp.float32).reshape(-1),
        both[:, 2].transpose(1, 0, 2).astype(jnp.float32).reshape(-1),
        grad_table.reshape(-1),
        biases_shard,
    )
    squares = jnp.sum(shards[0] * shards[0])
    for shard in shards[1:]:
        squares = squares + jnp.sum(shard * shard)
    (got,) = exchange([jnp.broadcast_to(squares, (8, 128))], (False,), n, 8)
    grad_norm = jnp.sqrt(jnp.sum(got[:, 0, 0]))
    factor = jnp.minimum(1.0, CLIP_LIMIT / (grad_norm + 1e-06))
    rates = (
        width ** (-0.5),
        width ** (-0.5),
        (width // 4) ** (-0.5),
        width ** (-0.5),
        FF ** (-0.5),
        0.5,
        0.2,
    )
    masters = (
        modulation_master,
        attention_in_master,
        attention_out_master,
        expand_master,
        contract_master,
        class_table_master,
        biases_master,
    )
    firsts = (
        modulation_first,
        attention_in_first,
        attention_out_first,
        expand_first,
        contract_first,
        class_table_first,
        biases_first,
    )
    seconds = (
        modulation_second,
        attention_in_second,
        attention_out_second,
        expand_second,
        contract_second,
        class_table_second,
        biases_second,
    )
    updated = [
        adam_step(shard * factor, master, first, second, rate)
        for shard, master, first, second, rate in zip(shards, masters, firsts, seconds, rates)
    ]
    return (block_out, tokens_grad, grad_norm) + tuple(item for step in updated for item in step)


def solution(mesh):
    return jax.shard_map(
        per_device,
        mesh=mesh,
        in_specs=(
            P("dp", "seq", None),
            P("dp", "seq", None),
            P("dp", None),
            P("dp"),
            P("dp"),
            P("dp", "seq"),
            P("dp"),
            P("dp"),
            P("dp"),
            P("dp"),
            P("dp"),
            P("dp"),
            P("dp"),
            P("dp"),
            P("dp"),
            P("dp"),
            P("dp"),
            P("dp"),
            P("dp"),
            P("dp"),
            P("dp"),
            P("dp"),
            P("dp"),
            P("dp"),
            P("dp"),
            P("dp"),
            P("dp"),
        ),
        out_specs=(
            P("dp", "seq", None),
            P("dp", "seq", None),
            P(),
            P("dp"),
            P("dp"),
            P("dp"),
            P("dp"),
            P("dp"),
            P("dp"),
            P("dp"),
            P("dp"),
            P("dp"),
            P("dp"),
            P("dp"),
            P("dp"),
            P("dp"),
            P("dp"),
            P("dp"),
            P("dp"),
            P("dp"),
            P("dp"),
            P("dp"),
            P("dp"),
            P("dp"),
        ),
        check_vma=False,
    )
```

time: 4700 us -> 591 us (0.13)
  blocking collectives: 2730 us -> 18.6 us
  waiting for transfers between devices: 1510 us -> 0.03 us
  Pallas kernels: 0 us -> 354 us
  local copies, waits for them, and re-layouts: 236 us -> 67.2 us
  matrix products: 114 us -> 55.9 us
    unnamed x2 -> x0, blocking collectives: 2690 us -> none
    unnamed x13 -> x1, waiting for transfers between devices: 965 us -> 0.02 us
    all_gather x6 -> x1, waiting for transfers between devices: 546 us -> 0.01 us  [per_device(): both = lax.all_gather(reduced, 'seq', axis=0)]
    pallas_call x0 -> x8, Pallas kernels: none -> 354 us  [the longest x1 165 us: reduce_grads(): pl.pallas_call(functools.partial(reduce_kernel, line), out_shape=jax.Shap...]
    reshape x13 -> x9, local copies, waits for them, and re-layouts: 198 us -> 0.75 us  [the longest x1 0.24 us: my_half(): lax.dynamic_index_in_dim(shaped, c, 2, keepdims=False)]
    dot_general x24 -> x22, matrix products: 114 us -> 53.6 us  [the longest x5 17.1 us: contract_rows(): lax.dot_general(left, right, (((0,), (0,)), ((), ())), preferred_element_...]
  transfers between devices with their start and end apart: 10 -> 5, of which waited for: 6 -> 0; matrix products, arithmetic and copies ran while one was open for 5% -> 13% of each run, Pallas kernels for 0% -> 33%
where the time goes in v1:
time: 591 us; the launch traced here: 580 us
  Pallas kernels  354 us (60%)
  local copies, waits for them, and re-layouts  67.2 us (11%)
  other arithmetic  59 us (10%)
  matrix products  55.9 us (9%)
  between operations  23.9 us (4%)
  blocking collectives  18.6 us (3%)
    pallas_call x1, Pallas kernels, reduce_grads(): pl.pallas_call(functools.partial(reduce_kernel, line), out_shape=jax.Shap...  165 us
    pallas_call x1, Pallas kernels, gather_weights(): pl.pallas_call(functools.partial(gather_kernel, line), out_shape=jax.Shap...  123 us
    pallas_call x6, Pallas kernels, exchange(): pl.pallas_call(functools.partial(exchange_kernel, n, spread), out_shape=[...  66.1 us
    mul x8, local copies, waits for them, and re-layouts, per_device(): shard * factor  17.8 us
    dot_general x5, matrix products, contract_rows(): lax.dot_general(left, right, (((0,), (0,)), ((), ())), preferred_element_...  17.1 us
    sub x7, other arithmetic, adam_step(): master - rate * (first_hat / (jnp.sqrt(second_hat) + ADAM_EPS) + WEIGHT_D...  16.8 us
    dot_general x5, matrix products, times_transposed(): lax.dot_general(left, right, (((1,), (1,)), ((), ())), preferred_element_...  12.4 us
  transfers between devices with their start and end apart: 5, of which 0 were waited for; matrix products, arithmetic and copies ran while one was open for 13% of the time, Pallas kernels for 33%

profile of v1, /device:TPU:12, one launch (start us, length us, event | category | flops | bytes accessed | tf_op | source)
XLA Modules:
  0.0 579.9 jit_solution(6482256924105700833)
XLA Ops:
  9.4 8.6 %exchange.6 = f32[16,16,128]{2,1,0:T(8,128)S(1)} custom-call(f32[16,128]{1,0:T(8,128)S(1)} %concatenate.28.refs_0_), custom_call_target="tpu_custom_call" | custom-call | tf_op jit(solution)/shard_map/exchange/pallas_call | solution.py:388
  19.1 2.0 reshape_reshape.19
  27.7 123.1 %gather_weights.1 = bf16[3,4,2,2,72,2304]{5,4,3,2,1,0:T(8,128)(2,1)} custom-call(bf16[3,72,2304]{2,1,0:T(8,128)(2,1)} %pad_maximum_fusion.1.src), custom_call_target="tpu_custom_call" | custom-call | bytes 31850496 | tf_op jit(solution)/shard_map/gather_weights/pallas_call | solution.py:169
  151.5 16.0 %exchange.7 = f32[16,16,128]{2,1,0:T(8,128)S(1)} custom-call(f32[16,16,128]{2,1,0:T(8,128)S(1)} %pad.27.refs_0_), custom_call_target="tpu_custom_call" | custom-call | tf_op jit(solution)/shard_map/exchange/pallas_call | solution.py:388
  167.9 2.0 dynamic-slice_convert_fusion
  171.4 9.0 %exchange.8 = f32[16,32,128]{2,1,0:T(8,128)S(1)} custom-call(f32[16,32,128]{2,1,0:T(8,128)S(1)} %pad.28.refs_0_), custom_call_target="tpu_custom_call" | custom-call | tf_op jit(solution)/shard_map/exchange/pallas_call | solution.py:388
  180.6 2.0 all_gather.21
  186.6 2.2 all_gather.22
  189.6 4.0 fusion.2
  193.9 2.2 fusion.96
  196.1 1.9 convolution_convert_fusion.5
  198.8 3.5 fusion.19
  202.3 1.9 constant_dynamic-slice_fusion.3
  204.9 8.8 %fusion.93 = (bf16[1,4,2,2,72,2304]{5,4,3,2,1,0:T(8,128)(2,1)}, bf16[1,4,2,2,72,2304]{5,4,3,2,1,0:T(8,128)(2,1)}) fusion(bf16[3,4,2,2,72,2304]{5,4,3,2,1,0:T(8,128)(2,1)} %gather_weights.1), kind=kLoop, calls=%fused_computation.236 | loop fusion | bytes 21233664 | tf_op jit(solution)/shard_map/slice | solution.py:500
  215.1 2.4 all_gather.24
  219.3 4.5 fusion.97
  226.4 2.8 all_gather.23
  229.1 5.6 convert_reduce_fusion
  236.5 3.9 convolution_convert_fusion.1
  240.4 2.1 fusion.80
  245.3 5.9 %convolution_convert_fusion = bf16[1152,2304]{1,0:T(8,128)(2,1)} fusion(bf16[256,1152]{1,0:T(8,128)(2,1)} %all_gather.24, f32[256,2304]{1,0:T(8,128)} %copy-done.92), kind=kOutput, calls=%fused_computation.1 | convolution fusion | flops 1366917120 | bytes 8257536 | tf_op jit(solution)/shard_map/dot_general | solution.py:557
  253.9 2.5 all_gather.25
  256.5 3.1 fusion.22
  262.8 3.7 fusion.1
  266.8 3.2 convolution_convert_fusion.2
  272.3 2.1 copy.105
  274.4 6.4 %copy.104 = bf16[1152,1728]{1,0:T(8,128)(2,1)} copy(bf16[1152,1728]{0,1:T(8,128)(2,1)} %convolution_convert_fusion.2) | data formatting | bytes 7962624 | tf_op jit(solution)/shard_map/convert.8
  282.6 5.6 pad_maximum_fusion.refs_0_
  288.3 165.2 %reduce_grads.1 = bf16[3,72,2304]{2,1,0:T(8,128)(2,1)} custom-call(bf16[4,2,2,72,2304]{4,3,2,1,0:T(8,128)(2,1)} %pad_maximum_fusion.refs_0_, bf16[4,2,2,72,2304]{4,3,2,1,0:T(8,128)(2,1)} %bitcast.187, bf16[4,2,2,72,2304]{4,3,2,1,0:T(8,128)(2,1)} %bitcast.192), custom_call_target="tpu_custom_call" | custom-call | bytes 31850496 | tf_op jit(solution)/shard_map/reduce_grads/pallas_call | solution.py:342
  461.1 2.5 fusion.34
  463.7 3.4 psum.21
  468.1 16.3 %exchange.9 = (f32[16,56,128]{2,1,0:T(8,128)S(1)}, f32[16,8,128]{2,1,0:T(8,128)S(1)}) custom-call(f32[56,128]{1,0:T(8,128)S(1)} %pad.29.refs_0_, f32[16,8,128]{2,1,0:T(8,128)S(1)} %bitcast.182), custom_call_target="tpu_custom_call" | custom-call | tf_op jit(solution)/shard_map/exchange/pallas_call | solution.py:388
  485.9 3.3 all-reduce.7
  489.3 8.4 %exchange.10 = f32[16,16,128]{2,1,0:T(8,128)S(1)} custom-call(f32[16,128]{1,0:T(8,128)S(1)} %pad.31.refs_0_), custom_call_target="tpu_custom_call" | custom-call | tf_op jit(solution)/shard_map/exchange/pallas_call | solution.py:388
  500.1 2.3 multiply_reduce_fusion.1
  507.8 2.0 fusion.12
  509.7 2.0 fusion.14
  516.3 7.8 %exchange.11 = f32[16,8,128]{2,1,0:T(8,128)S(1)} custom-call(f32[8,128]{1,0:T(8,128)S(1)} %broadcast_in_dim.130.refs_0_), custom_call_target="tpu_custom_call" | custom-call | tf_op jit(solution)/shard_map/exchange/pallas_call | solution.py:388
  525.4 2.1 convert_multiply_fusion.4
  532.9 2.6 mul.698
  539.1 3.2 mul.711
  542.3 2.0 mul.724
  544.3 2.1 mul.737
  546.4 2.6 mul.748
  553.1 6.5 %multiply_subtract_fusion = (f32[497664]{0:T(1024)}, f32[497664]{0:T(1024)}, f32[497664]{0:T(1024)}) fusion(f32[497664]{0:T(1024)S(1)} %copy-done, f32[497664]{0:T(1024)} %mul.698, f32[497664]{0:T(1024)} %param.35, f32[497664]{0:T(1024)} %param.34), kind=kLoop, calls=%fused_computation.28 | loop fusion | flops 6967296 | bytes 13934592 | tf_op jit(solution)/shard_map/sub | solution.py:428
  559.8 2.2 multiply_subtract_fusion.3
  564.2 2.6 multiply_subtract_fusion.2
  567.8 2.6 multiply_subtract_fusion.1
  (348 shorter events, 73.3 us)
Async XLA Ops:
  7.2 14.0 %copy-start.4 = (f32[331776]{0:T(1024)S(1)}, f32[331776]{0:T(1024)}, u32[]{:S(2)}) copy-start(f32[331776]{0:T(1024)} %param.42) | copy-start | bytes 3981316
  7.2 495.3 %all-gather.3.cloned.1.call-start = ((), (), s32[]{:S(2)}) async-start(), calls=%async_computation | async-start | bytes 2985984 | tf_op jit(solution)/shard_map/all_gather | solution.py:605
  18.4 132.7 %copy-start.71 = (s32[16]{0:T(128)}, s32[16]{0:T(128)S(1)}, u32[]{:S(2)}) copy-start(s32[16]{0:T(128)S(1)} %convert_reduce_fusion.5) | copy-start | bytes 196
  27.7 123.1 %copy-start.36 = (f32[73728]{0:T(1024)S(1)}, f32[73728]{0:T(1024)}, u32[]{:S(2)}) copy-start(f32[73728]{0:T(1024)} %param.48) | copy-start | bytes 884740
  27.7 123.3 %copy-start.73 = (bf16[1,1152]{1,0:T(2,128)(2,1)S(1)}, bf16[1,1152]{1,0:T(2,128)(2,1)}, u32[]{:S(2)}) copy-start(bf16[1,1152]{1,0:T(2,128)(2,1)} %param.29) | copy-start | bytes 6916
  27.7 139.8 %copy-start = (f32[497664]{0:T(1024)S(1)}, f32[497664]{0:T(1024)}, u32[]{:S(2)}) copy-start(f32[497664]{0:T(1024)} %param.33) | copy-start | bytes 5971972
  151.1 16.8 %copy-start.82 = (s32[64]{0:T(128)}, s32[64]{0:T(128)S(1)}, u32[]{:S(2)}) copy-start(s32[64]{0:T(128)S(1)} %iota_add_fusion) | copy-start | bytes 772
  167.8 12.6 %slice-start.4 = ((f32[16128]{0:T(1024)}), f32[6912]{0:T(1024)S(1)}, s32[]{:S(2)}) async-start(f32[16128]{0:T(1024)} %copy-done.45), calls=%async_computation.5 | async-start | bytes 57344 | tf_op jit(solution)/shard_map/slice | solution.py:508
  169.8 13.5 %copy-start.91 = (s32[1,128]{1,0:T(1,128)S(1)}, s32[1,128]{1,0:T(1,128)}, u32[]{:S(2)}) copy-start(s32[1,128]{1,0:T(1,128)} %param.32) | copy-start | bytes 1540
  186.1 7.4 %copy-start.69 = (f32[128]{0:T(128)}, f32[128]{0:T(128)S(1)}, u32[]{:S(2)}) copy-start(f32[128]{0:T(128)S(1)} %broadcast_multiply_fusion.3) | copy-start | bytes 1540
  186.4 7.2 %copy-start.86 = (f32[128]{0:T(128)}, f32[128]{0:T(128)S(1)}, u32[]{:S(2)}) copy-start(f32[128]{0:T(128)S(1)} %multiply_reduce_fusion.8) | copy-start | bytes 1540
  186.4 7.2 %copy-start.76 = (f32[128]{0:T(128)}, f32[128]{0:T(128)S(1)}, u32[]{:S(2)}) copy-start(f32[128]{0:T(128)S(1)} %fusion.74) | copy-start | bytes 1540
  204.2 19.6 %collective-permute-start = (f32[128,1152]{1,0:T(8,128)}, f32[128,1152]{1,0:T(8,128)S(1)}, u32[]{:S(2)}, u32[]{:S(2)}) collective-permute-start(f32[128,1152]{1,0:T(8,128)} %constant_dynamic-slice_fusion.3), channel_id=1, source_target_pairs={{0,1},{1,0},{2,3},{3,2},{4,5},{5,4},{6,7},{7,6},{8,9},{9,8},{10,11... | collective-permute-start | bytes 1769480 | tf_op jit(solution)/shard_map/ppermute | solution.py:471
  204.9 8.8 %copy-start.46 = (f32[16128]{0:T(1024)S(1)}, f32[16128]{0:T(1024)}, u32[]{:S(2)}) copy-start(f32[16128]{0:T(1024)} %copy-done.45) | copy-start | bytes 193540
  204.9 9.4 %copy-start.15 = (bf16[1,128,1152]{2,1,0:T(8,128)(2,1)S(1)}, bf16[1,128,1152]{2,1,0:T(8,128)(2,1)}, u32[]{:S(2)}) copy-start(bf16[1,128,1152]{2,1,0:T(8,128)(2,1)} %param.28) | copy-start | bytes 884740
  219.3 5.3 copy-start.51
  219.3 5.3 copy-start.52
  226.1 8.7 %copy-start.89 = (f32[128]{0:T(128)}, f32[128]{0:T(128)S(1)}, u32[]{:S(2)}) copy-start(f32[128]{0:T(128)S(1)} %multiply_reduce_fusion.7) | copy-start | bytes 1540
  226.1 8.6 %copy-start.78 = (f32[128]{0:T(128)}, f32[128]{0:T(128)S(1)}, u32[]{:S(2)}) copy-start(f32[128]{0:T(128)S(1)} %fusion.75) | copy-start | bytes 1540
  226.3 8.4 %slice-start.2 = ((s8[5308416]{0:T(1024)(128)(4,1)}), s8[4194304]{0:T(1024)(128)(4,1)S(1)}, s32[]{:S(2)}) async-start(s8[5308416]{0:T(1024)(128)(4,1)} %bitcast.198), calls=%async_computation.3 | async-start | bytes 8388608
  226.3 14.1 %slice-start = ((s8[5308416]{0:T(1024)(128)(4,1)}), s8[4194304]{0:T(1024)(128)(4,1)S(1)}, s32[]{:S(2)}) async-start(s8[5308416]{0:T(1024)(128)(4,1)} %bitcast.194), calls=%async_computation.1 | async-start | bytes 8388608
  229.1 5.7 slice-start.3
  229.1 11.3 %slice-start.1 = ((s8[5308416]{0:T(1024)(128)(4,1)}), s8[1114112]{0:T(1024)(128)(4,1)S(1)}, s32[]{:S(2)}) async-start(s8[5308416]{0:T(1024)(128)(4,1)} %bitcast.194), calls=%async_computation.2 | async-start | bytes 2228224
  234.8 5.6 copy-start.92
  236.5 6.0 %copy-start.34 = (f32[256,1152]{1,0:T(8,128)}, f32[256,1152]{1,0:T(8,128)S(1)}, u32[]{:S(2)}) copy-start(f32[256,1152]{1,0:T(8,128)S(1)} %fusion.98) | copy-start | bytes 3538948
  243.5 7.7 %collective-permute-start.2 = (f32[128,1152]{1,0:T(8,128)}, f32[128,1152]{1,0:T(8,128)}, u32[]{:S(2)}, u32[]{:S(2)}) collective-permute-start(f32[128,1152]{1,0:T(8,128)} %constant_dynamic-slice_fusion.1), channel_id=1, source_target_pairs={{0,1},{1,0},{2,3},{3,2},{4,5},{5,4},{6,7},{7,6},{8,9},{9,8},{10,11... | collective-permute-start | bytes 1769480 | tf_op jit(solution)/shard_map/ppermute | solution.py:471
  244.7 216.2 %collective-permute-start.1 = (f32[128,1152]{1,0:T(8,128)}, f32[128,1152]{1,0:T(8,128)}, u32[]{:S(2)}, u32[]{:S(2)}) collective-permute-start(f32[128,1152]{1,0:T(8,128)} %constant_dynamic-slice_fusion.2), channel_id=1, source_target_pairs={{0,1},{1,0},{2,3},{3,2},{4,5},{5,4},{6,7},{7,6},{8,9},{9,8},{10,11... | collective-permute-start | bytes 1769480 | tf_op jit(solution)/shard_map/ppermute | solution.py:471
  245.2 6.0 %copy-start.35 = (f32[256,1152]{1,0:T(8,128)S(1)}, f32[256,1152]{1,0:T(8,128)}, u32[]{:S(2)}) copy-start(f32[256,1152]{1,0:T(8,128)} %copy-done.34) | copy-start | bytes 3538948
  245.2 6.0 %copy-start.79 = (f32[128]{0:T(128)S(1)}, f32[128]{0:T(128)}, u32[]{:S(2)}) copy-start(f32[128]{0:T(128)} %copy-done.78) | copy-start | bytes 1540
  252.9 6.6 %copy-start.84 = (f32[128]{0:T(128)}, f32[128]{0:T(128)S(1)}, u32[]{:S(2)}) copy-start(f32[128]{0:T(128)S(1)} %negate_multiply_fusion.1) | copy-start | bytes 1540
  253.9 5.6 copy-start.18
  253.9 5.6 copy-start.68
  270.9 186.7 %collective-permute-start.3 = (f32[128,1152]{1,0:T(8,128)}, f32[128,1152]{1,0:T(8,128)}, u32[]{:S(2)}, u32[]{:S(2)}) collective-permute-start(f32[128,1152]{1,0:T(8,128)} %constant_dynamic-slice_fusion), channel_id=1, source_target_pairs={{0,1},{1,0},{2,3},{3,2},{4,5},{5,4},{6,7},{7,6},{8,9},{9,8},{10,11... | collective-permute-start | bytes 1769480 | tf_op jit(solution)/shard_map/ppermute | solution.py:471
  288.3 169.3 %copy-start.70 = (f32[128]{0:T(128)S(1)}, f32[128]{0:T(128)}, u32[]{:S(2)}) copy-start(f32[128]{0:T(128)} %copy-done.69) | copy-start | bytes 1540
  453.5 5.9 %copy-start.87 = (f32[128]{0:T(128)S(1)}, f32[128]{0:T(128)}, u32[]{:S(2)}) copy-start(f32[128]{0:T(128)} %copy-done.86) | copy-start | bytes 1540
  453.5 7.1 %copy-start.77 = (f32[128]{0:T(128)S(1)}, f32[128]{0:T(128)}, u32[]{:S(2)}) copy-start(f32[128]{0:T(128)} %copy-done.76) | copy-start | bytes 1540
  461.0 6.1 %copy-start.55 = (f32[16128]{0:T(1024)S(1)}, f32[16128]{0:T(1024)}, u32[]{:S(2)}) copy-start(f32[16128]{0:T(1024)} %custom-call) | copy-start | bytes 193540
  461.1 6.8 %copy-start.60 = (f32[1152]{0:T(1024)S(1)}, f32[1152]{0:T(1024)}, u32[]{:S(2)}) copy-start(f32[1152]{0:T(1024)} %copy-done.59) | copy-start | bytes 13828
  463.6 25.6 %copy-start.54 = (f32[16,128]{1,0:T(8,128)S(1)}, f32[16,128]{1,0:T(8,128)}, u32[]{:S(2)}) copy-start(f32[16,128]{1,0:T(8,128)} %copy-done.53) | copy-start | bytes 24580
  463.6 34.8 %copy-start.72 = (s32[16]{0:T(128)S(1)}, s32[16]{0:T(128)}, u32[]{:S(2)}) copy-start(s32[16]{0:T(128)} %copy-done.71) | copy-start | bytes 196
  463.6 34.8 %copy-start.83 = (s32[64]{0:T(128)S(1)}, s32[64]{0:T(128)}, u32[]{:S(2)}) copy-start(s32[64]{0:T(128)} %copy-done.82) | copy-start | bytes 772
  546.4 6.0 %copy-start.65 = (f32[1008]{0:T(1024)S(1)}, f32[1008]{0:T(1024)}, u32[]{:S(2)}) copy-start(f32[1008]{0:T(1024)} %param.51) | copy-start | bytes 12100
  546.4 6.0 %copy-start.80 = (f32[1008]{0:T(1024)S(1)}, f32[1008]{0:T(1024)}, u32[]{:S(2)}) copy-start(f32[1008]{0:T(1024)} %param.53) | copy-start | bytes 12100
  546.4 6.0 %copy-start.81 = (f32[1008]{0:T(1024)S(1)}, f32[1008]{0:T(1024)}, u32[]{:S(2)}) copy-start(f32[1008]{0:T(1024)} %param.52) | copy-start | bytes 12100
  553.1 6.6 %copy-start.13 = (f32[248832]{0:T(1024)S(1)}, f32[248832]{0:T(1024)}, u32[]{:S(2)}) copy-start(f32[248832]{0:T(1024)} %param.36) | copy-start | bytes 2985988
  553.1 6.6 %copy-start.14 = (f32[248832]{0:T(1024)S(1)}, f32[248832]{0:T(1024)}, u32[]{:S(2)}) copy-start(f32[248832]{0:T(1024)} %mul.711) | copy-start | bytes 2985988
  553.1 6.6 %copy-start.39 = (f32[248832]{0:T(1024)S(1)}, f32[248832]{0:T(1024)}, u32[]{:S(2)}) copy-start(f32[248832]{0:T(1024)} %param.38) | copy-start | bytes 2985988
  553.1 6.6 %copy-start.40 = (f32[248832]{0:T(1024)S(1)}, f32[248832]{0:T(1024)}, u32[]{:S(2)}) copy-start(f32[248832]{0:T(1024)} %param.37) | copy-start | bytes 2985988
  (55 other events, 145.3 us)
Sparse Core Ops, SparseCore 0:
  453.6 9.7 all-gather.2

commit v2 on v1

--- a/solution.py
+++ b/solution.py
@@ -179,18 +179,16 @@
 
 
 def reduce_kernel(line, *refs):
-    count = len(refs) - 1 - 4 - 4 - 4 - 4 - 8
+    count = len(refs) - 1 - 16 - 7
     grads = refs[:count]
     out = refs[count]
     s = count + 1
-    acc = refs[s:s + 4]
-    got_b = refs[s + 4:s + 8]
-    got_z = refs[s + 8:s + 12]
-    got_a = refs[s + 12:s + 16]
-    load, send_b, send_z, send_a, recv_b, recv_z, recv_a, spare = refs[s + 16:]
+    acc, got_b, got_z, got_a = (refs[s + 4 * i:s + 4 * i + 4] for i in range(4))
+    load, send_b, send_z, send_a, recv_b, recv_z, recv_a = refs[s + 16:]
     me = Place(line)
     x, y, z = me.x, me.y, me.z
     up, down = z < line - 1, z > 0
+    above, below = me.dev(z=jnp.minimum(z + 1, line - 1)), me.dev(z=jnp.maximum(z - 1, 0))
 
     def cols(g):
         return pl.ds(GROUPS[g][0], GROUPS[g][1])
@@ -198,53 +196,30 @@
     def last(g):
         return "y" if GROUPS[g][3] == "x" else "x"
 
-    def half(m, g, zz, mine):
+    def half(grad, g, zz, mine):
         if last(g) == "y":
-            return grads[m].at[zz, y if mine else 1 - y, :, :, cols(g)]
-        return grads[m].at[zz, :, x if mine else 1 - x, :, cols(g)]
+            return grad.at[zz, y if mine else 1 - y, :, :, cols(g)]
+        return grad.at[zz, :, x if mine else 1 - x, :, cols(g)]
 
     def first(g):
         return x if GROUPS[g][3] == "x" else y
 
-    def loading(m, g, zz):
-        return pltpu.make_async_copy(half(m, g, zz, True), acc[g].at[m, zz], load.at[m, g, zz])
+    def loading(m, g, zz, grad=grads[0]):
+        return pltpu.make_async_copy(half(grad, g, zz, True), acc[g].at[m, zz], load.at[m, g, zz])
 
     def remote(src, dst, send, recv, dev):
-        return pltpu.make_async_remote_copy(src_ref=src, dst_ref=dst, send_sem=send, recv_sem=recv, device_id=dev, device_id_type=MESH)
-
-    def b_copy(m, g, zz):
-        return remote(half(m, g, zz, False), got_b[g].at[m, zz], send_b.at[m, g, zz], recv_b.at[m, g, zz], me.peer(last(g)))
-
-    def a_copy(m, g, zz, slot):
-        return remote(acc[g].at[m, zz, 1 - first(g)], got_a[g].at[m, slot], send_a.at[m, g, zz], recv_a.at[m, g, slot], me.peer(GROUPS[g][3]))
-
-    def z_part(m, g, zz):
-        return acc[g].at[m, zz] if GROUPS[g][2] == 0 else acc[g].at[m, zz, first(g)]
+        return pltpu.make_async_remote_copy(
+            src_ref=src, dst_ref=dst, send_sem=send, recv_sem=recv, device_id=dev, device_id_type=MESH)
+
+    def b_copy(m, g, zz, grad=grads[0]):
+        return remote(half(grad, g, zz, False), got_b[g].at[m, zz], send_b.at[m, g, zz], recv_b.at[m, g, zz], me.peer(last(g)))
+
+    def a_copy(m, g, zz):
+        return remote(acc[g].at[m, zz, 1 - first(g)], got_a[g].at[m, zz], send_a.at[m, g, zz], recv_a.at[m, g, zz], me.peer(GROUPS[g][3]))
 
     def z_copy(m, g, zz, slot, dev):
-        return remote(z_part(m, g, zz), got_z[g].at[m, slot], send_z.at[m, g, zz], recv_z.at[m, g, slot], dev)
-
-    def z_recv(m, g, slot):
-        z_copy(m, g, z, slot, me.dev(z=jnp.maximum(z - 1, 0))).wait_recv()
-
-    above, below = me.dev(z=jnp.minimum(z + 1, line - 1)), me.dev(z=jnp.maximum(z - 1, 0))
-
-    me.barrier()
-
-    def start(m, zz):
-        for g in range(4):
-            b_copy(m, g, zz).start()
-            loading(m, g, zz).start()
-
-    def each(fn):
-        @pl.loop(0, line)
-        def _(j):
-            k = line - 1 - j
-            for m in range(count):
-                when(z + k < line, lambda: fn(m, jnp.minimum(z + k, line - 1)))
-                when((z >= k) & (k > 0), lambda: fn(m, jnp.maximum(z - k, 0)))
-
-    each(start)
+        part = acc[g].at[m, zz] if GROUPS[g][2] == 0 else acc[g].at[m, zz, first(g)]
+        return remote(part, got_z[g].at[m, slot], send_z.at[m, g, zz], recv_z.at[m, g, slot], dev)
 
     def add_b(m, g, zz):
         loading(m, g, zz).wait()
@@ -252,82 +227,105 @@
         acc[g][m, zz] = acc[g][m, zz] + got_b[g][m, zz]
 
     def add_z(m, g, zz, slot):
-        z_recv(m, g, slot)
+        z_copy(m, g, z, slot, below).wait_recv()
         if GROUPS[g][2] == 0:
             acc[g][m, zz] = acc[g][m, zz] + got_z[g][m, slot]
         else:
             acc[g][m, zz, first(g)] = acc[g][m, zz, first(g)] + got_z[g][m, slot]
 
     def add_a(m, g, zz):
-        a_copy(m, g, zz, zz).wait_recv()
+        a_copy(m, g, zz).wait_recv()
         acc[g][m, zz, first(g)] = acc[g][m, zz, first(g)] + got_a[g][m, zz]
 
-    def move_up(m, g, zz):
-        when(down, lambda: add_z(m, g, zz, zz))
-        z_copy(m, g, zz, zz, above).start()
-
-    def move_down(m, g, zz, k):
-        when(up, lambda: add_z(m, g, zz, zz))
-        z_copy(m, g, zz, jnp.where(k == 1, line, zz), below).start()
-
-    @pl.loop(0, line)
-    def _(j):
+    def planes(k, fn):
+        when(z + k < line, lambda: fn(jnp.minimum(z + k, line - 1), True))
+        when((z >= k) & (k > 0), lambda: fn(jnp.maximum(z - k, 0), False))
+
+    def begin(m, j):
+        def one(grad, zz):
+            for g in range(4):
+                b_copy(m, g, zz, grad).start()
+                loading(m, g, zz, grad).start()
+
+        for index, grad in enumerate(grads):
+            when(m == index, lambda: planes(line - 1 - j, lambda zz, upward: one(grad, zz)))
+
+    def onward(m, g, zz, k, upward):
+        if upward:
+            when(down, lambda: add_z(m, g, zz, zz))
+            z_copy(m, g, zz, zz, above).start()
+        else:
+            when(up, lambda: add_z(m, g, zz, zz))
+            z_copy(m, g, zz, jnp.where(k == 1, line, zz), below).start()
+
+    def near(m, j):
         k = line - 1 - j
 
-        def near(m, zz):
+        def one(zz, upward):
             for g in range(4):
                 add_b(m, g, zz)
                 if GROUPS[g][2] == 1:
-                    a_copy(m, g, zz, zz).start()
-
-        def go_up(m, gs, k):
-            zz = jnp.minimum(z + k, line - 1)
-            for g in gs:
-                if GROUPS[g][2] == 1:
-                    add_a(m, g, zz)
-                move_up(m, g, zz)
-
-        def go_down(m, gs, k):
-            zz = jnp.maximum(z - k, 0)
-            for g in gs:
-                if GROUPS[g][2] == 1:
-                    add_a(m, g, zz)
-                move_down(m, g, zz, k)
-
-        for m in range(count):
-            when(z + k < line, lambda: near(m, jnp.minimum(z + k, line - 1)))
-            when((z >= k) & (k > 0), lambda: near(m, jnp.maximum(z - k, 0)))
-            when((k > 0) & (z + k < line), lambda: go_up(m, (0, 1), k))
-            when((k > 0) & (z >= k), lambda: go_down(m, (0, 1), k))
-            when((j > 0) & (z + k + 1 < line), lambda: go_up(m, (2, 3), k + 1))
-            when((j > 0) & (z >= k + 1), lambda: go_down(m, (2, 3), k + 1))
-
-    for m in range(count):
+                    a_copy(m, g, zz).start()
+                else:
+                    when(k > 0, lambda g=g: onward(m, g, zz, k, upward))
+
+        planes(k, one)
+
+    def far(m, j):
+        k = line - j
+
+        def one(zz, upward):
+            for g in (2, 3):
+                add_a(m, g, zz)
+                onward(m, g, zz, k, upward)
+
+        when((k > 0) & (k < line), lambda: planes(k, one))
+
+    def close(m):
         for g in (0, 1):
-            when(down, lambda: add_z(m, g, z, z))
-            when(up, lambda: add_z(m, g, z, line))
-            a_copy(m, g, z, z).start()
-    for m in range(count):
+            when(down, lambda g=g: add_z(m, g, z, z))
+            when(up, lambda g=g: add_z(m, g, z, line))
+            a_copy(m, g, z).start()
+
+    def final(m):
         for g in (2, 3):
             add_a(m, g, z)
-            when(down, lambda: add_z(m, g, z, z))
-            when(up, lambda: add_z(m, g, z, line))
+            when(down, lambda g=g: add_z(m, g, z, z))
+            when(up, lambda g=g: add_z(m, g, z, line))
             out[m, :, cols(g)] = acc[g][m, z, first(g)]
         for g in (0, 1):
-            a_copy(m, g, z, z).wait_recv()
+            a_copy(m, g, z).wait_recv()
             out[m, :, cols(g)] = acc[g][m, z, first(g)] + got_a[g][m, z]
 
-    def finish(m, zz):
-        for g in range(4):
-            b_copy(m, g, zz).wait_send()
-            if GROUPS[g][2] == 1:
-                a_copy(m, g, zz, zz).wait_send()
-            when(zz != z, lambda: z_copy(m, g, zz, zz, above).wait_send())
-
-    each(finish)
-    for m in range(count):
+    me.barrier()
+    begin(0, 0)
+    if line > 1:
+        begin(0, 1)
+    units = count * line
+
+    @pl.loop(0, units)
+    def _(u):
+        m, j = u // line, u % line
+        v = u + 2
+        when(v < units, lambda: begin(jnp.minimum(v // line, count - 1), v % line))
+        near(m, j)
+        far(m, j)
+        when(j == line - 1, lambda: close(m))
+        when((j == 0) & (m > 0), lambda: final(jnp.maximum(m - 1, 0)))
+
+    final(count - 1)
+
+    @pl.loop(0, count)
+    def _(m):
+        @pl.loop(0, line)
+        def _(zz):
+            for g in range(4):
+                b_copy(m, g, zz).wait_send()
+                if GROUPS[g][2] == 1:
+                    a_copy(m, g, zz).wait_send()
+                when(zz != z, lambda g=g: z_copy(m, g, zz, zz, above).wait_send())
         for g in (0, 1):
-            a_copy(m, g, z, z).wait_send()
+            a_copy(m, g, z).wait_send()
 
 
 def reduce_grads(grads, n, collective_id):
@@ -344,7 +342,7 @@
         out_shape=jax.ShapeDtypeStruct((count, rows, cols), dt),
         in_specs=[pl.BlockSpec(memory_space=pltpu.HBM)] * count,
         out_specs=pl.BlockSpec(memory_space=pltpu.VMEM),
-        scratch_shapes=acc + acc + got_z + got_a + [dma((count, 4, line))] * 5 + [dma((count, 4, line + 1))] + [dma((count, 4, line))] + [dma((1,))],
+        scratch_shapes=acc + acc + got_z + got_a + [dma((count, 4, line))] * 5 + [dma((count, 4, line + 1))] + [dma((count, 4, line))],
         compiler_params=pltpu.CompilerParams(collective_id=collective_id, has_side_effects=True, vmem_limit_bytes=48 * 2**20),
         cost_estimate=pl.CostEstimate(flops=0, bytes_accessed=2 * count * n * rows * cols * 2, transcendentals=0),
         name="reduce_grads",
@@ -396,6 +394,175 @@
     )(*blocks)
 
 
+def adam_step(grad, master, first, second, rate):
+    first_new = BETA_FIRST * first + (1.0 - BETA_FIRST) * grad
+    second_new = BETA_SECOND * second + (1.0 - BETA_SECOND) * grad * grad
+    first_hat = first_new / (1.0 - BETA_FIRST**STEP)
+    second_hat = second_new / (1.0 - BETA_SECOND**STEP)
+    master_new = master - rate * (
+        first_hat / (jnp.sqrt(second_hat) + ADAM_EPS) + WEIGHT_DECAY * master
+    )
+    return (first_new, second_new, master_new)
+
+
+def chunk_rows(rows):
+    sizes = [d for d in range(8, 257, 8) if rows % d == 0]
+    return sizes[-1] if sizes else rows
+
+
+def finish_kernel(n, rates, *refs):
+    kinds = len(rates)
+    reduced, silu, d_mod, d_cond, bias_grad, onehot, same = refs[:7]
+    states = [refs[7 + 3 * a : 10 + 3 * a] for a in range(kinds)]
+    at = 7 + 3 * kinds
+    news = [refs[at + 3 * a : at + 3 * a + 3] for a in range(kinds)]
+    at += 3 * kinds
+    norm_out, at = refs[at], at + 1
+    held = refs[at : at + kinds]
+    flat = refs[at + kinds : at + 2 * kinds]
+    both, wide, block, got, in_sem, out_sem, pair_send, pair_recv, send, recv = refs[at + 2 * kinds :]
+    me, c = lax.axis_index("dp"), lax.axis_index("seq")
+    rows = reduced.shape[1]
+    half = reduced.shape[2]
+    head = half // 4
+
+    def loads(a, k):
+        return pltpu.make_async_copy(states[a][k], held[a].at[k], in_sem.at[a, k])
+
+    for a in range(kinds):
+        for k in range(3):
+            loads(a, k).start()
+
+    bar = pltpu.get_barrier_semaphore()
+    pl.semaphore_signal(bar, inc=1, device_id=(me, 1 - c), device_id_type=MESH)
+
+    @pl.loop(1, n)
+    def _(j):
+        pl.semaphore_signal(bar, inc=1, device_id=((me + j) % n, c), device_id_type=MESH)
+
+    both[c] = reduced[...]
+    pl.semaphore_wait(bar, n)
+    pair = pltpu.make_async_remote_copy(
+        src_ref=reduced, dst_ref=both.at[c], send_sem=pair_send, recv_sem=pair_recv,
+        device_id=(me, 1 - c), device_id_type=MESH)
+    pair.start()
+
+    def spread(a, width):
+        total = None
+        tiles = width // 128
+        for t in range(tiles):
+            part = wide[:, 128 * t : 128 * t + 128]
+            flat[a][pl.ds(t, rows, stride=tiles), :] = part
+            square = part * part
+            total = square if total is None else total + square
+        return jnp.sum(total)
+
+    wide[...] = lax.dot_general(
+        silu[...], d_mod[...], (((0,), (0,)), ((), ())), preferred_element_type=jnp.float32)
+    squares = spread(0, wide.shape[1]) + jnp.sum(bias_grad[...] * bias_grad[...])
+    pair.wait()
+    for core in range(2):
+        for part in range(3):
+            lo = (2 * part + core) * head
+            wide[:, lo : lo + head] = both[core, 0, :, part * head : (part + 1) * head].astype(jnp.float32)
+    squares = squares + spread(1, 6 * head)
+    for core in range(2):
+        wide[:, core * head : (core + 1) * head] = both[core, 0, :, 3 * head :].astype(jnp.float32)
+    squares = squares + spread(2, 2 * head)
+    for a in (3, 4):
+        for core in range(2):
+            wide[:, core * half : (core + 1) * half] = both[core, a - 2].astype(jnp.float32)
+        squares = squares + spread(a, 2 * half)
+
+    slots = d_cond.shape[0]
+    block[:slots] = d_cond[...]
+    block[slots:] = jnp.full((8, 128), squares, jnp.float32)
+    got[me] = block[...]
+
+    def copy(j, there, slot):
+        return pltpu.make_async_remote_copy(
+            src_ref=block, dst_ref=got.at[slot], send_sem=send.at[j], recv_sem=recv.at[slot],
+            device_id=(there, c), device_id_type=MESH)
+
+    @pl.loop(1, n)
+    def _(j):
+        copy(j, (me + j) % n, me).start()
+
+    @pl.loop(1, n)
+    def _(j):
+        copy(j, (me + j) % n, (me + n - j) % n).wait()
+
+    total = jnp.sum(got[:, slots:], axis=0)[:1, :1]
+    gram = jnp.zeros((slots, slots), jnp.float32)
+    for i in range(n):
+        part = got[i, :slots]
+        gram = gram + lax.dot_general(
+            part, part, (((1,), (1,)), ((), ())), preferred_element_type=jnp.float32, precision=lax.Precision.HIGHEST)
+        wide[: onehot.shape[1], i * rows : (i + 1) * rows] = lax.dot_general(
+            onehot[...], part, (((0,), (0,)), ((), ())), preferred_element_type=jnp.float32,
+            precision=lax.Precision.HIGHEST)[:, :rows]
+    total = total + jnp.sum(gram * same[...], keepdims=True)
+    norm = jnp.sqrt(total)
+    norm_out[...] = jnp.broadcast_to(norm, (8, 128))
+    factor = jnp.minimum(1.0, CLIP_LIMIT / (norm + 1e-06))
+    tiles = n * rows // 128
+    for t in range(tiles):
+        flat[5][pl.ds(t, onehot.shape[1], stride=tiles), :] = wide[: onehot.shape[1], 128 * t : 128 * t + 128]
+
+    for a in range(kinds):
+        for k in range(3):
+            loads(a, k).wait()
+        size = chunk_rows(flat[a].shape[0])
+
+        @pl.loop(0, flat[a].shape[0] // size)
+        def _(i, a=a, size=size):
+            part = pl.ds(pl.multiple_of(i * size, size), size)
+            grad = flat[a][part] * factor
+            master, first, second = held[a][0, part], held[a][1, part], held[a][2, part]
+            first, second, master = adam_step(grad, master, first, second, rates[a])
+            held[a][0, part], held[a][1, part], held[a][2, part] = master, first, second
+            for k in range(3):
+                pltpu.make_async_copy(held[a].at[k, part], news[a][k].at[part], out_sem.at[a, k]).start()
+
+    for a in range(kinds):
+        for k in range(3):
+            pltpu.make_async_copy(held[a].at[k], news[a][k], out_sem.at[a, k]).wait()
+
+
+def finish(reduced, silu, d_mod, d_cond, bias_grad, onehot, same, states, rates, n, collective_id):
+    vmem, hbm = pl.BlockSpec(memory_space=pltpu.VMEM), pl.BlockSpec(memory_space=pltpu.HBM)
+    dma = pltpu.SemaphoreType.DMA
+    kinds = len(states)
+    rows = reduced.shape[1]
+    flats = [jax.ShapeDtypeStruct(s[0].shape, jnp.float32) for s in states]
+    block = d_cond.shape[0] + 8
+    outs = pl.pallas_call(
+        functools.partial(finish_kernel, n, rates),
+        out_shape=[f for f in flats for _ in range(3)] + [jax.ShapeDtypeStruct((8, 128), jnp.float32)],
+        in_specs=[vmem] * 7 + [hbm] * (3 * kinds),
+        out_specs=[hbm] * (3 * kinds) + [vmem],
+        scratch_shapes=[pltpu.VMEM((3,) + f.shape, jnp.float32) for f in flats]
+        + [pltpu.VMEM(f.shape, jnp.float32) for f in flats]
+        + [
+            pltpu.VMEM((2,) + reduced.shape, reduced.dtype),
+            pltpu.VMEM((rows, d_mod.shape[1]), jnp.float32),
+            pltpu.VMEM((block, 128), jnp.float32),
+            pltpu.VMEM((n, block, 128), jnp.float32),
+            dma((kinds, 3)),
+            dma((kinds, 3)),
+            dma,
+            dma,
+            dma((n,)),
+            dma((n,)),
+        ],
+        compiler_params=pltpu.CompilerParams(
+            collective_id=collective_id, has_side_effects=True, vmem_limit_bytes=56 * 2**20),
+        name="finish",
+    )(reduced, silu, d_mod, d_cond, bias_grad, onehot, same, *[item for s in states for item in s])
+    order = [3 * a + k for a in range(kinds) for k in (1, 2, 0)]
+    return [outs[i] for i in order], outs[-1][0, 0]
+
+
 def grid_embed(keep_index, width):
     quarter = width // 4
     freqs = 10000.0 ** (-jnp.arange(quarter).astype(jnp.float32) / quarter)
@@ -418,17 +585,6 @@
 
 def gelu_tanh(values):
     return jax.nn.gelu(values, approximate=True)
-
-
-def adam_step(grad, master, first, second, rate):
-    first_new = BETA_FIRST * first + (1.0 - BETA_FIRST) * grad
-    second_new = BETA_SECOND * second + (1.0 - BETA_SECOND) * grad * grad
-    first_hat = first_new / (1.0 - BETA_FIRST**STEP)
-    second_hat = second_new / (1.0 - BETA_SECOND**STEP)
-    master_new = master - rate * (
-        first_hat / (jnp.sqrt(second_hat) + ADAM_EPS) + WEIGHT_DECAY * master
-    )
-    return (first_new, second_new, master_new)
 
 
 def per_device(
@@ -602,7 +758,6 @@
 
     shape = (n // 4, 2, 2, own_rows, pieces_own.shape[2])
     reduced = reduce_grads([g.reshape(shape) for g in (grad_attn, grad_expand, grad_contract)], n, 2)
-    both = lax.all_gather(reduced, "seq", axis=0)
 
     d_pieces = jnp.concatenate(
         [d_shift_attn, d_scale_attn, d_gate_attn, d_shift_mlp, d_scale_mlp, d_gate_mlp], axis=0
@@ -627,35 +782,15 @@
     bias_parts = jnp.pad(grad_biases.reshape(n, bias_share), ((0, 0), (0, 1024 - bias_share))).reshape(n, 8, 128)
     d_mod_block = jnp.pad(d_mod.reshape(-1, 128), ((0, -(6 * width // 128) % 8), (0, 0)))
     d_mod_got, bias_got = exchange([d_mod_block, bias_parts], (False, True), n, 6)
-    biases_shard = lax.psum(jnp.sum(bias_got, axis=0), "seq").reshape(1024)[:bias_share]
+    biases_shard = lax.psum(jnp.sum(bias_got, axis=0), "seq")
     d_mod_all = d_mod_got[:, : 6 * width // 128].reshape(n, 6 * width).astype(low)
     d_silu = times_transposed(
         lax.dynamic_slice_in_dim(d_mod_all, c * 3 * width, 3 * width, 1), own_modulation
     )
     d_silu = lax.psum(d_silu, "seq")
     d_cond_own = jax.vjp(jax.nn.silu, cond_own)[1](d_silu)[0]
-    (got,) = exchange([jnp.pad(d_cond_own, ((0, 0), (0, 128 - own_rows)))], (False,), n, 7)
-    d_cond = got[:, :, :own_rows].transpose(1, 0, 2).reshape(n, width)
-    grad_table = jnp.dot(onehot.astype(jnp.float32).T, d_cond, precision=lax.Precision.HIGHEST)
-    grad_modulation = contract_rows(silu_own, d_mod_all)
-
-    in_shard = both[:, 0, :, : 3 * half_width].reshape(pairs, own_rows, 3, half_width).transpose(1, 2, 0, 3)
-    out_shard = both[:, 0, :, 3 * half_width :].transpose(1, 0, 2)
-    shards = (
-        grad_modulation.reshape(-1),
-        in_shard.astype(jnp.float32).reshape(-1),
-        out_shard.astype(jnp.float32).reshape(-1),
-        both[:, 1].transpose(1, 0, 2).astype(jnp.float32).reshape(-1),
-        both[:, 2].transpose(1, 0, 2).astype(jnp.float32).reshape(-1),
-        grad_table.reshape(-1),
-        biases_shard,
-    )
-    squares = jnp.sum(shards[0] * shards[0])
-    for shard in shards[1:]:
-        squares = squares + jnp.sum(shard * shard)
-    (got,) = exchange([jnp.broadcast_to(squares, (8, 128))], (False,), n, 8)
-    grad_norm = jnp.sqrt(jnp.sum(got[:, 0, 0]))
-    factor = jnp.minimum(1.0, CLIP_LIMIT / (grad_norm + 1e-06))
+    d_cond_block = jnp.pad(d_cond_own, ((0, 0), (0, 128 - own_rows)))
+    same = (labels_all[:, None] == labels_all[None, :]).astype(jnp.float32)
     rates = (
         width ** (-0.5),
         width ** (-0.5),
@@ -692,11 +827,24 @@
         class_table_second,
         biases_second,
     )
-    updated = [
-        adam_step(shard * factor, master, first, second, rate)
-        for shard, master, first, second, rate in zip(shards, masters, firsts, seconds, rates)
-    ]
-    return (block_out, tokens_grad, grad_norm) + tuple(item for step in updated for item in step)
+    states = list(zip(masters, firsts, seconds))
+    updated, grad_norm = finish(
+        reduced,
+        silu_own,
+        d_mod_all,
+        d_cond_block,
+        biases_shard,
+        onehot.astype(jnp.float32),
+        same,
+        [tuple(item.reshape(-1, 128) for item in state) for state in states[:-1]],
+        rates[:-1],
+        n,
+        8,
+    )
+    factor = jnp.minimum(1.0, CLIP_LIMIT / (grad_norm + 1e-06))
+    bias_grad = biases_shard.reshape(1024)[:bias_share] * factor
+    updated = [item.reshape(-1) for item in updated] + list(adam_step(bias_grad, *states[-1], rates[-1]))
+    return (block_out, tokens_grad, grad_norm) + tuple(updated)
 
 
 def solution(mesh):

time: 591 us -> 489 us (0.83)
  other arithmetic: 59 us -> 23.8 us
  Pallas kernels: 354 us -> 320 us
  between operations: 23.9 us -> 4.63 us
  matrix products: 55.9 us -> 47.4 us
    pallas_call x1, Pallas kernels: 165 us -> 123 us  [reduce_grads(): pl.pallas_call(functools.partial(reduce_kernel, line), out_shape=jax.Shap...]
    pallas_call x0 -> x1, Pallas kernels: none -> 23.8 us  [finish(): pl.pallas_call(functools.partial(finish_kernel, n, rates), out_shape=[f f...]
    mul x8 -> x0, local copies, waits for them, and re-layouts: 17.8 us -> none  [per_device(): shard * factor]
    unnamed x204 -> x236, local copies, waits for them, and re-layouts: 8.62 us -> 25.6 us
    sub x7 -> x1, other arithmetic: 16.8 us -> 0.62 us  [adam_step(): master - rate * (first_hat / (jnp.sqrt(second_hat) + ADAM_EPS) + WEIGHT_D...]
    pallas_call x6 -> x4, Pallas kernels: 66.1 us -> 50.3 us  [exchange(): pl.pallas_call(functools.partial(exchange_kernel, n, spread), out_shape=[...]
    mul x6 -> x0, other arithmetic: 9.21 us -> none  [per_device(): shard * factor]
    reduce_sum x7 -> x1, other arithmetic: 8.05 us -> 0.02 us  [per_device(): biases_shard = lax.psum(jnp.sum(bias_got, axis=0), 'seq')]
  transfers between devices with their start and end apart: 5 -> 4, of which waited for: 0 -> 0; matrix products, arithmetic and copies ran while one was open for 13% -> 13% of each run, Pallas kernels for 33% -> 26%
where the time goes in v2:
time: 489 us; the launch traced here: 480 us
  Pallas kernels  320 us (65%)
  local copies, waits for them, and re-layouts  63.4 us (13%)
  matrix products  47.4 us (10%)
  other arithmetic  23.8 us (5%)
  blocking collectives  19.3 us (4%)
    pallas_call x1, Pallas kernels, reduce_grads(): pl.pallas_call(functools.partial(reduce_kernel, line), out_shape=jax.Shap...  123 us
    pallas_call x1, Pallas kernels, gather_weights(): pl.pallas_call(functools.partial(gather_kernel, line), out_shape=jax.Shap...  123 us
    pallas_call x4, Pallas kernels, exchange(): pl.pallas_call(functools.partial(exchange_kernel, n, spread), out_shape=[...  50.3 us
    unnamed x236, local copies, waits for them, and re-layouts  25.6 us
    pallas_call x1, Pallas kernels, finish(): pl.pallas_call(functools.partial(finish_kernel, n, rates), out_shape=[f f...  23.8 us
    dot_general x4, matrix products, contract_rows(): lax.dot_general(left, right, (((0,), (0,)), ((), ())), preferred_element_...  14.5 us
    dot_general x5, matrix products, times_transposed(): lax.dot_general(left, right, (((1,), (1,)), ((), ())), preferred_element_...  11.5 us
  transfers between devices with their start and end apart: 4, of which 0 were waited for; matrix products, arithmetic and copies ran while one was open for 13% of the time, Pallas kernels for 26%

profile of v2, /device:TPU:12, one launch (start us, length us, event | category | flops | bytes accessed | tf_op | source)
XLA Modules:
  0.0 479.8 jit_solution(15884733523828828974)
XLA Ops:
  2.8 8.6 %exchange.4 = f32[16,16,128]{2,1,0:T(8,128)S(1)} custom-call(f32[16,128]{1,0:T(8,128)S(1)} %concatenate.28.refs_0_), custom_call_target="tpu_custom_call" | custom-call | tf_op jit(solution)/shard_map/exchange/pallas_call | solution.py:386
  12.6 2.0 reshape_reshape.19
  14.8 1.4 constant_dynamic-slice_fusion.4
  17.8 1.9 convert_reduce_fusion.4
  21.1 123.1 %gather_weights.1 = bf16[3,4,2,2,72,2304]{5,4,3,2,1,0:T(8,128)(2,1)} custom-call(bf16[3,72,2304]{2,1,0:T(8,128)(2,1)} %pad_maximum_fusion.1.src), custom_call_target="tpu_custom_call" | custom-call | bytes 31850496 | tf_op jit(solution)/shard_map/gather_weights/pallas_call | solution.py:169
  145.0 16.0 %exchange.5 = f32[16,16,128]{2,1,0:T(8,128)S(1)} custom-call(f32[16,16,128]{2,1,0:T(8,128)S(1)} %pad.27.refs_0_), custom_call_target="tpu_custom_call" | custom-call | tf_op jit(solution)/shard_map/exchange/pallas_call | solution.py:386
  164.0 9.0 %exchange.6 = f32[16,32,128]{2,1,0:T(8,128)S(1)} custom-call(f32[16,32,128]{2,1,0:T(8,128)S(1)} %pad.28.refs_0_), custom_call_target="tpu_custom_call" | custom-call | tf_op jit(solution)/shard_map/exchange/pallas_call | solution.py:386
  173.1 2.0 all_gather.15
  175.9 1.4 multiply_cosine_fusion
  178.2 2.2 all_gather.16
  180.6 4.0 fusion.2
  186.5 1.5 convolution_convert_fusion.5
  188.7 2.5 fusion.12
  192.3 8.8 %fusion.69 = (bf16[1,4,2,2,72,2304]{5,4,3,2,1,0:T(8,128)(2,1)}, bf16[1,4,2,2,72,2304]{5,4,3,2,1,0:T(8,128)(2,1)}) fusion(bf16[3,4,2,2,72,2304]{5,4,3,2,1,0:T(8,128)(2,1)} %gather_weights.1), kind=kLoop, calls=%fused_computation.187 | loop fusion | bytes 21233664 | tf_op jit(solution)/shard_map/slice | solution.py:656
  203.2 2.2 all_gather.18
  206.2 1.4 dynamic_slice.68
  208.2 4.2 fusion.72
  213.3 2.8 all_gather.17
  216.2 5.7 %convert_reduce_fusion = (f32[2304]{0:T(1024)}, bf16[256,2304]{1,0:T(8,128)(2,1)S(1)}, f32[256,2304]{1,0:T(8,128)S(1)}) fusion(f32[256,2304]{1,0:T(8,128)S(1)} %fusion.72, f32[2304]{0:T(1024)S(1)} %copy-done.72, bf16[256,1152]{1,0:T(8,128)(2,1)S(1)} %all_gather.17, bf16[1152,2304]{1,0:T(8,128)(2,1)} %bitcast.206), kind=kOutput, calls=%fused_computation.18 | convolution fusion | flops 1372518144 | bytes 11814912 | tf_op jit(solution)/shard_map/dot_general | solution.py:720
  221.8 1.7 fusion.73
  223.6 3.9 convolution_convert_fusion.1
  227.5 2.1 fusion.62
  232.6 1.5 dynamic_update_slice.11
  234.1 5.8 %convolution_convert_fusion = bf16[1152,2304]{1,0:T(8,128)(2,1)} fusion(bf16[256,1152]{1,0:T(8,128)(2,1)S(1)} %copy-done.12, f32[256,2304]{1,0:T(8,128)} %copy-done.99), kind=kOutput, calls=%fused_computation.1 | convolution fusion | flops 1366917120 | bytes 8257536 | tf_op jit(solution)/shard_map/dot_general | solution.py:713
  239.9 2.0 multiply_reduce_fusion.1
  242.7 2.5 all_gather.19
  245.2 3.1 fusion.15
  251.1 3.7 fusion.1
  254.8 3.2 convolution_convert_fusion.2
  259.9 1.3 copy.93
  261.2 6.5 %copy.92 = bf16[1152,1728]{1,0:T(8,128)(2,1)} copy(bf16[1152,1728]{0,1:T(8,128)(2,1)} %convolution_convert_fusion.2) | data formatting | bytes 7962624 | tf_op jit(solution)/shard_map/convert.9
  267.7 1.3 reshape.479
  269.6 1.6 convolution_convert_fusion.3
  271.2 5.7 %pad_maximum_fusion.refs_0_ = bf16[4,2,2,72,2304]{4,3,2,1,0:T(8,128)(2,1)} fusion(bf16[4,2,2,72,576]{4,3,2,1,0:T(8,128)(2,1)S(1)} %convolution_convert_fusion.3, bf16[4,2,2,72,1728]{4,3,2,1,0:T(8,128)(2,1)} %bitcast.197), kind=kLoop, calls=%fused_computation.4 | loop fusion | flops 10616832 | bytes 10616832 | tf_op jit(solution)/shard_map/concatenate | solution.py:754
  276.9 123.1 %reduce_grads.1.refs_0_ = bf16[3,72,2304]{2,1,0:T(8,128)(2,1)S(1)} custom-call(bf16[4,2,2,72,2304]{4,3,2,1,0:T(8,128)(2,1)} %pad_maximum_fusion.refs_0_, bf16[4,2,2,72,2304]{4,3,2,1,0:T(8,128)(2,1)} %bitcast.196, bf16[4,2,2,72,2304]{4,3,2,1,0:T(8,128)(2,1)} %bitcast.201), custom_call_target="tpu_custom_call" | custom-call | bytes 31850496 | tf_op jit(solution)/shard_map/reduce_grads/pallas_call | solution.py:340
  400.5 1.5 multiply_reduce_fusion.3
  402.5 2.4 fusion.25
  405.0 3.7 psum.21
  408.9 16.6 %exchange.7 = (f32[16,56,128]{2,1,0:T(8,128)S(1)}, f32[16,8,128]{2,1,0:T(8,128)S(1)}) custom-call(f32[56,128]{1,0:T(8,128)S(1)} %pad.29.refs_0_, f32[16,8,128]{2,1,0:T(8,128)S(1)} %bitcast.191), custom_call_target="tpu_custom_call" | custom-call | tf_op jit(solution)/shard_map/exchange/pallas_call | solution.py:386
  425.7 1.5 fusion.31
  427.2 3.9 all-reduce.7
  431.8 23.8 %finish.1 = (f32[3888,128]{1,0:T(8,128)}, f32[3888,128]{1,0:T(8,128)}, f32[3888,128]{1,0:T(8,128)}, f32[1944,128]{1,0:T(8,128)}, f32[1944,128]{1,0:T(8,128)}, /*...) custom-call(bf16[3,72,2304]{2,1,0:T(8,128)(2,1)} %copy-done, ...), custom_call_target="tpu_custom_call" | custom-call | tf_op jit(solution)/shard_map/finish/pallas_call | solution.py:539
  455.6 1.3 slice.122
  458.3 3.0 copy.172
  461.2 1.4 copy.173
  463.5 1.4 copy.174
  472.7 1.1 copy.183
  475.0 1.1 copy.185
  (346 shorter events, 42.8 us)
Async XLA Ops:
  0.7 13.9 %copy-start.4 = (f32[331776]{0:T(1024)S(1)}, f32[331776]{0:T(1024)}, u32[]{:S(2)}) copy-start(f32[331776]{0:T(1024)} %param.42) | copy-start | bytes 3981316
  11.8 132.7 %copy-start.70 = (s32[16]{0:T(128)}, s32[16]{0:T(128)S(1)}, u32[]{:S(2)}) copy-start(s32[16]{0:T(128)S(1)} %convert_reduce_fusion.5) | copy-start | bytes 196
  21.1 123.1 %copy-start.34 = (f32[73728]{0:T(1024)S(1)}, f32[73728]{0:T(1024)}, u32[]{:S(2)}) copy-start(f32[73728]{0:T(1024)} %param.48) | copy-start | bytes 884740
  21.1 123.3 %copy-start.79 = (bf16[1,1152]{1,0:T(2,128)(2,1)S(1)}, bf16[1,1152]{1,0:T(2,128)(2,1)}, u32[]{:S(2)}) copy-start(bf16[1,1152]{1,0:T(2,128)(2,1)} %param.29) | copy-start | bytes 6916
  144.2 17.4 %copy-start.1 = (f32[497664]{0:T(1024)S(1)}, f32[497664]{0:T(1024)}, u32[]{:S(2)}) copy-start(f32[497664]{0:T(1024)} %param.33) | copy-start | bytes 5971972
  144.5 16.5 %copy-start.91 = (s32[64]{0:T(128)}, s32[64]{0:T(128)S(1)}, u32[]{:S(2)}) copy-start(s32[64]{0:T(128)S(1)} %iota_add_fusion) | copy-start | bytes 772
  161.9 11.1 %slice-start.4 = ((f32[16128]{0:T(1024)}), f32[6912]{0:T(1024)S(1)}, s32[]{:S(2)}) async-start(f32[16128]{0:T(1024)} %copy-done.43), calls=%async_computation.4 | async-start | bytes 57344 | tf_op jit(solution)/shard_map/slice | solution.py:664
  161.9 13.9 %copy-start.98 = (s32[1,128]{1,0:T(1,128)S(1)}, s32[1,128]{1,0:T(1,128)}, u32[]{:S(2)}) copy-start(s32[1,128]{1,0:T(1,128)} %param.32) | copy-start | bytes 1540
  163.2 14.4 %copy-start.49 = (bf16[1,128,1152]{2,1,0:T(8,128)(2,1)S(1)}, bf16[1,128,1152]{2,1,0:T(8,128)(2,1)}, u32[]{:S(2)}) copy-start(bf16[1,128,1152]{2,1,0:T(8,128)(2,1)} %param.27) | copy-start | bytes 884740
  177.8 6.8 %copy-start.75 = (f32[128]{0:T(128)}, f32[128]{0:T(128)S(1)}, u32[]{:S(2)}) copy-start(f32[128]{0:T(128)S(1)} %broadcast_multiply_fusion.1) | copy-start | bytes 1540
  178.0 6.6 %copy-start.93 = (f32[128]{0:T(128)}, f32[128]{0:T(128)S(1)}, u32[]{:S(2)}) copy-start(f32[128]{0:T(128)S(1)} %multiply_reduce_fusion.7) | copy-start | bytes 1540
  178.0 6.6 %copy-start.83 = (f32[128]{0:T(128)}, f32[128]{0:T(128)S(1)}, u32[]{:S(2)}) copy-start(f32[128]{0:T(128)S(1)} %fusion.57) | copy-start | bytes 1540
  192.1 20.4 %collective-permute-start = (f32[128,1152]{1,0:T(8,128)}, f32[128,1152]{1,0:T(8,128)S(1)}, u32[]{:S(2)}, u32[]{:S(2)}) collective-permute-start(f32[128,1152]{1,0:T(8,128)} %constant_dynamic-slice_fusion.3), channel_id=1, source_target_pairs={{0,1},{1,0},{2,3},{3,2},{4,5},{5,4},{6,7},{7,6},{8,9},{9,8},{10,11... | collective-permute-start | bytes 1769480 | tf_op jit(solution)/shard_map/ppermute | solution.py:627
  192.3 10.8 %copy-start.80 = (f32[128]{0:T(128)}, f32[128]{0:T(128)S(1)}, u32[]{:S(2)}) copy-start(f32[128]{0:T(128)S(1)} %fusion.61) | copy-start | bytes 1540
  192.3 8.9 %copy-start.44 = (f32[16128]{0:T(1024)S(1)}, f32[16128]{0:T(1024)}, u32[]{:S(2)}) copy-start(f32[16128]{0:T(1024)} %copy-done.43) | copy-start | bytes 193540
  192.3 9.5 %copy-start.71 = (s32[16]{0:T(128)S(1)}, s32[16]{0:T(128)}, u32[]{:S(2)}) copy-start(s32[16]{0:T(128)} %copy-done.70) | copy-start | bytes 196
  192.3 9.5 %copy-start.92 = (s32[64]{0:T(128)S(1)}, s32[64]{0:T(128)}, u32[]{:S(2)}) copy-start(s32[64]{0:T(128)} %copy-done.91) | copy-start | bytes 772
  192.3 10.8 %copy-start.7 = (bf16[1,128,1152]{2,1,0:T(8,128)(2,1)S(1)}, bf16[1,128,1152]{2,1,0:T(8,128)(2,1)}, u32[]{:S(2)}) copy-start(bf16[1,128,1152]{2,1,0:T(8,128)(2,1)} %param.28) | copy-start | bytes 884740
  192.3 10.8 %copy-start.51 = (f32[1152]{0:T(1024)S(1)}, f32[1152]{0:T(1024)}, u32[]{:S(2)}) copy-start(f32[1152]{0:T(1024)} %get-tuple-element.76) | copy-start | bytes 13828
  205.5 7.0 %copy-start.11 = (bf16[256,1152]{1,0:T(8,128)(2,1)}, bf16[256,1152]{1,0:T(8,128)(2,1)S(1)}, u32[]{:S(2)}) copy-start(bf16[256,1152]{1,0:T(8,128)(2,1)S(1)} %all_gather.18) | copy-start | bytes 1769476
  213.3 8.5 %slice-start.2 = ((s8[5308416]{0:T(1024)(128)(4,1)}), s8[4194304]{0:T(1024)(128)(4,1)S(1)}, s32[]{:S(2)}) async-start(s8[5308416]{0:T(1024)(128)(4,1)} %bitcast.207), calls=%async_computation.2 | async-start | bytes 8388608
  213.3 14.1 %slice-start = ((s8[5308416]{0:T(1024)(128)(4,1)}), s8[4194304]{0:T(1024)(128)(4,1)S(1)}, s32[]{:S(2)}) async-start(s8[5308416]{0:T(1024)(128)(4,1)} %bitcast.203), calls=%async_computation | async-start | bytes 8388608
  216.1 5.7 %slice-start.3 = ((s8[5308416]{0:T(1024)(128)(4,1)}), s8[1114112]{0:T(1024)(128)(4,1)S(1)}, s32[]{:S(2)}) async-start(s8[5308416]{0:T(1024)(128)(4,1)} %bitcast.207), calls=%async_computation.3 | async-start | bytes 2228224
  216.2 11.3 %slice-start.1 = ((s8[5308416]{0:T(1024)(128)(4,1)}), s8[1114112]{0:T(1024)(128)(4,1)S(1)}, s32[]{:S(2)}) async-start(s8[5308416]{0:T(1024)(128)(4,1)} %bitcast.203), calls=%async_computation.1 | async-start | bytes 2228224
  221.8 5.7 %copy-start.99 = (f32[256,2304]{1,0:T(8,128)}, f32[256,2304]{1,0:T(8,128)S(1)}, u32[]{:S(2)}) copy-start(f32[256,2304]{1,0:T(8,128)S(1)} %get-tuple-element.117) | copy-start | bytes 7077892
  223.6 6.0 %copy-start.32 = (f32[256,1152]{1,0:T(8,128)}, f32[256,1152]{1,0:T(8,128)S(1)}, u32[]{:S(2)}) copy-start(f32[256,1152]{1,0:T(8,128)S(1)} %fusion.73) | copy-start | bytes 3538948
  230.5 9.4 %collective-permute-start.2 = (f32[128,1152]{1,0:T(8,128)}, f32[128,1152]{1,0:T(8,128)}, u32[]{:S(2)}, u32[]{:S(2)}) collective-permute-start(f32[128,1152]{1,0:T(8,128)} %constant_dynamic-slice_fusion.1), channel_id=1, source_target_pairs={{0,1},{1,0},{2,3},{3,2},{4,5},{5,4},{6,7},{7,6},{8,9},{9,8},{10,11... | collective-permute-start | bytes 1769480 | tf_op jit(solution)/shard_map/ppermute | solution.py:627
  231.7 170.7 %collective-permute-start.1 = (f32[128,1152]{1,0:T(8,128)}, f32[128,1152]{1,0:T(8,128)}, u32[]{:S(2)}, u32[]{:S(2)}) collective-permute-start(f32[128,1152]{1,0:T(8,128)} %constant_dynamic-slice_fusion.2), channel_id=1, source_target_pairs={{0,1},{1,0},{2,3},{3,2},{4,5},{5,4},{6,7},{7,6},{8,9},{9,8},{10,11... | collective-permute-start | bytes 1769480 | tf_op jit(solution)/shard_map/ppermute | solution.py:627
  234.1 5.8 %copy-start.33 = (f32[256,1152]{1,0:T(8,128)S(1)}, f32[256,1152]{1,0:T(8,128)}, u32[]{:S(2)}) copy-start(f32[256,1152]{1,0:T(8,128)} %copy-done.32) | copy-start | bytes 3538948
  234.1 5.8 %copy-start.78 = (f32[128]{0:T(128)S(1)}, f32[128]{0:T(128)}, u32[]{:S(2)}) copy-start(f32[128]{0:T(128)} %copy-done.77) | copy-start | bytes 1540
  234.1 5.8 %copy-start.86 = (f32[128]{0:T(128)S(1)}, f32[128]{0:T(128)}, u32[]{:S(2)}) copy-start(f32[128]{0:T(128)} %copy-done.85) | copy-start | bytes 1540
  259.7 140.7 %collective-permute-start.3 = (f32[128,1152]{1,0:T(8,128)}, f32[128,1152]{1,0:T(8,128)}, u32[]{:S(2)}, u32[]{:S(2)}) collective-permute-start(f32[128,1152]{1,0:T(8,128)} %constant_dynamic-slice_fusion), channel_id=1, source_target_pairs={{0,1},{1,0},{2,3},{3,2},{4,5},{5,4},{6,7},{7,6},{8,9},{9,8},{10,11... | collective-permute-start | bytes 1769480 | tf_op jit(solution)/shard_map/ppermute | solution.py:627
  261.2 7.8 %copy-start.63 = (f32[1152]{0:T(1024)S(1)}, f32[1152]{0:T(1024)}, u32[]{:S(2)}) copy-start(f32[1152]{0:T(1024)} %get-tuple-element.66) | copy-start | bytes 13828
  276.9 123.1 %copy-start.3 = (bf16[256,1152]{1,0:T(8,128)(2,1)S(1)}, bf16[256,1152]{1,0:T(8,128)(2,1)}, u32[]{:S(2)}) copy-start(bf16[256,1152]{1,0:T(8,128)(2,1)} %copy-done.2) | copy-start | bytes 1769476
  276.9 123.3 %copy-start.64 = (f32[1728]{0:T(1024)S(1)}, f32[1728]{0:T(1024)}, u32[]{:S(2)}) copy-start(f32[1728]{0:T(1024)} %convert_reduce_fusion.1) | copy-start | bytes 20740
  276.9 123.6 %copy-start.31 = (f32[256,1152]{1,0:T(8,128)S(1)}, f32[256,1152]{1,0:T(8,128)}, u32[]{:S(2)}) copy-start(f32[256,1152]{1,0:T(8,128)} %copy-done.30) | copy-start | bytes 3538948
  276.9 123.6 %copy-start.76 = (f32[128]{0:T(128)S(1)}, f32[128]{0:T(128)}, u32[]{:S(2)}) copy-start(f32[128]{0:T(128)} %copy-done.75) | copy-start | bytes 1540
  276.9 123.6 %copy-start.84 = (f32[128]{0:T(128)S(1)}, f32[128]{0:T(128)}, u32[]{:S(2)}) copy-start(f32[128]{0:T(128)} %copy-done.83) | copy-start | bytes 1540
  402.5 6.2 %copy-start.59 = (f32[16128]{0:T(1024)S(1)}, f32[16128]{0:T(1024)}, u32[]{:S(2)}) copy-start(f32[16128]{0:T(1024)} %custom-call) | copy-start | bytes 193540
  402.5 6.2 %copy-start.50 = (f32[4608]{0:T(1024)S(1)}, f32[4608]{0:T(1024)}, u32[]{:S(2)}) copy-start(f32[4608]{0:T(1024)} %dynamic_update_slice.11) | copy-start | bytes 55300
  402.5 6.3 %copy-start.62 = (f32[1152]{0:T(1024)S(1)}, f32[1152]{0:T(1024)}, u32[]{:S(2)}) copy-start(f32[1152]{0:T(1024)} %convert_reduce_fusion.2) | copy-start | bytes 13828
  404.9 26.2 %copy-start.58 = (f32[16,128]{1,0:T(8,128)S(1)}, f32[16,128]{1,0:T(8,128)}, u32[]{:S(2)}) copy-start(f32[16,128]{1,0:T(8,128)} %copy-done.57) | copy-start | bytes 24580
  425.6 6.1 %copy-start.17 = (bf16[2,8,54,128]{3,1,2,0:T(8,128)(2,1)}, bf16[2,8,54,128]{3,1,2,0:T(8,128)(2,1)S(1)}, u32[]{:S(2)}) copy-start(bf16[2,8,54,128]{3,1,2,0:T(8,128)(2,1)S(1)} %copy.132) | copy-start | bytes 663556
  431.7 25.9 %copy-start.68 = (f32[8,128]{1,0:T(8,128)S(1)}, f32[8,128]{1,0:T(8,128)}, u32[]{:S(2)}) copy-start(f32[8,128]{1,0:T(8,128)} %get-tuple-element.81.refs_4_) | copy-start | bytes 12292
  431.7 25.9 %copy-start.69 = (f32[1008]{0:T(1024)S(1)}, f32[1008]{0:T(1024)}, u32[]{:S(2)}) copy-start(f32[1008]{0:T(1024)} %param.51) | copy-start | bytes 12100
  431.7 25.9 %copy-start.87 = (f32[1008]{0:T(1024)S(1)}, f32[1008]{0:T(1024)}, u32[]{:S(2)}) copy-start(f32[1008]{0:T(1024)} %param.53) | copy-start | bytes 12100
  431.7 25.9 %copy-start.88 = (f32[1008]{0:T(1024)S(1)}, f32[1008]{0:T(1024)}, u32[]{:S(2)}) copy-start(f32[1008]{0:T(1024)} %param.52) | copy-start | bytes 12100
  455.6 5.6 %copy-start.16 = (f32[3888,128]{1,0:T(8,128)S(1)}, f32[3888,128]{1,0:T(8,128)}, u32[]{:S(2)}) copy-start(f32[3888,128]{1,0:T(8,128)} %get-tuple-element.49) | copy-start | bytes 5971972
  (61 other events, 148.4 us)

commit v3 on v2

--- a/solution.py
+++ b/solution.py
@@ -178,175 +178,411 @@
     )(src)
 
 
-def reduce_kernel(line, *refs):
-    count = len(refs) - 1 - 16 - 7
-    grads = refs[:count]
-    out = refs[count]
-    s = count + 1
-    acc, got_b, got_z, got_a = (refs[s + 4 * i:s + 4 * i + 4] for i in range(4))
-    load, send_b, send_z, send_a, recv_b, recv_z, recv_a = refs[s + 16:]
-    me = Place(line)
-    x, y, z = me.x, me.y, me.z
-    up, down = z < line - 1, z > 0
-    above, below = me.dev(z=jnp.minimum(z + 1, line - 1)), me.dev(z=jnp.maximum(z - 1, 0))
-
-    def cols(g):
-        return pl.ds(GROUPS[g][0], GROUPS[g][1])
-
-    def last(g):
+class Reducer:
+    def __init__(self, line, grads, out, own, got_b, got_z, got_a, sems):
+        self.line, self.grads, self.out = line, grads, out
+        self.own, self.acc, self.got_z, self.got_a = own, got_b, got_z, got_a
+        self.load, self.send_b, self.send_z, self.send_a, self.recv_b, self.recv_z, self.recv_a = sems
+        self.me = me = Place(line)
+        self.up, self.down = me.z < line - 1, me.z > 0
+        self.above, self.below = me.dev(z=jnp.minimum(me.z + 1, line - 1)), me.dev(z=jnp.maximum(me.z - 1, 0))
+        self.units = len(grads) * line
+
+    def last(self, g):
         return "y" if GROUPS[g][3] == "x" else "x"
 
-    def half(grad, g, zz, mine):
-        if last(g) == "y":
-            return grad.at[zz, y if mine else 1 - y, :, :, cols(g)]
-        return grad.at[zz, :, x if mine else 1 - x, :, cols(g)]
-
-    def first(g):
-        return x if GROUPS[g][3] == "x" else y
-
-    def loading(m, g, zz, grad=grads[0]):
-        return pltpu.make_async_copy(half(grad, g, zz, True), acc[g].at[m, zz], load.at[m, g, zz])
-
-    def remote(src, dst, send, recv, dev):
+    def first(self, g):
+        return self.me.x if GROUPS[g][3] == "x" else self.me.y
+
+    def half(self, grad, g, zz, mine):
+        cols = pl.ds(GROUPS[g][0], GROUPS[g][1])
+        if self.last(g) == "y":
+            return grad.at[zz, self.me.y if mine else 1 - self.me.y, :, :, cols]
+        return grad.at[zz, :, self.me.x if mine else 1 - self.me.x, :, cols]
+
+    def loading(self, u, g, zz, side, grad=None):
+        grad = self.grads[0] if grad is None else grad
+        return pltpu.make_async_copy(
+            self.half(grad, g, zz, True), self.own[g].at[u % 3, side], self.load.at[u % 3, g, side])
+
+    def remote(self, src, dst, send, recv, dev):
         return pltpu.make_async_remote_copy(
             src_ref=src, dst_ref=dst, send_sem=send, recv_sem=recv, device_id=dev, device_id_type=MESH)
 
-    def b_copy(m, g, zz, grad=grads[0]):
-        return remote(half(grad, g, zz, False), got_b[g].at[m, zz], send_b.at[m, g, zz], recv_b.at[m, g, zz], me.peer(last(g)))
-
-    def a_copy(m, g, zz):
-        return remote(acc[g].at[m, zz, 1 - first(g)], got_a[g].at[m, zz], send_a.at[m, g, zz], recv_a.at[m, g, zz], me.peer(GROUPS[g][3]))
-
-    def z_copy(m, g, zz, slot, dev):
-        part = acc[g].at[m, zz] if GROUPS[g][2] == 0 else acc[g].at[m, zz, first(g)]
-        return remote(part, got_z[g].at[m, slot], send_z.at[m, g, zz], recv_z.at[m, g, slot], dev)
-
-    def add_b(m, g, zz):
-        loading(m, g, zz).wait()
-        b_copy(m, g, zz).wait_recv()
-        acc[g][m, zz] = acc[g][m, zz] + got_b[g][m, zz]
-
-    def add_z(m, g, zz, slot):
-        z_copy(m, g, z, slot, below).wait_recv()
+    def b_copy(self, m, g, zz, grad=None):
+        grad = self.grads[0] if grad is None else grad
+        return self.remote(
+            self.half(grad, g, zz, False), self.acc[g].at[m, zz], self.send_b.at[m, g, zz], self.recv_b.at[m, g, zz],
+            self.me.peer(self.last(g)))
+
+    def slot_a(self, g, zz):
+        return zz if GROUPS[g][2] == 1 else 0
+
+    def a_copy(self, m, g, zz):
+        return self.remote(
+            self.acc[g].at[m, zz, 1 - self.first(g)], self.got_a[g].at[m, self.slot_a(g, zz)], self.send_a.at[m, g, zz],
+            self.recv_a.at[m, g, zz], self.me.peer(GROUPS[g][3]))
+
+    def z_copy(self, m, g, zz, slot, dev):
+        part = self.acc[g].at[m, zz] if GROUPS[g][2] == 0 else self.acc[g].at[m, zz, self.first(g)]
+        return self.remote(part, self.got_z[g].at[m, slot], self.send_z.at[m, g, zz], self.recv_z.at[m, g, slot], dev)
+
+    def add_b(self, m, g, zz, u, side):
+        self.loading(u, g, zz, side).wait()
+        self.b_copy(m, g, zz).wait_recv()
+        self.acc[g][m, zz] = self.acc[g][m, zz] + self.own[g][u % 3, side]
+
+    def add_z(self, m, g, zz, slot):
+        acc, got = self.acc[g], self.got_z[g]
+        self.z_copy(m, g, self.me.z, slot, self.below).wait_recv()
         if GROUPS[g][2] == 0:
-            acc[g][m, zz] = acc[g][m, zz] + got_z[g][m, slot]
+            acc[m, zz] = acc[m, zz] + got[m, slot]
         else:
-            acc[g][m, zz, first(g)] = acc[g][m, zz, first(g)] + got_z[g][m, slot]
-
-    def add_a(m, g, zz):
-        a_copy(m, g, zz).wait_recv()
-        acc[g][m, zz, first(g)] = acc[g][m, zz, first(g)] + got_a[g][m, zz]
-
-    def planes(k, fn):
+            acc[m, zz, self.first(g)] = acc[m, zz, self.first(g)] + got[m, slot]
+
+    def add_a(self, m, g, zz):
+        self.a_copy(m, g, zz).wait_recv()
+        acc, first = self.acc[g], self.first(g)
+        acc[m, zz, first] = acc[m, zz, first] + self.got_a[g][m, self.slot_a(g, zz)]
+
+    def planes(self, k, fn):
+        z, line = self.me.z, self.line
         when(z + k < line, lambda: fn(jnp.minimum(z + k, line - 1), True))
         when((z >= k) & (k > 0), lambda: fn(jnp.maximum(z - k, 0), False))
 
-    def begin(m, j):
-        def one(grad, zz):
+    def begin(self, v):
+        m, j = v // self.line, v % self.line
+
+        def one(grad, zz, upward):
             for g in range(4):
-                b_copy(m, g, zz, grad).start()
-                loading(m, g, zz, grad).start()
-
-        for index, grad in enumerate(grads):
-            when(m == index, lambda: planes(line - 1 - j, lambda zz, upward: one(grad, zz)))
-
-    def onward(m, g, zz, k, upward):
+                self.b_copy(m, g, zz, grad).start()
+                self.loading(v, g, zz, 0 if upward else 1, grad).start()
+
+        for index, grad in enumerate(self.grads):
+            when(m == index, lambda: self.planes(self.line - 1 - j, lambda zz, upward: one(grad, zz, upward)))
+
+    def onward(self, m, g, zz, k, upward):
         if upward:
-            when(down, lambda: add_z(m, g, zz, zz))
-            z_copy(m, g, zz, zz, above).start()
+            when(self.down, lambda: self.add_z(m, g, zz, zz))
+            self.z_copy(m, g, zz, zz, self.above).start()
         else:
-            when(up, lambda: add_z(m, g, zz, zz))
-            z_copy(m, g, zz, jnp.where(k == 1, line, zz), below).start()
-
-    def near(m, j):
-        k = line - 1 - j
+            when(self.up, lambda: self.add_z(m, g, zz, zz))
+            self.z_copy(m, g, zz, jnp.where(k == 1, self.line, zz), self.below).start()
+
+    def near(self, u, m, j):
+        k = self.line - 1 - j
 
         def one(zz, upward):
             for g in range(4):
-                add_b(m, g, zz)
+                self.add_b(m, g, zz, u, 0 if upward else 1)
                 if GROUPS[g][2] == 1:
-                    a_copy(m, g, zz).start()
+                    self.a_copy(m, g, zz).start()
                 else:
-                    when(k > 0, lambda g=g: onward(m, g, zz, k, upward))
-
-        planes(k, one)
-
-    def far(m, j):
-        k = line - j
+                    when(k > 0, lambda g=g: self.onward(m, g, zz, k, upward))
+
+        self.planes(k, one)
+
+    def far(self, m, j):
+        k = self.line - j
 
         def one(zz, upward):
             for g in (2, 3):
-                add_a(m, g, zz)
-                onward(m, g, zz, k, upward)
-
-        when((k > 0) & (k < line), lambda: planes(k, one))
-
-    def close(m):
+                self.add_a(m, g, zz)
+                self.onward(m, g, zz, k, upward)
+
+        when((k > 0) & (k < self.line), lambda: self.planes(k, one))
+
+    def close(self, m):
+        z = self.me.z
         for g in (0, 1):
-            when(down, lambda g=g: add_z(m, g, z, z))
-            when(up, lambda g=g: add_z(m, g, z, line))
-            a_copy(m, g, z).start()
-
-    def final(m):
-        for g in (2, 3):
-            add_a(m, g, z)
-            when(down, lambda g=g: add_z(m, g, z, z))
-            when(up, lambda g=g: add_z(m, g, z, line))
-            out[m, :, cols(g)] = acc[g][m, z, first(g)]
-        for g in (0, 1):
-            a_copy(m, g, z).wait_recv()
-            out[m, :, cols(g)] = acc[g][m, z, first(g)] + got_a[g][m, z]
-
-    me.barrier()
-    begin(0, 0)
-    if line > 1:
-        begin(0, 1)
-    units = count * line
-
-    @pl.loop(0, units)
+            when(self.down, lambda g=g: self.add_z(m, g, z, z))
+            when(self.up, lambda g=g: self.add_z(m, g, z, self.line))
+            self.a_copy(m, g, z).start()
+
+    def final(self, m):
+        z = self.me.z
+        for g in range(4):
+            cols = pl.ds(GROUPS[g][0], GROUPS[g][1])
+            self.add_a(m, g, z)
+            if GROUPS[g][2] == 1:
+                when(self.down, lambda g=g: self.add_z(m, g, z, z))
+                when(self.up, lambda g=g: self.add_z(m, g, z, self.line))
+            self.out[m, :, cols] = self.acc[g][m, z, self.first(g)]
+
+    def unit(self, u):
+        line = self.line
+        m, j = u // line, u % line
+        when(u + 2 < self.units, lambda: self.begin(jnp.minimum(u + 2, self.units - 1)))
+        self.near(u, m, j)
+        self.far(m, j)
+        when(j == line - 1, lambda: self.close(m))
+        when((j == 0) & (m > 0), lambda: self.final(jnp.maximum(m - 1, 0)))
+
+    def drain(self):
+        z = self.me.z
+
+        @pl.loop(0, len(self.grads))
+        def _(m):
+            @pl.loop(0, self.line)
+            def _(zz):
+                for g in range(4):
+                    self.b_copy(m, g, zz).wait_send()
+                    if GROUPS[g][2] == 1:
+                        self.a_copy(m, g, zz).wait_send()
+                    when(zz != z, lambda g=g: self.z_copy(m, g, zz, zz, self.above).wait_send())
+            for g in (0, 1):
+                self.a_copy(m, g, z).wait_send()
+
+
+def reducer_scratch(count, line, rows, dt):
+    dma = pltpu.SemaphoreType.DMA
+    own = [pltpu.VMEM((3, 2, 2, rows, GROUPS[g][1]), dt) for g in range(4)]
+    got_b = [pltpu.VMEM((count, line, 2, rows, GROUPS[g][1]), dt) for g in range(4)]
+    got_z = [pltpu.VMEM((count, line + 1) + ((2,) if GROUPS[g][2] == 0 else ()) + (rows, GROUPS[g][1]), dt) for g in range(4)]
+    got_a = [pltpu.VMEM((count, line if GROUPS[g][2] == 1 else 1, rows, GROUPS[g][1]), dt) for g in range(4)]
+    sems = [dma((3, 4, 2))] + [dma((count, 4, line))] * 4 + [dma((count, 4, line + 1))] + [dma((count, 4, line))]
+    return own + got_b + got_z + got_a + sems
+
+
+def make_reducer(line, grads, out, refs):
+    return Reducer(line, grads, out, refs[:4], refs[4:8], refs[8:12], refs[12:16], refs[16:])
+
+
+def dot(left, right, a=1, b=0):
+    return lax.dot_general(left, right, (((a,), (b,)), ((), ())), preferred_element_type=jnp.float32)
+
+
+def backward_kernel(line, *refs):
+    (g_contract, g_expand, weight, pair_t, d_att, q, k, v, o, key_ok, x, d_mid, scale_a, d_pieces, v_rows, modulation, cond,
+     out, tokens_grad, d_mod_all, d_cond, bias_sum) = refs[:22]
+    (w, grads, rhs, d_o, d_q, d_k, d_v, d_h, d_h_got, dp, dp_got, msg, msg_got, vec, vec_got, d_silu, d_silu_got, chunk,
+     w_sem, pair_send, pair_recv, msg_send, msg_recv, vec_send, vec_recv) = refs[22:47]
+    n = line * 4
+    low = jnp.bfloat16
+    me, c = lax.axis_index("dp"), lax.axis_index("seq")
+    red = make_reducer(line, (g_contract, g_expand, grads), out, refs[47:])
+    rows, width = x.shape
+    half = weight.shape[1] // 4
+    heads = half // HEAD_DIM
+    edge = 3 * half // 128 * 128
+    partner = (me, 1 - c)
+
+    def swap(i, src, dst):
+        return pltpu.make_async_remote_copy(
+            src_ref=src, dst_ref=dst, send_sem=pair_send.at[i], recv_sem=pair_recv.at[i], device_id=partner, device_id_type=MESH)
+
+    def to_all(src, dst, send, recv, spread):
+        def copy(j, there, slot):
+            return pltpu.make_async_remote_copy(
+                src_ref=src.at[there] if spread else src, dst_ref=dst.at[slot], send_sem=send.at[j], recv_sem=recv.at[slot],
+                device_id=(there, c), device_id_type=MESH)
+
+        def start():
+            @pl.loop(1, n)
+            def _(j):
+                copy(j, (me + j) % n, me).start()
+
+        def wait():
+            @pl.loop(1, n)
+            def _(j):
+                copy(j, (me + j) % n, (me + n - j) % n).wait()
+
+        return start, wait
+
+    w_copy = pltpu.make_async_copy(weight, w, w_sem)
+    w_copy.start()
+    bar = pltpu.get_barrier_semaphore()
+    pl.semaphore_signal(bar, inc=1, device_id=partner, device_id_type=MESH)
+
+    @pl.loop(1, n)
+    def _(j):
+        pl.semaphore_signal(bar, inc=1, device_id=((me + j) % n, c), device_id_type=MESH)
+
+    pl.semaphore_wait(bar, n)
+    red.begin(0)
+    red.begin(1)
+
+    w_copy.wait()
+    d_o[:, :half] = dot(d_att[...], w[:, edge:])[:, 3 * half - edge :].astype(low)
+    d_o[:, half:] = jnp.zeros((2 * rows, d_o.shape[1] - half), low)
+    for item in (d_q, d_k, d_v):
+        item[...] = jnp.zeros_like(item)
+
+    seen = jnp.broadcast_to(key_ok[...], (2 * rows, 2 * rows)) > 0.0
+
+    def head(h):
+        lo = pl.multiple_of(h * HEAD_DIM // 128 * 128, 128)
+        win = pl.ds(lo, 256)
+        lane = lax.broadcasted_iota(jnp.int32, (1, 256), 1) + lo - h * HEAD_DIM
+        mine = ((lane >= 0) & (lane < HEAD_DIM)).astype(low)
+        qh, kh, doh = q[:, win] * mine, k[:, win] * mine, d_o[:, win] * mine
+        logits = jnp.where(seen, dot(qh, kh, 1, 1) * HEAD_DIM ** (-0.5), MASK_FILL)
+        expo = jnp.exp(logits - jnp.max(logits, axis=-1, keepdims=True))
+        probs = expo / jnp.sum(expo, axis=-1, keepdims=True)
+        d_probs = dot(doh, v[:, win], 1, 1)
+        inner = jnp.sum(probs * d_probs, axis=-1, keepdims=True)
+        d_logits = (probs * (d_probs - inner)).astype(low)
+        d_q[:, win] = d_q[:, win] + dot(d_logits, kh) * HEAD_DIM ** (-0.5)
+        d_k[:, win] = d_k[:, win] + dot(d_logits, qh, 0, 0) * HEAD_DIM ** (-0.5)
+        d_v[:, win] = d_v[:, win] + dot(probs.astype(low), doh, 0, 0)
+
+    def weight_grads():
+        for i, item in enumerate((d_q, d_k, d_v)):
+            rhs[: 2 * rows, i * half : (i + 1) * half] = item[:, :half].astype(low)
+        rhs[: 2 * rows, 3 * half :] = jnp.zeros((2 * rows, half), low)
+        rhs[2 * rows :, edge : 3 * half] = jnp.zeros((2 * rows, 3 * half - edge), low)
+        rhs[2 * rows :, 3 * half :] = o[:, :half]
+        vec[0:1, :half] = jnp.sum(rhs[: 2 * rows, :half].astype(jnp.float32), axis=0, keepdims=True)
+        vec[0:1, half:] = jnp.sum(rhs[: 2 * rows, 2 * half : 3 * half].astype(jnp.float32), axis=0, keepdims=True)
+        vec[1:] = v_rows[1:]
+
+        @pl.loop(0, n)
+        def _(i):
+            block = grads.at[i // 4, i // 2 % 2, i % 2]
+            block[:, :edge] = dot(pair_t[i, :, : 2 * rows], rhs[: 2 * rows, :edge]).astype(low)
+            block[:, edge:] = dot(pair_t[i], rhs[:, edge:]).astype(low)
+
+    def input_grad():
+        @pl.loop(0, width // 128)
+        def _(t):
+            cols = pl.ds(pl.multiple_of(t * 128, 128), 128)
+            part = dot(rhs[: 2 * rows, : edge + 128], w[cols, : edge + 128], 1, 1)
+            d_h[0, :, cols] = part[:rows]
+            d_h[1, :, cols] = part[rows:]
+
+        swap(0, d_h.at[1 - c], d_h_got).start()
+
+    def norm_grad():
+        swap(0, d_h.at[1 - c], d_h_got).wait()
+        d_n = d_h[c] + d_h_got[...]
+        centre = x[...] - jnp.mean(x[...], axis=-1, keepdims=True)
+        inv = lax.rsqrt(jnp.mean(centre * centre, axis=-1, keepdims=True) + LAYER_EPS)
+        normed = centre * inv
+        e = d_n * (1.0 + scale_a[...])
+        d_x = (e - jnp.mean(e, axis=-1, keepdims=True) - normed * jnp.mean(e * normed, axis=-1, keepdims=True)) * inv
+        tokens_grad[...] = (d_x + d_mid[...]).astype(low)
+        dp[...] = d_pieces[...]
+        dp[0:1] = jnp.sum(d_n, axis=0, keepdims=True)
+        dp[1:2] = jnp.sum(d_n * normed, axis=0, keepdims=True)
+        swap(1, dp, dp_got).start()
+
+    msg_start, msg_wait = to_all(msg, msg_got, msg_send, msg_recv, False)
+    vec_start, vec_wait = to_all(chunk, vec_got, vec_send, vec_recv, True)
+    per = chunk_tiles(n, width)
+
+    def send_mod():
+        swap(1, dp, dp_got).wait()
+        d_mod = (dp[...] + dp_got[...]).astype(low).astype(jnp.float32)
+        own = jnp.where(c == 0, d_mod[0:3], d_mod[3:6])
+        for r in range(3):
+            msg[r] = own[r : r + 1]
+        msg_got[me] = msg[...]
+        chunk[...] = jnp.zeros_like(chunk)
+        tiles = width // 128
+        for t in range(5 * tiles):
+            chunk[t // per, t % per] = vec[t // tiles : t // tiles + 1, t % tiles * 128 : t % tiles * 128 + 128]
+        vec_got[me] = chunk[me]
+        msg_start()
+        vec_start()
+
+    def mod_grad():
+        msg_wait()
+        vec_wait()
+
+        @pl.loop(0, n)
+        def _(s):
+            for r in range(3):
+                d_mod_all[c, pl.ds(s, 1), r * width : (r + 1) * width] = msg_got[s, r]
+
+        bias_sum[c] = jnp.zeros((8, 128), jnp.float32)
+        for r in range(per):
+            bias_sum[c, r : r + 1] = jnp.sum(vec_got[:, r], axis=0)
+        d_silu[...] = dot(d_mod_all[c].astype(low), modulation[...], 1, 1)
+        swap(2, d_silu, d_silu_got).start()
+        swap(3, d_mod_all.at[c], d_mod_all.at[c]).start()
+        swap(4, bias_sum.at[c], bias_sum.at[c]).start()
+
+    def cond_grad():
+        swap(2, d_silu, d_silu_got).wait()
+        swap(3, d_mod_all.at[c], d_mod_all.at[c]).wait()
+        swap(4, bias_sum.at[c], bias_sum.at[c]).wait()
+        gate = 1.0 / (1.0 + jnp.exp(-cond[...]))
+        d_cond[...] = (d_silu[...] + d_silu_got[...]) * (gate + cond[...] * gate * (1.0 - gate))
+
+    steps = (weight_grads, input_grad, norm_grad, send_mod, mod_grad, cond_grad)
+
+    @pl.loop(0, red.units)
     def _(u):
-        m, j = u // line, u % line
-        v = u + 2
-        when(v < units, lambda: begin(jnp.minimum(v // line, count - 1), v % line))
-        near(m, j)
-        far(m, j)
-        when(j == line - 1, lambda: close(m))
-        when((j == 0) & (m > 0), lambda: final(jnp.maximum(m - 1, 0)))
-
-    final(count - 1)
-
-    @pl.loop(0, count)
-    def _(m):
-        @pl.loop(0, line)
-        def _(zz):
-            for g in range(4):
-                b_copy(m, g, zz).wait_send()
-                if GROUPS[g][2] == 1:
-                    a_copy(m, g, zz).wait_send()
-                when(zz != z, lambda g=g: z_copy(m, g, zz, zz, above).wait_send())
-        for g in (0, 1):
-            a_copy(m, g, z).wait_send()
-
-
-def reduce_grads(grads, n, collective_id):
+        @pl.loop(0, jnp.where(u < heads // 2, 2, 0))
+        def _(i):
+            head(2 * u + i)
+
+        red.unit(u)
+        for i, step in enumerate(steps):
+            when(u == heads // 2 - 1 + i, step)
+
+    red.final(2)
+    red.drain()
+
+
+def chunk_tiles(n, width):
+    return -(-5 * (width // 128) // n)
+
+
+def backward(hbm_args, vmem_args, n, collective_id):
     line = n // 4
-    count = len(grads)
-    rows, cols = grads[0].shape[-2:]
-    dt = grads[0].dtype
+    grad = hbm_args[0]
+    rows, cols = grad.shape[-2:]
+    pair_t, d_att, q = vmem_args[0], vmem_args[1], vmem_args[2]
+    all_rows, width = d_att.shape
+    low, f32 = jnp.bfloat16, jnp.float32
     dma = pltpu.SemaphoreType.DMA
-    acc = [pltpu.VMEM((count, line, 2, rows, GROUPS[g][1]), dt) for g in range(4)]
-    got_z = [pltpu.VMEM((count, line + 1) + ((2,) if GROUPS[g][2] == 0 else ()) + (rows, GROUPS[g][1]), dt) for g in range(4)]
-    got_a = [pltpu.VMEM((count, line, rows, GROUPS[g][1]), dt) for g in range(4)]
+    vmem, hbm = pl.BlockSpec(memory_space=pltpu.VMEM), pl.BlockSpec(memory_space=pltpu.HBM)
+    wide = q.shape
+    per = chunk_tiles(n, width)
     return pl.pallas_call(
-        functools.partial(reduce_kernel, line),
-        out_shape=jax.ShapeDtypeStruct((count, rows, cols), dt),
-        in_specs=[pl.BlockSpec(memory_space=pltpu.HBM)] * count,
-        out_specs=pl.BlockSpec(memory_space=pltpu.VMEM),
-        scratch_shapes=acc + acc + got_z + got_a + [dma((count, 4, line))] * 5 + [dma((count, 4, line + 1))] + [dma((count, 4, line))],
-        compiler_params=pltpu.CompilerParams(collective_id=collective_id, has_side_effects=True, vmem_limit_bytes=48 * 2**20),
-        cost_estimate=pl.CostEstimate(flops=0, bytes_accessed=2 * count * n * rows * cols * 2, transcendentals=0),
-        name="reduce_grads",
-    )(*grads)
+        functools.partial(backward_kernel, line),
+        out_shape=[
+            jax.ShapeDtypeStruct((3, rows, cols), low),
+            jax.ShapeDtypeStruct((all_rows // 2, width), low),
+            jax.ShapeDtypeStruct((2, n, 3 * width), f32),
+            jax.ShapeDtypeStruct((n, 128), f32),
+            jax.ShapeDtypeStruct((2, 8, 128), f32),
+        ],
+        in_specs=[hbm] * len(hbm_args) + [vmem] * len(vmem_args),
+        out_specs=[vmem] * 5,
+        scratch_shapes=[
+            pltpu.VMEM((width, cols), low),
+            pltpu.VMEM((line, 2, 2, rows, cols), low),
+            pltpu.VMEM((2 * all_rows, cols), low),
+            pltpu.VMEM(wide, low),
+            pltpu.VMEM(wide, f32),
+            pltpu.VMEM(wide, f32),
+            pltpu.VMEM(wide, f32),
+            pltpu.VMEM((2, all_rows // 2, width), f32),
+            pltpu.VMEM((all_rows // 2, width), f32),
+            pltpu.VMEM((8, width), f32),
+            pltpu.VMEM((8, width), f32),
+            pltpu.VMEM((3, 1, width), f32),
+            pltpu.VMEM((n, 3, 1, width), f32),
+            pltpu.VMEM((8, width), f32),
+            pltpu.VMEM((n, per, 1, 128), f32),
+            pltpu.VMEM((n, 128), f32),
+            pltpu.VMEM((n, 128), f32),
+            pltpu.VMEM((n, per, 1, 128), f32),
+            dma,
+            dma((5,)),
+            dma((5,)),
+            dma((n,)),
+            dma((n,)),
+            dma((n,)),
+            dma((n,)),
+        ]
+        + reducer_scratch(3, line, rows, low),
+        compiler_params=pltpu.CompilerParams(
+            collective_id=collective_id, has_side_effects=True, vmem_limit_bytes=63 * 2**20),
+        name="backward",
+    )(*hbm_args, *vmem_args)
 
 
 def exchange_kernel(n, spread, *refs):
@@ -410,28 +646,14 @@
     return sizes[-1] if sizes else rows
 
 
-def finish_kernel(n, rates, *refs):
-    kinds = len(rates)
-    reduced, silu, d_mod, d_cond, bias_grad, onehot, same = refs[:7]
-    states = [refs[7 + 3 * a : 10 + 3 * a] for a in range(kinds)]
-    at = 7 + 3 * kinds
-    news = [refs[at + 3 * a : at + 3 * a + 3] for a in range(kinds)]
-    at += 3 * kinds
-    norm_out, at = refs[at], at + 1
-    held = refs[at : at + kinds]
-    flat = refs[at + kinds : at + 2 * kinds]
-    both, wide, block, got, in_sem, out_sem, pair_send, pair_recv, send, recv = refs[at + 2 * kinds :]
+def norm_kernel(n, *refs):
+    reduced, silu, d_mod, d_cond, bias_sum, onehot, same = refs[:7]
+    flat, factor_out, norm_out, bias_out = refs[7:13], refs[13], refs[14], refs[15]
+    both, wide, block, got, pair_send, pair_recv, send, recv = refs[16:]
     me, c = lax.axis_index("dp"), lax.axis_index("seq")
     rows = reduced.shape[1]
     half = reduced.shape[2]
     head = half // 4
-
-    def loads(a, k):
-        return pltpu.make_async_copy(states[a][k], held[a].at[k], in_sem.at[a, k])
-
-    for a in range(kinds):
-        for k in range(3):
-            loads(a, k).start()
 
     bar = pltpu.get_barrier_semaphore()
     pl.semaphore_signal(bar, inc=1, device_id=(me, 1 - c), device_id_type=MESH)
@@ -457,26 +679,35 @@
             total = square if total is None else total + square
         return jnp.sum(total)
 
-    wide[...] = lax.dot_general(
-        silu[...], d_mod[...], (((0,), (0,)), ((), ())), preferred_element_type=jnp.float32)
-    squares = spread(0, wide.shape[1]) + jnp.sum(bias_grad[...] * bias_grad[...])
+    part_mod = d_mod.shape[2]
+    for core in range(2):
+        wide[:, core * part_mod : (core + 1) * part_mod] = dot(silu[...], d_mod[core].astype(silu.dtype), 0, 0)
+    squares = spread(0, wide.shape[1])
+    mod_sums = jnp.sum(d_mod[...], axis=1)
+    squares = squares + jnp.where(me == 0, jnp.sum(mod_sums * mod_sums), 0.0)
+    width = n * rows
+    tile = chunk_tiles(n, width) * me + lax.broadcasted_iota(jnp.int32, (8, 128), 0)
+    squares = squares + jnp.sum(bias_sum[0] * bias_sum[0])
+    squares = squares + jnp.sum(jnp.where(tile < 3 * (width // 128), bias_sum[1] * bias_sum[1], 0.0))
     pair.wait()
     for core in range(2):
         for part in range(3):
             lo = (2 * part + core) * head
-            wide[:, lo : lo + head] = both[core, 0, :, part * head : (part + 1) * head].astype(jnp.float32)
+            wide[:, lo : lo + head] = both[core, 2, :, part * head : (part + 1) * head].astype(jnp.float32)
     squares = squares + spread(1, 6 * head)
     for core in range(2):
-        wide[:, core * head : (core + 1) * head] = both[core, 0, :, 3 * head :].astype(jnp.float32)
+        wide[:, core * head : (core + 1) * head] = both[core, 2, :, 3 * head :].astype(jnp.float32)
     squares = squares + spread(2, 2 * head)
     for a in (3, 4):
         for core in range(2):
-            wide[:, core * half : (core + 1) * half] = both[core, a - 2].astype(jnp.float32)
+            wide[:, core * half : (core + 1) * half] = both[core, 4 - a].astype(jnp.float32)
         squares = squares + spread(a, 2 * half)
 
     slots = d_cond.shape[0]
     block[:slots] = d_cond[...]
-    block[slots:] = jnp.full((8, 128), squares, jnp.float32)
+    block[slots : slots + 8] = jnp.full((8, 128), squares, jnp.float32)
+    block[slots + 8 : slots + 16] = bias_sum[0]
+    block[slots + 16 :] = bias_sum[1]
     got[me] = block[...]
 
     def copy(j, there, slot):
@@ -492,7 +723,8 @@
     def _(j):
         copy(j, (me + j) % n, (me + n - j) % n).wait()
 
-    total = jnp.sum(got[:, slots:], axis=0)[:1, :1]
+    bias_out[...] = got[:, slots + 8 :]
+    total = jnp.sum(got[:, slots : slots + 8], axis=0)[:1, :1]
     gram = jnp.zeros((slots, slots), jnp.float32)
     for i in range(n):
         part = got[i, :slots]
@@ -504,14 +736,33 @@
     total = total + jnp.sum(gram * same[...], keepdims=True)
     norm = jnp.sqrt(total)
     norm_out[...] = jnp.broadcast_to(norm, (8, 128))
-    factor = jnp.minimum(1.0, CLIP_LIMIT / (norm + 1e-06))
+    factor_out[...] = jnp.broadcast_to(jnp.minimum(1.0, CLIP_LIMIT / (norm + 1e-06)), (8, 128))
     tiles = n * rows // 128
     for t in range(tiles):
         flat[5][pl.ds(t, onehot.shape[1], stride=tiles), :] = wide[: onehot.shape[1], 128 * t : 128 * t + 128]
 
+
+def adam_kernel(rates, *refs):
+    kinds = len(rates)
+    factor_ref, flat = refs[0], refs[1 : 1 + kinds]
+    at = 1 + kinds
+    states = [refs[at + 3 * a : at + 3 * a + 3] for a in range(kinds)]
+    at += 3 * kinds
+    news = [refs[at + 3 * a : at + 3 * a + 3] for a in range(kinds)]
+    at += 3 * kinds
+    held = refs[at : at + kinds]
+    in_sem, out_sem = refs[at + kinds :]
+
+    def loads(a):
+        return [pltpu.make_async_copy(states[a][k], held[a].at[k], in_sem.at[a, k]) for k in range(3)]
+
     for a in range(kinds):
-        for k in range(3):
-            loads(a, k).wait()
+        for copy in loads(a):
+            copy.start()
+    factor = factor_ref[:1, :]
+    for a in range(kinds):
+        for copy in loads(a):
+            copy.wait()
         size = chunk_rows(flat[a].shape[0])
 
         @pl.loop(0, flat[a].shape[0] // size)
@@ -529,38 +780,46 @@
             pltpu.make_async_copy(held[a].at[k], news[a][k], out_sem.at[a, k]).wait()
 
 
-def finish(reduced, silu, d_mod, d_cond, bias_grad, onehot, same, states, rates, n, collective_id):
+def finish(reduced, silu, d_mod, d_cond, bias_sum, onehot, same, states, rates, n, collective_id):
     vmem, hbm = pl.BlockSpec(memory_space=pltpu.VMEM), pl.BlockSpec(memory_space=pltpu.HBM)
     dma = pltpu.SemaphoreType.DMA
     kinds = len(states)
     rows = reduced.shape[1]
     flats = [jax.ShapeDtypeStruct(s[0].shape, jnp.float32) for s in states]
-    block = d_cond.shape[0] + 8
+    small = jax.ShapeDtypeStruct((8, 128), jnp.float32)
+    block = d_cond.shape[0] + 24
     outs = pl.pallas_call(
-        functools.partial(finish_kernel, n, rates),
-        out_shape=[f for f in flats for _ in range(3)] + [jax.ShapeDtypeStruct((8, 128), jnp.float32)],
-        in_specs=[vmem] * 7 + [hbm] * (3 * kinds),
-        out_specs=[hbm] * (3 * kinds) + [vmem],
-        scratch_shapes=[pltpu.VMEM((3,) + f.shape, jnp.float32) for f in flats]
-        + [pltpu.VMEM(f.shape, jnp.float32) for f in flats]
-        + [
+        functools.partial(norm_kernel, n),
+        out_shape=flats + [small, small, jax.ShapeDtypeStruct((n, 16, 128), jnp.float32)],
+        in_specs=[vmem] * 7,
+        out_specs=[vmem] * (kinds + 3),
+        scratch_shapes=[
             pltpu.VMEM((2,) + reduced.shape, reduced.dtype),
-            pltpu.VMEM((rows, d_mod.shape[1]), jnp.float32),
+            pltpu.VMEM((rows, 2 * d_mod.shape[2]), jnp.float32),
             pltpu.VMEM((block, 128), jnp.float32),
             pltpu.VMEM((n, block, 128), jnp.float32),
-            dma((kinds, 3)),
-            dma((kinds, 3)),
             dma,
             dma,
             dma((n,)),
             dma((n,)),
         ],
         compiler_params=pltpu.CompilerParams(
-            collective_id=collective_id, has_side_effects=True, vmem_limit_bytes=56 * 2**20),
-        name="finish",
-    )(reduced, silu, d_mod, d_cond, bias_grad, onehot, same, *[item for s in states for item in s])
+            collective_id=collective_id, has_side_effects=True, vmem_limit_bytes=40 * 2**20),
+        name="norm",
+    )(reduced, silu, d_mod, d_cond, bias_sum, onehot, same)
+    grads, factor, norm = outs[:kinds], outs[kinds], outs[kinds + 1]
+    news = pl.pallas_call(
+        functools.partial(adam_kernel, rates),
+        out_shape=[f for f in flats for _ in range(3)],
+        in_specs=[vmem] * (1 + kinds) + [hbm] * (3 * kinds),
+        out_specs=[hbm] * (3 * kinds),
+        scratch_shapes=[pltpu.VMEM((3,) + f.shape, jnp.float32) for f in flats]
+        + [dma((kinds, 3)), dma((kinds, 3))],
+        compiler_params=pltpu.CompilerParams(vmem_limit_bytes=56 * 2**20),
+        name="adam",
+    )(factor, *grads, *[item for s in states for item in s])
     order = [3 * a + k for a in range(kinds) for k in (1, 2, 0)]
-    return [outs[i] for i in order], outs[-1][0, 0]
+    return [news[i] for i in order], norm[0, 0], outs[kinds + 2]
 
 
 def grid_embed(keep_index, width):
@@ -694,9 +953,10 @@
     def split_heads(values):
         return values.reshape(values.shape[0], half_width // HEAD_DIM, HEAD_DIM)
 
-    queries = split_heads((projected[:, :half_width] + part_of(bias_query)).astype(low))
-    keys = split_heads(projected[:, half_width : 2 * half_width].astype(low))
-    values = split_heads((projected[:, 2 * half_width :] + part_of(bias_value)).astype(low))
+    flat_query = (projected[:, :half_width] + part_of(bias_query)).astype(low)
+    flat_key = projected[:, half_width : 2 * half_width].astype(low)
+    flat_value = (projected[:, 2 * half_width :] + part_of(bias_value)).astype(low)
+    queries, keys, values = split_heads(flat_query), split_heads(flat_key), split_heads(flat_value)
     scale = HEAD_DIM ** (-0.5)
     logits = jnp.einsum("rhe,ghe->hrg", queries, keys, preferred_element_type=jnp.float32) * scale
     logits = jnp.where(key_ok[None, None, :], logits, MASK_FILL)
@@ -737,59 +997,50 @@
     d_middle = d_middle + grad_out
     d_attended = rows_all((pieces[2] * d_middle).astype(low))
     d_gate_attn = jnp.sum(d_middle * attended, axis=0, keepdims=True)
-    grad_attention_out = contract_rows(d_attended, mixed)
     grad_bias_out = jnp.sum(d_attended.astype(jnp.float32), axis=0)
-    d_mixed = split_heads(jnp.dot(d_attended, weight_out, preferred_element_type=jnp.float32).astype(low))
-    d_probs = jnp.einsum("rhe,ghe->hrg", d_mixed, values, preferred_element_type=jnp.float32)
-    inner = jnp.sum(probs * d_probs, axis=-1, keepdims=True)
-    d_logits = (probs * (d_probs - inner)).astype(low)
-    d_query = jnp.einsum("hrg,ghe->rhe", d_logits, keys, preferred_element_type=jnp.float32) * scale
-    d_key = jnp.einsum("hrg,rhe->ghe", d_logits, queries, preferred_element_type=jnp.float32) * scale
-    d_value = jnp.einsum("hrg,rhe->ghe", probs_low, d_mixed, preferred_element_type=jnp.float32)
-    d_projected = jnp.concatenate(
-        [item.reshape(rows * pairs, half_width) for item in (d_query, d_key, d_value)], axis=-1
-    ).astype(low)
-    grad_attention_in = contract_rows(normed_in, d_projected)
-    bias_sums = jnp.sum(d_projected.astype(jnp.float32), axis=0)
-    grad_attn = jnp.concatenate([grad_attention_in, grad_attention_out], axis=1).astype(low)
-    d_normed_in = rows_own(times_transposed(d_projected, weight_in))
-    d_inputs, d_shift_attn, d_scale_attn = jax.vjp(modulated, inputs, pieces[0], pieces[1])[1](d_normed_in)
-    tokens_grad = (d_inputs + d_middle).astype(low)[None]
-
+
+    def to_tiles(values):
+        return jnp.pad(values, ((0, 0), (0, -values.shape[1] % 128)))
+
+    pair_t = jnp.concatenate([normed_in.T, d_attended.T], axis=1).reshape(n, own_rows, 2 * pairs * rows)
+    zero_row = jnp.zeros((1, width), jnp.float32)
+    d_pieces = jnp.concatenate(
+        [zero_row, zero_row, d_gate_attn, d_shift_mlp, d_scale_mlp, d_gate_mlp, zero_row, zero_row]
+    )
+    v_rows = jnp.concatenate(
+        [
+            zero_row,
+            grad_bias_expand.reshape(2, width),
+            grad_bias_out[None],
+            grad_bias_contract[None],
+            zero_row,
+            zero_row,
+            zero_row,
+        ]
+    )
     shape = (n // 4, 2, 2, own_rows, pieces_own.shape[2])
-    reduced = reduce_grads([g.reshape(shape) for g in (grad_attn, grad_expand, grad_contract)], n, 2)
-
-    d_pieces = jnp.concatenate(
-        [d_shift_attn, d_scale_attn, d_gate_attn, d_shift_mlp, d_scale_mlp, d_gate_mlp], axis=0
-    ).reshape(6 * width)
-    d_mod = lax.psum(d_pieces, "seq").astype(low).astype(jnp.float32)
-
-    def at_half(vector):
-        whole = jnp.zeros((vector.shape[0] * pairs,), jnp.float32)
-        return lax.dynamic_update_slice_in_dim(whole, vector, c * vector.shape[0], 0)
-
-    once = (c == 0).astype(jnp.float32)
-    grad_biases = jnp.concatenate(
-        [
-            d_mod * once,
-            at_half(bias_sums[:half_width]),
-            at_half(bias_sums[2 * half_width :]),
-            grad_bias_out * once,
-            at_half(grad_bias_expand),
-            grad_bias_contract * once,
-        ]
-    )
-    bias_parts = jnp.pad(grad_biases.reshape(n, bias_share), ((0, 0), (0, 1024 - bias_share))).reshape(n, 8, 128)
-    d_mod_block = jnp.pad(d_mod.reshape(-1, 128), ((0, -(6 * width // 128) % 8), (0, 0)))
-    d_mod_got, bias_got = exchange([d_mod_block, bias_parts], (False, True), n, 6)
-    biases_shard = lax.psum(jnp.sum(bias_got, axis=0), "seq")
-    d_mod_all = d_mod_got[:, : 6 * width // 128].reshape(n, 6 * width).astype(low)
-    d_silu = times_transposed(
-        lax.dynamic_slice_in_dim(d_mod_all, c * 3 * width, 3 * width, 1), own_modulation
-    )
-    d_silu = lax.psum(d_silu, "seq")
-    d_cond_own = jax.vjp(jax.nn.silu, cond_own)[1](d_silu)[0]
-    d_cond_block = jnp.pad(d_cond_own, ((0, 0), (0, 128 - own_rows)))
+    reduced, tokens_grad, d_mod_all, d_cond, bias_sum = backward(
+        (grad_contract.reshape(shape), grad_expand.reshape(shape), weights[0]),
+        (
+            pair_t,
+            d_attended,
+            to_tiles(flat_query),
+            to_tiles(flat_key),
+            to_tiles(flat_value),
+            to_tiles(mixed),
+            key_ok.astype(jnp.float32)[None],
+            inputs,
+            d_middle,
+            pieces[1],
+            d_pieces,
+            v_rows,
+            jnp.pad(own_modulation, ((0, 128 - own_rows), (0, 0))),
+            jnp.pad(cond_own, ((0, 0), (0, 128 - own_rows))),
+        ),
+        n,
+        2,
+    )
+    tokens_grad = tokens_grad[None]
     same = (labels_all[:, None] == labels_all[None, :]).astype(jnp.float32)
     rates = (
         width ** (-0.5),
@@ -828,12 +1079,12 @@
         biases_second,
     )
     states = list(zip(masters, firsts, seconds))
-    updated, grad_norm = finish(
+    updated, grad_norm, bias_parts = finish(
         reduced,
         silu_own,
         d_mod_all,
-        d_cond_block,
-        biases_shard,
+        d_cond,
+        bias_sum,
         onehot.astype(jnp.float32),
         same,
         [tuple(item.reshape(-1, 128) for item in state) for state in states[:-1]],
@@ -842,7 +1093,19 @@
         8,
     )
     factor = jnp.minimum(1.0, CLIP_LIMIT / (grad_norm + 1e-06))
-    bias_grad = biases_shard.reshape(1024)[:bias_share] * factor
+    bias_parts = bias_parts.reshape(n, pairs, 8, 128)[:, :, : chunk_tiles(n, width)].transpose(1, 0, 2, 3)
+    bias_parts = bias_parts.reshape(pairs, -1)[:, : 5 * width].reshape(pairs, 5, width)
+    grad_biases = jnp.concatenate(
+        [
+            jnp.sum(d_mod_all, axis=1).reshape(-1),
+            bias_parts[:, 0, :half_width].reshape(-1),
+            bias_parts[:, 0, half_width:].reshape(-1),
+            bias_parts[0, 3],
+            bias_parts[:, 1:3].reshape(-1),
+            bias_parts[0, 4],
+        ]
+    )
+    bias_grad = lax.dynamic_slice_in_dim(grad_biases, me * bias_share, bias_share, 0) * factor
     updated = [item.reshape(-1) for item in updated] + list(adam_step(bias_grad, *states[-1], rates[-1]))
     return (block_out, tokens_grad, grad_norm) + tuple(updated)
 

time: 489 us -> 460 us (0.941)
  matrix products: 47.4 us -> 31.9 us
  Pallas kernels: 320 us -> 330 us
  local copies, waits for them, and re-layouts: 63.4 us -> 55.2 us
  blocking collectives: 19.3 us -> 11.5 us
  other arithmetic: 23.8 us -> 17.1 us
    pallas_call x2 -> x3, Pallas kernels: 147 us -> 180 us  [the longest x1 147 us: backward(): pl.pallas_call(functools.partial(backward_kernel, line), out_shape=[jax.S...]
    pallas_call x4 -> x3, Pallas kernels: 50.3 us -> 27 us  [exchange(): pl.pallas_call(functools.partial(exchange_kernel, n, spread), out_shape=[...]
    unnamed x236 -> x112, local copies, waits for them, and re-layouts: 25.6 us -> 14.1 us
    psum x2 -> x0, blocking collectives: 7.54 us -> none  [the longest x1 3.88 us: per_device(): d_silu = lax.psum(d_silu, 'seq')]
    dot_general x4 -> x2, matrix products: 14.5 us -> 7.93 us  [contract_rows(): lax.dot_general(left, right, (((0,), (0,)), ((), ())), preferred_element_...]
    concatenate x2 -> x1, other arithmetic: 5.66 us -> 0.09 us  [per_device(): jnp.concatenate([normed_in.T, d_attended.T], axis=1)]
    pad x2 -> x5, local copies, waits for them, and re-layouts: 0.62 us -> 5.94 us  [the longest x4 4.97 us: to_tiles(): return jnp.pad(values, ((0, 0), (0, -values.shape[1] % 128)))]
    dot_general x5 -> x3, matrix products: 11.5 us -> 6.27 us  [times_transposed(): lax.dot_general(left, right, (((1,), (1,)), ((), ())), preferred_element_...]
  transfers between devices with their start and end apart: 4 -> 3, of which waited for: 0 -> 0; matrix products, arithmetic and copies ran while one was open for 13% -> 7% of each run, Pallas kernels for 26% -> 0%
where the time goes in v3:
time: 460 us; the launch traced here: 451 us
  Pallas kernels  330 us (72%)
  local copies, waits for them, and re-layouts  55.2 us (12%)
  matrix products  31.9 us (7%)
  other arithmetic  17.1 us (4%)
  blocking collectives  11.5 us (2%)
    pallas_call x1, Pallas kernels, backward(): pl.pallas_call(functools.partial(backward_kernel, line), out_shape=[jax.S...  147 us
    pallas_call x1, Pallas kernels, gather_weights(): pl.pallas_call(functools.partial(gather_kernel, line), out_shape=jax.Shap...  124 us
    pallas_call x3, Pallas kernels, exchange(): pl.pallas_call(functools.partial(exchange_kernel, n, spread), out_shape=[...  27 us
    pallas_call x1, Pallas kernels, finish(): pl.pallas_call(functools.partial(norm_kernel, n), out_shape=flats + [smal...  16.5 us
    pallas_call x1, Pallas kernels, finish(): pl.pallas_call(functools.partial(adam_kernel, rates), out_shape=[f for f...  16.4 us
    unnamed x112, local copies, waits for them, and re-layouts  14.1 us
    slice x1, local copies, waits for them, and re-layouts, per_device(): weights[0]  12.2 us
    all_gather x4, blocking collectives, rows_all(): return lax.all_gather(values, 'seq', axis=0, tiled=True)  9.64 us
  transfers between devices with their start and end apart: 3, of which 0 were waited for; matrix products, arithmetic and copies ran while one was open for 7% of the time, Pallas kernels for 0%

profile of v3, /device:TPU:12, one launch (start us, length us, event | category | flops | bytes accessed | tf_op | source)
XLA Modules:
  0.0 450.8 jit_solution(16795748396643589231)
XLA Ops:
  2.0 8.6 %exchange.3 = f32[16,16,128]{2,1,0:T(8,128)S(1)} custom-call(f32[16,128]{1,0:T(8,128)S(1)} %concatenate.26.refs_0_), custom_call_target="tpu_custom_call" | custom-call | tf_op jit(solution)/shard_map/exchange/pallas_call | solution.py:622
  11.8 2.4 reshape_reshape.15
  14.2 1.0 constant_dynamic-slice_fusion.6
  16.1 8.5 %exchange.4 = f32[16,16,128]{2,1,0:T(8,128)S(1)} custom-call(f32[16,16,128]{2,1,0:T(8,128)S(1)} %pad.36.refs_0_), custom_call_target="tpu_custom_call" | custom-call | tf_op jit(solution)/shard_map/exchange/pallas_call | solution.py:622
  25.0 9.9 %exchange.5 = f32[16,32,128]{2,1,0:T(8,128)S(1)} custom-call(f32[16,32,128]{2,1,0:T(8,128)S(1)} %pad.37.refs_0_), custom_call_target="tpu_custom_call" | custom-call | tf_op jit(solution)/shard_map/exchange/pallas_call | solution.py:622
  35.0 1.8 all_gather.15
  36.9 1.2 fusion.32
  38.1 1.4 multiply_cosine_fusion
  40.4 2.5 all_gather.16
  42.9 1.3 reshape_reshape.16
  44.2 3.8 convert_reduce_fusion.3
  48.0 1.3 reshape.460
  49.2 1.8 reshape_reshape.17
  51.0 1.1 constant_dynamic-slice_fusion.5
  52.8 1.0 reshape_reshape.18
  54.9 1.4 constant_dynamic-slice_fusion.3
  56.5 1.1 pad_maximum_fusion.1.src
  57.6 123.7 %gather_weights.1 = bf16[3,4,2,2,72,2304]{5,4,3,2,1,0:T(8,128)(2,1)} custom-call(bf16[3,72,2304]{2,1,0:T(8,128)(2,1)} %pad_maximum_fusion.1.src), custom_call_target="tpu_custom_call" | custom-call | bytes 31850496 | tf_op jit(solution)/shard_map/gather_weights/pallas_call | solution.py:169
  181.2 4.0 fusion.1
  187.2 2.2 fusion.54
  189.3 1.9 convolution_convert_fusion.2
  191.3 2.5 fusion.10
  194.6 12.2 %fusion.51 = (bf16[1,4,2,2,72,2304]{5,4,3,2,1,0:T(8,128)(2,1)}, bf16[1,4,2,2,72,2304]{5,4,3,2,1,0:T(8,128)(2,1)}, bf16[1,4,2,2,72,2304]{5,4,3,2,1,0:T(8,128)(2,1)}) fusion(bf16[3,4,2,2,72,2304]{5,4,3,2,1,0:T(8,128)(2,1)} %gather_weights.1), kind=kLoop, calls=%fused_computation.152 | loop fusion | bytes 31850496 | tf_op jit(solution)/shard_map/slice | solution.py:1023
  211.7 2.3 all_gather.18
  214.2 1.7 pad.41.refs_8_
  215.9 1.7 pad.39.refs_6_
  219.3 4.2 fusion.55
  223.6 1.3 fusion.49
  225.3 2.6 all_gather.17
  227.9 5.0 %convert_reduce_fusion = (f32[2304]{0:T(1024)S(1)}, bf16[256,2304]{1,0:T(8,128)(2,1)S(1)}, f32[256,2304]{1,0:T(8,128)S(1)}) fusion(f32[256,2304]{1,0:T(8,128)S(1)} %fusion.55, f32[2304]{0:T(1024)S(1)} %dynamic_slice.62, bf16[256,1152]{1,0:T(8,128)(2,1)S(1)} %all_gather.17, bf16[1152,2304]{1,0:T(8,128)(2,1)} %bitcast.160), kind=kOutput, calls=%fused_computation.15 | convolution fusion | flops 1372518144 | bytes 11814912 | tf_op jit(solution)/shard_map/dot_general | solution.py:980
  232.9 2.1 fusion.44
  235.0 4.0 convolution_convert_fusion.1
  239.0 1.7 fusion.56
  241.5 4.0 convolution_convert_fusion
  245.5 1.6 multiply_reduce_fusion
  247.1 2.4 fusion.18
  249.5 1.4 multiply_reduce_fusion.1
  250.9 2.2 all_gather.19.refs_4_
  253.5 1.4 copy.110
  256.2 146.8 %backward.1 = (bf16[3,72,2304]{2,1,0:T(8,128)(2,1)}, bf16[128,1152]{1,0:T(8,128)(2,1)}, f32[2,16,3456]{2,1,0:T(8,128)}, f32[16,128]{1,0:T(8,128)}, f32[2,8,128]{2,1,0:T(8,128)}) custom-call(bf16[4,2,2,72,2304]{4,3,2,1,0:T(8,128)(2,1)} %bitcast.157, bf16[4,2,2,72,2304]{4,3,2,1,0:T(8,128)(2,1)} %bitcast.153, bf16[1152,2304]{1,0:T(8,128)(2,1)} %bitcast.154, ...), custom_call_target="tpu_custom_call" | custom-call | tf_op jit(solution)/shard_map/backward/pallas_call | solution.py:543
  403.1 1.1 reduce_sum.185
  404.2 1.0 copy-done.1
  405.2 1.2 copy-done.4
  407.8 16.5 %norm.1 = (f32[3888,128]{1,0:T(8,128)S(1)}, f32[1944,128]{1,0:T(8,128)S(1)}, f32[648,128]{1,0:T(8,128)S(1)}, f32[2592,128]{1,0:T(8,128)S(1)}, f32[2592,128]{1,0:...) custom-call(bf16[3,72,2304]{2,1,0:T(8,128)(2,1)S(1)} %copy-done.4, ...), custom_call_target="tpu_custom_call" | custom-call | tf_op jit(solution)/shard_map/norm/pallas_call | solution.py:791
  424.3 1.3 copy-done
  425.6 1.1 copy-done.2
  426.6 1.1 copy-done.3
  433.3 16.4 %adam.1 = (f32[3888,128]{1,0:T(8,128)}, f32[3888,128]{1,0:T(8,128)}, f32[3888,128]{1,0:T(8,128)}, f32[1944,128]{1,0:T(8,128)}, f32[1944,128]{1,0:T(8,128)}, /*in...) custom-call(f32[8,128]{1,0:T(8,128)} %copy-done.10, ...), custom_call_target="tpu_custom_call" | custom-call | tf_op jit(solution)/shard_map/adam/pallas_call | solution.py:811
  (214 shorter events, 24.1 us)
Async XLA Ops:
  11.2 4.1 copy-start.27
  14.2 1.2 copy-start.25
  14.2 1.4 copy-start.36
  15.3 9.6 %copy-start.16 = (bf16[72,1,1,3456]{3,0,2,1:T(8,128)(2,1)}, bf16[72,1,1,3456]{3,0,2,1:T(8,128)(2,1)S(1)}, u32[]{:S(2)}) copy-start(bf16[72,1,1,3456]{3,0,2,1:T(8,128)(2,1)S(1)} %copy.147) | copy-start | bytes 1492996
  15.3 19.6 %slice-start.4 = ((f32[16128]{0:T(1024)}), f32[6912]{0:T(1024)S(1)}, s32[]{:S(2)}) async-start(f32[16128]{0:T(1024)} %copy-done.27), calls=%async_computation.4 | async-start | bytes 57344 | tf_op jit(solution)/shard_map/slice | solution.py:923
  15.4 9.2 %copy-start.41 = (s32[64]{0:T(128)}, s32[64]{0:T(128)S(1)}, u32[]{:S(2)}) copy-start(s32[64]{0:T(128)S(1)} %iota_add_fusion) | copy-start | bytes 772
  15.4 22.7 %copy-start.44 = (s32[1,128]{1,0:T(1,128)S(1)}, s32[1,128]{1,0:T(1,128)}, u32[]{:S(2)}) copy-start(s32[1,128]{1,0:T(1,128)} %param.32) | copy-start | bytes 1540
  24.6 15.2 %copy-start.30 = (bf16[1,128,1152]{2,1,0:T(8,128)(2,1)S(1)}, bf16[1,128,1152]{2,1,0:T(8,128)(2,1)}, u32[]{:S(2)}) copy-start(bf16[1,128,1152]{2,1,0:T(8,128)(2,1)} %param.27) | copy-start | bytes 884740
  39.6 3.4 copy-start.18
  40.0 183.6 %copy-start.11 = (f32[128,1152]{1,0:T(8,128)}, f32[128,1152]{1,0:T(8,128)S(1)}, u32[]{:S(2)}) copy-start(f32[128,1152]{1,0:T(8,128)S(1)} %get-tuple-element.114.refs_10_) | copy-start | bytes 1769476
  40.4 12.4 %copy-start.15 = (f32[331776]{0:T(1024)S(1)}, f32[331776]{0:T(1024)}, u32[]{:S(2)}) copy-start(f32[331776]{0:T(1024)} %param.42) | copy-start | bytes 3981316
  44.2 9.6 %copy-start.14 = (f32[331776]{0:T(1024)S(1)}, f32[331776]{0:T(1024)}, u32[]{:S(2)}) copy-start(f32[331776]{0:T(1024)} %param.45) | copy-start | bytes 3981316
  53.8 1.1 copy-start.19
  54.9 1.5 copy-start.26
  57.6 123.7 %copy-start.21 = (bf16[256,1152]{1,0:T(8,128)(2,1)S(1)}, bf16[256,1152]{1,0:T(8,128)(2,1)}, u32[]{:S(2)}) copy-start(bf16[256,1152]{1,0:T(8,128)(2,1)} %all_gather.16) | copy-start | bytes 1769476
  185.2 1.0 copy-start.34
  185.3 1.5 copy-start.33
  194.6 28.9 %collective-permute-start = (f32[128,1152]{1,0:T(8,128)}, f32[128,1152]{1,0:T(8,128)}, u32[]{:S(2)}, u32[]{:S(2)}) collective-permute-start(f32[128,1152]{1,0:T(8,128)} %constant_dynamic-slice_fusion.2), channel_id=1, source_target_pairs={{0,1},{1,0},{2,3},{3,2},{4,5},{5,4},{6,7},{7,6},{8,9},{9,8},{10,11... | collective-permute-start | bytes 1769480 | tf_op jit(solution)/shard_map/ppermute | solution.py:886
  194.6 16.9 %copy-start.37 = (f32[128]{0:T(128)}, f32[128]{0:T(128)S(1)}, u32[]{:S(2)}) copy-start(f32[128]{0:T(128)S(1)} %fusion.43) | copy-start | bytes 1540
  194.6 12.2 %copy-start.28 = (f32[16128]{0:T(1024)S(1)}, f32[16128]{0:T(1024)}, u32[]{:S(2)}) copy-start(f32[16128]{0:T(1024)} %copy-done.27) | copy-start | bytes 193540
  206.9 4.7 %copy-start.20 = (bf16[1,128,1152]{2,1,0:T(8,128)(2,1)S(1)}, bf16[1,128,1152]{2,1,0:T(8,128)(2,1)}, u32[]{:S(2)}) copy-start(bf16[1,128,1152]{2,1,0:T(8,128)(2,1)} %param.28) | copy-start | bytes 884740
  208.5 9.1 %copy-start.17 = (bf16[72,1,1,3456]{3,0,2,1:T(8,128)(2,1)S(1)}, bf16[72,1,1,3456]{3,0,2,1:T(8,128)(2,1)}, u32[]{:S(2)}) copy-start(bf16[72,1,1,3456]{3,0,2,1:T(8,128)(2,1)} %copy-done.16) | copy-start | bytes 1492996
  211.6 7.1 %copy-start.42 = (pred[128]{0:T(512)(128)(4,1)S(1)}, pred[128]{0:T(512)(128)(4,1)}, u32[]{:S(2)}) copy-start(pred[128]{0:T(512)(128)(4,1)} %constant.170.clone.1) | copy-start | bytes 388
  223.5 1.6 copy-start.31
  225.3 7.6 %slice-start.2 = ((s8[5308416]{0:T(1024)(128)(4,1)}), s8[4194304]{0:T(1024)(128)(4,1)S(1)}, s32[]{:S(2)}) async-start(s8[5308416]{0:T(1024)(128)(4,1)} %bitcast.165), calls=%async_computation.2 | async-start | bytes 8388608
  227.9 5.1 %slice-start.3 = ((s8[5308416]{0:T(1024)(128)(4,1)}), s8[1114112]{0:T(1024)(128)(4,1)S(1)}, s32[]{:S(2)}) async-start(s8[5308416]{0:T(1024)(128)(4,1)} %bitcast.165), calls=%async_computation.3 | async-start | bytes 2228224
  227.9 11.2 %slice-start = ((s8[5308416]{0:T(1024)(128)(4,1)}), s8[4194304]{0:T(1024)(128)(4,1)S(1)}, s32[]{:S(2)}) async-start(s8[5308416]{0:T(1024)(128)(4,1)} %bitcast.161), calls=%async_computation | async-start | bytes 8388608
  232.9 6.1 %slice-start.1 = ((s8[5308416]{0:T(1024)(128)(4,1)}), s8[1114112]{0:T(1024)(128)(4,1)S(1)}, s32[]{:S(2)}) async-start(s8[5308416]{0:T(1024)(128)(4,1)} %bitcast.161), calls=%async_computation.1 | async-start | bytes 2228224
  235.0 6.2 %copy-start.23 = (f32[256,1152]{1,0:T(8,128)}, f32[256,1152]{1,0:T(8,128)S(1)}, u32[]{:S(2)}) copy-start(f32[256,1152]{1,0:T(8,128)S(1)} %fusion.44) | copy-start | bytes 3538948
  240.8 4.7 %copy-start.24 = (f32[256,1152]{1,0:T(8,128)}, f32[256,1152]{1,0:T(8,128)S(1)}, u32[]{:S(2)}) copy-start(f32[256,1152]{1,0:T(8,128)S(1)} %fusion.56) | copy-start | bytes 3538948
  240.8 4.7 %collective-permute-start.2 = (f32[128,1152]{1,0:T(8,128)S(1)}, f32[128,1152]{1,0:T(8,128)}, u32[]{:S(2)}, u32[]{:S(2)}) collective-permute-start(f32[128,1152]{1,0:T(8,128)S(1)} %constant_dynamic-slice_fusion), channel_id=1, source_target_pairs={{0,1},{1,0},{2,3},{3,2},{4,5},{5,4},{6,7},{7,6},{8,9},{9,8},{10,11... | collective-permute-start | bytes 1769480 | tf_op jit(solution)/shard_map/ppermute | solution.py:886
  241.3 5.8 %collective-permute-start.1 = (f32[128,1152]{1,0:T(8,128)S(1)}, f32[128,1152]{1,0:T(8,128)}, u32[]{:S(2)}, u32[]{:S(2)}) collective-permute-start(f32[128,1152]{1,0:T(8,128)S(1)} %constant_dynamic-slice_fusion.1), channel_id=1, source_target_pairs={{0,1},{1,0},{2,3},{3,2},{4,5},{5,4},{6,7},{7,6},{8,9},{9,8},{10,11... | collective-permute-start | bytes 1769480 | tf_op jit(solution)/shard_map/ppermute | solution.py:886
  245.5 1.6 copy-start.32
  245.5 1.6 copy-start.38
  249.5 3.8 copy-start.22
  250.9 2.6 copy-start.13
  253.2 1.7 copy-start.12
  403.0 29.4 %copy-start.43 = (f32[16128]{0:T(1024)S(1)}, f32[16128]{0:T(1024)}, u32[]{:S(2)}) copy-start(f32[16128]{0:T(1024)} %custom-call) | copy-start | bytes 193540
  403.0 29.5 %copy-start.35 = (f32[1008]{0:T(1024)S(1)}, f32[1008]{0:T(1024)}, u32[]{:S(2)}) copy-start(f32[1008]{0:T(1024)} %param.51) | copy-start | bytes 12100
  403.1 29.5 %copy-start.39 = (f32[1008]{0:T(1024)S(1)}, f32[1008]{0:T(1024)}, u32[]{:S(2)}) copy-start(f32[1008]{0:T(1024)} %param.53) | copy-start | bytes 12100
  403.1 29.5 %copy-start.40 = (f32[1008]{0:T(1024)S(1)}, f32[1008]{0:T(1024)}, u32[]{:S(2)}) copy-start(f32[1008]{0:T(1024)} %param.52) | copy-start | bytes 12100
  404.2 1.0 copy-start.1
  405.2 1.2 copy-start.4
  424.3 1.3 copy-start
  425.6 1.1 copy-start.2
  426.6 1.1 copy-start.3
  427.7 1.0 copy-start.5
  433.3 16.4 %copy-start.29 = (bf16[128,1152]{1,0:T(8,128)(2,1)S(1)}, bf16[128,1152]{1,0:T(8,128)(2,1)}, u32[]{:S(2)}) copy-start(bf16[128,1152]{1,0:T(8,128)(2,1)} %get-tuple-element.56) | copy-start | bytes 884740
  (5 other events, 3.4 us)

commit v4 on v3

--- a/solution.py
+++ b/solution.py
@@ -56,126 +56,408 @@
         pl.semaphore_wait(bar, 2 + (self.z > 0).astype(jnp.int32) + (self.z < self.line - 1).astype(jnp.int32))
 
 
-def gather_kernel(line, src, out, own_sem, send_a, send_u, send_d, send_b, recv_a, recv_z, recv_b):
-    me = Place(line)
-    count = src.shape[0]
-    x, y, z = me.x, me.y, me.z
-
-    def single(m, g, zz, yy=None, xx=None):
+class Gatherer:
+    def __init__(self, line, own, out, keep_sem, sems):
+        self.line, self.own, self.out, self.keep_sem = line, own, out, keep_sem
+        self.send_a, self.send_u, self.send_d, self.send_b, self.recv_a, self.recv_z, self.recv_b = sems
+        self.me = Place(line)
+        self.up, self.down = self.me.z < line - 1, self.me.z > 0
+
+    def single(self, m, g, zz):
         lo, width = GROUPS[g][:2]
-        return out.at[m, zz, y if yy is None else yy, x if xx is None else xx, :, pl.ds(lo, width)]
-
-    def pair(m, g, zz):
+        return self.out.at[m, zz, self.me.y, self.me.x, :, pl.ds(lo, width)]
+
+    def pair(self, m, g, zz):
         lo, width, _, first = GROUPS[g]
         if first == "x":
-            return out.at[m, zz, y, :, :, pl.ds(lo, width)]
-        return out.at[m, zz, :, x, :, pl.ds(lo, width)]
-
-    def remote(ref, send, recv, dev, source=None):
+            return self.out.at[m, zz, self.me.y, :, :, pl.ds(lo, width)]
+        return self.out.at[m, zz, :, self.me.x, :, pl.ds(lo, width)]
+
+    def remote(self, ref, send, recv, dev, source):
         return pltpu.make_async_remote_copy(
             src_ref=ref if source is None else source, dst_ref=ref, send_sem=send, recv_sem=recv,
             device_id=dev, device_id_type=MESH)
 
-    def own(m, g):
+    def source(self, m, g):
         lo, width = GROUPS[g][:2]
-        return src.at[m, :, pl.ds(lo, width)]
-
-    def a_copy(m, g, zz, source=None):
-        return remote(single(m, g, zz), send_a.at[m, g, zz], recv_a.at[m, g, zz], me.peer(GROUPS[g][3]), source)
-
-    def z_ref(m, g, zz):
-        return pair(m, g, zz) if GROUPS[g][2] == 0 else single(m, g, zz)
-
-    def u_copy(m, g, zz, source=None):
-        return remote(z_ref(m, g, zz), send_u.at[m, g, zz], recv_z.at[m, g, zz], me.dev(z=jnp.minimum(z + 1, line - 1)), source)
-
-    def d_copy(m, g, zz, source=None):
-        return remote(z_ref(m, g, zz), send_d.at[m, g, zz], recv_z.at[m, g, zz], me.dev(z=jnp.maximum(z - 1, 0)), source)
-
-    def b_copy(m, g, zz):
+        return self.own.at[m, :, pl.ds(lo, width)]
+
+    def a_copy(self, m, g, zz, source=None):
+        return self.remote(
+            self.single(m, g, zz), self.send_a.at[m, g, zz], self.recv_a.at[m, g, zz], self.me.peer(GROUPS[g][3]), source)
+
+    def z_ref(self, m, g, zz):
+        return self.pair(m, g, zz) if GROUPS[g][2] == 0 else self.single(m, g, zz)
+
+    def u_copy(self, m, g, zz, source=None):
+        dev = self.me.dev(z=jnp.minimum(self.me.z + 1, self.line - 1))
+        return self.remote(self.z_ref(m, g, zz), self.send_u.at[m, g, zz], self.recv_z.at[m, g, zz], dev, source)
+
+    def d_copy(self, m, g, zz, source=None):
+        dev = self.me.dev(z=jnp.maximum(self.me.z - 1, 0))
+        return self.remote(self.z_ref(m, g, zz), self.send_d.at[m, g, zz], self.recv_z.at[m, g, zz], dev, source)
+
+    def b_copy(self, m, g, zz):
         last = "y" if GROUPS[g][3] == "x" else "x"
-        return remote(pair(m, g, zz), send_b.at[m, g, zz], recv_b.at[m, g, zz], me.peer(last))
-
-    def keep(m):
-        return pltpu.make_async_copy(src.at[m], out.at[m, z, y, x], own_sem.at[m])
-
-    up, down = z < line - 1, z > 0
-
-    @pl.loop(0, count)
-    def _(m):
-        keep(m).start()
-
-    me.barrier()
-
-    @pl.loop(0, count)
-    def _(m):
+        return self.remote(self.pair(m, g, zz), self.send_b.at[m, g, zz], self.recv_b.at[m, g, zz], self.me.peer(last), None)
+
+    def keep(self, m):
+        me = self.me
+        return pltpu.make_async_copy(self.own.at[m], self.out.at[m, me.z, me.y, me.x], self.keep_sem.at[m])
+
+    def begin(self, m):
+        z = self.me.z
+        self.keep(m).start()
         for g in range(4):
-            a_copy(m, g, z, own(m, g)).start()
+            self.a_copy(m, g, z, self.source(m, g)).start()
         for g in (2, 3):
-            when(up, lambda g=g: u_copy(m, g, z, own(m, g)).start())
-            when(down, lambda g=g: d_copy(m, g, z, own(m, g)).start())
-
-    @pl.loop(0, count)
-    def _(m):
-        keep(m).wait()
+            when(self.up, lambda g=g: self.u_copy(m, g, z, self.source(m, g)).start())
+            when(self.down, lambda g=g: self.d_copy(m, g, z, self.source(m, g)).start())
+
+    def paired(self, m):
+        z = self.me.z
+        self.keep(m).wait()
         for g in (0, 1):
-            a_copy(m, g, z).wait_recv()
-            when(up, lambda g=g: u_copy(m, g, z).start())
-            when(down, lambda g=g: d_copy(m, g, z).start())
-            b_copy(m, g, z).start()
-
-    def arrive(m, k, zz, onward, go):
+            self.a_copy(m, g, z).wait_recv()
+            when(self.up, lambda g=g: self.u_copy(m, g, z).start())
+            when(self.down, lambda g=g: self.d_copy(m, g, z).start())
+            self.b_copy(m, g, z).start()
+
+    def arrive(self, m, zz, upward):
         for g in range(4):
-            copy = u_copy if go == "u" else d_copy
+            copy = self.u_copy if upward else self.d_copy
             copy(m, g, zz).wait_recv()
-            when(onward, lambda g=g: copy(m, g, zz).start())
+            when(self.up if upward else self.down, lambda g=g: copy(m, g, zz).start())
             if GROUPS[g][2] == 0:
-                b_copy(m, g, zz).start()
+                self.b_copy(m, g, zz).start()
             else:
-                a_copy(m, g, zz).start()
-
-    def crossed(m, zz):
+                self.a_copy(m, g, zz).start()
+
+    def crossed(self, m, zz):
         for g in (2, 3):
-            a_copy(m, g, zz).wait_recv()
-            b_copy(m, g, zz).start()
-
-    @pl.loop(1, line + 1)
-    def _(k):
-        @pl.loop(0, count)
-        def _(m):
-            when(k <= z, lambda: arrive(m, k, jnp.maximum(z - k, 0), up, "u"))
-            when(z + k < line, lambda: arrive(m, k, jnp.minimum(z + k, line - 1), down, "d"))
-            when(k - 1 <= z, lambda: crossed(m, jnp.maximum(z - k + 1, 0)))
-            when((k > 1) & (z + k - 1 < line), lambda: crossed(m, jnp.minimum(z + k - 1, line - 1)))
-
-    @pl.loop(0, count)
-    def _(m):
-        @pl.loop(0, line)
+            self.a_copy(m, g, zz).wait_recv()
+            self.b_copy(m, g, zz).start()
+
+    def step(self, m, k):
+        z, line = self.me.z, self.line
+        when(k <= z, lambda: self.arrive(m, jnp.maximum(z - k, 0), True))
+        when(z + k < line, lambda: self.arrive(m, jnp.minimum(z + k, line - 1), False))
+        when(k - 1 <= z, lambda: self.crossed(m, jnp.maximum(z - k + 1, 0)))
+        when((k > 1) & (z + k - 1 < line), lambda: self.crossed(m, jnp.minimum(z + k - 1, line - 1)))
+
+    def complete(self, m):
+        @pl.loop(0, self.line)
         def _(zz):
             for g in range(4):
-                b_copy(m, g, zz).wait()
+                self.b_copy(m, g, zz).wait_recv()
+
+    def drain(self, m):
+        z = self.me.z
+
+        @pl.loop(0, self.line)
+        def _(zz):
+            for g in range(4):
+                self.b_copy(m, g, zz).wait_send()
                 if GROUPS[g][2] == 1:
-                    a_copy(m, g, zz).wait_send()
-                when(up & (zz <= z), lambda g=g: u_copy(m, g, zz).wait_send())
-                when(down & (zz >= z), lambda g=g: d_copy(m, g, zz).wait_send())
+                    self.a_copy(m, g, zz).wait_send()
+                when(self.up & (zz <= z), lambda g=g: self.u_copy(m, g, zz).wait_send())
+                when(self.down & (zz >= z), lambda g=g: self.d_copy(m, g, zz).wait_send())
+
         for g in (0, 1):
-            a_copy(m, g, z).wait_send()
-
-
-def gather_weights(src, n, collective_id):
-    count, rows, cols = src.shape
+            self.a_copy(m, g, z).wait_send()
+
+
+def dot(left, right, a=1, b=0):
+    return lax.dot_general(left, right, (((a,), (b,)), ((), ())), preferred_element_type=jnp.float32)
+
+
+def normal(values):
+    centre = values - jnp.mean(values, axis=-1, keepdims=True)
+    return centre * lax.rsqrt(jnp.mean(centre * centre, axis=-1, keepdims=True) + LAYER_EPS)
+
+
+def all_peers(n, src, dst, send, recv, spread):
+    me, c = lax.axis_index("dp"), lax.axis_index("seq")
+
+    def copy(j, there, slot):
+        return pltpu.make_async_remote_copy(
+            src_ref=src.at[there] if spread else src, dst_ref=dst.at[slot], send_sem=send.at[j], recv_sem=recv.at[slot],
+            device_id=(there, c), device_id_type=MESH)
+
+    def start():
+        @pl.loop(1, n)
+        def _(j):
+            copy(j, (me + j) % n, me).start()
+
+    def wait():
+        @pl.loop(1, n)
+        def _(j):
+            copy(j, (me + j) % n, (me + n - j) % n).wait()
+
+    return start, wait
+
+
+def greet_all(n):
+    me, c = lax.axis_index("dp"), lax.axis_index("seq")
+    bar = pltpu.get_barrier_semaphore()
+    pl.semaphore_signal(bar, inc=1, device_id=(me, 1 - c), device_id_type=MESH)
+
+    @pl.loop(1, n)
+    def _(j):
+        pl.semaphore_signal(bar, inc=1, device_id=((me + j) % n, c), device_id_type=MESH)
+
+    return bar
+
+
+def head_window(h):
+    lo = pl.multiple_of(h * HEAD_DIM // 128 * 128, 128)
+    lane = lax.broadcasted_iota(jnp.int32, (1, 256), 1) + lo - h * HEAD_DIM
+    return pl.ds(lo, 256), ((lane >= 0) & (lane < HEAD_DIM)).astype(jnp.bfloat16)
+
+
+def head_probs(qh, kh, seen):
+    logits = jnp.where(seen, dot(qh, kh, 1, 1) * HEAD_DIM ** (-0.5), MASK_FILL)
+    expo = jnp.exp(logits - jnp.max(logits, axis=-1, keepdims=True))
+    return expo / jnp.sum(expo, axis=-1, keepdims=True)
+
+
+def forward_kernel(line, *refs):
+    (m_in, m_out, m_expand, m_contract, m_table, m_mod, onehot, time_vec, x, key_ok, b_mod, b_query, b_value, b_out,
+     weights, weight, h1, q, k, v, o, attended, middle, h2, pieces, cond, silu, mod_half) = refs[:28]
+    (f_in, f_out, f_expand, f_contract, f_table, f_mod, own, table, cond_part, cond_got, mods, mod_part, mod_got, blocks, w,
+     proj, mix, wide, partial, partial_got, in_sem, w_sem, pair_send, pair_recv, cond_send, cond_recv, mod_send, mod_recv,
+     keep_sem) = refs[28:57]
+    n = line * 4
+    low, f32 = jnp.bfloat16, jnp.float32
+    me, c = lax.axis_index("dp"), lax.axis_index("seq")
+    gat = Gatherer(line, own, weights, keep_sem, refs[57:])
+    rows, width = x.shape
+    own_rows, half = own.shape[1], own.shape[2] // 4
+    edge = 3 * half // 128 * 128
+    tiles = width // 128
+    sources, flats = (m_in, m_out, m_table, m_mod, m_expand, m_contract), (f_in, f_out, f_table, f_mod, f_expand, f_contract)
+
+    def load(i):
+        return pltpu.make_async_copy(sources[i], flats[i], in_sem.at[i])
+
+    for i in range(6):
+        load(i).start()
+    bar = greet_all(n)
+
+    def swap(i, src, dst):
+        return pltpu.make_async_remote_copy(
+            src_ref=src, dst_ref=dst, send_sem=pair_send.at[i], recv_sem=pair_recv.at[i], device_id=(me, 1 - c),
+            device_id_type=MESH)
+
+    def tile(flat, t, count, per_row):
+        return flat[pl.ds(t, count, stride=per_row), :]
+
+    def cut_heads(flat, part, per_row):
+        start = part * tiles + c * (tiles // 2)
+        found = jnp.concatenate([tile(flat, start + j, own_rows, per_row) for j in range(tiles // 2 + 1)], axis=1)
+        return jnp.where(c == 0, found[:, :half], found[:, found.shape[1] - half :]).astype(low)
+
+    def cut(flat, target, count):
+        for j in range(count):
+            target[:own_rows, 128 * j : 128 * j + 128] = tile(flat, c * count + j, own_rows, 2 * count).astype(low)
+
+    load(0).wait()
+    load(1).wait()
+    for part in range(3):
+        own[0, :, part * half : (part + 1) * half] = cut_heads(f_in, part, 3 * tiles)
+    own[0, :, 3 * half :] = cut_heads(f_out, 0, tiles)
+    load(2).wait()
+    class_rows = table.shape[0]
+    for t in range(tiles):
+        table[:, 128 * t : 128 * t + 128] = tile(f_table, t, class_rows, tiles).astype(low)
+    found = dot(onehot[...], table[...])
+    mine = lax.broadcasted_iota(jnp.int32, (n, width), 0) == me
+    found = found + jnp.where(mine, jnp.broadcast_to(time_vec[...].astype(f32), (n, width)), 0.0)
+    cond_part[...] = jnp.zeros_like(cond_part)
+    for i in range(n):
+        cond_part[i, :, :own_rows] = found[:, i * own_rows : (i + 1) * own_rows]
+    cond_got[me] = cond_part[me]
+
+    pl.semaphore_wait(bar, n)
+    cond_start, cond_wait = all_peers(n, cond_part, cond_got, cond_send, cond_recv, True)
+    mod_start, mod_wait = all_peers(n, mod_part, mod_got, mod_send, mod_recv, True)
+    cond_start()
+    gat.begin(0)
+    load(3).wait()
+    mod_half[own_rows:] = jnp.zeros((mod_half.shape[0] - own_rows, mod_half.shape[1]), low)
+    cut(f_mod, mod_half, 3 * tiles)
+    load(4).wait()
+    cut(f_expand, own.at[1], 4 * half // 128)
+
+    cond_wait()
+    value = jnp.sum(cond_got[...], axis=0)
+    cond[...] = value
+    silu[...] = (value / (1.0 + jnp.exp(-value))).astype(low)
+    mods[...] = dot(silu[...], mod_half[...])
+
+    @pl.loop(0, n)
+    def _(s):
+        mod_part[s] = mods[pl.ds(s, 1), :]
+
+    mod_got[me] = mod_part[me]
+    mod_start()
+    gat.paired(0)
+    gat.begin(1)
+    load(5).wait()
+    cut(f_contract, own.at[2], 4 * half // 128)
+    mod_wait()
+    pieces[c] = jnp.sum(mod_got[...], axis=0) + b_mod[...]
+    swap(0, pieces.at[c], pieces.at[c]).start()
+    gat.step(0, 1)
+    gat.begin(2)
+    swap(0, pieces.at[c], pieces.at[c]).wait()
+    shift, scale, gate = (pieces[0, :, i * width : (i + 1) * width] for i in range(3))
+    h1[c] = (normal(x[...]) * (1.0 + scale) + shift).astype(low)
+    swap(1, h1.at[c], h1.at[c]).start()
+
+    @pl.loop(2, line + 1)
+    def _(k):
+        gat.step(0, k)
+
+    gat.paired(1)
+    gat.complete(0)
+
+    def fetch():
+        return pltpu.make_async_copy(weights.at[0], blocks, w_sem.at[0])
+
+    fetch().start()
+    gat.paired(2)
+    swap(1, h1.at[c], h1.at[c]).wait()
+    fetch().wait()
+    for i in range(n):
+        w[i * own_rows : (i + 1) * own_rows, :] = blocks[i // 4, i // 2 % 2, i % 2]
+    keep_w = pltpu.make_async_copy(w, weight, w_sem.at[1])
+    keep_w.start()
+    both = jnp.concatenate([h1[0], h1[1]], axis=0)
+
+    @pl.loop(0, proj.shape[1] // 256)
+    def _(t):
+        cols = pl.ds(pl.multiple_of(t * 256, 256), 256)
+        proj[:, cols] = dot(both, w[:, cols])
+
+    spare = q.shape[1] - half
+    for item, value in (
+        (q, proj[:, :half] + b_query[...]),
+        (k, proj[:, half : 2 * half]),
+        (v, proj[:, 2 * half : 3 * half] + b_value[...]),
+    ):
+        item[:, :half] = value.astype(low)
+        item[:, half:] = jnp.zeros((2 * rows, spare), low)
+    mix[...] = jnp.zeros_like(mix)
+    seen = jnp.broadcast_to(key_ok[...], (2 * rows, 2 * rows)) > 0.0
+    heads = half // HEAD_DIM
+
+    def head(h):
+        win, lanes = head_window(h)
+        probs = head_probs(q[:, win] * lanes, k[:, win], seen)
+        mix[:, win] = mix[:, win] + dot(probs.astype(low), v[:, win] * lanes)
+
+    @pl.loop(0, max(heads, 2 * line))
+    def _(t):
+        when(t < heads, lambda: head(t))
+        when(t < 2 * line, lambda: gat.step(1 + t % 2, t // 2 + 1))
+
+    o[...] = mix[...].astype(low)
+    wide[:, : 3 * half - edge] = jnp.zeros((2 * rows, 3 * half - edge), low)
+    wide[:, 3 * half - edge :] = mix[:, :half].astype(low)
+
+    @pl.loop(0, tiles)
+    def _(t):
+        cols = pl.ds(pl.multiple_of(t * 128, 128), 128)
+        part = dot(wide[...], w[cols, edge:], 1, 1)
+        partial[0, :, cols] = part[:rows]
+        partial[1, :, cols] = part[rows:]
+
+    swap(2, partial.at[1 - c], partial_got).start()
+    swap(2, partial.at[1 - c], partial_got).wait()
+    attended[...] = partial[c] + partial_got[...] + b_out[...]
+    middle[...] = x[...] + gate * attended[...]
+    shift, scale = (pieces[1, :, i * width : (i + 1) * width] for i in range(2))
+    h2[c] = (normal(middle[...]) * (1.0 + scale) + shift).astype(low)
+    swap(3, h2.at[c], h2.at[c]).start()
+    gat.complete(1)
+    gat.complete(2)
+    swap(3, h2.at[c], h2.at[c]).wait()
+    keep_w.wait()
+
+    @pl.loop(0, 3)
+    def _(m):
+        gat.drain(m)
+
+
+def forward(hbm_args, vmem_args, n, collective_id):
     line = n // 4
+    onehot, time_vec, x = vmem_args[:3]
+    rows, width = x.shape
+    own_rows, half = width // n, width // 2
+    low, f32 = jnp.bfloat16, jnp.float32
     dma = pltpu.SemaphoreType.DMA
+    vmem, hbm = pl.BlockSpec(memory_space=pltpu.VMEM), pl.BlockSpec(memory_space=pltpu.HBM)
+    heads = (2 * rows, -(-half // 128) * 128)
+    edge = 3 * half // 128 * 128
+
+    def shape(dims, kind):
+        return jax.ShapeDtypeStruct(dims, kind)
+
+    def scratch(dims, kind):
+        return pltpu.VMEM(dims, kind)
+
     return pl.pallas_call(
-        functools.partial(gather_kernel, line),
-        out_shape=jax.ShapeDtypeStruct((count, line, 2, 2, rows, cols), src.dtype),
-        in_specs=[pl.BlockSpec(memory_space=pltpu.HBM)],
-        out_specs=pl.BlockSpec(memory_space=pltpu.HBM),
-        scratch_shapes=[dma((count,))] + [dma((count, 4, line))] * 7,
-        compiler_params=pltpu.CompilerParams(collective_id=collective_id, has_side_effects=True),
-        cost_estimate=pl.CostEstimate(flops=0, bytes_accessed=2 * count * n * rows * cols * 2, transcendentals=0),
-        name="gather_weights",
-    )(src)
+        functools.partial(forward_kernel, line),
+        out_shape=[
+            shape((3, line, 2, 2, own_rows, 4 * half), low),
+            shape((width, 4 * half), low),
+            shape((2, rows, width), low),
+            shape(heads, low),
+            shape(heads, low),
+            shape(heads, low),
+            shape(heads, low),
+            shape((rows, width), f32),
+            shape((rows, width), f32),
+            shape((2, rows, width), low),
+            shape((2, 1, 3 * width), f32),
+            shape((n, 128), f32),
+            shape((n, 128), low),
+            shape((128, 3 * width), low),
+        ],
+        in_specs=[hbm] * len(hbm_args) + [vmem] * len(vmem_args),
+        out_specs=[hbm] * 2 + [vmem] * 12,
+        scratch_shapes=[scratch(item.shape, f32) for item in hbm_args]
+        + [
+            scratch((3, own_rows, 4 * half), low),
+            scratch((onehot.shape[1], width), low),
+            scratch((n, n, 128), f32),
+            scratch((n, n, 128), f32),
+            scratch((n, 3 * width), f32),
+            scratch((n, 1, 3 * width), f32),
+            scratch((n, 1, 3 * width), f32),
+            scratch((line, 2, 2, own_rows, 4 * half), low),
+            scratch((width, 4 * half), low),
+            scratch((2 * rows, edge + 128), f32),
+            scratch(heads, f32),
+            scratch(heads, low),
+            scratch((2, rows, width), f32),
+            scratch((rows, width), f32),
+            dma((6,)),
+            dma((2,)),
+            dma((4,)),
+            dma((4,)),
+            dma((n,)),
+            dma((n,)),
+            dma((n,)),
+            dma((n,)),
+            dma((3,)),
+        ]
+        + [dma((3, 4, line))] * 7,
+        compiler_params=pltpu.CompilerParams(
+            collective_id=collective_id, has_side_effects=True, vmem_limit_bytes=60 * 2**20),
+        name="forward",
+    )(*hbm_args, *vmem_args)
 
 
 class Reducer:
@@ -346,10 +628,6 @@
 
 def make_reducer(line, grads, out, refs):
     return Reducer(line, grads, out, refs[:4], refs[4:8], refs[8:12], refs[12:16], refs[16:])
-
-
-def dot(left, right, a=1, b=0):
-    return lax.dot_general(left, right, (((a,), (b,)), ((), ())), preferred_element_type=jnp.float32)
 
 
 def backward_kernel(line, *refs):
@@ -371,33 +649,9 @@
         return pltpu.make_async_remote_copy(
             src_ref=src, dst_ref=dst, send_sem=pair_send.at[i], recv_sem=pair_recv.at[i], device_id=partner, device_id_type=MESH)
 
-    def to_all(src, dst, send, recv, spread):
-        def copy(j, there, slot):
-            return pltpu.make_async_remote_copy(
-                src_ref=src.at[there] if spread else src, dst_ref=dst.at[slot], send_sem=send.at[j], recv_sem=recv.at[slot],
-                device_id=(there, c), device_id_type=MESH)
-
-        def start():
-            @pl.loop(1, n)
-            def _(j):
-                copy(j, (me + j) % n, me).start()
-
-        def wait():
-            @pl.loop(1, n)
-            def _(j):
-                copy(j, (me + j) % n, (me + n - j) % n).wait()
-
-        return start, wait
-
     w_copy = pltpu.make_async_copy(weight, w, w_sem)
     w_copy.start()
-    bar = pltpu.get_barrier_semaphore()
-    pl.semaphore_signal(bar, inc=1, device_id=partner, device_id_type=MESH)
-
-    @pl.loop(1, n)
-    def _(j):
-        pl.semaphore_signal(bar, inc=1, device_id=((me + j) % n, c), device_id_type=MESH)
-
+    bar = greet_all(n)
     pl.semaphore_wait(bar, n)
     red.begin(0)
     red.begin(1)
@@ -411,14 +665,9 @@
     seen = jnp.broadcast_to(key_ok[...], (2 * rows, 2 * rows)) > 0.0
 
     def head(h):
-        lo = pl.multiple_of(h * HEAD_DIM // 128 * 128, 128)
-        win = pl.ds(lo, 256)
-        lane = lax.broadcasted_iota(jnp.int32, (1, 256), 1) + lo - h * HEAD_DIM
-        mine = ((lane >= 0) & (lane < HEAD_DIM)).astype(low)
-        qh, kh, doh = q[:, win] * mine, k[:, win] * mine, d_o[:, win] * mine
-        logits = jnp.where(seen, dot(qh, kh, 1, 1) * HEAD_DIM ** (-0.5), MASK_FILL)
-        expo = jnp.exp(logits - jnp.max(logits, axis=-1, keepdims=True))
-        probs = expo / jnp.sum(expo, axis=-1, keepdims=True)
+        win, lanes = head_window(h)
+        qh, kh, doh = q[:, win] * lanes, k[:, win] * lanes, d_o[:, win] * lanes
+        probs = head_probs(qh, kh, seen)
         d_probs = dot(doh, v[:, win], 1, 1)
         inner = jnp.sum(probs * d_probs, axis=-1, keepdims=True)
         d_logits = (probs * (d_probs - inner)).astype(low)
@@ -466,8 +715,8 @@
         dp[1:2] = jnp.sum(d_n * normed, axis=0, keepdims=True)
         swap(1, dp, dp_got).start()
 
-    msg_start, msg_wait = to_all(msg, msg_got, msg_send, msg_recv, False)
-    vec_start, vec_wait = to_all(chunk, vec_got, vec_send, vec_recv, True)
+    msg_start, msg_wait = all_peers(n, msg, msg_got, msg_send, msg_recv, False)
+    vec_start, vec_wait = all_peers(n, chunk, vec_got, vec_send, vec_recv, True)
     per = chunk_tiles(n, width)
 
     def send_mod():
@@ -892,27 +1141,8 @@
         mine = lax.dynamic_slice_in_dim(partial, c * rows, rows, 0)
         return mine + flipped(lax.dynamic_slice_in_dim(partial, (1 - c) * rows, rows, 0))
 
-    def my_half(values, parts):
-        shaped = values.reshape(values.shape[0], parts, pairs, -1)
-        return lax.dynamic_index_in_dim(shaped, c, 2, keepdims=False).reshape(values.shape[0], -1)
-
     def part_of(vector):
         return lax.dynamic_slice_in_dim(vector, c * (vector.shape[0] // pairs), vector.shape[0] // pairs, 0)
-
-    own_attn = jnp.concatenate(
-        [
-            my_half(attention_in_master.reshape(own_rows, 3 * width), 3),
-            my_half(attention_out_master.reshape(own_rows, width), 1),
-        ],
-        axis=1,
-    )
-    own_expand = my_half(expand_master.reshape(own_rows, FF), 1)
-    own_contract = my_half(contract_master.reshape(own_rows, FF), 1)
-    pieces_own = jnp.stack([own_attn, own_expand, own_contract]).astype(low)
-    weights = gather_weights(pieces_own, n, 1).reshape(3, width, pieces_own.shape[2])
-    weight_in = weights[0, :, : 3 * half_width]
-    weight_out = weights[0, :, 3 * half_width :]
-    weight_expand, weight_contract = weights[1], weights[2]
 
     bias_share = biases_master.shape[0]
     bias_block = jnp.pad(biases_master.astype(low).astype(jnp.float32), (0, 1024 - bias_share)).reshape(8, 128)
@@ -928,43 +1158,41 @@
     bias_contract = biases[9 * width + FF :]
 
     class_rows = CLASSES // n
-    table = class_table_master.reshape(class_rows, width).astype(low)
     onehot = labels_all[:, None] == me * class_rows + jnp.arange(class_rows)[None, :]
-    part = jnp.dot(onehot.astype(low), table, preferred_element_type=jnp.float32)
-    part = part + jnp.where(jnp.arange(n)[:, None] == me, time_vec.astype(jnp.float32), 0.0)
-    part = part.reshape(n, n, own_rows).transpose(1, 0, 2)
-    part = jnp.pad(part, ((0, 0), (0, 0), (0, 128 - own_rows)))
-    (got,) = exchange([part], (True,), n, 4)
-    cond_own = jnp.sum(got, axis=0)[:, :own_rows]
-    silu_own = jax.nn.silu(cond_own).astype(low)
-    own_modulation = my_half(modulation_master.reshape(own_rows, 6 * width), 1).astype(low)
-    part = jnp.dot(silu_own, own_modulation, preferred_element_type=jnp.float32).reshape(n, 3 * width // 128, 128)
-    (got,) = exchange([jnp.pad(part, ((0, 0), (0, -part.shape[1] % 8), (0, 0)))], (True,), n, 5)
-    mod_half = jnp.sum(got, axis=0)[: 3 * width // 128].reshape(-1) + part_of(bias_mod)
-    pieces = lax.all_gather(mod_half.reshape(1, 3, width), "seq", axis=0, tiled=True).reshape(6, 1, width)
-
     inputs = tokens[0].astype(jnp.float32) + grid_embed(keep_index[0], width)
     half_kept = kept // pairs
     row_ok = jnp.arange(rows) < half_kept
-    key_ok = (jnp.arange(rows * pairs) % rows) < half_kept
-    normed_in = rows_all(modulated(inputs, pieces[0], pieces[1]).astype(low))
-    projected = jnp.dot(normed_in, weight_in, preferred_element_type=jnp.float32)
-
-    def split_heads(values):
-        return values.reshape(values.shape[0], half_width // HEAD_DIM, HEAD_DIM)
-
-    flat_query = (projected[:, :half_width] + part_of(bias_query)).astype(low)
-    flat_key = projected[:, half_width : 2 * half_width].astype(low)
-    flat_value = (projected[:, 2 * half_width :] + part_of(bias_value)).astype(low)
-    queries, keys, values = split_heads(flat_query), split_heads(flat_key), split_heads(flat_value)
-    scale = HEAD_DIM ** (-0.5)
-    logits = jnp.einsum("rhe,ghe->hrg", queries, keys, preferred_element_type=jnp.float32) * scale
-    logits = jnp.where(key_ok[None, None, :], logits, MASK_FILL)
-    expo = jnp.exp(logits - jnp.max(logits, axis=-1, keepdims=True))
-    probs = expo / jnp.sum(expo, axis=-1, keepdims=True)
-    probs_low = probs.astype(low)
-    mixed = jnp.einsum("hrg,ghe->rhe", probs_low, values, preferred_element_type=jnp.float32)
-    mixed = mixed.reshape(rows * pairs, half_width).astype(low)
+    key_ok = ((jnp.arange(rows * pairs) % rows) < half_kept).astype(jnp.float32)[None]
+    (weights, weight_attn, normed_in, flat_query, flat_key, flat_value, mixed, attended, middle, normed_mid, pieces, cond_own,
+     silu_own, own_modulation) = forward(
+        [
+            item.reshape(-1, 128)
+            for item in (
+                attention_in_master,
+                attention_out_master,
+                expand_master,
+                contract_master,
+                class_table_master,
+                modulation_master,
+            )
+        ],
+        [
+            onehot.astype(low),
+            time_vec,
+            inputs,
+            key_ok,
+            part_of(bias_mod)[None],
+            part_of(bias_query)[None],
+            part_of(bias_value)[None],
+            bias_out[None],
+        ],
+        n,
+        1,
+    )
+    weights = weights.reshape(3, width, 4 * half_width)
+    weight_expand, weight_contract = weights[1], weights[2]
+    pieces = pieces.reshape(6, 1, width)
+    normed_in, normed_mid = normed_in.reshape(-1, width), normed_mid.reshape(-1, width)
 
     def times_transposed(left, right):
         return lax.dot_general(left, right, (((1,), (1,)), ((), ())), preferred_element_type=jnp.float32)
@@ -974,9 +1202,6 @@
             left, right, (((0,), (0,)), ((), ())), preferred_element_type=jnp.float32
         )
 
-    attended = rows_own(times_transposed(mixed, weight_out)) + bias_out
-    middle = inputs + pieces[2] * attended
-    normed_mid = rows_all(modulated(middle, pieces[3], pieces[4]).astype(low))
     hidden = jnp.dot(normed_mid, weight_expand, preferred_element_type=jnp.float32) + part_of(bias_expand)
     activated = gelu_tanh(hidden).astype(low)
     branch = rows_own(times_transposed(activated, weight_contract)) + bias_contract
@@ -998,9 +1223,6 @@
     d_attended = rows_all((pieces[2] * d_middle).astype(low))
     d_gate_attn = jnp.sum(d_middle * attended, axis=0, keepdims=True)
     grad_bias_out = jnp.sum(d_attended.astype(jnp.float32), axis=0)
-
-    def to_tiles(values):
-        return jnp.pad(values, ((0, 0), (0, -values.shape[1] % 128)))
 
     pair_t = jnp.concatenate([normed_in.T, d_attended.T], axis=1).reshape(n, own_rows, 2 * pairs * rows)
     zero_row = jnp.zeros((1, width), jnp.float32)
@@ -1018,24 +1240,24 @@
             zero_row,
         ]
     )
-    shape = (n // 4, 2, 2, own_rows, pieces_own.shape[2])
+    shape = (n // 4, 2, 2, own_rows, 4 * half_width)
     reduced, tokens_grad, d_mod_all, d_cond, bias_sum = backward(
-        (grad_contract.reshape(shape), grad_expand.reshape(shape), weights[0]),
+        (grad_contract.reshape(shape), grad_expand.reshape(shape), weight_attn),
         (
             pair_t,
             d_attended,
-            to_tiles(flat_query),
-            to_tiles(flat_key),
-            to_tiles(flat_value),
-            to_tiles(mixed),
-            key_ok.astype(jnp.float32)[None],
+            flat_query,
+            flat_key,
+            flat_value,
+            mixed,
+            key_ok,
             inputs,
             d_middle,
             pieces[1],
             d_pieces,
             v_rows,
-            jnp.pad(own_modulation, ((0, 128 - own_rows), (0, 0))),
-            jnp.pad(cond_own, ((0, 0), (0, 128 - own_rows))),
+            own_modulation,
+            cond_own,
         ),
         n,
         2,
@@ -1081,7 +1303,7 @@
     states = list(zip(masters, firsts, seconds))
     updated, grad_norm, bias_parts = finish(
         reduced,
-        silu_own,
+        silu_own[:, :own_rows],
         d_mod_all,
         d_cond,
         bias_sum,

time: 460 us -> 399 us (0.87); the launches traced: 451 us -> 398 us
  local copies, waits for them, and re-layouts: 55.2 us -> 30.8 us
  Pallas kernels: 330 us -> 315 us
  blocking collectives: 11.5 us -> 4.86 us
    pallas_call x3 -> x1, Pallas kernels: 27 us -> 8.62 us  [exchange(): pl.pallas_call(functools.partial(exchange_kernel, n, spread), out_shape=[...]
    another operation x7 -> x1, local copies, waits for them, and re-layouts: 10.4 us -> 0.01 us  [the longest x5 6.65 us: my_half(): shaped = values.reshape(values.shape[0], parts, pairs, -1)]
    dot_general x4 -> x0, matrix products: 6.31 us -> none  [the longest x1 3.98 us: per_device(): jnp.dot(normed_in, weight_in, preferred_element_type=jnp.float32)]
    pad x7 -> x0, local copies, waits for them, and re-layouts: 5.97 us -> none  [the longest x4 4.97 us: to_tiles(): return jnp.pad(values, ((0, 0), (0, -values.shape[1] % 128)))]
    all_gather x4 -> x2, blocking collectives: 9.64 us -> 4.86 us  [rows_all(): return lax.all_gather(values, 'seq', axis=0, tiled=True)]
    slice x3 -> x1, local copies, waits for them, and re-layouts: 12.3 us -> 8.82 us  [per_device(): weight_expand, weight_contract = (weights[1], weights[2])]
    unnamed x112 -> x71, local copies, waits for them, and re-layouts: 14.1 us -> 12.3 us
  transfers between devices with their start and end apart: 3 -> 2, of which waited for: 0 -> 0; matrix products, arithmetic and copies ran while one was open for 7% -> 4% of each run, Pallas kernels for 0% -> 0%
where the time goes in v4:
time: 399 us; the launch traced here: 398 us
  Pallas kernels  315 us (79%)
  local copies, waits for them, and re-layouts  30.8 us (8%)
  matrix products  30.7 us (8%)
  other arithmetic  12.6 us (3%)
  blocking collectives  4.86 us (1%)
    pallas_call x1, Pallas kernels, backward(): pl.pallas_call(functools.partial(backward_kernel, line), out_shape=[jax.S...  148 us
    pallas_call x1, Pallas kernels, forward(): pl.pallas_call(functools.partial(forward_kernel, line), out_shape=[shape(...  126 us
    pallas_call x1, Pallas kernels, finish(): pl.pallas_call(functools.partial(norm_kernel, n), out_shape=flats + [smal...  16.5 us
    pallas_call x1, Pallas kernels, finish(): pl.pallas_call(functools.partial(adam_kernel, rates), out_shape=[f for f...  16.4 us
    unnamed x71, local copies, waits for them, and re-layouts  12.3 us
    dot_general x2, matrix products, contract_rows(): lax.dot_general(left, right, (((0,), (0,)), ((), ())), preferred_element_...  9.68 us
    slice x1, local copies, waits for them, and re-layouts, per_device(): weight_expand, weight_contract = (weights[1], weights[2])  8.82 us
    pallas_call x1, Pallas kernels, exchange(): pl.pallas_call(functools.partial(exchange_kernel, n, spread), out_shape=[...  8.62 us
  transfers between devices with their start and end apart: 2, of which 0 were waited for; matrix products, arithmetic and copies ran while one was open for 4% of the time, Pallas kernels for 0%

profile of v4, /device:TPU:12, one launch (start us, length us, event | category | flops | bytes accessed | tf_op | source)
XLA Modules:
  0.0 398.0 jit_solution(2692004516489589004)
XLA Ops:
  1.4 0.7 convert_element_type.115
  2.7 8.6 %exchange.1 = f32[16,16,128]{2,1,0:T(8,128)S(1)} custom-call(f32[16,128]{1,0:T(8,128)S(1)} %concatenate.21.refs_0_), custom_call_target="tpu_custom_call" | custom-call | tf_op jit(solution)/shard_map/exchange/pallas_call | solution.py:871
  11.8 0.6 compare_convert_fusion.3.refs_9_
  12.5 0.7 fusion.15
  13.3 0.6 broadcast_in_dim.74.refs_10_
  14.0 0.6 broadcast_in_dim.75.refs_11_
  14.6 0.6 broadcast_in_dim.76.refs_12_
  15.2 0.6 broadcast_in_dim.77.refs_13_
  15.8 0.7 compare_convert_fusion
  16.5 1.4 multiply_cosine_fusion
  18.2 0.9 convert_add_fusion.refs_8_.refs_10_
  19.1 126.2 %forward.1 = (bf16[3,4,2,2,72,2304]{5,4,3,2,1,0:T(8,128)(2,1)}, bf16[1152,2304]{1,0:T(8,128)(2,1)}, bf16[2,128,1152]{2,1,0:T(8,128)(2,1)}, bf16[256,640]{1,0:T(8...) custom-call(f32[1944,128]{1,0:T(8,128)} %bitcast.120, ...), custom_call_target="tpu_custom_call" | custom-call | tf_op jit(solution)/shard_map/forward/pallas_call | solution.py:410
  145.3 8.8 %fusion.24 = (bf16[1,4,2,2,72,2304]{5,4,3,2,1,0:T(8,128)(2,1)}, bf16[1,4,2,2,72,2304]{5,4,3,2,1,0:T(8,128)(2,1)}) fusion(bf16[3,4,2,2,72,2304]{5,4,3,2,1,0:T(8,128)(2,1)} %get-tuple-element.73), kind=kLoop, calls=%fused_computation.88 | loop fusion | bytes 21233664 | tf_op jit(solution)/shard_map/slice | solution.py:1193
  154.2 0.6 slice_reduce_fusion.4
  155.0 2.4 all_gather.6
  157.4 5.7 %fusion.26 = f32[256,2304]{1,0:T(8,128)} fusion(bf16[256,1152]{1,0:T(8,128)(2,1)S(1)} %all_gather.6, bf16[1152,2304]{1,0:T(8,128)(2,1)} %bitcast.111), kind=kOutput, calls=%fused_computation.90 | convolution fusion | flops 1358954496 | bytes 8257536 | tf_op jit(solution)/shard_map/dot_general | solution.py:1216
  163.2 7.5 %convert_reduce_fusion = (f32[2304]{0:T(1024)S(1)}, bf16[256,2304]{1,0:T(8,128)(2,1)}, f32[256,2304]{1,0:T(8,128)S(1)}) fusion(f32[256,2304]{1,0:T(8,128)} %fusion.26, f32[2304]{0:T(1024)S(1)} %dynamic_slice.30, bf16[256,1152]{1,0:T(8,128)(2,1)S(1)} %bitcast.132, bf16[1152,2304]{1,0:T(8,128)(2,1)} %bitcast.109), kind=kOutput, calls=%fused_computation.12 | convolution fusion | flops 1372518144 | bytes 11814912 | tf_op jit(solution)/shard_map/dot_general | solution.py:1205
  170.7 1.4 copy-done.29
  172.1 3.1 fusion.19
  175.2 1.9 constant_dynamic-slice_fusion.1
  177.3 4.7 %fusion.27 = f32[256,1152]{1,0:T(8,128)S(1)} fusion(bf16[256,2304]{1,0:T(8,128)(2,1)} %get-tuple-element.130, bf16[1152,2304]{1,0:T(8,128)(2,1)} %bitcast.110), kind=kOutput, calls=%fused_computation.91 | convolution fusion | flops 1358954496 | bytes 7667712 | tf_op jit(solution)/shard_map/dot_general | solution.py:1198
  182.0 0.9 constant_dynamic-slice_fusion
  183.3 3.9 convolution_convert_fusion
  187.8 5.8 %convolution_convert_fusion.1 = bf16[1152,2304]{1,0:T(8,128)(2,1)} fusion(bf16[256,1152]{1,0:T(8,128)(2,1)S(1)} %all_gather.6, f32[256,2304]{1,0:T(8,128)} %copy-done.29), kind=kOutput, calls=%fused_computation.1 | convolution fusion | flops 1366917120 | bytes 8257536 | tf_op jit(solution)/shard_map/dot_general | solution.py:1201
  193.6 1.5 multiply_reduce_fusion
  195.1 2.3 fusion.11
  197.6 2.4 all_gather.7.refs_4_
  200.3 1.4 copy.52
  201.8 0.7 concatenate.24.refs_13_
  202.5 0.7 concatenate.26.refs_14_
  203.1 147.5 %backward.1 = (bf16[3,72,2304]{2,1,0:T(8,128)(2,1)}, bf16[128,1152]{1,0:T(8,128)(2,1)}, f32[2,16,3456]{2,1,0:T(8,128)}, f32[16,128]{1,0:T(8,128)}, f32[2,8,128]{2,1,0:T(8,128)}) custom-call(bf16[4,2,2,72,2304]{4,3,2,1,0:T(8,128)(2,1)} %bitcast.108, bf16[4,2,2,72,2304]{4,3,2,1,0:T(8,128)(2,1)} %bitcast.104, bf16[1152,2304]{1,0:T(8,128)(2,1)} %get-tuple-element.74.refs_2_, ...), custom_call_target="tpu_custom_call" | custom-call | tf_op jit(solution)/shard_map/backward/pallas_call | solution.py:792
  350.7 1.1 reduce_sum.127
  351.8 1.0 copy-done.1
  352.8 1.2 copy-done.4
  354.0 0.7 copy-done.8
  354.7 0.7 copy-done.9
  355.4 16.5 %norm.1 = (f32[3888,128]{1,0:T(8,128)S(1)}, f32[1944,128]{1,0:T(8,128)S(1)}, f32[648,128]{1,0:T(8,128)S(1)}, f32[2592,128]{1,0:T(8,128)S(1)}, f32[2592,128]{1,0:...) custom-call(bf16[3,72,2304]{2,1,0:T(8,128)(2,1)S(1)} %copy-done.4, ...), custom_call_target="tpu_custom_call" | custom-call | tf_op jit(solution)/shard_map/norm/pallas_call | solution.py:1040
  371.9 1.3 copy-done
  373.2 1.1 copy-done.2
  374.3 1.1 copy-done.3
  375.3 1.0 copy-done.5
  376.3 0.7 copy-done.6
  377.1 0.7 copy-done.7
  377.8 0.6 copy-done.11
  378.7 0.5 slice.91
  380.2 0.7 multiply_subtract_fusion
  380.9 16.4 %adam.1 = (f32[3888,128]{1,0:T(8,128)}, f32[3888,128]{1,0:T(8,128)}, f32[3888,128]{1,0:T(8,128)}, f32[1944,128]{1,0:T(8,128)}, f32[1944,128]{1,0:T(8,128)}, /*in...) custom-call(f32[8,128]{1,0:T(8,128)} %copy-done.11, ...), custom_call_target="tpu_custom_call" | custom-call | tf_op jit(solution)/shard_map/adam/pallas_call | solution.py:1060
  397.3 0.7 copy.68
  (118 shorter events, 3.5 us)
Async XLA Ops:
  0.7 17.5 %copy-start.24 = (bf16[1,128,1152]{2,1,0:T(8,128)(2,1)S(1)}, bf16[1,128,1152]{2,1,0:T(8,128)(2,1)}, u32[]{:S(2)}) copy-start(bf16[1,128,1152]{2,1,0:T(8,128)(2,1)} %param.27) | copy-start | bytes 884740
  145.3 8.8 %copy-start.25 = (f32[2,1,3456]{2,1,0:T(1,128)S(1)}, f32[2,1,3456]{2,1,0:T(1,128)}, u32[]{:S(2)}) copy-start(f32[2,1,3456]{2,1,0:T(1,128)} %get-tuple-element.71) | copy-start | bytes 82948
  145.3 9.6 %copy-start.15 = (bf16[1,128,1152]{2,1,0:T(8,128)(2,1)S(1)}, bf16[1,128,1152]{2,1,0:T(8,128)(2,1)}, u32[]{:S(2)}) copy-start(bf16[1,128,1152]{2,1,0:T(8,128)(2,1)} %param.28) | copy-start | bytes 884740
  157.4 5.8 %copy-start.20 = (bf16[2,128,1152]{2,1,0:T(8,128)(2,1)S(1)}, bf16[2,128,1152]{2,1,0:T(8,128)(2,1)}, u32[]{:S(2)}) copy-start(bf16[2,128,1152]{2,1,0:T(8,128)(2,1)} %get-tuple-element.72) | copy-start | bytes 1769476
  157.4 14.7 %slice-start = ((s8[5308416]{0:T(1024)(128)(4,1)}), s8[1114112]{0:T(1024)(128)(4,1)S(1)}, s32[]{:S(2)}) async-start(s8[5308416]{0:T(1024)(128)(4,1)} %bitcast.112), calls=%async_computation | async-start | bytes 2228224
  163.2 8.9 %slice-start.1 = ((s8[5308416]{0:T(1024)(128)(4,1)}), s8[4194304]{0:T(1024)(128)(4,1)S(1)}, s32[]{:S(2)}) async-start(s8[5308416]{0:T(1024)(128)(4,1)} %bitcast.112), calls=%async_computation.1 | async-start | bytes 8388608
  170.7 1.4 copy-start.29
  177.2 17.9 %collective-permute-start = (f32[128,1152]{1,0:T(8,128)}, f32[128,1152]{1,0:T(8,128)}, u32[]{:S(2)}, u32[]{:S(2)}) collective-permute-start(f32[128,1152]{1,0:T(8,128)} %constant_dynamic-slice_fusion.1), channel_id=1, source_target_pairs={{0,1},{1,0},{2,3},{3,2},{4,5},{5,4},{6,7},{7,6},{8,9},{9,8},{10,11... | collective-permute-start | bytes 1769480 | tf_op jit(solution)/shard_map/ppermute | solution.py:1135
  177.3 6.0 %copy-start.16 = (bf16[256,2304]{1,0:T(8,128)(2,1)S(1)}, bf16[256,2304]{1,0:T(8,128)(2,1)}, u32[]{:S(2)}) copy-start(bf16[256,2304]{1,0:T(8,128)(2,1)} %get-tuple-element.130) | copy-start | bytes 3538948
  182.0 5.2 %copy-start.18 = (f32[256,1152]{1,0:T(8,128)}, f32[256,1152]{1,0:T(8,128)S(1)}, u32[]{:S(2)}) copy-start(f32[256,1152]{1,0:T(8,128)S(1)} %fusion.27) | copy-start | bytes 3538948
  182.9 4.4 %copy-start.13 = (f32[128,1152]{1,0:T(8,128)S(1)}, f32[128,1152]{1,0:T(8,128)}, u32[]{:S(2)}) copy-start(f32[128,1152]{1,0:T(8,128)} %get-tuple-element.70) | copy-start | bytes 1769476
  182.9 10.7 %collective-permute-start.1 = (f32[128,1152]{1,0:T(8,128)}, f32[128,1152]{1,0:T(8,128)}, u32[]{:S(2)}, u32[]{:S(2)}) collective-permute-start(f32[128,1152]{1,0:T(8,128)} %constant_dynamic-slice_fusion), channel_id=1, source_target_pairs={{0,1},{1,0},{2,3},{3,2},{4,5},{5,4},{6,7},{7,6},{8,9},{9,8},{10,11... | collective-permute-start | bytes 1769480 | tf_op jit(solution)/shard_map/ppermute | solution.py:1135
  187.8 5.8 %copy-start.19 = (f32[256,1152]{1,0:T(8,128)S(1)}, f32[256,1152]{1,0:T(8,128)}, u32[]{:S(2)}) copy-start(f32[256,1152]{1,0:T(8,128)} %copy-done.18) | copy-start | bytes 3538948
  193.6 1.5 copy-start.17
  195.0 2.3 copy-start.21
  197.4 2.8 copy-start.22
  197.6 2.7 copy-start.14
  200.1 1.7 copy-start.12
  203.1 148.7 %copy-start.10 = (bf16[16,128]{1,0:T(8,128)(2,1)S(1)}, bf16[16,128]{1,0:T(8,128)(2,1)}, u32[]{:S(2)}) copy-start(bf16[16,128]{1,0:T(8,128)(2,1)} %get-tuple-element.85) | copy-start | bytes 12292
  350.7 29.5 %copy-start.26 = (f32[1008]{0:T(1024)S(1)}, f32[1008]{0:T(1024)}, u32[]{:S(2)}) copy-start(f32[1008]{0:T(1024)} %param.51) | copy-start | bytes 12100
  350.7 29.5 %copy-start.27 = (f32[1008]{0:T(1024)S(1)}, f32[1008]{0:T(1024)}, u32[]{:S(2)}) copy-start(f32[1008]{0:T(1024)} %param.53) | copy-start | bytes 12100
  350.7 29.5 %copy-start.28 = (f32[1008]{0:T(1024)S(1)}, f32[1008]{0:T(1024)}, u32[]{:S(2)}) copy-start(f32[1008]{0:T(1024)} %param.52) | copy-start | bytes 12100
  351.8 1.0 copy-start.1
  352.8 1.2 copy-start.4
  354.0 0.7 copy-start.8
  354.7 0.7 copy-start.9
  371.9 1.3 copy-start
  373.2 1.1 copy-start.2
  374.3 1.1 copy-start.3
  375.3 1.0 copy-start.5
  376.3 0.7 copy-start.6
  377.1 0.7 copy-start.7
  377.8 0.6 copy-start.11
  380.9 16.4 %copy-start.23 = (bf16[128,1152]{1,0:T(8,128)(2,1)S(1)}, bf16[128,1152]{1,0:T(8,128)(2,1)}, u32[]{:S(2)}) copy-start(bf16[128,1152]{1,0:T(8,128)(2,1)} %get-tuple-element.83) | copy-start | bytes 884740

commit v5 on v4

--- a/solution.py
+++ b/solution.py
@@ -20,6 +20,8 @@
 CLIP_LIMIT = 1.0
 
 MESH = pl.DeviceIdType.MESH
+GELU_A = (2.0 / 3.141592653589793) ** 0.5
+GELU_B = 0.044715
 GROUPS = ((0, 768, 0, "x"), (768, 768, 0, "y"), (1536, 384, 1, "x"), (1920, 384, 1, "y"))
 
 
@@ -221,16 +223,39 @@
     return expo / jnp.sum(expo, axis=-1, keepdims=True)
 
 
+def to_blocks(values, ref):
+    count, size = ref.shape[:2]
+    turned = values.T
+    for i in range(count):
+        ref[i] = turned[i * size : (i + 1) * size]
+
+
+def write_blocks(n, target, stage, sem, block):
+    def copy(i):
+        return pltpu.make_async_copy(stage.at[i % 2], target.at[i // 4, i // 2 % 2, i % 2], sem.at[i % 2])
+
+    @pl.loop(0, n)
+    def _(i):
+        when(i >= 2, lambda: copy(i).wait())
+        stage[i % 2] = block(i).astype(stage.dtype)
+        copy(i).start()
+
+    copy(0).wait()
+    copy(1).wait()
+
+
 def forward_kernel(line, *refs):
     (m_in, m_out, m_expand, m_contract, m_table, m_mod, onehot, time_vec, x, key_ok, b_mod, b_query, b_value, b_out,
-     weights, weight, h1, q, k, v, o, attended, middle, h2, pieces, cond, silu, mod_half) = refs[:28]
+     b_expand, cot, row_ok) = refs[:17]
+    (weights, g_contract, h1_t, h2_t, q, k, v, o, attended, middle, act, slope, d_branch, pieces, cond, silu,
+     mod_half) = refs[17:34]
     (f_in, f_out, f_expand, f_contract, f_table, f_mod, own, table, cond_part, cond_got, mods, mod_part, mod_got, blocks, w,
-     proj, mix, wide, partial, partial_got, in_sem, w_sem, pair_send, pair_recv, cond_send, cond_recv, mod_send, mod_recv,
-     keep_sem) = refs[28:57]
+     proj, mix, wide, partial, partial_got, h1, h2, d_branch_t, stage, in_sem, w_sem, pair_send, pair_recv, cond_send,
+     cond_recv, mod_send, mod_recv, keep_sem, stage_sem) = refs[34:68]
     n = line * 4
     low, f32 = jnp.bfloat16, jnp.float32
     me, c = lax.axis_index("dp"), lax.axis_index("seq")
-    gat = Gatherer(line, own, weights, keep_sem, refs[57:])
+    gat = Gatherer(line, own, weights, keep_sem, refs[68:])
     rows, width = x.shape
     own_rows, half = own.shape[1], own.shape[2] // 4
     edge = 3 * half // 128 * 128
@@ -314,6 +339,8 @@
     shift, scale, gate = (pieces[0, :, i * width : (i + 1) * width] for i in range(3))
     h1[c] = (normal(x[...]) * (1.0 + scale) + shift).astype(low)
     swap(1, h1.at[c], h1.at[c]).start()
+    d_branch[c] = (pieces[1, :, 2 * width :] * (cot[...].astype(f32) * row_ok[...])).astype(low)
+    swap(4, d_branch.at[c], d_branch.at[c]).start()
 
     @pl.loop(2, line + 1)
     def _(k):
@@ -322,18 +349,20 @@
     gat.paired(1)
     gat.complete(0)
 
-    def fetch():
-        return pltpu.make_async_copy(weights.at[0], blocks, w_sem.at[0])
-
-    fetch().start()
+    def fetch(m):
+        return pltpu.make_async_copy(weights.at[m], blocks, w_sem.at[m])
+
+    def unpack():
+        for i in range(n):
+            w[i * own_rows : (i + 1) * own_rows, :] = blocks[i // 4, i // 2 % 2, i % 2]
+
+    fetch(0).start()
     gat.paired(2)
     swap(1, h1.at[c], h1.at[c]).wait()
-    fetch().wait()
-    for i in range(n):
-        w[i * own_rows : (i + 1) * own_rows, :] = blocks[i // 4, i // 2 % 2, i % 2]
-    keep_w = pltpu.make_async_copy(w, weight, w_sem.at[1])
-    keep_w.start()
+    fetch(0).wait()
+    unpack()
     both = jnp.concatenate([h1[0], h1[1]], axis=0)
+    to_blocks(both, h1_t)
 
     @pl.loop(0, proj.shape[1] // 256)
     def _(t):
@@ -360,7 +389,7 @@
     @pl.loop(0, max(heads, 2 * line))
     def _(t):
         when(t < heads, lambda: head(t))
-        when(t < 2 * line, lambda: gat.step(1 + t % 2, t // 2 + 1))
+        when((t % 2 == 1) & (t < 2 * line), lambda: gat.step(1, t // 2 + 1))
 
     o[...] = mix[...].astype(low)
     wide[:, : 3 * half - edge] = jnp.zeros((2 * rows, 3 * half - edge), low)
@@ -374,6 +403,7 @@
         partial[1, :, cols] = part[rows:]
 
     swap(2, partial.at[1 - c], partial_got).start()
+    gat.step(2, 1)
     swap(2, partial.at[1 - c], partial_got).wait()
     attended[...] = partial[c] + partial_got[...] + b_out[...]
     middle[...] = x[...] + gate * attended[...]
@@ -381,9 +411,32 @@
     h2[c] = (normal(middle[...]) * (1.0 + scale) + shift).astype(low)
     swap(3, h2.at[c], h2.at[c]).start()
     gat.complete(1)
+    fetch(1).start()
+    swap(4, d_branch.at[c], d_branch.at[c]).wait()
+    to_blocks(jnp.concatenate([d_branch[0], d_branch[1]], axis=0), d_branch_t)
+    gat.step(2, 2)
+    swap(3, h2.at[c], h2.at[c]).wait()
+    both = jnp.concatenate([h2[0], h2[1]], axis=0)
+    to_blocks(both, h2_t)
+    fetch(1).wait()
+    unpack()
+
+    @pl.loop(0, act.shape[1] // 256)
+    def _(t):
+        cols = pl.ds(pl.multiple_of(t * 256, 256), 256)
+        z = dot(both, w[:, cols]) + b_expand[:, cols]
+        bend = jnp.tanh(GELU_A * (z + GELU_B * z * z * z))
+        act[:, cols] = (0.5 * z * (1.0 + bend)).astype(low)
+        slope[:, cols] = 0.5 * (1.0 + bend) + 0.5 * z * (1.0 - bend * bend) * (GELU_A * (1.0 + 3.0 * GELU_B * z * z))
+
+    gat.step(2, 3)
+    write_blocks(n, g_contract, stage, stage_sem, lambda i: dot(d_branch_t[i], act[...]))
+
+    @pl.loop(4, line + 1)
+    def _(k):
+        gat.step(2, k)
+
     gat.complete(2)
-    swap(3, h2.at[c], h2.at[c]).wait()
-    keep_w.wait()
 
     @pl.loop(0, 3)
     def _(m):
@@ -411,14 +464,17 @@
         functools.partial(forward_kernel, line),
         out_shape=[
             shape((3, line, 2, 2, own_rows, 4 * half), low),
-            shape((width, 4 * half), low),
-            shape((2, rows, width), low),
+            shape((line, 2, 2, own_rows, 4 * half), low),
+            shape((n, own_rows, 2 * rows), low),
+            shape((n, own_rows, 2 * rows), low),
             shape(heads, low),
             shape(heads, low),
             shape(heads, low),
             shape(heads, low),
             shape((rows, width), f32),
             shape((rows, width), f32),
+            shape((2 * rows, 4 * half), low),
+            shape((2 * rows, 4 * half), f32),
             shape((2, rows, width), low),
             shape((2, 1, 3 * width), f32),
             shape((n, 128), f32),
@@ -426,7 +482,7 @@
             shape((128, 3 * width), low),
         ],
         in_specs=[hbm] * len(hbm_args) + [vmem] * len(vmem_args),
-        out_specs=[hbm] * 2 + [vmem] * 12,
+        out_specs=[hbm] * 2 + [vmem] * 15,
         scratch_shapes=[scratch(item.shape, f32) for item in hbm_args]
         + [
             scratch((3, own_rows, 4 * half), low),
@@ -443,19 +499,24 @@
             scratch(heads, low),
             scratch((2, rows, width), f32),
             scratch((rows, width), f32),
+            scratch((2, rows, width), low),
+            scratch((2, rows, width), low),
+            scratch((n, own_rows, 2 * rows), low),
+            scratch((2, own_rows, 4 * half), low),
             dma((6,)),
             dma((2,)),
-            dma((4,)),
-            dma((4,)),
+            dma((5,)),
+            dma((5,)),
             dma((n,)),
             dma((n,)),
             dma((n,)),
             dma((n,)),
             dma((3,)),
+            dma((2,)),
         ]
         + [dma((3, 4, line))] * 7,
         compiler_params=pltpu.CompilerParams(
-            collective_id=collective_id, has_side_effects=True, vmem_limit_bytes=60 * 2**20),
+            collective_id=collective_id, has_side_effects=True, vmem_limit_bytes=63 * 2**20),
         name="forward",
     )(*hbm_args, *vmem_args)
 
@@ -631,36 +692,104 @@
 
 
 def backward_kernel(line, *refs):
-    (g_contract, g_expand, weight, pair_t, d_att, q, k, v, o, key_ok, x, d_mid, scale_a, d_pieces, v_rows, modulation, cond,
-     out, tokens_grad, d_mod_all, d_cond, bias_sum) = refs[:22]
-    (w, grads, rhs, d_o, d_q, d_k, d_v, d_h, d_h_got, dp, dp_got, msg, msg_got, vec, vec_got, d_silu, d_silu_got, chunk,
-     w_sem, pair_send, pair_recv, msg_send, msg_recv, vec_send, vec_recv) = refs[22:47]
+    (weights, g_contract, h1_t, h2_t, act, slope, d_branch, q, k, v, o, key_ok, x, middle, attended, cot, row_ok, pieces,
+     b_contract, modulation, cond) = refs[:21]
+    (g_expand, g_attn, d_mod_all, out, block_out, tokens_grad, d_cond, bias_sum) = refs[21:29]
+    (w, rhs, d_o, d_q, d_k, d_v, d_h, d_h_got, branch_got, d_mid, d_att, d_att_t, stage, dp, dp_got, msg, msg_got, d_mod, vec,
+     vec_got, d_silu, d_silu_got, chunk, w_sem, mod_sem, stage_sem, pair_send, pair_recv, msg_send, msg_recv, vec_send,
+     vec_recv) = refs[29:61]
     n = line * 4
-    low = jnp.bfloat16
+    low, f32 = jnp.bfloat16, jnp.float32
     me, c = lax.axis_index("dp"), lax.axis_index("seq")
-    red = make_reducer(line, (g_contract, g_expand, grads), out, refs[47:])
+    red = make_reducer(line, (g_contract, g_expand, g_attn), out, refs[61:])
     rows, width = x.shape
-    half = weight.shape[1] // 4
+    half = weights.shape[2] // 4
     heads = half // HEAD_DIM
     edge = 3 * half // 128 * 128
-    partner = (me, 1 - c)
+    tiles = width // 128
+    d_z = rhs.at[2 * rows :]
 
     def swap(i, src, dst):
         return pltpu.make_async_remote_copy(
-            src_ref=src, dst_ref=dst, send_sem=pair_send.at[i], recv_sem=pair_recv.at[i], device_id=partner, device_id_type=MESH)
-
-    w_copy = pltpu.make_async_copy(weight, w, w_sem)
-    w_copy.start()
+            src_ref=src, dst_ref=dst, send_sem=pair_send.at[i], recv_sem=pair_recv.at[i], device_id=(me, 1 - c),
+            device_id_type=MESH)
+
+    def fetch(i):
+        return pltpu.make_async_copy(weights.at[(2, 1, 0, 2)[i]], w, w_sem.at[i])
+
+    def back(values, lanes):
+        @pl.loop(0, tiles)
+        def _(t):
+            cols = pl.ds(pl.multiple_of(t * 128, 128), 128)
+            part = dot(values[...], w[cols, :lanes], 1, 1)
+            d_h[0, :, cols] = part[:rows]
+            d_h[1, :, cols] = part[rows:]
+
+    def column_sums(values):
+        return jnp.sum(values.astype(f32), axis=0, keepdims=True)
+
+    def norm_back(values, scale, d_n):
+        centre = values - jnp.mean(values, axis=-1, keepdims=True)
+        inv = lax.rsqrt(jnp.mean(centre * centre, axis=-1, keepdims=True) + LAYER_EPS)
+        normed = centre * inv
+        e = d_n * (1.0 + scale)
+        d_x = (e - jnp.mean(e, axis=-1, keepdims=True) - normed * jnp.mean(e * normed, axis=-1, keepdims=True)) * inv
+        return d_x, jnp.sum(d_n, axis=0, keepdims=True), jnp.sum(d_n * normed, axis=0, keepdims=True)
+
+    def piece(i):
+        return pieces[i // 3, :, i % 3 * width : (i % 3 + 1) * width]
+
+    fetch(0).start()
     bar = greet_all(n)
+    for item in (d_q, d_k, d_v):
+        item[...] = jnp.zeros_like(item)
+    dp[...] = jnp.zeros_like(dp)
+    vec[...] = jnp.zeros_like(vec)
+    vec[4:5] = column_sums(d_branch[0]) + column_sums(d_branch[1])
     pl.semaphore_wait(bar, n)
     red.begin(0)
     red.begin(1)
 
-    w_copy.wait()
-    d_o[:, :half] = dot(d_att[...], w[:, edge:])[:, 3 * half - edge :].astype(low)
-    d_o[:, half:] = jnp.zeros((2 * rows, d_o.shape[1] - half), low)
-    for item in (d_q, d_k, d_v):
-        item[...] = jnp.zeros_like(item)
+    fetch(0).wait()
+    d_out = jnp.concatenate([d_branch[0], d_branch[1]], axis=0)
+
+    @pl.loop(0, act.shape[1] // 256)
+    def _(t):
+        cols = pl.ds(pl.multiple_of(t * 256, 256), 256)
+        d_z[:, cols] = (dot(d_out, w[:, cols]) * slope[:, cols]).astype(low)
+
+    fetch(1).start()
+
+    def expand_grads():
+        write_blocks(n, g_expand, stage, stage_sem, lambda i: dot(h2_t[i], d_z[...]))
+        sums = column_sums(d_z[...])
+        vec[1:2] = sums[:, :width]
+        vec[2:3] = sums[:, width:]
+
+    def hidden_back():
+        fetch(1).wait()
+        back(d_z, 4 * half)
+        swap(0, d_h.at[1 - c], d_h_got).start()
+        fetch(2).start()
+
+    def middle_back():
+        swap(0, d_h.at[1 - c], d_h_got).wait()
+        d_x, shift, scale = norm_back(middle[...], piece(4), d_h[c] + d_h_got[...])
+        d_mid[...] = d_x + cot[...].astype(f32) * row_ok[...]
+        dp[2:3] = jnp.sum(d_mid[...] * attended[...], axis=0, keepdims=True)
+        dp[3:4] = shift
+        dp[4:5] = scale
+        d_att[c] = (piece(2) * d_mid[...]).astype(low)
+        swap(1, d_att.at[c], d_att.at[c]).start()
+
+    def mixed_back():
+        swap(1, d_att.at[c], d_att.at[c]).wait()
+        d_all = jnp.concatenate([d_att[0], d_att[1]], axis=0)
+        to_blocks(d_all, d_att_t)
+        vec[3:4] = column_sums(d_att[0]) + column_sums(d_att[1])
+        fetch(2).wait()
+        d_o[:, :half] = dot(d_all, w[:, edge:])[:, 3 * half - edge :].astype(low)
+        d_o[:, half:] = jnp.zeros((2 * rows, d_o.shape[1] - half), low)
 
     seen = jnp.broadcast_to(key_ok[...], (2 * rows, 2 * rows)) > 0.0
 
@@ -675,65 +804,66 @@
         d_k[:, win] = d_k[:, win] + dot(d_logits, qh, 0, 0) * HEAD_DIM ** (-0.5)
         d_v[:, win] = d_v[:, win] + dot(probs.astype(low), doh, 0, 0)
 
-    def weight_grads():
+    def attention_grads():
         for i, item in enumerate((d_q, d_k, d_v)):
             rhs[: 2 * rows, i * half : (i + 1) * half] = item[:, :half].astype(low)
         rhs[: 2 * rows, 3 * half :] = jnp.zeros((2 * rows, half), low)
         rhs[2 * rows :, edge : 3 * half] = jnp.zeros((2 * rows, 3 * half - edge), low)
         rhs[2 * rows :, 3 * half :] = o[:, :half]
-        vec[0:1, :half] = jnp.sum(rhs[: 2 * rows, :half].astype(jnp.float32), axis=0, keepdims=True)
-        vec[0:1, half:] = jnp.sum(rhs[: 2 * rows, 2 * half : 3 * half].astype(jnp.float32), axis=0, keepdims=True)
-        vec[1:] = v_rows[1:]
-
-        @pl.loop(0, n)
-        def _(i):
-            block = grads.at[i // 4, i // 2 % 2, i % 2]
-            block[:, :edge] = dot(pair_t[i, :, : 2 * rows], rhs[: 2 * rows, :edge]).astype(low)
-            block[:, edge:] = dot(pair_t[i], rhs[:, edge:]).astype(low)
-
-    def input_grad():
-        @pl.loop(0, width // 128)
-        def _(t):
-            cols = pl.ds(pl.multiple_of(t * 128, 128), 128)
-            part = dot(rhs[: 2 * rows, : edge + 128], w[cols, : edge + 128], 1, 1)
-            d_h[0, :, cols] = part[:rows]
-            d_h[1, :, cols] = part[rows:]
-
-        swap(0, d_h.at[1 - c], d_h_got).start()
-
-    def norm_grad():
-        swap(0, d_h.at[1 - c], d_h_got).wait()
-        d_n = d_h[c] + d_h_got[...]
-        centre = x[...] - jnp.mean(x[...], axis=-1, keepdims=True)
-        inv = lax.rsqrt(jnp.mean(centre * centre, axis=-1, keepdims=True) + LAYER_EPS)
-        normed = centre * inv
-        e = d_n * (1.0 + scale_a[...])
-        d_x = (e - jnp.mean(e, axis=-1, keepdims=True) - normed * jnp.mean(e * normed, axis=-1, keepdims=True)) * inv
+        sums = column_sums(rhs[: 2 * rows, : 3 * half])
+        vec[0:1, :half] = sums[:, :half]
+        vec[0:1, half:] = sums[:, 2 * half :]
+
+        def block(i):
+            left = dot(h1_t[i], rhs[: 2 * rows, :edge])
+            right = dot(h1_t[i], rhs[: 2 * rows, edge:]) + dot(d_att_t[i], rhs[2 * rows :, edge:])
+            return jnp.concatenate([left, right], axis=1)
+
+        write_blocks(n, g_attn, stage, stage_sem, block)
+
+    def input_back():
+        back(rhs.at[: 2 * rows, : edge + 128], edge + 128)
+        swap(2, d_h.at[1 - c], d_h_got).start()
+        fetch(3).start()
+
+    def first_back():
+        swap(2, d_h.at[1 - c], d_h_got).wait()
+        d_x, shift, scale = norm_back(x[...], piece(1), d_h[c] + d_h_got[...])
         tokens_grad[...] = (d_x + d_mid[...]).astype(low)
-        dp[...] = d_pieces[...]
-        dp[0:1] = jnp.sum(d_n, axis=0, keepdims=True)
-        dp[1:2] = jnp.sum(d_n * normed, axis=0, keepdims=True)
-        swap(1, dp, dp_got).start()
+        dp[0:1] = shift
+        dp[1:2] = scale
+        fetch(3).wait()
+        back(act, 4 * half)
+        swap(3, d_h.at[1 - c], branch_got).start()
+
+    def branch_out():
+        swap(3, d_h.at[1 - c], branch_got).wait()
+        branch = d_h[c] + branch_got[...] + b_contract[...]
+        result = middle[...] + piece(5) * branch
+        block_out[...] = jnp.where(jnp.broadcast_to(row_ok[...], result.shape) > 0.0, result, 0.0).astype(low)
+        dp[5:6] = jnp.sum(cot[...].astype(f32) * row_ok[...] * branch, axis=0, keepdims=True)
+        swap(4, dp, dp_got).start()
 
     msg_start, msg_wait = all_peers(n, msg, msg_got, msg_send, msg_recv, False)
     vec_start, vec_wait = all_peers(n, chunk, vec_got, vec_send, vec_recv, True)
     per = chunk_tiles(n, width)
 
     def send_mod():
-        swap(1, dp, dp_got).wait()
-        d_mod = (dp[...] + dp_got[...]).astype(low).astype(jnp.float32)
-        own = jnp.where(c == 0, d_mod[0:3], d_mod[3:6])
+        swap(4, dp, dp_got).wait()
+        total = (dp[...] + dp_got[...]).astype(low).astype(f32)
+        own = jnp.where(c == 0, total[0:3], total[3:6])
         for r in range(3):
             msg[r] = own[r : r + 1]
         msg_got[me] = msg[...]
         chunk[...] = jnp.zeros_like(chunk)
-        tiles = width // 128
         for t in range(5 * tiles):
             chunk[t // per, t % per] = vec[t // tiles : t // tiles + 1, t % tiles * 128 : t % tiles * 128 + 128]
         vec_got[me] = chunk[me]
         msg_start()
         vec_start()
 
+    keep_mod = pltpu.make_async_copy(d_mod, d_mod_all.at[c], mod_sem)
+
     def mod_grad():
         msg_wait()
         vec_wait()
@@ -741,34 +871,60 @@
         @pl.loop(0, n)
         def _(s):
             for r in range(3):
-                d_mod_all[c, pl.ds(s, 1), r * width : (r + 1) * width] = msg_got[s, r]
-
-        bias_sum[c] = jnp.zeros((8, 128), jnp.float32)
+                d_mod[pl.ds(s, 1), r * width : (r + 1) * width] = msg_got[s, r]
+
+        bias_sum[c] = jnp.zeros((8, 128), f32)
         for r in range(per):
             bias_sum[c, r : r + 1] = jnp.sum(vec_got[:, r], axis=0)
-        d_silu[...] = dot(d_mod_all[c].astype(low), modulation[...], 1, 1)
-        swap(2, d_silu, d_silu_got).start()
-        swap(3, d_mod_all.at[c], d_mod_all.at[c]).start()
-        swap(4, bias_sum.at[c], bias_sum.at[c]).start()
+        d_silu[...] = dot(d_mod[...].astype(low), modulation[...], 1, 1)
+        swap(5, d_silu, d_silu_got).start()
+        swap(6, d_mod, d_mod_all.at[c]).start()
+        swap(7, bias_sum.at[c], bias_sum.at[c]).start()
+        keep_mod.start()
 
     def cond_grad():
-        swap(2, d_silu, d_silu_got).wait()
-        swap(3, d_mod_all.at[c], d_mod_all.at[c]).wait()
-        swap(4, bias_sum.at[c], bias_sum.at[c]).wait()
+        swap(5, d_silu, d_silu_got).wait()
+        swap(6, d_mod, d_mod_all.at[c]).wait()
+        swap(7, bias_sum.at[c], bias_sum.at[c]).wait()
+        keep_mod.wait()
         gate = 1.0 / (1.0 + jnp.exp(-cond[...]))
         d_cond[...] = (d_silu[...] + d_silu_got[...]) * (gate + cond[...] * gate * (1.0 - gate))
 
-    steps = (weight_grads, input_grad, norm_grad, send_mod, mod_grad, cond_grad)
+    def heads_at(first, count):
+        @pl.loop(first, first + count)
+        def _(h):
+            head(h)
+
+    third = -(-heads // 3)
+
+    def first_heads():
+        mixed_back()
+        heads_at(0, third)
+
+    def last_heads():
+        heads_at(2 * third, heads - 2 * third)
+        attention_grads()
+
+    steps = (
+        expand_grads,
+        hidden_back,
+        middle_back,
+        first_heads,
+        lambda: heads_at(third, third),
+        last_heads,
+        input_back,
+        first_back,
+        branch_out,
+        send_mod,
+        mod_grad,
+        cond_grad,
+    )
 
     @pl.loop(0, red.units)
     def _(u):
-        @pl.loop(0, jnp.where(u < heads // 2, 2, 0))
-        def _(i):
-            head(2 * u + i)
-
         red.unit(u)
         for i, step in enumerate(steps):
-            when(u == heads // 2 - 1 + i, step)
+            when(u == i, step)
 
     red.final(2)
     red.drain()
@@ -780,48 +936,58 @@
 
 def backward(hbm_args, vmem_args, n, collective_id):
     line = n // 4
-    grad = hbm_args[0]
+    grad = hbm_args[1]
     rows, cols = grad.shape[-2:]
-    pair_t, d_att, q = vmem_args[0], vmem_args[1], vmem_args[2]
-    all_rows, width = d_att.shape
+    two, own, width = vmem_args[4].shape
+    all_rows = two * own
+    heads = vmem_args[5].shape
     low, f32 = jnp.bfloat16, jnp.float32
     dma = pltpu.SemaphoreType.DMA
     vmem, hbm = pl.BlockSpec(memory_space=pltpu.VMEM), pl.BlockSpec(memory_space=pltpu.HBM)
-    wide = q.shape
     per = chunk_tiles(n, width)
     return pl.pallas_call(
         functools.partial(backward_kernel, line),
         out_shape=[
+            jax.ShapeDtypeStruct(grad.shape, low),
+            jax.ShapeDtypeStruct(grad.shape, low),
+            jax.ShapeDtypeStruct((2, n, 3 * width), f32),
             jax.ShapeDtypeStruct((3, rows, cols), low),
-            jax.ShapeDtypeStruct((all_rows // 2, width), low),
-            jax.ShapeDtypeStruct((2, n, 3 * width), f32),
+            jax.ShapeDtypeStruct((own, width), low),
+            jax.ShapeDtypeStruct((own, width), low),
             jax.ShapeDtypeStruct((n, 128), f32),
             jax.ShapeDtypeStruct((2, 8, 128), f32),
         ],
         in_specs=[hbm] * len(hbm_args) + [vmem] * len(vmem_args),
-        out_specs=[vmem] * 5,
+        out_specs=[hbm] * 3 + [vmem] * 5,
         scratch_shapes=[
             pltpu.VMEM((width, cols), low),
-            pltpu.VMEM((line, 2, 2, rows, cols), low),
             pltpu.VMEM((2 * all_rows, cols), low),
-            pltpu.VMEM(wide, low),
-            pltpu.VMEM(wide, f32),
-            pltpu.VMEM(wide, f32),
-            pltpu.VMEM(wide, f32),
-            pltpu.VMEM((2, all_rows // 2, width), f32),
-            pltpu.VMEM((all_rows // 2, width), f32),
+            pltpu.VMEM(heads, low),
+            pltpu.VMEM(heads, f32),
+            pltpu.VMEM(heads, f32),
+            pltpu.VMEM(heads, f32),
+            pltpu.VMEM((2, own, width), f32),
+            pltpu.VMEM((own, width), f32),
+            pltpu.VMEM((own, width), f32),
+            pltpu.VMEM((own, width), f32),
+            pltpu.VMEM((2, own, width), low),
+            pltpu.VMEM((n, rows, all_rows), low),
+            pltpu.VMEM((2, rows, cols), low),
             pltpu.VMEM((8, width), f32),
             pltpu.VMEM((8, width), f32),
             pltpu.VMEM((3, 1, width), f32),
             pltpu.VMEM((n, 3, 1, width), f32),
+            pltpu.VMEM((n, 3 * width), f32),
             pltpu.VMEM((8, width), f32),
             pltpu.VMEM((n, per, 1, 128), f32),
             pltpu.VMEM((n, 128), f32),
             pltpu.VMEM((n, 128), f32),
             pltpu.VMEM((n, per, 1, 128), f32),
+            dma((4,)),
             dma,
-            dma((5,)),
-            dma((5,)),
+            dma((2,)),
+            dma((8,)),
+            dma((8,)),
             dma((n,)),
             dma((n,)),
             dma((n,)),
@@ -1081,20 +1247,6 @@
     )
 
 
-def normalize(values):
-    centre = values - jnp.mean(values, axis=-1, keepdims=True)
-    spread = jnp.mean(centre * centre, axis=-1, keepdims=True)
-    return centre * lax.rsqrt(spread + LAYER_EPS)
-
-
-def modulated(values, shift, scale):
-    return normalize(values) * (1.0 + scale) + shift
-
-
-def gelu_tanh(values):
-    return jax.nn.gelu(values, approximate=True)
-
-
 def per_device(
     tokens,
     cotangent,
@@ -1131,16 +1283,6 @@
     half_width, half_ff = width // pairs, FF // pairs
     low = jnp.bfloat16
 
-    def flipped(values):
-        return lax.ppermute(values, "seq", [(i, (i + 1) % pairs) for i in range(pairs)])
-
-    def rows_all(values):
-        return lax.all_gather(values, "seq", axis=0, tiled=True)
-
-    def rows_own(partial):
-        mine = lax.dynamic_slice_in_dim(partial, c * rows, rows, 0)
-        return mine + flipped(lax.dynamic_slice_in_dim(partial, (1 - c) * rows, rows, 0))
-
     def part_of(vector):
         return lax.dynamic_slice_in_dim(vector, c * (vector.shape[0] // pairs), vector.shape[0] // pairs, 0)
 
@@ -1163,8 +1305,9 @@
     half_kept = kept // pairs
     row_ok = jnp.arange(rows) < half_kept
     key_ok = ((jnp.arange(rows * pairs) % rows) < half_kept).astype(jnp.float32)[None]
-    (weights, weight_attn, normed_in, flat_query, flat_key, flat_value, mixed, attended, middle, normed_mid, pieces, cond_own,
-     silu_own, own_modulation) = forward(
+    row_ok = row_ok.astype(jnp.float32)[:, None]
+    (weights, grad_contract, normed_in, normed_mid, queries, keys, values, mixed, attended, middle, activated, slope, d_branch,
+     pieces, cond_own, silu_own, own_modulation) = forward(
         [
             item.reshape(-1, 128)
             for item in (
@@ -1185,84 +1328,40 @@
             part_of(bias_query)[None],
             part_of(bias_value)[None],
             bias_out[None],
+            part_of(bias_expand)[None],
+            cotangent[0],
+            row_ok,
         ],
         n,
         1,
     )
-    weights = weights.reshape(3, width, 4 * half_width)
-    weight_expand, weight_contract = weights[1], weights[2]
-    pieces = pieces.reshape(6, 1, width)
-    normed_in, normed_mid = normed_in.reshape(-1, width), normed_mid.reshape(-1, width)
-
-    def times_transposed(left, right):
-        return lax.dot_general(left, right, (((1,), (1,)), ((), ())), preferred_element_type=jnp.float32)
-
-    def contract_rows(left, right):
-        return lax.dot_general(
-            left, right, (((0,), (0,)), ((), ())), preferred_element_type=jnp.float32
-        )
-
-    hidden = jnp.dot(normed_mid, weight_expand, preferred_element_type=jnp.float32) + part_of(bias_expand)
-    activated = gelu_tanh(hidden).astype(low)
-    branch = rows_own(times_transposed(activated, weight_contract)) + bias_contract
-    result = middle + pieces[5] * branch
-    block_out = jnp.where(row_ok[:, None], result, 0.0).astype(low)[None]
-
-    grad_out = cotangent[0].astype(jnp.float32) * row_ok[:, None].astype(jnp.float32)
-    d_branch = rows_all((pieces[5] * grad_out).astype(low))
-    d_gate_mlp = jnp.sum(grad_out * branch, axis=0, keepdims=True)
-    grad_contract = contract_rows(d_branch, activated).astype(low)
-    grad_bias_contract = jnp.sum(d_branch.astype(jnp.float32), axis=0)
-    d_activated = jnp.dot(d_branch, weight_contract, preferred_element_type=jnp.float32)
-    d_hidden = jax.vjp(gelu_tanh, hidden)[1](d_activated)[0].astype(low)
-    grad_expand = contract_rows(normed_mid, d_hidden).astype(low)
-    grad_bias_expand = jnp.sum(d_hidden.astype(jnp.float32), axis=0)
-    d_normed_mid = rows_own(times_transposed(d_hidden, weight_expand))
-    d_middle, d_shift_mlp, d_scale_mlp = jax.vjp(modulated, middle, pieces[3], pieces[4])[1](d_normed_mid)
-    d_middle = d_middle + grad_out
-    d_attended = rows_all((pieces[2] * d_middle).astype(low))
-    d_gate_attn = jnp.sum(d_middle * attended, axis=0, keepdims=True)
-    grad_bias_out = jnp.sum(d_attended.astype(jnp.float32), axis=0)
-
-    pair_t = jnp.concatenate([normed_in.T, d_attended.T], axis=1).reshape(n, own_rows, 2 * pairs * rows)
-    zero_row = jnp.zeros((1, width), jnp.float32)
-    d_pieces = jnp.concatenate(
-        [zero_row, zero_row, d_gate_attn, d_shift_mlp, d_scale_mlp, d_gate_mlp, zero_row, zero_row]
-    )
-    v_rows = jnp.concatenate(
+    _, _, d_mod_all, reduced, block_out, tokens_grad, d_cond, bias_sum = backward(
+        [weights.reshape(3, width, 4 * half_width), grad_contract],
         [
-            zero_row,
-            grad_bias_expand.reshape(2, width),
-            grad_bias_out[None],
-            grad_bias_contract[None],
-            zero_row,
-            zero_row,
-            zero_row,
-        ]
-    )
-    shape = (n // 4, 2, 2, own_rows, 4 * half_width)
-    reduced, tokens_grad, d_mod_all, d_cond, bias_sum = backward(
-        (grad_contract.reshape(shape), grad_expand.reshape(shape), weight_attn),
-        (
-            pair_t,
-            d_attended,
-            flat_query,
-            flat_key,
-            flat_value,
+            normed_in,
+            normed_mid,
+            activated,
+            slope,
+            d_branch,
+            queries,
+            keys,
+            values,
             mixed,
             key_ok,
             inputs,
-            d_middle,
-            pieces[1],
-            d_pieces,
-            v_rows,
+            middle,
+            attended,
+            cotangent[0],
+            row_ok,
+            pieces,
+            bias_contract[None],
             own_modulation,
             cond_own,
-        ),
+        ],
         n,
         2,
     )
-    tokens_grad = tokens_grad[None]
+    block_out, tokens_grad = block_out[None], tokens_grad[None]
     same = (labels_all[:, None] == labels_all[None, :]).astype(jnp.float32)
     rates = (
         width ** (-0.5),

time: 399 us -> 351 us (0.88)
  matrix products: 30.7 us -> 0 us
  local copies, waits for them, and re-layouts: 30.8 us -> 16.9 us
  Pallas kernels: 315 us -> 324 us
  other arithmetic: 12.6 us -> 6.77 us
  blocking collectives: 4.86 us -> 0 us
    dot_general x6 -> x0, matrix products: 30.7 us -> none  [the longest x2 9.68 us: contract_rows(): lax.dot_general(left, right, (((0,), (0,)), ((), ())), preferred_element_...]
    slice x1 -> x0, local copies, waits for them, and re-layouts: 8.82 us -> none  [per_device(): weight_expand, weight_contract = (weights[1], weights[2])]
    pallas_call x1, Pallas kernels: 126 us -> 132 us  [forward(): pl.pallas_call(functools.partial(forward_kernel, line), out_shape=[shape(...]
    all_gather x2 -> x0, blocking collectives: 4.86 us -> none  [rows_all(): return lax.all_gather(values, 'seq', axis=0, tiled=True)]
    reduce_sum x7 -> x0, other arithmetic: 4.48 us -> none  [the longest x1 2.27 us: per_device(): d_gate_mlp = jnp.sum(grad_out * branch, axis=0, keepdims=True)]
    unnamed x71 -> x46, local copies, waits for them, and re-layouts: 12.3 us -> 11.6 us
  transfers between devices with their start and end apart: 2 -> 0, of which waited for: 0 -> 0; matrix products, arithmetic and copies ran while one was open for 4% -> 0% of each run, Pallas kernels for 0% -> 0%
where the time goes in v5:
time: 351 us
  Pallas kernels  324 us (92%)
  local copies, waits for them, and re-layouts  16.9 us (5%)
  other arithmetic  6.77 us (2%)
    pallas_call x1, Pallas kernels, backward(): pl.pallas_call(functools.partial(backward_kernel, line), out_shape=[jax.S...  150 us
    pallas_call x1, Pallas kernels, forward(): pl.pallas_call(functools.partial(forward_kernel, line), out_shape=[shape(...  132 us
    pallas_call x1, Pallas kernels, finish(): pl.pallas_call(functools.partial(norm_kernel, n), out_shape=flats + [smal...  17.4 us
    pallas_call x1, Pallas kernels, finish(): pl.pallas_call(functools.partial(adam_kernel, rates), out_shape=[f for f...  16.4 us
    unnamed x46, local copies, waits for them, and re-layouts  11.6 us
    pallas_call x1, Pallas kernels, exchange(): pl.pallas_call(functools.partial(exchange_kernel, n, spread), out_shape=[...  8.62 us

profile of v5, /device:TPU:12, one launch (start us, length us, event | category | flops | bytes accessed | tf_op | source)
XLA Modules:
  0.0 350.6 jit_solution(18154601871121576332)
XLA Ops:
  1.3 0.6 fusion.refs_16_
  2.0 0.6 compare_convert_fusion.3.refs_9_.refs_11_
  2.5 0.7 convert_element_type.81
  3.9 8.6 %exchange.1 = f32[16,16,128]{2,1,0:T(8,128)S(1)} custom-call(f32[16,128]{1,0:T(8,128)S(1)} %concatenate.9.refs_0_), custom_call_target="tpu_custom_call" | custom-call | tf_op jit(solution)/shard_map/exchange/pallas_call | solution.py:1037
  12.5 0.0 copy-start.15
  12.6 0.1 reshape.320
  12.7 0.1 dynamic_slice.16
  12.8 0.6 broadcast_in_dim.20.refs_11_
  13.3 0.1 dynamic_slice.17
  13.4 0.6 broadcast_in_dim.21.refs_12_
  14.0 0.7 fusion.2
  14.7 1.4 multiply_cosine_fusion
  16.1 0.3 concatenate.10
  16.4 0.0 copy-done.15
  16.4 0.9 convert_add_fusion.refs_8_.refs_12_
  17.3 0.1 dynamic_slice.15
  17.4 0.6 broadcast_in_dim.19.refs_10_
  18.0 0.1 dynamic_slice.18
  18.1 0.6 broadcast_in_dim.45.refs_14_
  18.7 0.6 broadcast_in_dim.44.refs_13_
  19.3 0.4 convert_reduce_fusion
  19.6 0.7 compare_convert_fusion
  20.3 131.8 %forward.1 = (bf16[3,4,2,2,72,2304]{5,4,3,2,1,0:T(8,128)(2,1)}, bf16[4,2,2,72,2304]{4,3,2,1,0:T(8,128)(2,1)}, bf16[16,72,256]{2,1,0:T(8,128)(2,1)}, bf16[16,72,2...) custom-call(f32[1944,128]{1,0:T(8,128)} %bitcast.84, ...), custom_call_target="tpu_custom_call" | custom-call | tf_op jit(solution)/shard_map/forward/pallas_call | solution.py:463
  152.1 0.6 broadcast_in_dim.46.refs_18_
  152.7 149.7 %backward.1 = (bf16[4,2,2,72,2304]{4,3,2,1,0:T(8,128)(2,1)}, bf16[4,2,2,72,2304]{4,3,2,1,0:T(8,128)(2,1)}, f32[2,16,3456]{2,1,0:T(8,128)}, bf16[3,72,2304]{2,1,0...) custom-call(bf16[3,1152,2304]{2,1,0:T(8,128)(2,1)} %bitcast.77, ...), custom_call_target="tpu_custom_call" | custom-call | tf_op jit(solution)/shard_map/backward/pallas_call | solution.py:948
  302.5 0.1 compare_convert_fusion.2.refs_6_
  302.5 0.0 copy-done.11
  302.5 1.0 copy-done.1
  303.6 1.2 copy-done.5
  304.8 0.7 copy-done.9
  305.5 0.7 copy-done.10
  306.2 17.4 %norm.1 = (f32[3888,128]{1,0:T(8,128)S(1)}, f32[1944,128]{1,0:T(8,128)S(1)}, f32[648,128]{1,0:T(8,128)S(1)}, f32[2592,128]{1,0:T(8,128)S(1)}, f32[2592,128]{1,0:...) custom-call(bf16[3,72,2304]{2,1,0:T(8,128)(2,1)S(1)} %copy-done.5, ...), custom_call_target="tpu_custom_call" | custom-call | tf_op jit(solution)/shard_map/norm/pallas_call | solution.py:1206
  323.6 1.3 copy-done
  324.9 1.1 copy-done.3
  326.0 1.1 copy-done.4
  327.1 1.0 copy-done.6
  328.1 0.7 copy-done.7
  328.8 0.7 copy-done.8
  329.6 0.6 copy-done.12
  330.3 0.1 slice_reduce_fusion
  330.4 0.1 reshape_squeeze.6
  330.4 0.1 reduce_sum.9
  330.6 0.1 reshape_squeeze.7
  330.8 0.5 slice.64
  332.0 0.7 multiply_subtract_fusion
  332.7 16.4 %adam.1 = (f32[3888,128]{1,0:T(8,128)}, f32[3888,128]{1,0:T(8,128)}, f32[3888,128]{1,0:T(8,128)}, f32[1944,128]{1,0:T(8,128)}, f32[1944,128]{1,0:T(8,128)}, /*in...) custom-call(f32[8,128]{1,0:T(8,128)} %copy-done.12, ...), custom_call_target="tpu_custom_call" | custom-call | tf_op jit(solution)/shard_map/adam/pallas_call | solution.py:1226
  349.2 0.7 copy.67
  349.9 0.7 copy.68
  (48 shorter events, 0.3 us)
Async XLA Ops:
  12.5 3.9 %copy-start.15 = (bf16[1,128,1152]{2,1,0:T(8,128)(2,1)S(1)}, bf16[1,128,1152]{2,1,0:T(8,128)(2,1)}, u32[]{:S(2)}) copy-start(bf16[1,128,1152]{2,1,0:T(8,128)(2,1)} %param.27) | copy-start | bytes 884740
  152.7 149.8 %copy-start.11 = (bf16[16,128]{1,0:T(8,128)(2,1)S(1)}, bf16[16,128]{1,0:T(8,128)(2,1)}, u32[]{:S(2)}) copy-start(bf16[16,128]{1,0:T(8,128)(2,1)} %get-tuple-element.93) | copy-start | bytes 12292
  302.5 1.0 copy-start.1
  303.6 1.2 copy-start.5
  304.8 0.7 copy-start.9
  305.5 0.7 copy-start.10
  306.2 24.3 %copy-start.2 = (f32[2,16,3456]{2,1,0:T(8,128)S(1)}, f32[2,16,3456]{2,1,0:T(8,128)}, u32[]{:S(2)}) copy-start(f32[2,16,3456]{2,1,0:T(8,128)} %get-tuple-element.94.refs_2_) | copy-start | bytes 1327108
  306.2 25.8 %copy-start.16 = (f32[1008]{0:T(1024)S(1)}, f32[1008]{0:T(1024)}, u32[]{:S(2)}) copy-start(f32[1008]{0:T(1024)} %param.51) | copy-start | bytes 12100
  306.2 25.9 %copy-start.17 = (f32[1008]{0:T(1024)S(1)}, f32[1008]{0:T(1024)}, u32[]{:S(2)}) copy-start(f32[1008]{0:T(1024)} %param.53) | copy-start | bytes 12100
  306.2 25.9 %copy-start.18 = (f32[1008]{0:T(1024)S(1)}, f32[1008]{0:T(1024)}, u32[]{:S(2)}) copy-start(f32[1008]{0:T(1024)} %param.52) | copy-start | bytes 12100
  323.6 1.3 copy-start
  324.9 1.1 copy-start.3
  326.0 1.1 copy-start.4
  327.1 1.0 copy-start.6
  328.1 0.7 copy-start.7
  328.8 0.7 copy-start.8
  329.6 0.6 copy-start.12
  332.7 16.4 %copy-start.14 = (bf16[128,1152]{1,0:T(8,128)(2,1)S(1)}, bf16[128,1152]{1,0:T(8,128)(2,1)}, u32[]{:S(2)}) copy-start(bf16[128,1152]{1,0:T(8,128)(2,1)} %get-tuple-element.90) | copy-start | bytes 884740
  332.7 17.1 %copy-start.13 = (bf16[128,1152]{1,0:T(8,128)(2,1)S(1)}, bf16[128,1152]{1,0:T(8,128)(2,1)}, u32[]{:S(2)}) copy-start(bf16[128,1152]{1,0:T(8,128)(2,1)} %get-tuple-element.91) | copy-start | bytes 884740

commit v6 on v5

--- a/solution.py
+++ b/solution.py
@@ -22,6 +22,7 @@
 MESH = pl.DeviceIdType.MESH
 GELU_A = (2.0 / 3.141592653589793) ** 0.5
 GELU_B = 0.044715
+UNIT_PLACES = ((0, 1, 2, 4, 6, 7, 9, 12, 14, 14, 16, 17), (1, 2, 4, 6, 7, 10, 13, 15, 16, 16, 17, 20))
 GROUPS = ((0, 768, 0, "x"), (768, 768, 0, "y"), (1536, 384, 1, "x"), (1920, 384, 1, "y"))
 
 
@@ -147,6 +148,11 @@
         when(k - 1 <= z, lambda: self.crossed(m, jnp.maximum(z - k + 1, 0)))
         when((k > 1) & (z + k - 1 < line), lambda: self.crossed(m, jnp.minimum(z + k - 1, line - 1)))
 
+    def steps(self, m, first, last):
+        @pl.loop(first, last + 1)
+        def _(k):
+            self.step(m, k)
+
     def complete(self, m):
         @pl.loop(0, self.line)
         def _(zz):
@@ -245,17 +251,16 @@
 
 
 def forward_kernel(line, *refs):
-    (m_in, m_out, m_expand, m_contract, m_table, m_mod, onehot, time_vec, x, key_ok, b_mod, b_query, b_value, b_out,
-     b_expand, cot, row_ok) = refs[:17]
+    (m_in, m_out, m_expand, m_contract, m_table, m_mod, block, time_vec, tokens, cells, freqs, kept, cot) = refs[:13]
     (weights, g_contract, h1_t, h2_t, q, k, v, o, attended, middle, act, slope, d_branch, pieces, cond, silu,
-     mod_half) = refs[17:34]
+     mod_half, x, key_ok, row_ok, onehot, same, biases) = refs[13:36]
     (f_in, f_out, f_expand, f_contract, f_table, f_mod, own, table, cond_part, cond_got, mods, mod_part, mod_got, blocks, w,
-     proj, mix, wide, partial, partial_got, h1, h2, d_branch_t, stage, in_sem, w_sem, pair_send, pair_recv, cond_send,
-     cond_recv, mod_send, mod_recv, keep_sem, stage_sem) = refs[34:68]
+     proj, mix, wide, partial, partial_got, h1, h2, d_branch_t, stage, block_got, wide_bias, in_sem, w_sem, pair_send, pair_recv,
+     block_send, block_recv, cond_send, cond_recv, mod_send, mod_recv, keep_sem, stage_sem) = refs[36:74]
     n = line * 4
     low, f32 = jnp.bfloat16, jnp.float32
     me, c = lax.axis_index("dp"), lax.axis_index("seq")
-    gat = Gatherer(line, own, weights, keep_sem, refs[68:])
+    gat = Gatherer(line, own, weights, keep_sem, refs[74:])
     rows, width = x.shape
     own_rows, half = own.shape[1], own.shape[2] // 4
     edge = 3 * half // 128 * 128
@@ -286,33 +291,73 @@
         for j in range(count):
             target[:own_rows, 128 * j : 128 * j + 128] = tile(flat, c * count + j, own_rows, 2 * count).astype(low)
 
+    block_start, block_wait = all_peers(n, block, block_got, block_send, block_recv, False)
+    cond_start, cond_wait = all_peers(n, cond_part, cond_got, cond_send, cond_recv, True)
+    mod_start, mod_wait = all_peers(n, mod_part, mod_got, mod_send, mod_recv, True)
+    block_got[me] = block[...]
     load(0).wait()
     load(1).wait()
     for part in range(3):
         own[0, :, part * half : (part + 1) * half] = cut_heads(f_in, part, 3 * tiles)
     own[0, :, 3 * half :] = cut_heads(f_out, 0, tiles)
+    pl.semaphore_wait(bar, n)
+    block_start()
+    gat.begin(0)
+    load(5).wait()
+    cut(f_contract, own.at[2], 4 * half // 128)
     load(2).wait()
     class_rows = table.shape[0]
     for t in range(tiles):
         table[:, 128 * t : 128 * t + 128] = tile(f_table, t, class_rows, tiles).astype(low)
-    found = dot(onehot[...], table[...])
+
+    block_wait()
+    labels = block_got[:, 8, :]
+    hot = (labels[:, :class_rows] - (me * class_rows).astype(f32)
+           == lax.broadcasted_iota(jnp.int32, (n, class_rows), 1).astype(f32)).astype(f32)
+    onehot[...] = hot
+    row = jnp.concatenate([block_got[s, 8:9, :1] for s in range(n)], axis=1)
+    same[...] = (labels[:, :1] == row).astype(f32)
+    found = dot(hot.astype(low), table[...])
     mine = lax.broadcasted_iota(jnp.int32, (n, width), 0) == me
     found = found + jnp.where(mine, jnp.broadcast_to(time_vec[...].astype(f32), (n, width)), 0.0)
     cond_part[...] = jnp.zeros_like(cond_part)
     for i in range(n):
         cond_part[i, :, :own_rows] = found[:, i * own_rows : (i + 1) * own_rows]
     cond_got[me] = cond_part[me]
-
-    pl.semaphore_wait(bar, n)
-    cond_start, cond_wait = all_peers(n, cond_part, cond_got, cond_send, cond_recv, True)
-    mod_start, mod_wait = all_peers(n, mod_part, mod_got, mod_send, mod_recv, True)
     cond_start()
-    gat.begin(0)
+    gat.begin(2)
     load(3).wait()
     mod_half[own_rows:] = jnp.zeros((mod_half.shape[0] - own_rows, mod_half.shape[1]), low)
     cut(f_mod, mod_half, 3 * tiles)
+    gat.paired(0)
     load(4).wait()
     cut(f_expand, own.at[1], 4 * half // 128)
+    gat.begin(1)
+
+    share = biases.shape[1] // n
+    for i in range(n):
+        for r in range(-(-share // 128)):
+            size = min(128, share - 128 * r)
+            biases[:, i * share + 128 * r : i * share + 128 * r + size] = block_got[i, r : r + 1, :size]
+
+    def bias(start, size):
+        return biases[:, start : start + size]
+
+    def bias_half(start, size):
+        return jnp.where(c == 0, bias(start, size // 2), bias(start + size // 2, size // 2))
+
+    half_kept = jnp.floor(kept[...] * 0.5)
+    rows_at = lax.broadcasted_iota(jnp.int32, (rows, 1), 0).astype(f32)
+    row_ok[...] = (rows_at < half_kept).astype(f32)
+    lanes_at = lax.broadcasted_iota(jnp.int32, (1, 2 * rows), 1)
+    lanes_at = jnp.where(lanes_at < rows, lanes_at, lanes_at - rows).astype(f32)
+    key_ok[...] = (lanes_at < half_kept).astype(f32)
+    quarter = width // 4
+    for i, place in enumerate((cells[:, :1], cells[:, 1:2])):
+        angle = place * freqs[...]
+        for j, wave in enumerate((jnp.sin(angle), jnp.cos(angle))):
+            cols = slice((2 * i + j) * quarter, (2 * i + j + 1) * quarter)
+            x[:, cols] = tokens[:, cols].astype(f32) + wave
 
     cond_wait()
     value = jnp.sum(cond_got[...], axis=0)
@@ -326,27 +371,19 @@
 
     mod_got[me] = mod_part[me]
     mod_start()
-    gat.paired(0)
-    gat.begin(1)
-    load(5).wait()
-    cut(f_contract, own.at[2], 4 * half // 128)
+    gat.steps(0, 1, 2)
     mod_wait()
-    pieces[c] = jnp.sum(mod_got[...], axis=0) + b_mod[...]
+    pieces[c] = jnp.sum(mod_got[...], axis=0) + bias_half(0, 6 * width)
     swap(0, pieces.at[c], pieces.at[c]).start()
-    gat.step(0, 1)
-    gat.begin(2)
+    gat.paired(1)
     swap(0, pieces.at[c], pieces.at[c]).wait()
     shift, scale, gate = (pieces[0, :, i * width : (i + 1) * width] for i in range(3))
     h1[c] = (normal(x[...]) * (1.0 + scale) + shift).astype(low)
     swap(1, h1.at[c], h1.at[c]).start()
     d_branch[c] = (pieces[1, :, 2 * width :] * (cot[...].astype(f32) * row_ok[...])).astype(low)
     swap(4, d_branch.at[c], d_branch.at[c]).start()
-
-    @pl.loop(2, line + 1)
-    def _(k):
-        gat.step(0, k)
-
-    gat.paired(1)
+    gat.steps(0, 3, line)
+    gat.steps(1, 1, 1)
     gat.complete(0)
 
     def fetch(m):
@@ -357,12 +394,12 @@
             w[i * own_rows : (i + 1) * own_rows, :] = blocks[i // 4, i // 2 % 2, i % 2]
 
     fetch(0).start()
-    gat.paired(2)
     swap(1, h1.at[c], h1.at[c]).wait()
+    both = jnp.concatenate([h1[0], h1[1]], axis=0)
+    to_blocks(both, h1_t)
     fetch(0).wait()
     unpack()
-    both = jnp.concatenate([h1[0], h1[1]], axis=0)
-    to_blocks(both, h1_t)
+    gat.steps(1, 2, 2)
 
     @pl.loop(0, proj.shape[1] // 256)
     def _(t):
@@ -371,9 +408,9 @@
 
     spare = q.shape[1] - half
     for item, value in (
-        (q, proj[:, :half] + b_query[...]),
+        (q, proj[:, :half] + bias_half(6 * width, width)),
         (k, proj[:, half : 2 * half]),
-        (v, proj[:, 2 * half : 3 * half] + b_value[...]),
+        (v, proj[:, 2 * half : 3 * half] + bias_half(7 * width, width)),
     ):
         item[:, :half] = value.astype(low)
         item[:, half:] = jnp.zeros((2 * rows, spare), low)
@@ -386,10 +423,13 @@
         probs = head_probs(q[:, win] * lanes, k[:, win], seen)
         mix[:, win] = mix[:, win] + dot(probs.astype(low), v[:, win] * lanes)
 
-    @pl.loop(0, max(heads, 2 * line))
+    @pl.loop(0, heads)
     def _(t):
-        when(t < heads, lambda: head(t))
-        when((t % 2 == 1) & (t < 2 * line), lambda: gat.step(1, t // 2 + 1))
+        head(t)
+        when(t == 0, lambda: gat.paired(2))
+        when(t == 3, lambda: gat.steps(1, 3, 3))
+        when(t == 5, lambda: gat.steps(1, 4, line))
+        when(t == heads - 1, lambda: gat.steps(2, 1, 1))
 
     o[...] = mix[...].astype(low)
     wide[:, : 3 * half - edge] = jnp.zeros((2 * rows, 3 * half - edge), low)
@@ -403,9 +443,8 @@
         partial[1, :, cols] = part[rows:]
 
     swap(2, partial.at[1 - c], partial_got).start()
-    gat.step(2, 1)
     swap(2, partial.at[1 - c], partial_got).wait()
-    attended[...] = partial[c] + partial_got[...] + b_out[...]
+    attended[...] = partial[c] + partial_got[...] + bias(8 * width, width)
     middle[...] = x[...] + gate * attended[...]
     shift, scale = (pieces[1, :, i * width : (i + 1) * width] for i in range(2))
     h2[c] = (normal(middle[...]) * (1.0 + scale) + shift).astype(low)
@@ -414,28 +453,30 @@
     fetch(1).start()
     swap(4, d_branch.at[c], d_branch.at[c]).wait()
     to_blocks(jnp.concatenate([d_branch[0], d_branch[1]], axis=0), d_branch_t)
-    gat.step(2, 2)
     swap(3, h2.at[c], h2.at[c]).wait()
     both = jnp.concatenate([h2[0], h2[1]], axis=0)
     to_blocks(both, h2_t)
     fetch(1).wait()
     unpack()
+    gat.steps(2, 2, 2)
+
+    wide_bias[...] = bias_half(9 * width, 8 * half)
 
     @pl.loop(0, act.shape[1] // 256)
     def _(t):
         cols = pl.ds(pl.multiple_of(t * 256, 256), 256)
-        z = dot(both, w[:, cols]) + b_expand[:, cols]
+        z = dot(both, w[:, cols]) + wide_bias[:, cols]
         bend = jnp.tanh(GELU_A * (z + GELU_B * z * z * z))
         act[:, cols] = (0.5 * z * (1.0 + bend)).astype(low)
         slope[:, cols] = 0.5 * (1.0 + bend) + 0.5 * z * (1.0 - bend * bend) * (GELU_A * (1.0 + 3.0 * GELU_B * z * z))
 
-    gat.step(2, 3)
-    write_blocks(n, g_contract, stage, stage_sem, lambda i: dot(d_branch_t[i], act[...]))
-
-    @pl.loop(4, line + 1)
-    def _(k):
-        gat.step(2, k)
-
+    gat.steps(2, 3, 3)
+
+    def contract_block(i):
+        when(i == n // 4, lambda: gat.steps(2, 4, line))
+        return dot(d_branch_t[i], act[...])
+
+    write_blocks(n, g_contract, stage, stage_sem, contract_block)
     gat.complete(2)
 
     @pl.loop(0, 3)
@@ -443,10 +484,11 @@
         gat.drain(m)
 
 
-def forward(hbm_args, vmem_args, n, collective_id):
+def forward(hbm_args, vmem_args, bias_size, n, collective_id):
     line = n // 4
-    onehot, time_vec, x = vmem_args[:3]
-    rows, width = x.shape
+    block, time_vec, tokens = vmem_args[:3]
+    rows, width = tokens.shape
+    class_rows = hbm_args[4].size // width
     own_rows, half = width // n, width // 2
     low, f32 = jnp.bfloat16, jnp.float32
     dma = pltpu.SemaphoreType.DMA
@@ -480,13 +522,19 @@
             shape((n, 128), f32),
             shape((n, 128), low),
             shape((128, 3 * width), low),
+            shape((rows, width), f32),
+            shape((1, 2 * rows), f32),
+            shape((rows, 1), f32),
+            shape((n, class_rows), f32),
+            shape((n, n), f32),
+            shape((1, bias_size), f32),
         ],
         in_specs=[hbm] * len(hbm_args) + [vmem] * len(vmem_args),
-        out_specs=[hbm] * 2 + [vmem] * 15,
+        out_specs=[hbm] * 2 + [vmem] * 21,
         scratch_shapes=[scratch(item.shape, f32) for item in hbm_args]
         + [
             scratch((3, own_rows, 4 * half), low),
-            scratch((onehot.shape[1], width), low),
+            scratch((class_rows, width), low),
             scratch((n, n, 128), f32),
             scratch((n, n, 128), f32),
             scratch((n, 3 * width), f32),
@@ -503,10 +551,14 @@
             scratch((2, rows, width), low),
             scratch((n, own_rows, 2 * rows), low),
             scratch((2, own_rows, 4 * half), low),
+            scratch((n,) + block.shape, f32),
+            scratch((1, 4 * half), f32),
             dma((6,)),
             dma((2,)),
             dma((5,)),
             dma((5,)),
+            dma((n,)),
+            dma((n,)),
             dma((n,)),
             dma((n,)),
             dma((n,)),
@@ -655,7 +707,6 @@
     def unit(self, u):
         line = self.line
         m, j = u // line, u % line
-        when(u + 2 < self.units, lambda: self.begin(jnp.minimum(u + 2, self.units - 1)))
         self.near(u, m, j)
         self.far(m, j)
         when(j == line - 1, lambda: self.close(m))
@@ -693,15 +744,16 @@
 
 def backward_kernel(line, *refs):
     (weights, g_contract, h1_t, h2_t, act, slope, d_branch, q, k, v, o, key_ok, x, middle, attended, cot, row_ok, pieces,
-     b_contract, modulation, cond) = refs[:21]
-    (g_expand, g_attn, d_mod_all, out, block_out, tokens_grad, d_cond, bias_sum) = refs[21:29]
+     b_contract, modulation, cond, silu, same) = refs[:23]
+    (g_expand, g_attn, d_mod_all, cond_all, both, block_out, tokens_grad, bias_all, norm_out, factor_out) = refs[23:33]
     (w, rhs, d_o, d_q, d_k, d_v, d_h, d_h_got, branch_got, d_mid, d_att, d_att_t, stage, dp, dp_got, msg, msg_got, d_mod, vec,
-     vec_got, d_silu, d_silu_got, chunk, w_sem, mod_sem, stage_sem, pair_send, pair_recv, msg_send, msg_recv, vec_send,
-     vec_recv) = refs[29:61]
+     vec_got, d_silu, d_silu_got, chunk, out, bias_sum, d_cond, squares, squares_got, table_squares, squares_pair, cond_some, w_sem,
+     mod_sem, stage_sem, pair_send, pair_recv, msg_send, msg_recv, vec_send, vec_recv, cond_send, cond_recv, bias_send, bias_recv, square_send,
+     square_recv) = refs[33:79]
     n = line * 4
     low, f32 = jnp.bfloat16, jnp.float32
     me, c = lax.axis_index("dp"), lax.axis_index("seq")
-    red = make_reducer(line, (g_contract, g_expand, g_attn), out, refs[61:])
+    red = make_reducer(line, (g_contract, g_expand, g_attn), out, refs[79:])
     rows, width = x.shape
     half = weights.shape[2] // 4
     heads = half // HEAD_DIM
@@ -747,18 +799,17 @@
     vec[...] = jnp.zeros_like(vec)
     vec[4:5] = column_sums(d_branch[0]) + column_sums(d_branch[1])
     pl.semaphore_wait(bar, n)
-    red.begin(0)
-    red.begin(1)
-
-    fetch(0).wait()
-    d_out = jnp.concatenate([d_branch[0], d_branch[1]], axis=0)
-
-    @pl.loop(0, act.shape[1] // 256)
-    def _(t):
-        cols = pl.ds(pl.multiple_of(t * 256, 256), 256)
-        d_z[:, cols] = (dot(d_out, w[:, cols]) * slope[:, cols]).astype(low)
-
-    fetch(1).start()
+
+    def hidden_grad():
+        fetch(0).wait()
+        d_out = jnp.concatenate([d_branch[0], d_branch[1]], axis=0)
+
+        @pl.loop(0, act.shape[1] // 256)
+        def _(t):
+            cols = pl.ds(pl.multiple_of(t * 256, 256), 256)
+            d_z[:, cols] = (dot(d_out, w[:, cols]) * slope[:, cols]).astype(low)
+
+        fetch(1).start()
 
     def expand_grads():
         write_blocks(n, g_expand, stage, stage_sem, lambda i: dot(h2_t[i], d_z[...]))
@@ -862,7 +913,8 @@
         msg_start()
         vec_start()
 
-    keep_mod = pltpu.make_async_copy(d_mod, d_mod_all.at[c], mod_sem)
+    keep_mod = pltpu.make_async_copy(d_mod, d_mod_all.at[c], mod_sem.at[0])
+    keep_cond = pltpu.make_async_copy(d_cond, cond_all.at[me], mod_sem.at[2])
 
     def mod_grad():
         msg_wait()
@@ -882,6 +934,10 @@
         swap(7, bias_sum.at[c], bias_sum.at[c]).start()
         keep_mod.start()
 
+    cond_start, cond_wait = all_peers(n, d_cond, cond_all, cond_send, cond_recv, False)
+    bias_start, bias_wait = all_peers(n, bias_sum, bias_all, bias_send, bias_recv, False)
+    square_start, square_wait = all_peers(n, squares, squares_got, square_send, square_recv, False)
+
     def cond_grad():
         swap(5, d_silu, d_silu_got).wait()
         swap(6, d_mod, d_mod_all.at[c]).wait()
@@ -889,45 +945,86 @@
         keep_mod.wait()
         gate = 1.0 / (1.0 + jnp.exp(-cond[...]))
         d_cond[...] = (d_silu[...] + d_silu_got[...]) * (gate + cond[...] * gate * (1.0 - gate))
-
-    def heads_at(first, count):
-        @pl.loop(first, first + count)
-        def _(h):
-            head(h)
-
-    third = -(-heads // 3)
-
-    def first_heads():
-        mixed_back()
-        heads_at(0, third)
-
-    def last_heads():
-        heads_at(2 * third, heads - 2 * third)
-        attention_grads()
-
-    steps = (
-        expand_grads,
-        hidden_back,
-        middle_back,
-        first_heads,
-        lambda: heads_at(third, third),
-        last_heads,
-        input_back,
-        first_back,
-        branch_out,
-        send_mod,
-        mod_grad,
-        cond_grad,
-    )
-
-    @pl.loop(0, red.units)
-    def _(u):
-        red.unit(u)
-        for i, step in enumerate(steps):
-            when(u == i, step)
-
+        keep_cond.start()
+        bias_all[me] = bias_sum[...]
+        cond_start()
+        bias_start()
+        d_low = d_mod[...].astype(low)
+        grad = dot(silu[...], d_low, 0, 0)[: out.shape[1]]
+        sums = jnp.sum(d_mod[...], axis=0, keepdims=True)
+        tile = per * me + lax.broadcasted_iota(jnp.int32, (8, 128), 0)
+        counted = (tile < 3 * tiles) | (c == 0)
+        total = jnp.sum(grad * grad) + jnp.where(me == 0, jnp.sum(sums * sums), 0.0)
+        total = total + jnp.sum(jnp.where(counted, bias_sum[c] * bias_sum[c], 0.0))
+        squares[...] = jnp.full((8, 128), total, f32)
+
+    def table_norm():
+        cond_wait()
+        bias_wait()
+        keep_cond.wait()
+        table_squares[...] = jnp.zeros((8, 128), f32)
+        size = cond_some.shape[0]
+
+        @pl.loop(0, n // size)
+        def _(j):
+            some = pltpu.make_async_copy(cond_all.at[pl.ds(j * size, size)], cond_some, mod_sem.at[1])
+            some.start()
+            some.wait()
+            gram = jnp.zeros((n, n), f32)
+            for i in range(size):
+                part = cond_some[i]
+                gram = gram + lax.dot_general(
+                    part, part, (((1,), (1,)), ((), ())), preferred_element_type=f32, precision=lax.Precision.HIGHEST)
+            table_squares[...] = table_squares[...] + jnp.sum(gram * same[...])
+
+    def reduced(m):
+        value = out[m].astype(f32)
+        squares[...] = squares[...] + jnp.sum(value * value)
+        both[c, m] = out[m]
+        swap(8 + m, out.at[m], both.at[c, m]).start()
+
+    parts = (hidden_grad, expand_grads, hidden_back, middle_back, mixed_back) + (None,) * heads
+    parts += (attention_grads, input_back, first_back, branch_out, send_mod, mod_grad, cond_grad, table_norm)
+    first_head = parts.index(None)
+    begun, carried = ([places[u // line * 4 + u % line * 4 // line] for u in range(red.units)] for places in UNIT_PLACES)
+
+    def upto(places, s):
+        total = jnp.int32(0)
+        for place in places:
+            total = total + (place <= s).astype(jnp.int32)
+        return total
+
+    @pl.loop(0, len(parts) + 1)
+    def _(s):
+        @pl.loop(upto(begun, s - 1), upto(begun, s))
+        def _(v):
+            red.begin(v)
+
+        @pl.loop(upto(carried, s - 1), upto(carried, s))
+        def _(u):
+            red.unit(u)
+
+        when((s >= first_head) & (s < first_head + heads), lambda: head(s - first_head))
+        for i, part in enumerate(parts):
+            if part is not None:
+                when(s == i, part)
+
+    reduced(0)
+    reduced(1)
     red.final(2)
+    reduced(2)
+    squares_got[me] = squares[...]
+    square_start()
     red.drain()
+    square_wait()
+    squares[...] = jnp.sum(squares_got[...], axis=0)
+    swap(11, squares, squares_pair).start()
+    for m in range(3):
+        swap(8 + m, out.at[m], both.at[c, m]).wait()
+    swap(11, squares, squares_pair).wait()
+    norm = jnp.sqrt(squares[...] + squares_pair[...] + table_squares[...])
+    norm_out[...] = norm
+    factor_out[...] = jnp.minimum(1.0, CLIP_LIMIT / (norm + 1e-06))
 
 
 def chunk_tiles(n, width):
@@ -951,14 +1048,16 @@
             jax.ShapeDtypeStruct(grad.shape, low),
             jax.ShapeDtypeStruct(grad.shape, low),
             jax.ShapeDtypeStruct((2, n, 3 * width), f32),
-            jax.ShapeDtypeStruct((3, rows, cols), low),
+            jax.ShapeDtypeStruct((n, n, 128), f32),
+            jax.ShapeDtypeStruct((2, 3, rows, cols), low),
             jax.ShapeDtypeStruct((own, width), low),
             jax.ShapeDtypeStruct((own, width), low),
-            jax.ShapeDtypeStruct((n, 128), f32),
-            jax.ShapeDtypeStruct((2, 8, 128), f32),
+            jax.ShapeDtypeStruct((n, 2, 8, 128), f32),
+            jax.ShapeDtypeStruct((8, 128), f32),
+            jax.ShapeDtypeStruct((8, 128), f32),
         ],
         in_specs=[hbm] * len(hbm_args) + [vmem] * len(vmem_args),
-        out_specs=[hbm] * 3 + [vmem] * 5,
+        out_specs=[hbm] * 4 + [vmem] * 6,
         scratch_shapes=[
             pltpu.VMEM((width, cols), low),
             pltpu.VMEM((2 * all_rows, cols), low),
@@ -983,66 +1082,26 @@
             pltpu.VMEM((n, 128), f32),
             pltpu.VMEM((n, 128), f32),
             pltpu.VMEM((n, per, 1, 128), f32),
+            pltpu.VMEM((3, rows, cols), low),
+            pltpu.VMEM((2, 8, 128), f32),
+            pltpu.VMEM((n, 128), f32),
+            pltpu.VMEM((8, 128), f32),
+            pltpu.VMEM((n, 8, 128), f32),
+            pltpu.VMEM((8, 128), f32),
+            pltpu.VMEM((8, 128), f32),
+            pltpu.VMEM((min(n, 16), n, 128), f32),
             dma((4,)),
-            dma,
+            dma((3,)),
             dma((2,)),
-            dma((8,)),
-            dma((8,)),
-            dma((n,)),
-            dma((n,)),
-            dma((n,)),
-            dma((n,)),
+            dma((12,)),
+            dma((12,)),
         ]
+        + [dma((n,))] * 10
         + reducer_scratch(3, line, rows, low),
         compiler_params=pltpu.CompilerParams(
             collective_id=collective_id, has_side_effects=True, vmem_limit_bytes=63 * 2**20),
         name="backward",
     )(*hbm_args, *vmem_args)
-
-
-def exchange_kernel(n, spread, *refs):
-    count = len(spread)
-    srcs, outs, (send, recv) = refs[:count], refs[count:2 * count], refs[2 * count:]
-    me, c = lax.axis_index("dp"), lax.axis_index("seq")
-    bar = pltpu.get_barrier_semaphore()
-
-    @pl.loop(1, n)
-    def _(j):
-        pl.semaphore_signal(bar, inc=1, device_id=((me + j) % n, c), device_id_type=MESH)
-
-    for a in range(count):
-        outs[a][me] = srcs[a][me] if spread[a] else srcs[a][...]
-    pl.semaphore_wait(bar, n - 1)
-
-    def copy(a, j, there, slot):
-        return pltpu.make_async_remote_copy(
-            src_ref=srcs[a].at[there] if spread[a] else srcs[a], dst_ref=outs[a].at[slot],
-            send_sem=send.at[a, j], recv_sem=recv.at[a, slot], device_id=(there, c), device_id_type=MESH)
-
-    @pl.loop(1, n)
-    def _(j):
-        for a in range(count):
-            copy(a, j, (me + j) % n, me).start()
-
-    @pl.loop(1, n)
-    def _(j):
-        for a in range(count):
-            copy(a, j, (me + j) % n, (me + n - j) % n).wait()
-
-
-def exchange(blocks, spread, n, collective_id):
-    count = len(blocks)
-    parts = [b.shape[1:] if s else b.shape for b, s in zip(blocks, spread)]
-    dma = pltpu.SemaphoreType.DMA
-    return pl.pallas_call(
-        functools.partial(exchange_kernel, n, spread),
-        out_shape=[jax.ShapeDtypeStruct((n,) + p, b.dtype) for p, b in zip(parts, blocks)],
-        in_specs=[pl.BlockSpec(memory_space=pltpu.VMEM)] * count,
-        out_specs=[pl.BlockSpec(memory_space=pltpu.VMEM)] * count,
-        scratch_shapes=[dma((count, n)), dma((count, n))],
-        compiler_params=pltpu.CompilerParams(collective_id=collective_id, has_side_effects=True, vmem_limit_bytes=32 * 2**20),
-        name="exchange",
-    )(*blocks)
 
 
 def adam_step(grad, master, first, second, rate):
@@ -1061,121 +1120,64 @@
     return sizes[-1] if sizes else rows
 
 
-def norm_kernel(n, *refs):
-    reduced, silu, d_mod, d_cond, bias_sum, onehot, same = refs[:7]
-    flat, factor_out, norm_out, bias_out = refs[7:13], refs[13], refs[14], refs[15]
-    both, wide, block, got, pair_send, pair_recv, send, recv = refs[16:]
-    me, c = lax.axis_index("dp"), lax.axis_index("seq")
-    rows = reduced.shape[1]
-    half = reduced.shape[2]
-    head = half // 4
-
-    bar = pltpu.get_barrier_semaphore()
-    pl.semaphore_signal(bar, inc=1, device_id=(me, 1 - c), device_id_type=MESH)
-
-    @pl.loop(1, n)
-    def _(j):
-        pl.semaphore_signal(bar, inc=1, device_id=((me + j) % n, c), device_id_type=MESH)
-
-    both[c] = reduced[...]
-    pl.semaphore_wait(bar, n)
-    pair = pltpu.make_async_remote_copy(
-        src_ref=reduced, dst_ref=both.at[c], send_sem=pair_send, recv_sem=pair_recv,
-        device_id=(me, 1 - c), device_id_type=MESH)
-    pair.start()
-
-    def spread(a, width):
-        total = None
-        tiles = width // 128
-        for t in range(tiles):
-            part = wide[:, 128 * t : 128 * t + 128]
-            flat[a][pl.ds(t, rows, stride=tiles), :] = part
-            square = part * part
-            total = square if total is None else total + square
-        return jnp.sum(total)
-
-    part_mod = d_mod.shape[2]
-    for core in range(2):
-        wide[:, core * part_mod : (core + 1) * part_mod] = dot(silu[...], d_mod[core].astype(silu.dtype), 0, 0)
-    squares = spread(0, wide.shape[1])
-    mod_sums = jnp.sum(d_mod[...], axis=1)
-    squares = squares + jnp.where(me == 0, jnp.sum(mod_sums * mod_sums), 0.0)
-    width = n * rows
-    tile = chunk_tiles(n, width) * me + lax.broadcasted_iota(jnp.int32, (8, 128), 0)
-    squares = squares + jnp.sum(bias_sum[0] * bias_sum[0])
-    squares = squares + jnp.sum(jnp.where(tile < 3 * (width // 128), bias_sum[1] * bias_sum[1], 0.0))
-    pair.wait()
-    for core in range(2):
-        for part in range(3):
-            lo = (2 * part + core) * head
-            wide[:, lo : lo + head] = both[core, 2, :, part * head : (part + 1) * head].astype(jnp.float32)
-    squares = squares + spread(1, 6 * head)
-    for core in range(2):
-        wide[:, core * head : (core + 1) * head] = both[core, 2, :, 3 * head :].astype(jnp.float32)
-    squares = squares + spread(2, 2 * head)
-    for a in (3, 4):
-        for core in range(2):
-            wide[:, core * half : (core + 1) * half] = both[core, 4 - a].astype(jnp.float32)
-        squares = squares + spread(a, 2 * half)
-
-    slots = d_cond.shape[0]
-    block[:slots] = d_cond[...]
-    block[slots : slots + 8] = jnp.full((8, 128), squares, jnp.float32)
-    block[slots + 8 : slots + 16] = bias_sum[0]
-    block[slots + 16 :] = bias_sum[1]
-    got[me] = block[...]
-
-    def copy(j, there, slot):
-        return pltpu.make_async_remote_copy(
-            src_ref=block, dst_ref=got.at[slot], send_sem=send.at[j], recv_sem=recv.at[slot],
-            device_id=(there, c), device_id_type=MESH)
-
-    @pl.loop(1, n)
-    def _(j):
-        copy(j, (me + j) % n, me).start()
-
-    @pl.loop(1, n)
-    def _(j):
-        copy(j, (me + j) % n, (me + n - j) % n).wait()
-
-    bias_out[...] = got[:, slots + 8 :]
-    total = jnp.sum(got[:, slots : slots + 8], axis=0)[:1, :1]
-    gram = jnp.zeros((slots, slots), jnp.float32)
-    for i in range(n):
-        part = got[i, :slots]
-        gram = gram + lax.dot_general(
-            part, part, (((1,), (1,)), ((), ())), preferred_element_type=jnp.float32, precision=lax.Precision.HIGHEST)
-        wide[: onehot.shape[1], i * rows : (i + 1) * rows] = lax.dot_general(
-            onehot[...], part, (((0,), (0,)), ((), ())), preferred_element_type=jnp.float32,
-            precision=lax.Precision.HIGHEST)[:, :rows]
-    total = total + jnp.sum(gram * same[...], keepdims=True)
-    norm = jnp.sqrt(total)
-    norm_out[...] = jnp.broadcast_to(norm, (8, 128))
-    factor_out[...] = jnp.broadcast_to(jnp.minimum(1.0, CLIP_LIMIT / (norm + 1e-06)), (8, 128))
-    tiles = n * rows // 128
-    for t in range(tiles):
-        flat[5][pl.ds(t, onehot.shape[1], stride=tiles), :] = wide[: onehot.shape[1], 128 * t : 128 * t + 128]
-
-
-def adam_kernel(rates, *refs):
+def adam_kernel(n, rates, *refs):
     kinds = len(rates)
-    factor_ref, flat = refs[0], refs[1 : 1 + kinds]
-    at = 1 + kinds
+    factor_ref, both, silu, d_mod, cond_all, onehot = refs[:6]
+    at = 6
     states = [refs[at + 3 * a : at + 3 * a + 3] for a in range(kinds)]
     at += 3 * kinds
     news = [refs[at + 3 * a : at + 3 * a + 3] for a in range(kinds)]
     at += 3 * kinds
-    held = refs[at : at + kinds]
-    in_sem, out_sem = refs[at + kinds :]
+    held, flat = refs[at : at + kinds], refs[at + kinds : at + 2 * kinds]
+    wide, in_sem, out_sem = refs[at + 2 * kinds :]
+    rows, half = both.shape[2:]
+    head = half // 4
+    order = (3, 4, 0, 1, 2, 5)
 
     def loads(a):
         return [pltpu.make_async_copy(states[a][k], held[a].at[k], in_sem.at[a, k]) for k in range(3)]
 
-    for a in range(kinds):
+    for a in order:
         for copy in loads(a):
             copy.start()
+
+    def spread(a, width, count=rows):
+        tiles = width // 128
+        for t in range(tiles):
+            flat[a][pl.ds(t, count, stride=tiles), :] = wide[:count, 128 * t : 128 * t + 128]
+
+    def gradient(a):
+        if a == 0:
+            part = d_mod.shape[2]
+            for core in range(2):
+                grad = dot(silu[...], d_mod[core].astype(silu.dtype), 0, 0)
+                wide[:, core * part : (core + 1) * part] = grad[:rows]
+            spread(a, 2 * part)
+        elif a == 1:
+            for core in range(2):
+                for part in range(3):
+                    lo = (2 * part + core) * head
+                    wide[:, lo : lo + head] = both[core, 2, :, part * head : (part + 1) * head].astype(jnp.float32)
+            spread(a, 6 * head)
+        elif a == 2:
+            for core in range(2):
+                wide[:, core * head : (core + 1) * head] = both[core, 2, :, 3 * head :].astype(jnp.float32)
+            spread(a, 2 * head)
+        elif a == 5:
+            count = onehot.shape[1]
+            for i in range(n):
+                wide[:count, i * rows : (i + 1) * rows] = lax.dot_general(
+                    onehot[...], cond_all[i], (((0,), (0,)), ((), ())), preferred_element_type=jnp.float32,
+                    precision=lax.Precision.HIGHEST)[:, :rows]
+            spread(a, n * rows, count)
+        else:
+            for core in range(2):
+                wide[:, core * half : (core + 1) * half] = both[core, 4 - a].astype(jnp.float32)
+            spread(a, 2 * half)
+
     factor = factor_ref[:1, :]
-    for a in range(kinds):
+    for a in order:
+        gradient(a)
         for copy in loads(a):
             copy.wait()
         size = chunk_rows(flat[a].shape[0])
@@ -1195,56 +1197,24 @@
             pltpu.make_async_copy(held[a].at[k], news[a][k], out_sem.at[a, k]).wait()
 
 
-def finish(reduced, silu, d_mod, d_cond, bias_sum, onehot, same, states, rates, n, collective_id):
+def adam(factor, both, silu, d_mod, cond_all, onehot, states, rates, n):
     vmem, hbm = pl.BlockSpec(memory_space=pltpu.VMEM), pl.BlockSpec(memory_space=pltpu.HBM)
     dma = pltpu.SemaphoreType.DMA
     kinds = len(states)
-    rows = reduced.shape[1]
     flats = [jax.ShapeDtypeStruct(s[0].shape, jnp.float32) for s in states]
-    small = jax.ShapeDtypeStruct((8, 128), jnp.float32)
-    block = d_cond.shape[0] + 24
-    outs = pl.pallas_call(
-        functools.partial(norm_kernel, n),
-        out_shape=flats + [small, small, jax.ShapeDtypeStruct((n, 16, 128), jnp.float32)],
-        in_specs=[vmem] * 7,
-        out_specs=[vmem] * (kinds + 3),
-        scratch_shapes=[
-            pltpu.VMEM((2,) + reduced.shape, reduced.dtype),
-            pltpu.VMEM((rows, 2 * d_mod.shape[2]), jnp.float32),
-            pltpu.VMEM((block, 128), jnp.float32),
-            pltpu.VMEM((n, block, 128), jnp.float32),
-            dma,
-            dma,
-            dma((n,)),
-            dma((n,)),
-        ],
-        compiler_params=pltpu.CompilerParams(
-            collective_id=collective_id, has_side_effects=True, vmem_limit_bytes=40 * 2**20),
-        name="norm",
-    )(reduced, silu, d_mod, d_cond, bias_sum, onehot, same)
-    grads, factor, norm = outs[:kinds], outs[kinds], outs[kinds + 1]
     news = pl.pallas_call(
-        functools.partial(adam_kernel, rates),
+        functools.partial(adam_kernel, n, rates),
         out_shape=[f for f in flats for _ in range(3)],
-        in_specs=[vmem] * (1 + kinds) + [hbm] * (3 * kinds),
+        in_specs=[vmem] * 6 + [hbm] * (3 * kinds),
         out_specs=[hbm] * (3 * kinds),
         scratch_shapes=[pltpu.VMEM((3,) + f.shape, jnp.float32) for f in flats]
-        + [dma((kinds, 3)), dma((kinds, 3))],
+        + [pltpu.VMEM(f.shape, jnp.float32) for f in flats]
+        + [pltpu.VMEM((both.shape[2], 2 * d_mod.shape[2]), jnp.float32), dma((kinds, 3)), dma((kinds, 3))],
         compiler_params=pltpu.CompilerParams(vmem_limit_bytes=56 * 2**20),
         name="adam",
-    )(factor, *grads, *[item for s in states for item in s])
+    )(factor, both, silu, d_mod, cond_all, onehot, *[item for s in states for item in s])
     order = [3 * a + k for a in range(kinds) for k in (1, 2, 0)]
-    return [news[i] for i in order], norm[0, 0], outs[kinds + 2]
-
-
-def grid_embed(keep_index, width):
-    quarter = width // 4
-    freqs = 10000.0 ** (-jnp.arange(quarter).astype(jnp.float32) / quarter)
-    across = (keep_index // SIDE).astype(jnp.float32)[..., None] * freqs
-    along = (keep_index % SIDE).astype(jnp.float32)[..., None] * freqs
-    return jnp.concatenate(
-        [jnp.sin(across), jnp.cos(across), jnp.sin(along), jnp.cos(along)], axis=-1
-    )
+    return [news[i] for i in order]
 
 
 def per_device(
@@ -1278,36 +1248,19 @@
 ):
     rows, width = tokens.shape[1:]
     n, pairs = lax.axis_size("dp"), lax.axis_size("seq")
-    me, c = lax.axis_index("dp"), lax.axis_index("seq")
-    own_rows = width // n
-    half_width, half_ff = width // pairs, FF // pairs
+    me = lax.axis_index("dp")
+    half_width = width // pairs
     low = jnp.bfloat16
-
-    def part_of(vector):
-        return lax.dynamic_slice_in_dim(vector, c * (vector.shape[0] // pairs), vector.shape[0] // pairs, 0)
 
     bias_share = biases_master.shape[0]
     bias_block = jnp.pad(biases_master.astype(low).astype(jnp.float32), (0, 1024 - bias_share)).reshape(8, 128)
     label_block = jnp.broadcast_to(labels.astype(jnp.float32)[:, None], (8, 128))
-    (got,) = exchange([jnp.concatenate([bias_block, label_block])], (False,), n, 3)
-    biases = got[:, :8].reshape(n, 1024)[:, :bias_share].reshape(-1)
-    labels_all = got[:, 8, 0].astype(jnp.int32)
-    bias_mod = biases[: 6 * width]
-    bias_query = biases[6 * width : 7 * width]
-    bias_value = biases[7 * width : 8 * width]
-    bias_out = biases[8 * width : 9 * width]
-    bias_expand = biases[9 * width : 9 * width + FF]
-    bias_contract = biases[9 * width + FF :]
-
-    class_rows = CLASSES // n
-    onehot = labels_all[:, None] == me * class_rows + jnp.arange(class_rows)[None, :]
-    inputs = tokens[0].astype(jnp.float32) + grid_embed(keep_index[0], width)
-    half_kept = kept // pairs
-    row_ok = jnp.arange(rows) < half_kept
-    key_ok = ((jnp.arange(rows * pairs) % rows) < half_kept).astype(jnp.float32)[None]
-    row_ok = row_ok.astype(jnp.float32)[:, None]
+    place = keep_index[0]
+    cells = jnp.stack([place // SIDE, place % SIDE], axis=1).astype(jnp.float32)
+    quarter = width // 4
+    freqs = 10000.0 ** (-jnp.arange(quarter).astype(jnp.float32) / quarter)
     (weights, grad_contract, normed_in, normed_mid, queries, keys, values, mixed, attended, middle, activated, slope, d_branch,
-     pieces, cond_own, silu_own, own_modulation) = forward(
+     pieces, cond_own, silu_own, own_modulation, inputs, key_ok, row_ok, onehot, same, biases) = forward(
         [
             item.reshape(-1, 128)
             for item in (
@@ -1320,22 +1273,19 @@
             )
         ],
         [
-            onehot.astype(low),
+            jnp.concatenate([bias_block, label_block]),
             time_vec,
-            inputs,
-            key_ok,
-            part_of(bias_mod)[None],
-            part_of(bias_query)[None],
-            part_of(bias_value)[None],
-            bias_out[None],
-            part_of(bias_expand)[None],
+            tokens[0],
+            cells,
+            freqs[None],
+            kept.astype(jnp.float32)[None],
             cotangent[0],
-            row_ok,
         ],
+        bias_share * n,
         n,
         1,
     )
-    _, _, d_mod_all, reduced, block_out, tokens_grad, d_cond, bias_sum = backward(
+    _, _, d_mod_all, cond_all, reduced, block_out, tokens_grad, bias_parts, norm, clip = backward(
         [weights.reshape(3, width, 4 * half_width), grad_contract],
         [
             normed_in,
@@ -1354,15 +1304,16 @@
             cotangent[0],
             row_ok,
             pieces,
-            bias_contract[None],
+            biases[:, 9 * width + FF :],
             own_modulation,
             cond_own,
+            silu_own,
+            same,
         ],
         n,
         2,
     )
-    block_out, tokens_grad = block_out[None], tokens_grad[None]
-    same = (labels_all[:, None] == labels_all[None, :]).astype(jnp.float32)
+    block_out, tokens_grad, grad_norm = block_out[None], tokens_grad[None], norm[0, 0]
     rates = (
         width ** (-0.5),
         width ** (-0.5),
@@ -1400,20 +1351,17 @@
         biases_second,
     )
     states = list(zip(masters, firsts, seconds))
-    updated, grad_norm, bias_parts = finish(
+    updated = adam(
+        clip,
         reduced,
-        silu_own[:, :own_rows],
+        silu_own,
         d_mod_all,
-        d_cond,
-        bias_sum,
-        onehot.astype(jnp.float32),
-        same,
+        cond_all,
+        onehot,
         [tuple(item.reshape(-1, 128) for item in state) for state in states[:-1]],
         rates[:-1],
         n,
-        8,
     )
-    factor = jnp.minimum(1.0, CLIP_LIMIT / (grad_norm + 1e-06))
     bias_parts = bias_parts.reshape(n, pairs, 8, 128)[:, :, : chunk_tiles(n, width)].transpose(1, 0, 2, 3)
     bias_parts = bias_parts.reshape(pairs, -1)[:, : 5 * width].reshape(pairs, 5, width)
     grad_biases = jnp.concatenate(
@@ -1426,7 +1374,7 @@
             bias_parts[0, 4],
         ]
     )
-    bias_grad = lax.dynamic_slice_in_dim(grad_biases, me * bias_share, bias_share, 0) * factor
+    bias_grad = lax.dynamic_slice_in_dim(grad_biases, me * bias_share, bias_share, 0) * clip[0, 0]
     updated = [item.reshape(-1) for item in updated] + list(adam_step(bias_grad, *states[-1], rates[-1]))
     return (block_out, tokens_grad, grad_norm) + tuple(updated)
 

time: 351 us -> 333 us (0.949)
  local copies, waits for them, and re-layouts: 16.9 us -> 7.88 us
  Pallas kernels: 324 us -> 315 us
    pallas_call x3 -> x1, Pallas kernels: 42.5 us -> 14.8 us  [adam(): pl.pallas_call(functools.partial(adam_kernel, n, rates), out_shape=[f for...]
    pallas_call x1, Pallas kernels: 150 us -> 167 us  [backward(): pl.pallas_call(functools.partial(backward_kernel, line), out_shape=[jax.S...]
    unnamed x46 -> x17, local copies, waits for them, and re-layouts: 11.6 us -> 1.49 us
    broadcast_in_dim x6 -> x0, local copies, waits for them, and re-layouts: 3.58 us -> none  [the longest x1 0.61 us: per_device(): part_of(bias_mod)[None]]
where the time goes in v6:
time: 333 us; the launch traced here: 329 us
  Pallas kernels  315 us (95%)
  local copies, waits for them, and re-layouts  7.88 us (2%)
  other arithmetic  4.38 us (1%)
    pallas_call x1, Pallas kernels, backward(): pl.pallas_call(functools.partial(backward_kernel, line), out_shape=[jax.S...  167 us
    pallas_call x1, Pallas kernels, forward(): pl.pallas_call(functools.partial(forward_kernel, line), out_shape=[shape(...  133 us
    pallas_call x1, Pallas kernels, adam(): pl.pallas_call(functools.partial(adam_kernel, n, rates), out_shape=[f for...  14.8 us

profile of v6, /device:TPU:12, one launch (start us, length us, event | category | flops | bytes accessed | tf_op | source)
XLA Modules:
  0.0 329.4 jit_solution(15178240734659642947)
XLA Ops:
  0.7 0.7 and_select_fusion.1
  1.3 0.7 copy.62.refs_9_
  2.1 0.7 convert_element_type.25
  3.4 0.6 concatenate.6.refs_6_
  4.0 0.6 multiply_power_fusion.refs_10_
  5.3 133.4 %forward.1 = (bf16[3,4,2,2,72,2304]{5,4,3,2,1,0:T(8,128)(2,1)}, bf16[4,2,2,72,2304]{4,3,2,1,0:T(8,128)(2,1)}, bf16[16,72,256]{2,1,0:T(8,128)(2,1)}, bf16[16,72,2...) custom-call(f32[1944,128]{1,0:T(8,128)} %bitcast.72, ...), custom_call_target="tpu_custom_call" | custom-call | tf_op jit(solution)/shard_map/forward/pallas_call | solution.py:505
  138.7 1.3 slice.30.refs_18_
  139.9 166.8 %backward.1 = (bf16[4,2,2,72,2304]{4,3,2,1,0:T(8,128)(2,1)}, bf16[4,2,2,72,2304]{4,3,2,1,0:T(8,128)(2,1)}, f32[2,16,3456]{2,1,0:T(8,128)}, f32[16,16,128]{2,1,0:...) custom-call(bf16[3,1152,2304]{2,1,0:T(8,128)(2,1)} %bitcast.65, ...), custom_call_target="tpu_custom_call" | custom-call | tf_op jit(solution)/shard_map/backward/pallas_call | solution.py:1045
  306.7 0.0 copy-start.2
  306.7 0.0 copy-start.3
  306.7 0.0 copy-start.4
  306.8 0.9 slice_bitcast_fusion
  307.8 0.1 slice_reduce_fusion
  307.9 0.1 reshape_squeeze.6
  308.0 1.1 reduce_sum.9
  309.2 0.1 reshape_squeeze.7
  309.4 1.2 slice.39
  310.6 0.0 copy-done.2
  310.6 0.0 copy-done.3
  310.6 0.0 copy-done.4
  310.6 1.3 multiply_subtract_fusion
  311.9 0.0 copy-start.1
  311.9 0.0 copy-start
  311.9 14.8 %adam.1 = (f32[3888,128]{1,0:T(8,128)}, f32[3888,128]{1,0:T(8,128)}, f32[3888,128]{1,0:T(8,128)}, f32[1944,128]{1,0:T(8,128)}, f32[1944,128]{1,0:T(8,128)}, /*in...) custom-call(f32[8,128]{1,0:T(8,128)} %get-tuple-element.98.refs_0_, ...), custom_call_target="tpu_custom_call" | custom-call | tf_op jit(solution)/shard_map/adam/pallas_call | solution.py:1205
  326.8 1.2 slice.31
  327.9 0.0 copy-done.1
  327.9 0.7 copy.74
  328.7 0.0 copy-done
  328.7 0.7 copy.75
  (17 shorter events, 0.2 us)
Async XLA Ops:
  306.7 3.8 %copy-start.2 = (f32[1008]{0:T(1024)S(1)}, f32[1008]{0:T(1024)}, u32[]{:S(2)}) copy-start(f32[1008]{0:T(1024)} %param.51) | copy-start | bytes 12100
  306.7 3.8 %copy-start.3 = (f32[1008]{0:T(1024)S(1)}, f32[1008]{0:T(1024)}, u32[]{:S(2)}) copy-start(f32[1008]{0:T(1024)} %param.53) | copy-start | bytes 12100
  306.7 3.8 %copy-start.4 = (f32[1008]{0:T(1024)S(1)}, f32[1008]{0:T(1024)}, u32[]{:S(2)}) copy-start(f32[1008]{0:T(1024)} %param.52) | copy-start | bytes 12100
  311.9 16.0 %copy-start.1 = (bf16[128,1152]{1,0:T(8,128)(2,1)S(1)}, bf16[128,1152]{1,0:T(8,128)(2,1)}, u32[]{:S(2)}) copy-start(bf16[128,1152]{1,0:T(8,128)(2,1)} %get-tuple-element.95) | copy-start | bytes 884740
  311.9 16.7 %copy-start = (bf16[128,1152]{1,0:T(8,128)(2,1)S(1)}, bf16[128,1152]{1,0:T(8,128)(2,1)}, u32[]{:S(2)}) copy-start(bf16[128,1152]{1,0:T(8,128)(2,1)} %get-tuple-element.96) | copy-start | bytes 884740

commit v7 on v6

--- a/solution.py
+++ b/solution.py
@@ -22,8 +22,8 @@
 MESH = pl.DeviceIdType.MESH
 GELU_A = (2.0 / 3.141592653589793) ** 0.5
 GELU_B = 0.044715
-UNIT_PLACES = ((0, 1, 2, 4, 6, 7, 9, 12, 14, 14, 16, 17), (1, 2, 4, 6, 7, 10, 13, 15, 16, 16, 17, 20))
-GROUPS = ((0, 768, 0, "x"), (768, 768, 0, "y"), (1536, 384, 1, "x"), (1920, 384, 1, "y"))
+UNIT_PLACES = ((0, 0, 2, 10, 12, 13, 13, 15), (1, 3, 11, 12, 13, 14, 15, 18))
+GROUPS = ((0, 640, 0, "x"), (640, 640, 0, "y"), (1280, 512, 1, "x"), (1792, 512, 1, "y"))
 
 
 def when(cond, fn):
@@ -62,7 +62,7 @@
 class Gatherer:
     def __init__(self, line, own, out, keep_sem, sems):
         self.line, self.own, self.out, self.keep_sem = line, own, out, keep_sem
-        self.send_a, self.send_u, self.send_d, self.send_b, self.recv_a, self.recv_z, self.recv_b = sems
+        self.send_a, self.send_z, self.send_b, self.recv_a, self.recv_z, self.recv_b = sems
         self.me = Place(line)
         self.up, self.down = self.me.z < line - 1, self.me.z > 0
 
@@ -94,11 +94,12 @@
 
     def u_copy(self, m, g, zz, source=None):
         dev = self.me.dev(z=jnp.minimum(self.me.z + 1, self.line - 1))
-        return self.remote(self.z_ref(m, g, zz), self.send_u.at[m, g, zz], self.recv_z.at[m, g, zz], dev, source)
+        return self.remote(self.z_ref(m, g, zz), self.send_z.at[m, g, zz], self.recv_z.at[m, g, zz], dev, source)
 
     def d_copy(self, m, g, zz, source=None):
         dev = self.me.dev(z=jnp.maximum(self.me.z - 1, 0))
-        return self.remote(self.z_ref(m, g, zz), self.send_d.at[m, g, zz], self.recv_z.at[m, g, zz], dev, source)
+        sem = self.send_z.at[m, g, jnp.where(zz == self.me.z, self.line, zz)]
+        return self.remote(self.z_ref(m, g, zz), sem, self.recv_z.at[m, g, zz], dev, source)
 
     def b_copy(self, m, g, zz):
         last = "y" if GROUPS[g][3] == "x" else "x"
@@ -252,15 +253,16 @@
 
 def forward_kernel(line, *refs):
     (m_in, m_out, m_expand, m_contract, m_table, m_mod, block, time_vec, tokens, cells, freqs, kept, cot) = refs[:13]
-    (weights, g_contract, h1_t, h2_t, q, k, v, o, attended, middle, act, slope, d_branch, pieces, cond, silu,
-     mod_half, x, key_ok, row_ok, onehot, same, biases) = refs[13:36]
-    (f_in, f_out, f_expand, f_contract, f_table, f_mod, own, table, cond_part, cond_got, mods, mod_part, mod_got, blocks, w,
-     proj, mix, wide, partial, partial_got, h1, h2, d_branch_t, stage, block_got, wide_bias, in_sem, w_sem, pair_send, pair_recv,
-     block_send, block_recv, cond_send, cond_recv, mod_send, mod_recv, keep_sem, stage_sem) = refs[36:74]
+    (weights, g_contract, g_expand, cond_got, h1_t, q, k, v, o, attended, middle, act, d_z, sums, out, pieces, cond, silu,
+     mod_half, x, key_ok, row_ok, onehot, same, biases) = refs[13:38]
+    (f_in, f_out, f_expand, f_contract, f_table, f_mod, own, table, cond_part, cond_some, mods, mod_part, mod_got, blocks, w,
+     proj, mix, wide, partial, partial_got, h1, h2, h2_t, slope, d_branch, d_branch_t, stage, block_got, wide_bias, in_sem,
+     w_sem, pair_send, pair_recv, peer_send, block_recv, cond_recv, mod_recv, keep_sem, stage_sem, cond_sem) = refs[38:78]
     n = line * 4
     low, f32 = jnp.bfloat16, jnp.float32
     me, c = lax.axis_index("dp"), lax.axis_index("seq")
-    gat = Gatherer(line, own, weights, keep_sem, refs[74:])
+    gat = Gatherer(line, own, weights, keep_sem, refs[78:84])
+    red = make_reducer(line, (g_contract,), out, refs[84:])
     rows, width = x.shape
     own_rows, half = own.shape[1], own.shape[2] // 4
     edge = 3 * half // 128 * 128
@@ -291,9 +293,9 @@
         for j in range(count):
             target[:own_rows, 128 * j : 128 * j + 128] = tile(flat, c * count + j, own_rows, 2 * count).astype(low)
 
-    block_start, block_wait = all_peers(n, block, block_got, block_send, block_recv, False)
-    cond_start, cond_wait = all_peers(n, cond_part, cond_got, cond_send, cond_recv, True)
-    mod_start, mod_wait = all_peers(n, mod_part, mod_got, mod_send, mod_recv, True)
+    block_start, block_wait = all_peers(n, block, block_got, peer_send, block_recv, False)
+    cond_start, cond_wait = all_peers(n, cond_part, cond_got, peer_send, cond_recv, True)
+    mod_start, mod_wait = all_peers(n, mod_part, mod_got, peer_send, mod_recv, True)
     block_got[me] = block[...]
     load(0).wait()
     load(1).wait()
@@ -323,13 +325,14 @@
     cond_part[...] = jnp.zeros_like(cond_part)
     for i in range(n):
         cond_part[i, :, :own_rows] = found[:, i * own_rows : (i + 1) * own_rows]
-    cond_got[me] = cond_part[me]
+    keep_cond = pltpu.make_async_copy(cond_part.at[me], cond_got.at[me], cond_sem.at[0])
+    keep_cond.start()
     cond_start()
     gat.begin(2)
+    gat.paired(0)
     load(3).wait()
     mod_half[own_rows:] = jnp.zeros((mod_half.shape[0] - own_rows, mod_half.shape[1]), low)
     cut(f_mod, mod_half, 3 * tiles)
-    gat.paired(0)
     load(4).wait()
     cut(f_expand, own.at[1], 4 * half // 128)
     gat.begin(1)
@@ -359,9 +362,20 @@
             cols = slice((2 * i + j) * quarter, (2 * i + j + 1) * quarter)
             x[:, cols] = tokens[:, cols].astype(f32) + wave
 
+    gat.steps(0, 1, 1)
     cond_wait()
-    value = jnp.sum(cond_got[...], axis=0)
-    cond[...] = value
+    keep_cond.wait()
+    cond[...] = jnp.zeros_like(cond)
+    some = cond_some.shape[0]
+
+    @pl.loop(0, n // some)
+    def _(j):
+        copy = pltpu.make_async_copy(cond_got.at[pl.ds(j * some, some)], cond_some, cond_sem.at[1])
+        copy.start()
+        copy.wait()
+        cond[...] = cond[...] + jnp.sum(cond_some[...], axis=0)
+
+    value = cond[...]
     silu[...] = (value / (1.0 + jnp.exp(-value))).astype(low)
     mods[...] = dot(silu[...], mod_half[...])
 
@@ -371,35 +385,33 @@
 
     mod_got[me] = mod_part[me]
     mod_start()
-    gat.steps(0, 1, 2)
+    gat.steps(0, 2, 2)
+    gat.paired(1)
+    gat.steps(0, 3, line)
+    gat.steps(1, 1, 1)
     mod_wait()
     pieces[c] = jnp.sum(mod_got[...], axis=0) + bias_half(0, 6 * width)
     swap(0, pieces.at[c], pieces.at[c]).start()
-    gat.paired(1)
+    def fetch(m):
+        return pltpu.make_async_copy(weights.at[m], blocks, w_sem.at[m])
+
+    def unpack():
+        for i in range(n):
+            w[i * own_rows : (i + 1) * own_rows, :] = blocks[i // 4, i // 2 % 2, i % 2]
+
+    gat.complete(0)
+    fetch(0).start()
     swap(0, pieces.at[c], pieces.at[c]).wait()
     shift, scale, gate = (pieces[0, :, i * width : (i + 1) * width] for i in range(3))
     h1[c] = (normal(x[...]) * (1.0 + scale) + shift).astype(low)
     swap(1, h1.at[c], h1.at[c]).start()
     d_branch[c] = (pieces[1, :, 2 * width :] * (cot[...].astype(f32) * row_ok[...])).astype(low)
     swap(4, d_branch.at[c], d_branch.at[c]).start()
-    gat.steps(0, 3, line)
-    gat.steps(1, 1, 1)
-    gat.complete(0)
-
-    def fetch(m):
-        return pltpu.make_async_copy(weights.at[m], blocks, w_sem.at[m])
-
-    def unpack():
-        for i in range(n):
-            w[i * own_rows : (i + 1) * own_rows, :] = blocks[i // 4, i // 2 % 2, i % 2]
-
-    fetch(0).start()
+    fetch(0).wait()
+    unpack()
     swap(1, h1.at[c], h1.at[c]).wait()
     both = jnp.concatenate([h1[0], h1[1]], axis=0)
     to_blocks(both, h1_t)
-    fetch(0).wait()
-    unpack()
-    gat.steps(1, 2, 2)
 
     @pl.loop(0, proj.shape[1] // 256)
     def _(t):
@@ -426,10 +438,9 @@
     @pl.loop(0, heads)
     def _(t):
         head(t)
-        when(t == 0, lambda: gat.paired(2))
-        when(t == 3, lambda: gat.steps(1, 3, 3))
-        when(t == 5, lambda: gat.steps(1, 4, line))
-        when(t == heads - 1, lambda: gat.steps(2, 1, 1))
+        when(t == 1, lambda: gat.steps(1, 2, 2))
+        when(t == 3, lambda: gat.paired(2))
+        when(t == heads - 1, lambda: gat.steps(1, 3, 3))
 
     o[...] = mix[...].astype(low)
     wide[:, : 3 * half - edge] = jnp.zeros((2 * rows, 3 * half - edge), low)
@@ -443,6 +454,7 @@
         partial[1, :, cols] = part[rows:]
 
     swap(2, partial.at[1 - c], partial_got).start()
+    gat.steps(1, 4, line)
     swap(2, partial.at[1 - c], partial_got).wait()
     attended[...] = partial[c] + partial_got[...] + bias(8 * width, width)
     middle[...] = x[...] + gate * attended[...]
@@ -451,6 +463,7 @@
     swap(3, h2.at[c], h2.at[c]).start()
     gat.complete(1)
     fetch(1).start()
+    gat.steps(2, 1, 1)
     swap(4, d_branch.at[c], d_branch.at[c]).wait()
     to_blocks(jnp.concatenate([d_branch[0], d_branch[1]], axis=0), d_branch_t)
     swap(3, h2.at[c], h2.at[c]).wait()
@@ -470,14 +483,43 @@
         act[:, cols] = (0.5 * z * (1.0 + bend)).astype(low)
         slope[:, cols] = 0.5 * (1.0 + bend) + 0.5 * z * (1.0 - bend * bend) * (GELU_A * (1.0 + 3.0 * GELU_B * z * z))
 
-    gat.steps(2, 3, 3)
-
     def contract_block(i):
-        when(i == n // 4, lambda: gat.steps(2, 4, line))
+        when(i == n // 4, lambda: gat.steps(2, 3, 3))
+        when(i == n // 2, lambda: gat.steps(2, 4, line))
         return dot(d_branch_t[i], act[...])
 
     write_blocks(n, g_contract, stage, stage_sem, contract_block)
+    quarter = line // 4
+    red.begin_some(0, 2 * quarter)
     gat.complete(2)
+    fetch(2).start()
+    sums[...] = jnp.zeros_like(sums)
+    sums[4:5] = jnp.sum(d_branch[...].astype(f32), axis=(0, 1))[None]
+    fetch(2).wait()
+    unpack()
+    red.unit_some(0, quarter)
+    d_out = jnp.concatenate([d_branch[0], d_branch[1]], axis=0)
+
+    @pl.loop(0, act.shape[1] // 256)
+    def _(t):
+        cols = pl.ds(pl.multiple_of(t * 256, 256), 256)
+        d_z[:, cols] = (dot(d_out, w[:, cols]) * slope[:, cols]).astype(low)
+
+    red.begin_some(2 * quarter, 3 * quarter)
+    red.unit_some(quarter, 2 * quarter)
+    totals = jnp.sum(d_z[...].astype(f32), axis=0, keepdims=True)
+    sums[1:2] = totals[:, :width]
+    sums[2:3] = totals[:, width:]
+
+    def expand_block(i):
+        when(i == n // 4, lambda: red.begin_some(3 * quarter, line))
+        when(i == n // 2, lambda: red.unit_some(2 * quarter, 3 * quarter))
+        return dot(h2_t[i], d_z[...])
+
+    write_blocks(n, g_expand, stage, stage_sem, expand_block)
+    red.unit_some(3 * quarter, line)
+    red.final(0)
+    red.drain()
 
     @pl.loop(0, 3)
     def _(m):
@@ -507,7 +549,8 @@
         out_shape=[
             shape((3, line, 2, 2, own_rows, 4 * half), low),
             shape((line, 2, 2, own_rows, 4 * half), low),
-            shape((n, own_rows, 2 * rows), low),
+            shape((line, 2, 2, own_rows, 4 * half), low),
+            shape((n, n, 128), f32),
             shape((n, own_rows, 2 * rows), low),
             shape(heads, low),
             shape(heads, low),
@@ -516,8 +559,9 @@
             shape((rows, width), f32),
             shape((rows, width), f32),
             shape((2 * rows, 4 * half), low),
-            shape((2 * rows, 4 * half), f32),
-            shape((2, rows, width), low),
+            shape((2 * rows, 4 * half), low),
+            shape((8, width), f32),
+            shape((1, own_rows, 4 * half), low),
             shape((2, 1, 3 * width), f32),
             shape((n, 128), f32),
             shape((n, 128), low),
@@ -530,13 +574,13 @@
             shape((1, bias_size), f32),
         ],
         in_specs=[hbm] * len(hbm_args) + [vmem] * len(vmem_args),
-        out_specs=[hbm] * 2 + [vmem] * 21,
+        out_specs=[hbm] * 4 + [vmem] * 21,
         scratch_shapes=[scratch(item.shape, f32) for item in hbm_args]
         + [
             scratch((3, own_rows, 4 * half), low),
             scratch((class_rows, width), low),
             scratch((n, n, 128), f32),
-            scratch((n, n, 128), f32),
+            scratch((min(n, 16), n, 128), f32),
             scratch((n, 3 * width), f32),
             scratch((n, 1, 3 * width), f32),
             scratch((n, 1, 3 * width), f32),
@@ -550,23 +594,26 @@
             scratch((2, rows, width), low),
             scratch((2, rows, width), low),
             scratch((n, own_rows, 2 * rows), low),
+            scratch((2 * rows, 4 * half), f32),
+            scratch((2, rows, width), low),
+            scratch((n, own_rows, 2 * rows), low),
             scratch((2, own_rows, 4 * half), low),
             scratch((n,) + block.shape, f32),
             scratch((1, 4 * half), f32),
             dma((6,)),
-            dma((2,)),
+            dma((3,)),
             dma((5,)),
             dma((5,)),
             dma((n,)),
             dma((n,)),
             dma((n,)),
             dma((n,)),
-            dma((n,)),
-            dma((n,)),
             dma((3,)),
             dma((2,)),
+            dma((2,)),
         ]
-        + [dma((3, 4, line))] * 7,
+        + [dma((3, 4, line)), dma((3, 4, line + 1))] + [dma((3, 4, line))] * 4
+        + reducer_scratch(1, line, own_rows, low),
         compiler_params=pltpu.CompilerParams(
             collective_id=collective_id, has_side_effects=True, vmem_limit_bytes=63 * 2**20),
         name="forward",
@@ -710,7 +757,18 @@
         self.near(u, m, j)
         self.far(m, j)
         when(j == line - 1, lambda: self.close(m))
-        when((j == 0) & (m > 0), lambda: self.final(jnp.maximum(m - 1, 0)))
+        if len(self.grads) > 1:
+            when((j == 0) & (m > 0), lambda: self.final(jnp.maximum(m - 1, 0)))
+
+    def begin_some(self, first, last):
+        @pl.loop(first, last)
+        def _(v):
+            self.begin(v)
+
+    def unit_some(self, first, last):
+        @pl.loop(first, last)
+        def _(u):
+            self.unit(u)
 
     def drain(self):
         z = self.me.z
@@ -743,23 +801,22 @@
 
 
 def backward_kernel(line, *refs):
-    (weights, g_contract, h1_t, h2_t, act, slope, d_branch, q, k, v, o, key_ok, x, middle, attended, cot, row_ok, pieces,
+    (weights, g_expand, h1_t, act, d_z, sums, out_contract, q, k, v, o, key_ok, x, middle, attended, cot, row_ok, pieces,
      b_contract, modulation, cond, silu, same) = refs[:23]
-    (g_expand, g_attn, d_mod_all, cond_all, both, block_out, tokens_grad, bias_all, norm_out, factor_out) = refs[23:33]
+    (g_attn, d_mod_all, cond_all, both, block_out, tokens_grad, bias_all, norm_out, factor_out) = refs[23:32]
     (w, rhs, d_o, d_q, d_k, d_v, d_h, d_h_got, branch_got, d_mid, d_att, d_att_t, stage, dp, dp_got, msg, msg_got, d_mod, vec,
      vec_got, d_silu, d_silu_got, chunk, out, bias_sum, d_cond, squares, squares_got, table_squares, squares_pair, cond_some, w_sem,
      mod_sem, stage_sem, pair_send, pair_recv, msg_send, msg_recv, vec_send, vec_recv, cond_send, cond_recv, bias_send, bias_recv, square_send,
-     square_recv) = refs[33:79]
+     square_recv) = refs[32:78]
     n = line * 4
     low, f32 = jnp.bfloat16, jnp.float32
     me, c = lax.axis_index("dp"), lax.axis_index("seq")
-    red = make_reducer(line, (g_contract, g_expand, g_attn), out, refs[79:])
+    red = make_reducer(line, (g_expand, g_attn), out, refs[78:])
     rows, width = x.shape
     half = weights.shape[2] // 4
     heads = half // HEAD_DIM
     edge = 3 * half // 128 * 128
     tiles = width // 128
-    d_z = rhs.at[2 * rows :]
 
     def swap(i, src, dst):
         return pltpu.make_async_remote_copy(
@@ -767,7 +824,7 @@
             device_id_type=MESH)
 
     def fetch(i):
-        return pltpu.make_async_copy(weights.at[(2, 1, 0, 2)[i]], w, w_sem.at[i])
+        return pltpu.make_async_copy(weights.at[(1, 0, 2)[i]], w, w_sem.at[i])
 
     def back(values, lanes):
         @pl.loop(0, tiles)
@@ -796,32 +853,14 @@
     for item in (d_q, d_k, d_v):
         item[...] = jnp.zeros_like(item)
     dp[...] = jnp.zeros_like(dp)
-    vec[...] = jnp.zeros_like(vec)
-    vec[4:5] = column_sums(d_branch[0]) + column_sums(d_branch[1])
+    vec[...] = sums[...]
     pl.semaphore_wait(bar, n)
 
-    def hidden_grad():
+    def hidden_back():
         fetch(0).wait()
-        d_out = jnp.concatenate([d_branch[0], d_branch[1]], axis=0)
-
-        @pl.loop(0, act.shape[1] // 256)
-        def _(t):
-            cols = pl.ds(pl.multiple_of(t * 256, 256), 256)
-            d_z[:, cols] = (dot(d_out, w[:, cols]) * slope[:, cols]).astype(low)
-
-        fetch(1).start()
-
-    def expand_grads():
-        write_blocks(n, g_expand, stage, stage_sem, lambda i: dot(h2_t[i], d_z[...]))
-        sums = column_sums(d_z[...])
-        vec[1:2] = sums[:, :width]
-        vec[2:3] = sums[:, width:]
-
-    def hidden_back():
-        fetch(1).wait()
         back(d_z, 4 * half)
         swap(0, d_h.at[1 - c], d_h_got).start()
-        fetch(2).start()
+        fetch(1).start()
 
     def middle_back():
         swap(0, d_h.at[1 - c], d_h_got).wait()
@@ -838,7 +877,7 @@
         d_all = jnp.concatenate([d_att[0], d_att[1]], axis=0)
         to_blocks(d_all, d_att_t)
         vec[3:4] = column_sums(d_att[0]) + column_sums(d_att[1])
-        fetch(2).wait()
+        fetch(1).wait()
         d_o[:, :half] = dot(d_all, w[:, edge:])[:, 3 * half - edge :].astype(low)
         d_o[:, half:] = jnp.zeros((2 * rows, d_o.shape[1] - half), low)
 
@@ -875,7 +914,7 @@
     def input_back():
         back(rhs.at[: 2 * rows, : edge + 128], edge + 128)
         swap(2, d_h.at[1 - c], d_h_got).start()
-        fetch(3).start()
+        fetch(2).start()
 
     def first_back():
         swap(2, d_h.at[1 - c], d_h_got).wait()
@@ -883,7 +922,7 @@
         tokens_grad[...] = (d_x + d_mid[...]).astype(low)
         dp[0:1] = shift
         dp[1:2] = scale
-        fetch(3).wait()
+        fetch(2).wait()
         back(act, 4 * half)
         swap(3, d_h.at[1 - c], branch_got).start()
 
@@ -977,13 +1016,17 @@
                     part, part, (((1,), (1,)), ((), ())), preferred_element_type=f32, precision=lax.Precision.HIGHEST)
             table_squares[...] = table_squares[...] + jnp.sum(gram * same[...])
 
+    def share(m):
+        return swap(8 + m, out_contract.at[0] if m == 0 else out.at[m - 1], both.at[c, m])
+
     def reduced(m):
-        value = out[m].astype(f32)
+        value = out_contract[0] if m == 0 else out[m - 1]
+        both[c, m] = value
+        share(m).start()
+        value = value.astype(f32)
         squares[...] = squares[...] + jnp.sum(value * value)
-        both[c, m] = out[m]
-        swap(8 + m, out.at[m], both.at[c, m]).start()
-
-    parts = (hidden_grad, expand_grads, hidden_back, middle_back, mixed_back) + (None,) * heads
+
+    parts = (hidden_back, middle_back, mixed_back) + (None,) * heads
     parts += (attention_grads, input_back, first_back, branch_out, send_mod, mod_grad, cond_grad, table_norm)
     first_head = parts.index(None)
     begun, carried = ([places[u // line * 4 + u % line * 4 // line] for u in range(red.units)] for places in UNIT_PLACES)
@@ -1011,7 +1054,7 @@
 
     reduced(0)
     reduced(1)
-    red.final(2)
+    red.final(1)
     reduced(2)
     squares_got[me] = squares[...]
     square_start()
@@ -1020,7 +1063,7 @@
     squares[...] = jnp.sum(squares_got[...], axis=0)
     swap(11, squares, squares_pair).start()
     for m in range(3):
-        swap(8 + m, out.at[m], both.at[c, m]).wait()
+        share(m).wait()
     swap(11, squares, squares_pair).wait()
     norm = jnp.sqrt(squares[...] + squares_pair[...] + table_squares[...])
     norm_out[...] = norm
@@ -1035,9 +1078,9 @@
     line = n // 4
     grad = hbm_args[1]
     rows, cols = grad.shape[-2:]
-    two, own, width = vmem_args[4].shape
-    all_rows = two * own
     heads = vmem_args[5].shape
+    own, width = vmem_args[10].shape
+    all_rows = 2 * own
     low, f32 = jnp.bfloat16, jnp.float32
     dma = pltpu.SemaphoreType.DMA
     vmem, hbm = pl.BlockSpec(memory_space=pltpu.VMEM), pl.BlockSpec(memory_space=pltpu.HBM)
@@ -1045,7 +1088,6 @@
     return pl.pallas_call(
         functools.partial(backward_kernel, line),
         out_shape=[
-            jax.ShapeDtypeStruct(grad.shape, low),
             jax.ShapeDtypeStruct(grad.shape, low),
             jax.ShapeDtypeStruct((2, n, 3 * width), f32),
             jax.ShapeDtypeStruct((n, n, 128), f32),
@@ -1057,7 +1099,7 @@
             jax.ShapeDtypeStruct((8, 128), f32),
         ],
         in_specs=[hbm] * len(hbm_args) + [vmem] * len(vmem_args),
-        out_specs=[hbm] * 4 + [vmem] * 6,
+        out_specs=[hbm] * 3 + [vmem] * 6,
         scratch_shapes=[
             pltpu.VMEM((width, cols), low),
             pltpu.VMEM((2 * all_rows, cols), low),
@@ -1082,7 +1124,7 @@
             pltpu.VMEM((n, 128), f32),
             pltpu.VMEM((n, 128), f32),
             pltpu.VMEM((n, per, 1, 128), f32),
-            pltpu.VMEM((3, rows, cols), low),
+            pltpu.VMEM((2, rows, cols), low),
             pltpu.VMEM((2, 8, 128), f32),
             pltpu.VMEM((n, 128), f32),
             pltpu.VMEM((8, 128), f32),
@@ -1090,14 +1132,14 @@
             pltpu.VMEM((8, 128), f32),
             pltpu.VMEM((8, 128), f32),
             pltpu.VMEM((min(n, 16), n, 128), f32),
-            dma((4,)),
+            dma((3,)),
             dma((3,)),
             dma((2,)),
             dma((12,)),
             dma((12,)),
         ]
         + [dma((n,))] * 10
-        + reducer_scratch(3, line, rows, low),
+        + reducer_scratch(2, line, rows, low),
         compiler_params=pltpu.CompilerParams(
             collective_id=collective_id, has_side_effects=True, vmem_limit_bytes=63 * 2**20),
         name="backward",
@@ -1259,7 +1301,7 @@
     cells = jnp.stack([place // SIDE, place % SIDE], axis=1).astype(jnp.float32)
     quarter = width // 4
     freqs = 10000.0 ** (-jnp.arange(quarter).astype(jnp.float32) / quarter)
-    (weights, grad_contract, normed_in, normed_mid, queries, keys, values, mixed, attended, middle, activated, slope, d_branch,
+    (weights, _, grad_expand, _, normed_in, queries, keys, values, mixed, attended, middle, activated, d_hidden, sums, contract_sum,
      pieces, cond_own, silu_own, own_modulation, inputs, key_ok, row_ok, onehot, same, biases) = forward(
         [
             item.reshape(-1, 128)
@@ -1285,14 +1327,14 @@
         n,
         1,
     )
-    _, _, d_mod_all, cond_all, reduced, block_out, tokens_grad, bias_parts, norm, clip = backward(
-        [weights.reshape(3, width, 4 * half_width), grad_contract],
+    _, d_mod_all, cond_all, reduced, block_out, tokens_grad, bias_parts, norm, clip = backward(
+        [weights.reshape(3, width, 4 * half_width), grad_expand],
         [
             normed_in,
-            normed_mid,
             activated,
-            slope,
-            d_branch,
+            d_hidden,
+            sums,
+            contract_sum,
             queries,
             keys,
             values,

time: 333 us -> 320 us (0.961)
  Pallas kernels: 315 us -> 303 us
    pallas_call x1, Pallas kernels: 167 us -> 110 us  [backward(): pl.pallas_call(functools.partial(backward_kernel, line), out_shape=[jax.S...]
    pallas_call x1, Pallas kernels: 133 us -> 178 us  [forward(): pl.pallas_call(functools.partial(forward_kernel, line), out_shape=[shape(...]
where the time goes in v7:
time: 320 us; the launch traced here: 317 us
  Pallas kernels  303 us (95%)
  local copies, waits for them, and re-layouts  7.88 us (2%)
  other arithmetic  4.38 us (1%)
    pallas_call x1, Pallas kernels, forward(): pl.pallas_call(functools.partial(forward_kernel, line), out_shape=[shape(...  178 us
    pallas_call x1, Pallas kernels, backward(): pl.pallas_call(functools.partial(backward_kernel, line), out_shape=[jax.S...  110 us
    pallas_call x1, Pallas kernels, adam(): pl.pallas_call(functools.partial(adam_kernel, n, rates), out_shape=[f for...  14.8 us

profile of v7, /device:TPU:12, one launch (start us, length us, event | category | flops | bytes accessed | tf_op | source)
XLA Modules:
  0.0 317.0 jit_solution(12378895729668633498)
XLA Ops:
  0.7 0.7 and_select_fusion.1
  1.3 0.7 copy.62.refs_9_
  2.1 0.7 convert_element_type.25
  3.4 0.6 concatenate.6.refs_6_
  4.0 0.6 multiply_power_fusion.refs_10_
  5.3 178.0 %forward.1 = (bf16[3,4,2,2,72,2304]{5,4,3,2,1,0:T(8,128)(2,1)}, bf16[4,2,2,72,2304]{4,3,2,1,0:T(8,128)(2,1)}, bf16[4,2,2,72,2304]{4,3,2,1,0:T(8,128)(2,1)}, f32[...) custom-call(f32[1944,128]{1,0:T(8,128)} %bitcast.72, ...), custom_call_target="tpu_custom_call" | custom-call | tf_op jit(solution)/shard_map/forward/pallas_call | solution.py:547
  183.3 1.3 slice.30.refs_18_
  184.6 109.8 %backward.1 = (bf16[4,2,2,72,2304]{4,3,2,1,0:T(8,128)(2,1)}, f32[2,16,3456]{2,1,0:T(8,128)}, f32[16,16,128]{2,1,0:T(8,128)}, bf16[2,3,72,2304]{3,2,1,0:T(8,128)(...) custom-call(bf16[3,1152,2304]{2,1,0:T(8,128)(2,1)} %bitcast.65, ...), custom_call_target="tpu_custom_call" | custom-call | tf_op jit(solution)/shard_map/backward/pallas_call | solution.py:1088
  294.4 0.0 copy-start.2
  294.4 0.0 copy-start.3
  294.4 0.0 copy-start.4
  294.4 0.9 slice_bitcast_fusion
  295.5 0.1 slice_reduce_fusion
  295.6 0.1 reshape_squeeze.6
  295.7 1.1 reduce_sum.9
  296.8 0.1 reshape_squeeze.7
  297.0 1.2 slice.39
  298.2 0.0 copy-done.2
  298.2 0.0 copy-done.3
  298.2 0.0 copy-done.4
  298.2 1.3 multiply_subtract_fusion
  299.6 0.0 copy-start.1
  299.6 0.0 copy-start
  299.6 14.8 %adam.1 = (f32[3888,128]{1,0:T(8,128)}, f32[3888,128]{1,0:T(8,128)}, f32[3888,128]{1,0:T(8,128)}, f32[1944,128]{1,0:T(8,128)}, f32[1944,128]{1,0:T(8,128)}, /*in...) custom-call(f32[8,128]{1,0:T(8,128)} %get-tuple-element.98.refs_0_, ...), custom_call_target="tpu_custom_call" | custom-call | tf_op jit(solution)/shard_map/adam/pallas_call | solution.py:1247
  314.4 1.2 slice.31
  315.6 0.0 copy-done.1
  315.6 0.7 copy.74
  316.3 0.0 copy-done
  316.3 0.7 copy.75
  (17 shorter events, 0.2 us)
Async XLA Ops:
  294.4 3.8 %copy-start.2 = (f32[1008]{0:T(1024)S(1)}, f32[1008]{0:T(1024)}, u32[]{:S(2)}) copy-start(f32[1008]{0:T(1024)} %param.51) | copy-start | bytes 12100
  294.4 3.8 %copy-start.3 = (f32[1008]{0:T(1024)S(1)}, f32[1008]{0:T(1024)}, u32[]{:S(2)}) copy-start(f32[1008]{0:T(1024)} %param.53) | copy-start | bytes 12100
  294.4 3.8 %copy-start.4 = (f32[1008]{0:T(1024)S(1)}, f32[1008]{0:T(1024)}, u32[]{:S(2)}) copy-start(f32[1008]{0:T(1024)} %param.52) | copy-start | bytes 12100
  299.6 16.0 %copy-start.1 = (bf16[128,1152]{1,0:T(8,128)(2,1)S(1)}, bf16[128,1152]{1,0:T(8,128)(2,1)}, u32[]{:S(2)}) copy-start(bf16[128,1152]{1,0:T(8,128)(2,1)} %get-tuple-element.95) | copy-start | bytes 884740
  299.6 16.7 %copy-start = (bf16[128,1152]{1,0:T(8,128)(2,1)S(1)}, bf16[128,1152]{1,0:T(8,128)(2,1)}, u32[]{:S(2)}) copy-start(bf16[128,1152]{1,0:T(8,128)(2,1)} %get-tuple-element.96) | copy-start | bytes 884740

commit v8 on v7

--- a/solution.py
+++ b/solution.py
@@ -4,6 +4,7 @@
 from jax import lax
 from jax.experimental import pallas as pl
 from jax.experimental.pallas import tpu as pltpu
+import numpy as np
 from jax.sharding import PartitionSpec as P
 
 HEAD_DIM = 72
@@ -252,17 +253,17 @@
 
 
 def forward_kernel(line, *refs):
-    (m_in, m_out, m_expand, m_contract, m_table, m_mod, block, time_vec, tokens, cells, freqs, kept, cot) = refs[:13]
+    (m_in, m_out, m_expand, m_contract, m_table, m_mod, own_bias, meta, time_vec, tokens, cells, freqs, cot) = refs[:13]
     (weights, g_contract, g_expand, cond_got, h1_t, q, k, v, o, attended, middle, act, d_z, sums, out, pieces, cond, silu,
      mod_half, x, key_ok, row_ok, onehot, same, biases) = refs[13:38]
     (f_in, f_out, f_expand, f_contract, f_table, f_mod, own, table, cond_part, cond_some, mods, mod_part, mod_got, blocks, w,
-     proj, mix, wide, partial, partial_got, h1, h2, h2_t, slope, d_branch, d_branch_t, stage, block_got, wide_bias, in_sem,
-     w_sem, pair_send, pair_recv, peer_send, block_recv, cond_recv, mod_recv, keep_sem, stage_sem, cond_sem) = refs[38:78]
+     proj, mix, wide, partial, partial_got, h1, h2, h2_t, slope, d_branch, d_branch_t, stage, block, block_got, wide_bias, in_sem,
+     w_sem, pair_send, pair_recv, peer_send, block_recv, cond_recv, mod_recv, keep_sem, stage_sem, cond_sem) = refs[38:79]
     n = line * 4
     low, f32 = jnp.bfloat16, jnp.float32
     me, c = lax.axis_index("dp"), lax.axis_index("seq")
-    gat = Gatherer(line, own, weights, keep_sem, refs[78:84])
-    red = make_reducer(line, (g_contract,), out, refs[84:])
+    gat = Gatherer(line, own, weights, keep_sem, refs[79:85])
+    red = make_reducer(line, (g_contract,), out, refs[85:])
     rows, width = x.shape
     own_rows, half = own.shape[1], own.shape[2] // 4
     edge = 3 * half // 128 * 128
@@ -296,6 +297,11 @@
     block_start, block_wait = all_peers(n, block, block_got, peer_send, block_recv, False)
     cond_start, cond_wait = all_peers(n, cond_part, cond_got, peer_send, cond_recv, True)
     mod_start, mod_wait = all_peers(n, mod_part, mod_got, peer_send, mod_recv, True)
+    share = own_bias.shape[1]
+    for r in range(-(-share // 128)):
+        size = min(128, share - 128 * r)
+        block[r : r + 1, :size] = own_bias[:, 128 * r : 128 * r + size].astype(low).astype(f32)
+    block[8:] = jnp.broadcast_to(meta[:, :1].astype(f32), (8, 128))
     block_got[me] = block[...]
     load(0).wait()
     load(1).wait()
@@ -337,7 +343,6 @@
     cut(f_expand, own.at[1], 4 * half // 128)
     gat.begin(1)
 
-    share = biases.shape[1] // n
     for i in range(n):
         for r in range(-(-share // 128)):
             size = min(128, share - 128 * r)
@@ -349,20 +354,24 @@
     def bias_half(start, size):
         return jnp.where(c == 0, bias(start, size // 2), bias(start + size // 2, size // 2))
 
-    half_kept = jnp.floor(kept[...] * 0.5)
+    half_kept = jnp.floor(meta[:, 1:2].astype(f32) * 0.5)
     rows_at = lax.broadcasted_iota(jnp.int32, (rows, 1), 0).astype(f32)
     row_ok[...] = (rows_at < half_kept).astype(f32)
     lanes_at = lax.broadcasted_iota(jnp.int32, (1, 2 * rows), 1)
     lanes_at = jnp.where(lanes_at < rows, lanes_at, lanes_at - rows).astype(f32)
     key_ok[...] = (lanes_at < half_kept).astype(f32)
     quarter = width // 4
-    for i, place in enumerate((cells[:, :1], cells[:, 1:2])):
+    at = lax.broadcasted_iota(jnp.int32, (rows, rows), 0) == lax.broadcasted_iota(jnp.int32, (rows, rows), 1)
+    cell = jnp.broadcast_to(cells[...].astype(f32), (rows, rows))
+    cell = jnp.sum(jnp.where(at, cell, 0.0), axis=1, keepdims=True)
+    across = jnp.floor(cell * (1.0 / SIDE))
+    for i, place in enumerate((across, cell - SIDE * across)):
         angle = place * freqs[...]
         for j, wave in enumerate((jnp.sin(angle), jnp.cos(angle))):
             cols = slice((2 * i + j) * quarter, (2 * i + j + 1) * quarter)
             x[:, cols] = tokens[:, cols].astype(f32) + wave
 
-    gat.steps(0, 1, 1)
+    gat.steps(0, 1, 2)
     cond_wait()
     keep_cond.wait()
     cond[...] = jnp.zeros_like(cond)
@@ -385,22 +394,22 @@
 
     mod_got[me] = mod_part[me]
     mod_start()
-    gat.steps(0, 2, 2)
     gat.paired(1)
     gat.steps(0, 3, line)
     gat.steps(1, 1, 1)
+    gat.steps(1, 2, 2)
+    def fetch(m):
+        return pltpu.make_async_copy(weights.at[m], blocks, w_sem.at[m])
+
+    def unpack():
+        for i in range(n):
+            w[i * own_rows : (i + 1) * own_rows, :] = blocks[i // 4, i // 2 % 2, i % 2]
+
+    gat.complete(0)
+    fetch(0).start()
     mod_wait()
     pieces[c] = jnp.sum(mod_got[...], axis=0) + bias_half(0, 6 * width)
     swap(0, pieces.at[c], pieces.at[c]).start()
-    def fetch(m):
-        return pltpu.make_async_copy(weights.at[m], blocks, w_sem.at[m])
-
-    def unpack():
-        for i in range(n):
-            w[i * own_rows : (i + 1) * own_rows, :] = blocks[i // 4, i // 2 % 2, i % 2]
-
-    gat.complete(0)
-    fetch(0).start()
     swap(0, pieces.at[c], pieces.at[c]).wait()
     shift, scale, gate = (pieces[0, :, i * width : (i + 1) * width] for i in range(3))
     h1[c] = (normal(x[...]) * (1.0 + scale) + shift).astype(low)
@@ -412,6 +421,7 @@
     swap(1, h1.at[c], h1.at[c]).wait()
     both = jnp.concatenate([h1[0], h1[1]], axis=0)
     to_blocks(both, h1_t)
+    gat.paired(2)
 
     @pl.loop(0, proj.shape[1] // 256)
     def _(t):
@@ -438,9 +448,8 @@
     @pl.loop(0, heads)
     def _(t):
         head(t)
-        when(t == 1, lambda: gat.steps(1, 2, 2))
-        when(t == 3, lambda: gat.paired(2))
-        when(t == heads - 1, lambda: gat.steps(1, 3, 3))
+        when(t == 0, lambda: gat.steps(1, 3, 3))
+        when(t == heads - 1, lambda: gat.steps(1, 4, line))
 
     o[...] = mix[...].astype(low)
     wide[:, : 3 * half - edge] = jnp.zeros((2 * rows, 3 * half - edge), low)
@@ -454,7 +463,7 @@
         partial[1, :, cols] = part[rows:]
 
     swap(2, partial.at[1 - c], partial_got).start()
-    gat.steps(1, 4, line)
+    gat.steps(2, 1, 1)
     swap(2, partial.at[1 - c], partial_got).wait()
     attended[...] = partial[c] + partial_got[...] + bias(8 * width, width)
     middle[...] = x[...] + gate * attended[...]
@@ -463,7 +472,6 @@
     swap(3, h2.at[c], h2.at[c]).start()
     gat.complete(1)
     fetch(1).start()
-    gat.steps(2, 1, 1)
     swap(4, d_branch.at[c], d_branch.at[c]).wait()
     to_blocks(jnp.concatenate([d_branch[0], d_branch[1]], axis=0), d_branch_t)
     swap(3, h2.at[c], h2.at[c]).wait()
@@ -484,7 +492,7 @@
         slope[:, cols] = 0.5 * (1.0 + bend) + 0.5 * z * (1.0 - bend * bend) * (GELU_A * (1.0 + 3.0 * GELU_B * z * z))
 
     def contract_block(i):
-        when(i == n // 4, lambda: gat.steps(2, 3, 3))
+        when(i == 0, lambda: gat.steps(2, 3, 3))
         when(i == n // 2, lambda: gat.steps(2, 4, line))
         return dot(d_branch_t[i], act[...])
 
@@ -528,7 +536,7 @@
 
 def forward(hbm_args, vmem_args, bias_size, n, collective_id):
     line = n // 4
-    block, time_vec, tokens = vmem_args[:3]
+    tokens = vmem_args[3]
     rows, width = tokens.shape
     class_rows = hbm_args[4].size // width
     own_rows, half = width // n, width // 2
@@ -598,7 +606,8 @@
             scratch((2, rows, width), low),
             scratch((n, own_rows, 2 * rows), low),
             scratch((2, own_rows, 4 * half), low),
-            scratch((n,) + block.shape, f32),
+            scratch((16, 128), f32),
+            scratch((n, 16, 128), f32),
             scratch((1, 4 * half), f32),
             dma((6,)),
             dma((3,)),
@@ -802,16 +811,17 @@
 
 def backward_kernel(line, *refs):
     (weights, g_expand, h1_t, act, d_z, sums, out_contract, q, k, v, o, key_ok, x, middle, attended, cot, row_ok, pieces,
-     b_contract, modulation, cond, silu, same) = refs[:23]
-    (g_attn, d_mod_all, cond_all, both, block_out, tokens_grad, bias_all, norm_out, factor_out) = refs[23:32]
+     biases, modulation, cond, silu, same) = refs[:23]
+    (g_attn, d_mod_all, cond_all, both, block_out, tokens_grad, bias_grad, norm_out, factor_out) = refs[23:32]
     (w, rhs, d_o, d_q, d_k, d_v, d_h, d_h_got, branch_got, d_mid, d_att, d_att_t, stage, dp, dp_got, msg, msg_got, d_mod, vec,
-     vec_got, d_silu, d_silu_got, chunk, out, bias_sum, d_cond, squares, squares_got, table_squares, squares_pair, cond_some, w_sem,
+     vec_got, d_silu, d_silu_got, chunk, out, bias_sum, d_cond, squares, squares_got, table_squares, squares_pair, cond_some, bias_all,
+     mod_sums, vec_all, w_sem,
      mod_sem, stage_sem, pair_send, pair_recv, msg_send, msg_recv, vec_send, vec_recv, cond_send, cond_recv, bias_send, bias_recv, square_send,
-     square_recv) = refs[32:78]
+     square_recv) = refs[32:81]
     n = line * 4
     low, f32 = jnp.bfloat16, jnp.float32
     me, c = lax.axis_index("dp"), lax.axis_index("seq")
-    red = make_reducer(line, (g_expand, g_attn), out, refs[78:])
+    red = make_reducer(line, (g_expand, g_attn), out, refs[81:])
     rows, width = x.shape
     half = weights.shape[2] // 4
     heads = half // HEAD_DIM
@@ -928,7 +938,7 @@
 
     def branch_out():
         swap(3, d_h.at[1 - c], branch_got).wait()
-        branch = d_h[c] + branch_got[...] + b_contract[...]
+        branch = d_h[c] + branch_got[...] + biases[:, 9 * width + 8 * half :]
         result = middle[...] + piece(5) * branch
         block_out[...] = jnp.where(jnp.broadcast_to(row_ok[...], result.shape) > 0.0, result, 0.0).astype(low)
         dp[5:6] = jnp.sum(cot[...].astype(f32) * row_ok[...] * branch, axis=0, keepdims=True)
@@ -991,6 +1001,8 @@
         d_low = d_mod[...].astype(low)
         grad = dot(silu[...], d_low, 0, 0)[: out.shape[1]]
         sums = jnp.sum(d_mod[...], axis=0, keepdims=True)
+        mod_sums[c] = sums
+        swap(12, mod_sums.at[c], mod_sums.at[c]).start()
         tile = per * me + lax.broadcasted_iota(jnp.int32, (8, 128), 0)
         counted = (tile < 3 * tiles) | (c == 0)
         total = jnp.sum(grad * grad) + jnp.where(me == 0, jnp.sum(sums * sums), 0.0)
@@ -1001,6 +1013,18 @@
         cond_wait()
         bias_wait()
         keep_cond.wait()
+        swap(12, mod_sums.at[c], mod_sums.at[c]).wait()
+        for core in range(2):
+            bias_grad[:, 3 * core * width : 3 * (core + 1) * width] = mod_sums[core]
+            for t in range(5 * tiles):
+                vec_all[core, :, 128 * t : 128 * t + 128] = bias_all[t // per, core, t % per : t % per + 1]
+            start = 6 * width + core * half
+            bias_grad[:, start : start + half] = vec_all[core, :, :half]
+            bias_grad[:, start + width : start + width + half] = vec_all[core, :, half:width]
+            start = 9 * width + core * 4 * half
+            bias_grad[:, start : start + 4 * half] = vec_all[core, :, width : 3 * width]
+        bias_grad[:, 8 * width : 9 * width] = vec_all[0, :, 3 * width : 4 * width]
+        bias_grad[:, 9 * width + 8 * half :] = vec_all[0, :, 4 * width :]
         table_squares[...] = jnp.zeros((8, 128), f32)
         size = cond_some.shape[0]
 
@@ -1066,7 +1090,7 @@
         share(m).wait()
     swap(11, squares, squares_pair).wait()
     norm = jnp.sqrt(squares[...] + squares_pair[...] + table_squares[...])
-    norm_out[...] = norm
+    norm_out[...] = norm[:1, :1]
     factor_out[...] = jnp.minimum(1.0, CLIP_LIMIT / (norm + 1e-06))
 
 
@@ -1094,8 +1118,8 @@
             jax.ShapeDtypeStruct((2, 3, rows, cols), low),
             jax.ShapeDtypeStruct((own, width), low),
             jax.ShapeDtypeStruct((own, width), low),
-            jax.ShapeDtypeStruct((n, 2, 8, 128), f32),
-            jax.ShapeDtypeStruct((8, 128), f32),
+            jax.ShapeDtypeStruct(vmem_args[16].shape, f32),
+            jax.ShapeDtypeStruct((1, 1), f32),
             jax.ShapeDtypeStruct((8, 128), f32),
         ],
         in_specs=[hbm] * len(hbm_args) + [vmem] * len(vmem_args),
@@ -1132,11 +1156,14 @@
             pltpu.VMEM((8, 128), f32),
             pltpu.VMEM((8, 128), f32),
             pltpu.VMEM((min(n, 16), n, 128), f32),
+            pltpu.VMEM((n, 2, 8, 128), f32),
+            pltpu.VMEM((2, 1, 3 * width), f32),
+            pltpu.VMEM((2, 1, 5 * width), f32),
             dma((3,)),
             dma((3,)),
             dma((2,)),
-            dma((12,)),
-            dma((12,)),
+            dma((13,)),
+            dma((13,)),
         ]
         + [dma((n,))] * 10
         + reducer_scratch(2, line, rows, low),
@@ -1295,12 +1322,8 @@
     low = jnp.bfloat16
 
     bias_share = biases_master.shape[0]
-    bias_block = jnp.pad(biases_master.astype(low).astype(jnp.float32), (0, 1024 - bias_share)).reshape(8, 128)
-    label_block = jnp.broadcast_to(labels.astype(jnp.float32)[:, None], (8, 128))
-    place = keep_index[0]
-    cells = jnp.stack([place // SIDE, place % SIDE], axis=1).astype(jnp.float32)
     quarter = width // 4
-    freqs = 10000.0 ** (-jnp.arange(quarter).astype(jnp.float32) / quarter)
+    freqs = np.float32(10000.0) ** (-np.arange(quarter, dtype=np.float32) / np.float32(quarter))
     (weights, _, grad_expand, _, normed_in, queries, keys, values, mixed, attended, middle, activated, d_hidden, sums, contract_sum,
      pieces, cond_own, silu_own, own_modulation, inputs, key_ok, row_ok, onehot, same, biases) = forward(
         [
@@ -1315,19 +1338,19 @@
             )
         ],
         [
-            jnp.concatenate([bias_block, label_block]),
+            biases_master[None],
+            jnp.stack([labels, kept], axis=1),
             time_vec,
             tokens[0],
-            cells,
-            freqs[None],
-            kept.astype(jnp.float32)[None],
+            keep_index,
+            jnp.asarray(freqs)[None],
             cotangent[0],
         ],
         bias_share * n,
         n,
         1,
     )
-    _, d_mod_all, cond_all, reduced, block_out, tokens_grad, bias_parts, norm, clip = backward(
+    _, d_mod_all, cond_all, reduced, block_out, tokens_grad, grad_biases, norm, clip = backward(
         [weights.reshape(3, width, 4 * half_width), grad_expand],
         [
             normed_in,
@@ -1346,7 +1369,7 @@
             cotangent[0],
             row_ok,
             pieces,
-            biases[:, 9 * width + FF :],
+            biases,
             own_modulation,
             cond_own,
             silu_own,
@@ -1355,7 +1378,7 @@
         n,
         2,
     )
-    block_out, tokens_grad, grad_norm = block_out[None], tokens_grad[None], norm[0, 0]
+    block_out, tokens_grad, grad_norm = block_out[None], tokens_grad[None], norm.reshape(())
     rates = (
         width ** (-0.5),
         width ** (-0.5),
@@ -1404,19 +1427,7 @@
         rates[:-1],
         n,
     )
-    bias_parts = bias_parts.reshape(n, pairs, 8, 128)[:, :, : chunk_tiles(n, width)].transpose(1, 0, 2, 3)
-    bias_parts = bias_parts.reshape(pairs, -1)[:, : 5 * width].reshape(pairs, 5, width)
-    grad_biases = jnp.concatenate(
-        [
-            jnp.sum(d_mod_all, axis=1).reshape(-1),
-            bias_parts[:, 0, :half_width].reshape(-1),
-            bias_parts[:, 0, half_width:].reshape(-1),
-            bias_parts[0, 3],
-            bias_parts[:, 1:3].reshape(-1),
-            bias_parts[0, 4],
-        ]
-    )
-    bias_grad = lax.dynamic_slice_in_dim(grad_biases, me * bias_share, bias_share, 0) * clip[0, 0]
+    bias_grad = lax.dynamic_slice_in_dim(grad_biases[0], me * bias_share, bias_share, 0) * clip.reshape(-1)[:bias_share]
     updated = [item.reshape(-1) for item in updated] + list(adam_step(bias_grad, *states[-1], rates[-1]))
     return (block_out, tokens_grad, grad_norm) + tuple(updated)
 

time: 320 us -> 312 us (0.975)
  local copies, waits for them, and re-layouts: 7.88 us -> 2.23 us
    slice x7 -> x0, local copies, waits for them, and re-layouts: 3.82 us -> none  [the longest x1 1.28 us: per_device(): biases[:, 9 * width + FF:]]
where the time goes in v8:
time: 312 us; the launch traced here: 308 us
  Pallas kernels  300 us (96%)
  between operations  3.78 us (1%)
    pallas_call x1, Pallas kernels, forward(): pl.pallas_call(functools.partial(forward_kernel, line), out_shape=[shape(...  176 us
    pallas_call x1, Pallas kernels, backward(): pl.pallas_call(functools.partial(backward_kernel, line), out_shape=[jax.S...  110 us
    pallas_call x1, Pallas kernels, adam(): pl.pallas_call(functools.partial(adam_kernel, n, rates), out_shape=[f for...  14.8 us

profile of v8, /device:TPU:12, one launch (start us, length us, event | category | flops | bytes accessed | tf_op | source)
XLA Modules:
  0.0 308.1 jit_solution(15401864447606205640)
XLA Ops:
  1.9 0.6 pad_add_fusion.refs_7_
  2.5 175.9 %forward.1 = (bf16[3,4,2,2,72,2304]{5,4,3,2,1,0:T(8,128)(2,1)}, bf16[4,2,2,72,2304]{4,3,2,1,0:T(8,128)(2,1)}, bf16[4,2,2,72,2304]{4,3,2,1,0:T(8,128)(2,1)}, f32[...) custom-call(f32[1944,128]{1,0:T(8,128)} %bitcast.56, ...), custom_call_target="tpu_custom_call" | custom-call | tf_op jit(solution)/shard_map/forward/pallas_call | solution.py:555
  178.4 0.0 copy-start.2
  178.5 0.0 copy-start.3
  178.5 0.0 copy-start.4
  178.5 109.5 %backward.1 = (bf16[4,2,2,72,2304]{4,3,2,1,0:T(8,128)(2,1)}, f32[2,16,3456]{2,1,0:T(8,128)}, f32[16,16,128]{2,1,0:T(8,128)}, bf16[2,3,72,2304]{3,2,1,0:T(8,128)(...) custom-call(bf16[3,1152,2304]{2,1,0:T(8,128)(2,1)} %bitcast.49, ...), custom_call_target="tpu_custom_call" | custom-call | tf_op jit(solution)/shard_map/backward/pallas_call | solution.py:1112
  288.0 0.8 constant_dynamic-slice_fusion
  288.8 0.0 copy-done.2
  288.8 0.0 copy-done.3
  288.8 0.0 copy-done.4
  288.8 1.3 multiply_subtract_fusion
  290.1 0.0 copy-start.1
  290.1 0.0 copy-start
  290.1 14.8 %adam.1 = (f32[3888,128]{1,0:T(8,128)}, f32[3888,128]{1,0:T(8,128)}, f32[3888,128]{1,0:T(8,128)}, f32[1944,128]{1,0:T(8,128)}, f32[1944,128]{1,0:T(8,128)}, /*in...) custom-call(f32[8,128]{1,0:T(8,128)} %get-tuple-element.98.refs_0_, ...), custom_call_target="tpu_custom_call" | custom-call | tf_op jit(solution)/shard_map/adam/pallas_call | solution.py:1274
  304.9 0.0 copy-done.1
  305.0 0.7 copy.57
  305.7 0.0 copy-done
  305.7 0.7 copy.58
Async XLA Ops:
  178.4 110.3 %copy-start.2 = (f32[1008]{0:T(1024)S(1)}, f32[1008]{0:T(1024)}, u32[]{:S(2)}) copy-start(f32[1008]{0:T(1024)} %param.52) | copy-start | bytes 12100
  178.5 110.3 %copy-start.3 = (f32[1008]{0:T(1024)S(1)}, f32[1008]{0:T(1024)}, u32[]{:S(2)}) copy-start(f32[1008]{0:T(1024)} %param.54) | copy-start | bytes 12100
  178.5 110.3 %copy-start.4 = (f32[1008]{0:T(1024)S(1)}, f32[1008]{0:T(1024)}, u32[]{:S(2)}) copy-start(f32[1008]{0:T(1024)} %param.53) | copy-start | bytes 12100
  290.1 14.8 %copy-start.1 = (bf16[128,1152]{1,0:T(8,128)(2,1)S(1)}, bf16[128,1152]{1,0:T(8,128)(2,1)}, u32[]{:S(2)}) copy-start(bf16[128,1152]{1,0:T(8,128)(2,1)} %get-tuple-element.95) | copy-start | bytes 884740
  290.1 15.6 %copy-start = (bf16[128,1152]{1,0:T(8,128)(2,1)S(1)}, bf16[128,1152]{1,0:T(8,128)(2,1)}, u32[]{:S(2)}) copy-start(bf16[128,1152]{1,0:T(8,128)(2,1)} %get-tuple-element.96) | copy-start | bytes 884740

commit v9 on v8

--- a/solution.py
+++ b/solution.py
@@ -23,7 +23,7 @@
 MESH = pl.DeviceIdType.MESH
 GELU_A = (2.0 / 3.141592653589793) ** 0.5
 GELU_B = 0.044715
-UNIT_PLACES = ((0, 0, 2, 10, 12, 13, 13, 15), (1, 3, 11, 12, 13, 14, 15, 18))
+UNIT_PLACES = ((0, 0, 2, 10, 12, 13, 14, 15), (1, 3, 11, 12, 14, 15, 16, 18))
 GROUPS = ((0, 640, 0, "x"), (640, 640, 0, "y"), (1280, 512, 1, "x"), (1792, 512, 1, "y"))
 
 
@@ -974,9 +974,8 @@
             for r in range(3):
                 d_mod[pl.ds(s, 1), r * width : (r + 1) * width] = msg_got[s, r]
 
-        bias_sum[c] = jnp.zeros((8, 128), f32)
         for r in range(per):
-            bias_sum[c, r : r + 1] = jnp.sum(vec_got[:, r], axis=0)
+            bias_sum[c, r] = jnp.sum(vec_got[:, r], axis=0)
         d_silu[...] = dot(d_mod[...].astype(low), modulation[...], 1, 1)
         swap(5, d_silu, d_silu_got).start()
         swap(6, d_mod, d_mod_all.at[c]).start()
@@ -1003,11 +1002,11 @@
         sums = jnp.sum(d_mod[...], axis=0, keepdims=True)
         mod_sums[c] = sums
         swap(12, mod_sums.at[c], mod_sums.at[c]).start()
-        tile = per * me + lax.broadcasted_iota(jnp.int32, (8, 128), 0)
-        counted = (tile < 3 * tiles) | (c == 0)
+        counted = [(per * me + r < 3 * tiles) | (c == 0) for r in range(per)]
         total = jnp.sum(grad * grad) + jnp.where(me == 0, jnp.sum(sums * sums), 0.0)
-        total = total + jnp.sum(jnp.where(counted, bias_sum[c] * bias_sum[c], 0.0))
-        squares[...] = jnp.full((8, 128), total, f32)
+        for r in range(per):
+            total = total + jnp.where(counted[r], jnp.sum(bias_sum[c, r] * bias_sum[c, r]), 0.0)
+        squares[...] = jnp.full((1, 128), total, f32)
 
     def table_norm():
         cond_wait()
@@ -1017,7 +1016,7 @@
         for core in range(2):
             bias_grad[:, 3 * core * width : 3 * (core + 1) * width] = mod_sums[core]
             for t in range(5 * tiles):
-                vec_all[core, :, 128 * t : 128 * t + 128] = bias_all[t // per, core, t % per : t % per + 1]
+                vec_all[core, :, 128 * t : 128 * t + 128] = bias_all[t // per, core, t % per]
             start = 6 * width + core * half
             bias_grad[:, start : start + half] = vec_all[core, :, :half]
             bias_grad[:, start + width : start + width + half] = vec_all[core, :, half:width]
@@ -1025,7 +1024,7 @@
             bias_grad[:, start : start + 4 * half] = vec_all[core, :, width : 3 * width]
         bias_grad[:, 8 * width : 9 * width] = vec_all[0, :, 3 * width : 4 * width]
         bias_grad[:, 9 * width + 8 * half :] = vec_all[0, :, 4 * width :]
-        table_squares[...] = jnp.zeros((8, 128), f32)
+        table_squares[...] = jnp.zeros((1, 128), f32)
         size = cond_some.shape[0]
 
         @pl.loop(0, n // size)
@@ -1090,8 +1089,8 @@
         share(m).wait()
     swap(11, squares, squares_pair).wait()
     norm = jnp.sqrt(squares[...] + squares_pair[...] + table_squares[...])
-    norm_out[...] = norm[:1, :1]
-    factor_out[...] = jnp.minimum(1.0, CLIP_LIMIT / (norm + 1e-06))
+    norm_out[...] = norm[:, :1]
+    factor_out[...] = jnp.broadcast_to(jnp.minimum(1.0, CLIP_LIMIT / (norm + 1e-06)), (8, 128))
 
 
 def chunk_tiles(n, width):
@@ -1149,14 +1148,14 @@
             pltpu.VMEM((n, 128), f32),
             pltpu.VMEM((n, per, 1, 128), f32),
             pltpu.VMEM((2, rows, cols), low),
-            pltpu.VMEM((2, 8, 128), f32),
+            pltpu.VMEM((2, per, 1, 128), f32),
             pltpu.VMEM((n, 128), f32),
-            pltpu.VMEM((8, 128), f32),
-            pltpu.VMEM((n, 8, 128), f32),
-            pltpu.VMEM((8, 128), f32),
-            pltpu.VMEM((8, 128), f32),
+            pltpu.VMEM((1, 128), f32),
+            pltpu.VMEM((n, 1, 128), f32),
+            pltpu.VMEM((1, 128), f32),
+            pltpu.VMEM((1, 128), f32),
             pltpu.VMEM((min(n, 16), n, 128), f32),
-            pltpu.VMEM((n, 2, 8, 128), f32),
+            pltpu.VMEM((n, 2, per, 1, 128), f32),
             pltpu.VMEM((2, 1, 3 * width), f32),
             pltpu.VMEM((2, 1, 5 * width), f32),
             dma((3,)),

time: 312 us -> 309 us (level)
  no operation moved by 1% of the time
where the time goes in v9:
time: 309 us; the launch traced here: 306 us
  Pallas kernels  298 us (96%)
  between operations  3.78 us (1%)
    pallas_call x1, Pallas kernels, forward(): pl.pallas_call(functools.partial(forward_kernel, line), out_shape=[shape(...  176 us
    pallas_call x1, Pallas kernels, backward(): pl.pallas_call(functools.partial(backward_kernel, line), out_shape=[jax.S...  108 us
    pallas_call x1, Pallas kernels, adam(): pl.pallas_call(functools.partial(adam_kernel, n, rates), out_shape=[f for...  14.8 us

profile of v9, /device:TPU:12, one launch (start us, length us, event | category | flops | bytes accessed | tf_op | source)
XLA Modules:
  0.0 306.3 jit_solution(17039713899909656213)
XLA Ops:
  1.9 0.6 pad_add_fusion.refs_7_
  2.5 175.9 %forward.1 = (bf16[3,4,2,2,72,2304]{5,4,3,2,1,0:T(8,128)(2,1)}, bf16[4,2,2,72,2304]{4,3,2,1,0:T(8,128)(2,1)}, bf16[4,2,2,72,2304]{4,3,2,1,0:T(8,128)(2,1)}, f32[...) custom-call(f32[1944,128]{1,0:T(8,128)} %bitcast.56, ...), custom_call_target="tpu_custom_call" | custom-call | tf_op jit(solution)/shard_map/forward/pallas_call | solution.py:555
  178.4 0.0 copy-start.2
  178.5 0.0 copy-start.3
  178.5 0.0 copy-start.4
  178.5 107.7 %backward.1 = (bf16[4,2,2,72,2304]{4,3,2,1,0:T(8,128)(2,1)}, f32[2,16,3456]{2,1,0:T(8,128)}, f32[16,16,128]{2,1,0:T(8,128)}, bf16[2,3,72,2304]{3,2,1,0:T(8,128)(...) custom-call(bf16[3,1152,2304]{2,1,0:T(8,128)(2,1)} %bitcast.49, ...), custom_call_target="tpu_custom_call" | custom-call | tf_op jit(solution)/shard_map/backward/pallas_call | solution.py:1111
  286.2 0.8 constant_dynamic-slice_fusion
  286.9 0.0 copy-done.2
  286.9 0.0 copy-done.3
  286.9 0.0 copy-done.4
  287.0 1.3 multiply_subtract_fusion
  288.3 0.0 copy-start.1
  288.3 0.0 copy-start
  288.3 14.8 %adam.1 = (f32[3888,128]{1,0:T(8,128)}, f32[3888,128]{1,0:T(8,128)}, f32[3888,128]{1,0:T(8,128)}, f32[1944,128]{1,0:T(8,128)}, f32[1944,128]{1,0:T(8,128)}, /*in...) custom-call(f32[8,128]{1,0:T(8,128)} %get-tuple-element.98.refs_0_, ...), custom_call_target="tpu_custom_call" | custom-call | tf_op jit(solution)/shard_map/adam/pallas_call | solution.py:1273
  303.1 0.0 copy-done.1
  303.1 0.7 copy.57
  303.8 0.0 copy-done
  303.8 0.7 copy.58
Async XLA Ops:
  178.4 108.5 %copy-start.2 = (f32[1008]{0:T(1024)S(1)}, f32[1008]{0:T(1024)}, u32[]{:S(2)}) copy-start(f32[1008]{0:T(1024)} %param.52) | copy-start | bytes 12100
  178.5 108.5 %copy-start.3 = (f32[1008]{0:T(1024)S(1)}, f32[1008]{0:T(1024)}, u32[]{:S(2)}) copy-start(f32[1008]{0:T(1024)} %param.54) | copy-start | bytes 12100
  178.5 108.5 %copy-start.4 = (f32[1008]{0:T(1024)S(1)}, f32[1008]{0:T(1024)}, u32[]{:S(2)}) copy-start(f32[1008]{0:T(1024)} %param.53) | copy-start | bytes 12100
  288.3 14.8 %copy-start.1 = (bf16[128,1152]{1,0:T(8,128)(2,1)S(1)}, bf16[128,1152]{1,0:T(8,128)(2,1)}, u32[]{:S(2)}) copy-start(bf16[128,1152]{1,0:T(8,128)(2,1)} %get-tuple-element.95) | copy-start | bytes 884740
  288.3 15.6 %copy-start = (bf16[128,1152]{1,0:T(8,128)(2,1)S(1)}, bf16[128,1152]{1,0:T(8,128)(2,1)}, u32[]{:S(2)}) copy-start(bf16[128,1152]{1,0:T(8,128)(2,1)} %get-tuple-element.96) | copy-start | bytes 884740
